TPU v7x, 512 devices: a whole 4x4x16 slice. The times are simulated.
512 devices in a mesh: dp: 32 (over y_lo, z), mp: 16 (over y_hi, x, core).
Axes of the slice: x: 4, y: 4 (y_hi: 2, y_lo: 2; y = y_hi * 2 + y_lo), z: 16, core: 2. Of those that a mesh axis runs over, the one named last changes fastest.
Arguments:
- queries_raw: bfloat16 [24576, 4096], P('dp', 'mp'), may hold values from -6 to 6
- keys_raw: bfloat16 [24576, 4096], P('dp', 'mp'), may hold values from -6 to 6
- values: bfloat16 [24576, 4096], P('dp', 'mp'), may hold values from -6 to 6
- grad_out: bfloat16 [24576, 6144], P('dp', 'mp'), may hold values from -16 to 16
- out_weight: bfloat16 [6144, 4096], P('dp', 'mp'), may hold values from -0.09375 to 0.09375
- norm_gains: float32 [2, 128], replicated, may hold values from 0.5 to 5
Outputs:
- queries_grad: bfloat16 [24576, 4096], P('dp', 'mp')
- keys_grad: bfloat16 [24576, 4096], P('dp', 'mp')
- values_grad: bfloat16 [24576, 4096], P('dp', 'mp')
- weight_grad: float32 [6144, 4096], P('dp', 'mp')
- gains_grad: float32 [2, 128], replicated
All inputs are finite; a program needn't handle non-finite values.
Results may differ from a plain program's by a relative error of at most 0.034.
The roundings to bfloat16 on the way count: a program that leaves them out, or rounds other values in their place, can miss the bound.
Values may be sent and summed in bfloat16 or wider, within the bound.
No kernel may reach another device: no remote copies, remote signals or barrier semaphores. Data moves between devices by JAX's collectives and lax.ppermute only.
A program may use at most 64 MiB of HBM per device.

v0:
```python
import jax
import jax.numpy as jnp
from jax import lax
from jax.sharding import PartitionSpec as P

HD = 128
PATCH = 256


EPSILON = 1e-06


def normalize(raw, gain):
    values32 = raw.astype(jnp.float32)
    center = values32 - jnp.mean(values32, axis=-1, keepdims=True)
    inverse = lax.rsqrt(jnp.mean(center * center, axis=-1, keepdims=True) + EPSILON)
    unit = center * inverse
    return (unit, inverse, (unit * gain).astype(jnp.bfloat16))


def unnormalize(grad, unit, inverse, gain):
    scaled = grad * gain
    centered = scaled - jnp.mean(scaled, axis=-1, keepdims=True)
    return ((centered - unit * jnp.mean(scaled * unit, axis=-1, keepdims=True)) * inverse).astype(
        jnp.bfloat16
    )


def heads_view(array):
    return array.reshape(array.shape[0] // PATCH, PATCH, array.shape[1] // HD, HD)


def attend(queries_raw, keys_raw, values, norm_gains):
    scale = HD ** (-0.5)
    q_unit, q_inverse, q_norm = normalize(heads_view(queries_raw), norm_gains[0])
    k_unit, k_inverse, k_norm = normalize(heads_view(keys_raw), norm_gains[1])
    value_view = heads_view(values)
    scores = (
        jnp.einsum("iphd,iqhd->ihpq", q_norm, k_norm, preferred_element_type=jnp.float32) * scale
    )
    peak = jnp.max(scores, axis=-1, keepdims=True)
    expo = jnp.exp(scores - peak)
    prob = expo / jnp.sum(expo, axis=-1, keepdims=True)
    prob_low = prob.astype(jnp.bfloat16)
    attn = jnp.einsum(
        "ihpq,iqhd->iphd", prob_low, value_view, preferred_element_type=jnp.float32
    ).astype(jnp.bfloat16)
    return (q_unit, q_inverse, q_norm, k_unit, k_inverse, k_norm, value_view, prob, prob_low, attn)


def backward(state, grad_attn, norm_gains):
    q_unit, q_inverse, q_norm, k_unit, k_inverse, k_norm, value_view, prob, prob_low, attn = state
    scale = HD ** (-0.5)
    tokens = grad_attn.shape[0]
    grad_view = heads_view(grad_attn)
    values_grad = jnp.einsum(
        "ihpq,iphd->iqhd", prob_low, grad_view, preferred_element_type=jnp.float32
    ).astype(jnp.bfloat16)
    product = jnp.einsum(
        "iphd,iqhd->ihpq", grad_view, value_view, preferred_element_type=jnp.float32
    )
    delta = jnp.sum(grad_view.astype(jnp.float32) * attn.astype(jnp.float32), axis=-1)
    delta = jnp.transpose(delta, (0, 2, 1))[..., None]
    score_grad = (prob * (product - delta)).astype(jnp.bfloat16)
    qn_grad = (
        jnp.einsum("ihpq,iqhd->iphd", score_grad, k_norm, preferred_element_type=jnp.float32)
        * scale
    )
    kn_grad = (
        jnp.einsum("ihpq,iphd->iqhd", score_grad, q_norm, preferred_element_type=jnp.float32)
        * scale
    )
    terms = jnp.stack(
        [jnp.sum(qn_grad * q_unit, axis=(0, 1, 2)), jnp.sum(kn_grad * k_unit, axis=(0, 1, 2))]
    )
    queries_grad = unnormalize(qn_grad, q_unit, q_inverse, norm_gains[0]).reshape(tokens, -1)
    keys_grad = unnormalize(kn_grad, k_unit, k_inverse, norm_gains[1]).reshape(tokens, -1)
    return (queries_grad, keys_grad, values_grad.reshape(tokens, -1), terms)


def per_device(queries_raw, keys_raw, values, grad_out, out_weight, norm_gains):
    state = attend(queries_raw, keys_raw, values, norm_gains)
    tokens = queries_raw.shape[0]
    attn_flat = state[-1].reshape(tokens, -1)
    contract = (((0,), (0,)), ((), ()))
    weights = lax.all_gather(out_weight, "dp", axis=0, tiled=True)
    full_grad = lax.all_gather(grad_out, "mp", axis=1, tiled=True)
    grad_sum = jnp.dot(full_grad, weights, preferred_element_type=jnp.float32)
    weight_grad = lax.psum_scatter(
        lax.dot_general(full_grad, attn_flat, contract, preferred_element_type=jnp.float32).astype(
            jnp.bfloat16
        ),
        "dp",
        scatter_dimension=0,
        tiled=True,
    ).astype(jnp.float32)
    grad_attn = grad_sum.astype(jnp.bfloat16)
    queries_grad, keys_grad, values_grad, terms = backward(state, grad_attn, norm_gains)
    gains_grad = lax.psum(terms, ("dp", "mp"))
    return (queries_grad, keys_grad, values_grad, weight_grad, gains_grad)


def solution(mesh):
    return jax.shard_map(
        per_device,
        mesh=mesh,
        in_specs=(P("dp", "mp"), P("dp", "mp"), P("dp", "mp"), P("dp", "mp"), P("dp", "mp"), P()),
        out_specs=(P("dp", "mp"), P("dp", "mp"), P("dp", "mp"), P("dp", "mp"), P()),
        check_vma=False,
    )
```

profile of v0, /device:TPU:2, one launch (start us, length us, event | category | flops | bytes accessed | tf_op | source)
XLA Modules:
  0.0 418.3 jit_solution(17238412232942012175)
XLA Ops:
  7.2 0.0 all-gather.5.cloned.1.call-start
  7.2 0.7 all-gather.5.cloned.1.call-update
  7.9 0.0 all-gather.3.cloned.1.call-start
  7.9 0.7 all-gather.3.cloned.1.call-update
  8.6 0.0 reduce-scatter.4.cloned.1.call-start
  8.7 1.4 reshape.86
  10.1 0.0 copy-start.1
  10.1 0.4 copy.102
  10.5 0.9 reduce_sum.110
  11.4 0.0 copy-done.1
  11.4 0.4 reshape.85
  11.8 0.0 copy-start
  11.8 0.9 reduce_sum.108
  12.7 0.4 copy.100
  13.1 0.0 copy-done
  13.1 0.1 reshape.80
  13.3 0.0 copy-start.2
  13.3 0.4 copy.109
  13.7 0.1 copy.101
  13.8 0.2 copy.99
  14.0 0.1 multiply_reduce_fusion.1
  14.1 0.1 multiply_reduce_fusion.2
  14.3 2.0 fusion.23
  16.3 133.7 %all-gather.5.cloned.1.call-done = bf16[6144,256]{1,0:T(8,128)(2,1)} async-done(((bf16[192,256]{1,0:T(8,128)(2,1)}), bf16[6144,256]{1,0:T(8,128)(2,1)}) %all-gather.5.cloned.1.call-update) | async-done | bytes 3145744 | tf_op jit(solution)/shard_map/all_gather | solution.py:86
  150.0 97.2 %all-gather.3.cloned.1.call-done = bf16[768,6144]{1,0:T(8,128)(2,1)} async-done(((bf16[768,384]{1,0:T(8,128)(2,1)}), bf16[768,6144]{1,0:T(8,128)(2,1)}) %all-gather.3.cloned.1.call-update) | async-done | bytes 9437200 | tf_op jit(solution)/shard_map/all_gather | solution.py:87
  247.2 7.2 %convolution_convert_fusion.3 = bf16[768,256]{1,0:T(8,128)(2,1)S(1)} fusion(bf16[768,6144]{1,0:T(8,128)(2,1)} %all-gather.3.cloned.1.call-done, bf16[6144,256]{1,0:T(8,128)(2,1)} %all-gather.5.cloned.1.call-done), kind=kOutput, calls=%fused_computation.9 | convolution fusion | flops 2416115712 | bytes 12976128 | tf_op jit(solution)/shard_map/dot_general | solution.py:88
  254.3 0.1 reshape.79
  254.4 0.4 copy.107
  254.9 1.7 multiply_reduce_fusion
  256.6 0.4 copy.118
  257.0 7.7 %fusion.1 = bf16[6144,256]{0,1:T(8,128)(2,1)} fusion(bf16[768,6144]{1,0:T(8,128)(2,1)} %all-gather.3.cloned.1.call-done, bf16[96,8,2,128]{3,2,1,0:T(2,128)(2,1)S(1)} %bitcast.79), kind=kOutput, calls=%fused_computation.2 | convolution fusion | flops 2417491968 | bytes 12976128 | tf_op jit(solution)/shard_map/dot_general | solution.py:90
  264.8 4.6 %copy.127 = bf16[6144,256]{1,0:T(8,128)(2,1)} copy(bf16[6144,256]{0,1:T(8,128)(2,1)} %fusion.1) | data formatting | bytes 6291456
  269.4 0.0 reduce-scatter.4.cloned.1.call-update
  269.5 1.8 fusion.4
  271.3 0.4 copy.117
  271.7 0.8 copy.140
  272.5 1.8 multiply_convert_fusion
  274.4 0.6 fusion.6
  275.0 0.6 fusion.7
  275.6 0.6 fusion.10
  276.1 0.4 copy.114
  276.6 0.8 copy.141
  277.4 0.4 copy.112
  277.9 0.8 copy.142
  278.7 105.2 %psum.7 = f32[2,128]{1,0:T(2,128)} all-reduce(f32[2,128]{1,0:T(2,128)S(1)} %pad_maximum_fusion), channel_id=1, replica_groups=mesh['dp'=32,'mp'=16] {'dp','mp'}, use_global_device_ids=true, to_apply=%region_14.0 | all-reduce | flops 256 | bytes 2048 | tf_op jit(solution)/shard_map/psum | solution.py:99
  383.8 26.2 %reduce-scatter.4.cloned.1.call-done = bf16[192,256]{1,0:T(8,128)(2,1)} async-done(((bf16[6144,256]{1,0:T(8,128)(2,1)}), bf16[192,256]{1,0:T(8,128)(2,1)}) %reduce-scatter.4.cloned.1.call-update) | async-done | bytes 98320
  410.0 1.0 copy.128
  411.0 0.8 copy.119
  (12 shorter events, 0.1 us)
Async XLA Ops:
  7.2 142.8 %all-gather.5.cloned.1.call-start = ((), (), s32[]{:S(2)}) async-start(), calls=%async_computation.2 | async-start | bytes 3244032 | tf_op jit(solution)/shard_map/all_gather | solution.py:86
  7.9 239.3 %all-gather.3.cloned.1.call-start = ((), (), s32[]{:S(2)}) async-start(), calls=%async_computation.1 | async-start | bytes 10027008 | tf_op jit(solution)/shard_map/all_gather | solution.py:87
  8.6 401.4 %reduce-scatter.4.cloned.1.call-start = ((), (), s32[]{:S(2)}) async-start(), calls=%async_computation.3 | async-start | bytes 3244032
  10.1 1.3 copy-start.1
  11.8 1.3 copy-start
  13.3 1.0 copy-start.2
Sparse Core Ops, SparseCore 0:
  10.1 139.8 all-gather.4
  153.1 93.9 all-gather.2
  269.6 140.4 reduce-scatter.3
where the time goes:
time: 419 us; the launch traced here: 418 us
  waiting for transfers between devices  259 us (62%)
  blocking collectives  105 us (25%)
  matrix products  23.4 us (6%)
  local copies, waits for them, and re-layouts  14.6 us (3%)
  between operations  14 us (3%)
    all_gather x1, waiting for transfers between devices, per_device(): weights = lax.all_gather(out_weight, 'dp', axis=0, tiled=True)  134 us
    psum x1, blocking collectives, per_device(): gains_grad = lax.psum(terms, ('dp', 'mp'))  105 us
    all_gather x1, waiting for transfers between devices, per_device(): full_grad = lax.all_gather(grad_out, 'mp', axis=1, tiled=True)  97.2 us
    unnamed x4, waiting for transfers between devices  27.6 us
    unnamed x12, local copies, waits for them, and re-layouts  8.84 us
  transfers between devices with their start and end apart: 3, of which 3 were waited for; matrix products, arithmetic and copies ran while one was open for 4% of the time, Pallas kernels for 0%

commit v1 on v0

--- a/solution.py
+++ b/solution.py
@@ -1,13 +1,15 @@
 import jax
 import jax.numpy as jnp
 from jax import lax
-from jax.sharding import PartitionSpec as P
+from jax.experimental import pallas as pl
+from jax.experimental.pallas import tpu as pltpu
+from jax.sharding import Mesh, PartitionSpec as P
 
 HD = 128
 PATCH = 256
-
-
 EPSILON = 1e-06
+AXES = ("yl", "z", "yh", "x", "c")
+SIZES = (2, 16, 2, 4, 2)
 
 
 def normalize(raw, gain):
@@ -78,33 +80,114 @@
     return (queries_grad, keys_grad, values_grad.reshape(tokens, -1), terms)
 
 
+def swap_y(array, target):
+    pairs = []
+    for low in range(2):
+        for high in range(2):
+            to_low, to_high = target(low, high)
+            pairs.append((low * 2 + high, to_low * 2 + to_high))
+    return lax.ppermute(array, ("yl", "yh"), pairs)
+
+
+def transpose_y(array):
+    return swap_y(array, lambda low, high: (high, low))
+
+
+def sum_over(array, axis, count):
+    spread = lax.all_to_all(jnp.broadcast_to(array[None], (count,) + array.shape), axis, 0, 0)
+    return jnp.sum(spread, axis=0)
+
+
+def product_kernel(grad_ref, weight_ref, attn_ref, part_ref, wgrad_ref, total):
+    step = pl.program_id(0)
+
+    @pl.when(step == 0)
+    def _():
+        total[...] = jnp.zeros_like(total)
+
+    weights = weight_ref[...]
+    flipped = None
+    for token in range(2):
+        block = grad_ref[token, 0]
+        total[token] += jnp.dot(block, weights, preferred_element_type=jnp.float32)
+        term = jnp.dot(attn_ref[token], block, preferred_element_type=jnp.float32)
+        flipped = term if flipped is None else flipped + term
+    wgrad_ref[...] = flipped.T.astype(wgrad_ref.dtype)
+
+    @pl.when(step == pl.num_programs(0) - 1)
+    def _():
+        part_ref[...] = total[...].astype(part_ref.dtype)
+
+
+def products(grads, weights, attn_flipped):
+    _, blocks, tokens, width = grads.shape
+    heads = weights.shape[1]
+    return pl.pallas_call(
+        product_kernel,
+        grid=(blocks,),
+        in_specs=[
+            pl.BlockSpec((2, 1, tokens, width), lambda k: (0, k, 0, 0)),
+            pl.BlockSpec((width, heads), lambda k: (k, 0)),
+            pl.BlockSpec((2, heads, tokens), lambda k: (0, 0, 0)),
+        ],
+        out_specs=[
+            pl.BlockSpec((2, tokens, heads), lambda k: (0, 0, 0)),
+            pl.BlockSpec((width, heads), lambda k: (k, 0)),
+        ],
+        out_shape=[
+            jax.ShapeDtypeStruct((2, tokens, heads), jnp.bfloat16),
+            jax.ShapeDtypeStruct((blocks * width, heads), jnp.bfloat16),
+        ],
+        scratch_shapes=[pltpu.VMEM((2, tokens, heads), jnp.float32)],
+        compiler_params=pltpu.CompilerParams(vmem_limit_bytes=32 * 1024 * 1024),
+        cost_estimate=pl.CostEstimate(
+            flops=8 * blocks * tokens * width * heads,
+            bytes_accessed=2 * (2 * blocks * tokens * width + 2 * blocks * width * heads),
+            transcendentals=0,
+        ),
+    )(grads, weights, attn_flipped)
+
+
 def per_device(queries_raw, keys_raw, values, grad_out, out_weight, norm_gains):
+    high = lax.axis_index("yh")
+    full_grad = lax.all_gather(grad_out, ("yl", "x", "c"), axis=0)
+    full_grad = full_grad.reshape((2, 8) + grad_out.shape)
+    own_rows = transpose_y(out_weight)
+    half = own_rows.shape[0] // 2
+    first = lax.all_gather(own_rows[:half], "z", axis=0)
+    second = lax.all_gather(own_rows[half:], "z", axis=0)
+    weights = jnp.concatenate([first, second], axis=1).reshape(-1, own_rows.shape[1])
+
     state = attend(queries_raw, keys_raw, values, norm_gains)
     tokens = queries_raw.shape[0]
     attn_flat = state[-1].reshape(tokens, -1)
-    contract = (((0,), (0,)), ((), ()))
-    weights = lax.all_gather(out_weight, "dp", axis=0, tiled=True)
-    full_grad = lax.all_gather(grad_out, "mp", axis=1, tiled=True)
-    grad_sum = jnp.dot(full_grad, weights, preferred_element_type=jnp.float32)
-    weight_grad = lax.psum_scatter(
-        lax.dot_general(full_grad, attn_flat, contract, preferred_element_type=jnp.float32).astype(
-            jnp.bfloat16
-        ),
-        "dp",
-        scatter_dimension=0,
-        tiled=True,
-    ).astype(jnp.float32)
-    grad_attn = grad_sum.astype(jnp.bfloat16)
+    attn_same = transpose_y(attn_flat)
+    attn_other = swap_y(attn_flat, lambda low, up: (up, 1 - low))
+    both = jnp.stack([attn_same.T, attn_other.T])
+    both = jnp.where(high == 0, both, both[::-1])
+
+    parts, wgrad = products(full_grad, weights, both)
+    shard = lax.psum_scatter(wgrad, "z", scatter_dimension=0, tiled=True)
+
+    parts = jnp.where(high == 0, parts, parts[::-1])
+    came_same = transpose_y(parts[0])
+    came_other = swap_y(parts[1], lambda low, up: (1 - up, low))
+    grad_attn = (came_same.astype(jnp.float32) + came_other.astype(jnp.float32)).astype(
+        jnp.bfloat16
+    )
     queries_grad, keys_grad, values_grad, terms = backward(state, grad_attn, norm_gains)
-    gains_grad = lax.psum(terms, ("dp", "mp"))
+    gains_grad = sum_over(sum_over(terms, "z", 16), ("yl", "yh", "x", "c"), 32)
+    weight_grad = transpose_y(shard).astype(jnp.float32)
     return (queries_grad, keys_grad, values_grad, weight_grad, gains_grad)
 
 
 def solution(mesh):
+    fine = Mesh(mesh.devices.reshape(SIZES), AXES)
+    spec = P(("yl", "z"), ("yh", "x", "c"))
     return jax.shard_map(
         per_device,
-        mesh=mesh,
-        in_specs=(P("dp", "mp"), P("dp", "mp"), P("dp", "mp"), P("dp", "mp"), P("dp", "mp"), P()),
-        out_specs=(P("dp", "mp"), P("dp", "mp"), P("dp", "mp"), P("dp", "mp"), P()),
+        mesh=fine,
+        in_specs=(spec, spec, spec, spec, spec, P()),
+        out_specs=(spec, spec, spec, spec, P()),
         check_vma=False,
     )

time: 419 us -> 204 us (0.49)
  the two profiles are of different devices: /device:TPU:2 before, /device:TPU:10 now
where the time goes in v1:
time: 204 us; the launch traced here: 203 us
  blocking collectives  71.3 us (35%)
  waiting for transfers between devices  38.4 us (19%)
  starting transfers between devices  36.5 us (18%)
  between operations  14.7 us (7%)
  local copies, waits for them, and re-layouts  14.5 us (7%)
  Pallas kernels  10.3 us (5%)
  other arithmetic  8.53 us (4%)
  matrix products  8.43 us (4%)
    all_gather x1, blocking collectives, per_device(): first = lax.all_gather(own_rows[:half], 'z', axis=0)  41 us
    all_gather x1, blocking collectives, per_device(): second = lax.all_gather(own_rows[half:], 'z', axis=0)  30.3 us
    reduce_scatter x1, waiting for transfers between devices, per_device(): shard = lax.psum_scatter(wgrad, 'z', scatter_dimension=0, tiled=True)  22.6 us
    ppermute x6, starting transfers between devices, swap_y(): return lax.ppermute(array, ('yl', 'yh'), pairs)  19.2 us
    all_to_all x2, starting transfers between devices, sum_over(): lax.all_to_all(jnp.broadcast_to(array[None], (count,) + array.shape), axi...  17.3 us
    pallas_call x1, Pallas kernels, products(): pl.pallas_call(product_kernel, grid=(blocks,), in_specs=[pl.BlockSpec((2,...  10.3 us
    all_to_all x2, waiting for transfers between devices, sum_over(): lax.all_to_all(jnp.broadcast_to(array[None], (count,) + array.shape), axi...  10.3 us
    unnamed x54, local copies, waits for them, and re-layouts  7.13 us
  transfers between devices with their start and end apart: 10, of which 4 were waited for; matrix products, arithmetic and copies ran while one was open for 13% of the time, Pallas kernels for 0%

profile of v1, /device:TPU:10, one launch (start us, length us, event | category | flops | bytes accessed | tf_op | source)
XLA Modules:
  0.0 202.6 jit_solution(10499667885479990828)
XLA Ops:
  7.2 0.7 all-gather.5.cloned.1.call-update
  7.9 3.5 %collective-permute-start = (bf16[192,256]{1,0:T(8,128)(2,1)}, bf16[192,256]{1,0:T(8,128)(2,1)}, u32[]{:S(2)}, u32[]{:S(2)}) collective-permute-start(bf16[192,256]{1,0:T(8,128)(2,1)} %param.10), channel_id=1, source_target_pairs={{0,0},{8,256},{256,8},{264,264},{1,1},{9,257},{257,9},{265,265},{2... | collective-permute-start | bytes 294920 | tf_op jit(solution)/shard_map/ppermute | solution.py:89
  11.4 1.4 reshape.96
  12.8 0.4 copy.167
  13.3 0.9 reduce_sum.128
  14.2 0.4 reshape.95
  14.6 0.4 copy.165
  15.0 0.9 reduce_sum.126
  16.1 0.2 copy.164
  16.7 1.9 fusion.23
  18.7 1.7 fusion.4
  20.4 0.3 copy.195
  20.7 0.8 copy.199
  21.6 1.9 collective-permute-start.2
  23.5 3.4 %collective-permute-start.1 = (bf16[768,256]{0,1:T(8,128)(2,1)}, bf16[768,256]{0,1:T(8,128)(2,1)}, u32[]{:S(2)}, u32[]{:S(2)}) collective-permute-start(bf16[768,256]{0,1:T(8,128)(2,1)} %bitcast.27), channel_id=1, source_target_pairs={{0,0},{8,256},{256,8},{264,264},{1,1},{9,257},{257,9},{265,265},{2... | collective-permute-start | bytes 1179656 | tf_op jit(solution)/shard_map/ppermute | solution.py:89
  26.9 0.8 fusion.22
  27.8 41.0 %all-gather.1 = bf16[1536,256]{1,0:T(8,128)(2,1)S(1)} all-gather(bf16[96,256]{1,0:T(8,128)(2,1)S(1)} %get-tuple-element.17), channel_id=3, replica_groups=mesh['yl'=2,'z'=16,'yh'=2,'x'=4,'c'=2] {'z'}, dimensions={0}, use_global_device_ids=true | all-gather | bytes 835584 | tf_op jit(solution)/shard_map/all_gather | solution.py:157
  68.7 30.3 %all-gather.2 = bf16[1536,256]{1,0:T(8,128)(2,1)S(1)} all-gather(bf16[96,256]{1,0:T(8,128)(2,1)S(1)} %get-tuple-element.18), channel_id=4, replica_groups=mesh['yl'=2,'z'=16,'yh'=2,'x'=4,'c'=2] {'z'}, dimensions={0}, use_global_device_ids=true | all-gather | bytes 835584 | tf_op jit(solution)/shard_map/all_gather | solution.py:158
  99.1 1.2 pad_maximum_fusion.1
  100.5 3.7 %copy-done = bf16[12288,384]{1,0:T(8,128)(2,1)S(1)} copy-done((bf16[12288,384]{1,0:T(8,128)(2,1)S(1)}, bf16[12288,384]{1,0:T(8,128)(2,1)}, u32[]{:S(2)}) %copy-start) | copy-done | bytes 9437208
  104.2 10.3 %shard_map.101 = (bf16[2,768,256]{2,1,0:T(8,128)(2,1)S(1)}, bf16[3072,256]{1,0:T(8,128)(2,1)}) custom-call(bf16[2,8,768,384]{3,2,1,0:T(8,128)(2,1)S(1)} %bitcast.86, bf16[3072,256]{1,0:T(8,128)(2,1)S(1)} %bitcast.85, bf16[2,256,768]{2,1,0:T(8,128)(2,1)S(1)} %reverse_select_fusion.1.attn_ref), custom_call_target="tpu_custom_call" | custom-call | flops 4831838208 | bytes 12582912 | tf_op jit(solution)/shard_map/pallas_call | solution.py:125
  114.8 2.4 %collective-permute-start.3 = (bf16[768,256]{1,0:T(8,128)(2,1)S(1)}, bf16[768,256]{1,0:T(8,128)(2,1)S(1)}, u32[]{:S(2)}, u32[]{:S(2)}) collective-permute-start(bf16[768,256]{1,0:T(8,128)(2,1)S(1)} %get-tuple-element.15), channel_id=1, source_target_pairs={{0,0},{8,256},{256,8},{264,264},{1,1},{9,257},{257,9},{265,265},{2... | collective-permute-start | bytes 1179656 | tf_op jit(solution)/shard_map/ppermute | solution.py:89
  117.2 4.4 %collective-permute-start.4 = (bf16[768,256]{1,0:T(8,128)(2,1)S(1)}, bf16[768,256]{1,0:T(8,128)(2,1)S(1)}, u32[]{:S(2)}, u32[]{:S(2)}) collective-permute-start(bf16[768,256]{1,0:T(8,128)(2,1)S(1)} %get-tuple-element.16), channel_id=1, source_target_pairs={{0,256},{8,0},{256,264},{264,8},{1,257},{9,1},{257,265},{265,9},{2... | collective-permute-start | bytes 1179656 | tf_op jit(solution)/shard_map/ppermute | solution.py:89
  121.5 0.5 broadcast_multiply_fusion.6
  122.1 2.4 %collective-permute-done.3 = bf16[768,256]{1,0:T(8,128)(2,1)S(1)} collective-permute-done((bf16[768,256]{1,0:T(8,128)(2,1)S(1)}, bf16[768,256]{1,0:T(8,128)(2,1)S(1)}, u32[]{:S(2)}, u32[]{:S(2)}) %collective-permute-start.3) | collective-permute-done | bytes 393248 | tf_op jit(solution)/shard_map/ppermute | solution.py:89
  124.4 2.4 %collective-permute-done.4 = bf16[768,256]{1,0:T(8,128)(2,1)S(1)} collective-permute-done((bf16[768,256]{1,0:T(8,128)(2,1)S(1)}, bf16[768,256]{1,0:T(8,128)(2,1)S(1)}, u32[]{:S(2)}, u32[]{:S(2)}) %collective-permute-start.4) | collective-permute-done | bytes 393248 | tf_op jit(solution)/shard_map/ppermute | solution.py:89
  127.0 0.4 copy.177
  127.7 1.8 multiply_convert_fusion
  129.6 0.5 fusion.6
  130.2 0.6 fusion.5
  130.8 0.6 broadcast_in_dim.4
  131.5 7.9 %all-to-all-start = ((f32[16,2,128]{2,1,0:T(2,128)}), f32[16,2,128]{2,1,0:T(2,128)}, u32[]{:S(2)}, u32[]{:S(2)}) async-start(f32[16,2,128]{2,1,0:T(2,128)} %broadcast_in_dim.4), calls=%async_computation.1 | async-start | bytes 32768 | tf_op jit(solution)/shard_map/all_to_all | solution.py:97
  139.4 2.2 %fusion.9 = (bf16[3,256,2,128]{1,3,2,0:T(8,128)(2,1)}, bf16[3,256,2,128]{1,3,2,0:T(8,128)(2,1)}) fusion(f32[3,2,128,256]{3,2,1,0:T(8,128)S(1)} %get-tuple-element.26, f32[3,256,2,128]{1,3,2,0:T(8,128)S(1)} %copy-done.2, f32[3,256,2]{1,2,0:T(2,128)S(1)} %broadcast_multiply_fusion, f32[3,256,2]{1,2,0:T(2,128)S(1)} %broadcast_multiply_fusion.1, ...), kind=kLoop, calls=%fused_computation.22 | loop fusion | flops 3145728 | bytes 3982336 | tf_op jit(solution)/shard_map/convert_element_type | solution.py:26
  141.6 10.3 %all-to-all-done = f32[16,2,128]{2,1,0:T(2,128)} async-done(((f32[16,2,128]{2,1,0:T(2,128)}), f32[16,2,128]{2,1,0:T(2,128)}, u32[]{:S(2)}, u32[]{:S(2)}) %all-to-all-start) | async-done | bytes 16416 | tf_op jit(solution)/shard_map/all_to_all | solution.py:97
  151.9 0.7 reduce_sum.138
  152.6 0.6 broadcast_in_dim.5
  153.2 9.4 %all-to-all-start.1 = ((f32[32,2,128]{2,1,0:T(2,128)}), f32[32,2,128]{2,1,0:T(2,128)S(1)}, u32[]{:S(2)}, u32[]{:S(2)}) async-start(f32[32,2,128]{2,1,0:T(2,128)} %broadcast_in_dim.5), calls=%async_computation.2 | async-start | bytes 65536 | tf_op jit(solution)/shard_map/all_to_all | solution.py:97
  162.6 22.6 %reduce-scatter.2.cloned.1.call-done = bf16[192,256]{1,0:T(8,128)(2,1)} async-done(((bf16[3072,256]{1,0:T(8,128)(2,1)}), bf16[192,256]{1,0:T(8,128)(2,1)}) %reduce-scatter.2.cloned.1.call-update) | async-done | bytes 98320 | tf_op jit(solution)/shard_map/reduce_scatter | solution.py:170
  185.2 3.6 %collective-permute-start.5 = (bf16[192,256]{1,0:T(8,128)(2,1)}, bf16[192,256]{1,0:T(8,128)(2,1)S(1)}, u32[]{:S(2)}, u32[]{:S(2)}) collective-permute-start(bf16[192,256]{1,0:T(8,128)(2,1)} %reduce-scatter.2.cloned.1.call-done), channel_id=1, source_target_pairs={{0,0},{8,256},{256,8},{264,264},{1,1},{9,257},{257,9},{265,265},{2... | collective-permute-start | bytes 294920 | tf_op jit(solution)/shard_map/ppermute | solution.py:89
  188.8 1.8 fusion.3
  190.7 0.4 copy.185
  191.1 0.8 copy.210
  191.9 0.4 copy.182
  192.4 0.8 copy.211
  193.2 0.4 copy.180
  193.6 0.8 copy.212
  194.5 0.6 reduce_sum.139
  195.1 0.7 convert_element_type.79
  (79 shorter events, 1.6 us)
Async XLA Ops:
  7.2 93.3 %all-gather.5.cloned.1.call-start = ((), (), s32[]{:S(2)}) async-start(), calls=%async_computation.4 | async-start | bytes 10027008 | tf_op jit(solution)/shard_map/all_gather | solution.py:153
  7.9 177.3 %reduce-scatter.2.cloned.1.call-start = ((), (), s32[]{:S(2)}) async-start(), calls=%async_computation.3 | async-start | bytes 1671168 | tf_op jit(solution)/shard_map/reduce_scatter | solution.py:170
  7.9 19.0 %collective-permute-start = (bf16[192,256]{1,0:T(8,128)(2,1)}, bf16[192,256]{1,0:T(8,128)(2,1)}, u32[]{:S(2)}, u32[]{:S(2)}) collective-permute-start(bf16[192,256]{1,0:T(8,128)(2,1)} %param.10), channel_id=1, source_target_pairs={{0,0},{8,256},{256,8},{264,264},{1,1},{9,257},{257,9},{265,265},{2... | collective-permute-start | bytes 294920 | tf_op jit(solution)/shard_map/ppermute | solution.py:89
  12.8 1.3 copy-start.10
  14.6 1.7 copy-start.7
  15.0 1.7 copy-start.1
  15.9 0.7 copy-start.17
  16.3 2.3 %copy-start.8 = (bf16[3,256,2,128]{3,2,1,0:T(2,128)(2,1)}, bf16[3,256,2,128]{3,2,1,0:T(2,128)(2,1)S(1)}, u32[]{:S(2)}) copy-start(bf16[3,256,2,128]{3,2,1,0:T(2,128)(2,1)S(1)} %reshape.89) | copy-start | bytes 1179652
  16.6 2.0 %copy-start.19 = (f32[128]{0:T(128)}, f32[128]{0:T(128)S(1)}, u32[]{:S(2)}) copy-start(f32[128]{0:T(128)S(1)} %get-tuple-element.21) | copy-start | bytes 1540
  16.6 2.0 %copy-start.21 = (f32[128]{0:T(128)}, f32[128]{0:T(128)S(1)}, u32[]{:S(2)}) copy-start(f32[128]{0:T(128)S(1)} %get-tuple-element.22) | copy-start | bytes 1540
  16.6 2.0 copy-start.11
  16.7 2.0 copy-start.13
  18.7 1.7 copy-start.23
  21.6 77.6 %collective-permute-start.2 = (bf16[768,256]{0,1:T(8,128)(2,1)}, bf16[768,256]{0,1:T(8,128)(2,1)}, u32[]{:S(2)}, u32[]{:S(2)}) collective-permute-start(bf16[768,256]{0,1:T(8,128)(2,1)} %bitcast.27), channel_id=1, source_target_pairs={{0,8},{8,264},{256,0},{264,256},{1,9},{9,265},{257,1},{265,257},{2... | collective-permute-start | bytes 1179656 | tf_op jit(solution)/shard_map/ppermute | solution.py:89
  23.5 75.6 %collective-permute-start.1 = (bf16[768,256]{0,1:T(8,128)(2,1)}, bf16[768,256]{0,1:T(8,128)(2,1)}, u32[]{:S(2)}, u32[]{:S(2)}) collective-permute-start(bf16[768,256]{0,1:T(8,128)(2,1)} %bitcast.27), channel_id=1, source_target_pairs={{0,0},{8,256},{256,8},{264,264},{1,1},{9,257},{257,9},{265,265},{2... | collective-permute-start | bytes 1179656 | tf_op jit(solution)/shard_map/ppermute | solution.py:89
  100.5 3.7 %copy-start = (bf16[12288,384]{1,0:T(8,128)(2,1)S(1)}, bf16[12288,384]{1,0:T(8,128)(2,1)}, u32[]{:S(2)}) copy-start(bf16[12288,384]{1,0:T(8,128)(2,1)} %all-gather.5.cloned.1.call-done) | copy-start | bytes 28311556
  114.7 6.9 %copy-start.18 = (f32[2,128]{1,0:T(2,128)S(1)}, f32[2,128]{1,0:T(2,128)}, u32[]{:S(2)}) copy-start(f32[2,128]{1,0:T(2,128)} %param.11) | copy-start | bytes 3076
  114.8 9.7 %collective-permute-start.3 = (bf16[768,256]{1,0:T(8,128)(2,1)S(1)}, bf16[768,256]{1,0:T(8,128)(2,1)S(1)}, u32[]{:S(2)}, u32[]{:S(2)}) collective-permute-start(bf16[768,256]{1,0:T(8,128)(2,1)S(1)} %get-tuple-element.15), channel_id=1, source_target_pairs={{0,0},{8,256},{256,8},{264,264},{1,1},{9,257},{257,9},{265,265},{2... | collective-permute-start | bytes 1179656 | tf_op jit(solution)/shard_map/ppermute | solution.py:89
  117.2 9.7 %collective-permute-start.4 = (bf16[768,256]{1,0:T(8,128)(2,1)S(1)}, bf16[768,256]{1,0:T(8,128)(2,1)S(1)}, u32[]{:S(2)}, u32[]{:S(2)}) collective-permute-start(bf16[768,256]{1,0:T(8,128)(2,1)S(1)} %get-tuple-element.16), channel_id=1, source_target_pairs={{0,256},{8,0},{256,264},{264,8},{1,257},{9,1},{257,265},{265,9},{2... | collective-permute-start | bytes 1179656 | tf_op jit(solution)/shard_map/ppermute | solution.py:89
  122.1 7.5 %copy-start.16 = (f32[128]{0:T(128)}, f32[128]{0:T(128)S(1)}, u32[]{:S(2)}) copy-start(f32[128]{0:T(128)S(1)} %get-tuple-element.20) | copy-start | bytes 1540
  122.1 5.6 %copy-start.9 = (bf16[3,256,2,128]{3,2,1,0:T(2,128)(2,1)S(1)}, bf16[3,256,2,128]{3,2,1,0:T(2,128)(2,1)}, u32[]{:S(2)}) copy-start(bf16[3,256,2,128]{3,2,1,0:T(2,128)(2,1)} %copy-done.8) | copy-start | bytes 1179652
  122.1 5.6 %copy-start.24 = (f32[3,2,256]{2,1,0:T(2,128)S(1)}, f32[3,2,256]{2,1,0:T(2,128)}, u32[]{:S(2)}) copy-start(f32[3,2,256]{2,1,0:T(2,128)} %copy-done.23) | copy-start | bytes 18436
  127.5 2.0 %copy-start.3 = (bf16[3,256,2,128]{1,3,2,0:T(8,128)(2,1)}, bf16[3,256,2,128]{1,3,2,0:T(8,128)(2,1)S(1)}, u32[]{:S(2)}) copy-start(bf16[3,256,2,128]{1,3,2,0:T(8,128)(2,1)S(1)} %copy.177) | copy-start | bytes 1179652
  127.6 1.9 copy-start.2
  127.6 1.9 copy-start.12
  127.7 1.9 copy-start.14
  127.7 1.9 copy-start.22
  129.6 0.7 copy-start.15
  129.6 0.7 copy-start.20
  131.5 20.4 %all-to-all-start = ((f32[16,2,128]{2,1,0:T(2,128)}), f32[16,2,128]{2,1,0:T(2,128)}, u32[]{:S(2)}, u32[]{:S(2)}) async-start(f32[16,2,128]{2,1,0:T(2,128)} %broadcast_in_dim.4), calls=%async_computation.1 | async-start | bytes 32768 | tf_op jit(solution)/shard_map/all_to_all | solution.py:97
  139.4 49.4 %copy-start.4 = (bf16[3,256,2,128]{1,3,2,0:T(8,128)(2,1)S(1)}, bf16[3,256,2,128]{1,3,2,0:T(8,128)(2,1)}, u32[]{:S(2)}) copy-start(bf16[3,256,2,128]{1,3,2,0:T(8,128)(2,1)} %copy-done.3) | copy-start | bytes 1179652
  153.2 41.2 %all-to-all-start.1 = ((f32[32,2,128]{2,1,0:T(2,128)}), f32[32,2,128]{2,1,0:T(2,128)S(1)}, u32[]{:S(2)}, u32[]{:S(2)}) async-start(f32[32,2,128]{2,1,0:T(2,128)} %broadcast_in_dim.5), calls=%async_computation.2 | async-start | bytes 65536 | tf_op jit(solution)/shard_map/all_to_all | solution.py:97
  185.2 9.9 %collective-permute-start.5 = (bf16[192,256]{1,0:T(8,128)(2,1)}, bf16[192,256]{1,0:T(8,128)(2,1)S(1)}, u32[]{:S(2)}, u32[]{:S(2)}) collective-permute-start(bf16[192,256]{1,0:T(8,128)(2,1)} %reduce-scatter.2.cloned.1.call-done), channel_id=1, source_target_pairs={{0,0},{8,256},{256,8},{264,264},{1,1},{9,257},{257,9},{265,265},{2... | collective-permute-start | bytes 294920 | tf_op jit(solution)/shard_map/ppermute | solution.py:89
  190.7 1.3 copy-start.6
  190.7 2.5 %copy-start.5 = (bf16[3,256,2,128]{1,3,2,0:T(8,128)(2,1)S(1)}, bf16[3,256,2,128]{1,3,2,0:T(8,128)(2,1)}, u32[]{:S(2)}) copy-start(bf16[3,256,2,128]{1,3,2,0:T(8,128)(2,1)} %get-tuple-element.28) | copy-start | bytes 1179652
Sparse Core Ops, SparseCore 0:
  10.1 69.0 all-gather.4
  114.8 70.3 reduce-scatter.1

commit v2 on v0

v2 whole, which is shorter than its diff:
```python
import jax
import jax.numpy as jnp
from jax import lax
from jax.experimental import pallas as pl
from jax.experimental.pallas import tpu as pltpu
from jax.sharding import Mesh, PartitionSpec as P

HD = 128
PATCH = 256
EPSILON = 1e-06
SCALE = HD ** (-0.5)
AXES = ("yl", "z", "yh", "x", "c")
SIZES = (2, 16, 2, 4, 2)
VMEM_LIMIT = 56 * 1024 * 1024


def normalize(raw, gain):
    values32 = raw.astype(jnp.float32)
    center = values32 - jnp.mean(values32, axis=-1, keepdims=True)
    inverse = lax.rsqrt(jnp.mean(center * center, axis=-1, keepdims=True) + EPSILON)
    unit = center * inverse
    return (unit, inverse, (unit * gain).astype(jnp.bfloat16))


def unnormalize(grad, unit, inverse, gain):
    scaled = grad * gain
    centered = scaled - jnp.mean(scaled, axis=-1, keepdims=True)
    return (centered - unit * jnp.mean(scaled * unit, axis=-1, keepdims=True)) * inverse


def product(left, right, left_dim, right_dim):
    return lax.dot_general(
        left, right, (((left_dim,), (right_dim,)), ((), ())), preferred_element_type=jnp.float32
    )


def softmax(q_norm, k_norm):
    scores = product(q_norm, k_norm, 1, 1) * SCALE
    expo = jnp.exp(scores - jnp.max(scores, axis=-1, keepdims=True))
    return expo / jnp.sum(expo, axis=-1, keepdims=True)


def forward_kernel(q_ref, k_ref, v_ref, gains_ref, attn_ref):
    for head in range(q_ref.shape[1] // HD):
        cols = slice(head * HD, (head + 1) * HD)
        _, _, q_norm = normalize(q_ref[:, cols], gains_ref[0:1, :])
        _, _, k_norm = normalize(k_ref[:, cols], gains_ref[1:2, :])
        prob_low = softmax(q_norm, k_norm).astype(jnp.bfloat16)
        attn = product(prob_low, v_ref[:, cols], 1, 0)
        attn_ref[cols, :] = attn.T.astype(jnp.bfloat16)


def forward(queries_raw, keys_raw, values, norm_gains):
    tokens, width = queries_raw.shape
    block = pl.BlockSpec((PATCH, width), lambda i: (i, 0))
    return pl.pallas_call(
        forward_kernel,
        grid=(tokens // PATCH,),
        in_specs=[block, block, block, pl.BlockSpec((2, HD), lambda i: (0, 0))],
        out_specs=pl.BlockSpec((width, PATCH), lambda i: (0, i)),
        out_shape=jax.ShapeDtypeStruct((width, tokens), jnp.bfloat16),
        compiler_params=pltpu.CompilerParams(vmem_limit_bytes=VMEM_LIMIT),
    )(queries_raw, keys_raw, values, norm_gains)


def backward_kernel(
    q_ref, k_ref, v_ref, one_ref, two_ref, gains_ref, qg_ref, kg_ref, vg_ref, terms_ref
):
    @pl.when(pl.program_id(0) == 0)
    def _():
        terms_ref[...] = jnp.zeros_like(terms_ref)

    q_gain, k_gain = gains_ref[0:1, :], gains_ref[1:2, :]
    for head in range(q_ref.shape[1] // HD):
        cols = slice(head * HD, (head + 1) * HD)
        value = v_ref[:, cols]
        q_unit, q_inverse, q_norm = normalize(q_ref[:, cols], q_gain)
        k_unit, k_inverse, k_norm = normalize(k_ref[:, cols], k_gain)
        prob = softmax(q_norm, k_norm)
        prob_low = prob.astype(jnp.bfloat16)
        attn = product(prob_low, value, 1, 0).astype(jnp.bfloat16)
        grad = one_ref[:, cols].astype(jnp.float32) + two_ref[:, cols].astype(jnp.float32)
        grad = grad.astype(jnp.bfloat16)
        vg_ref[:, cols] = product(prob_low, grad, 0, 0).astype(jnp.bfloat16)
        delta = jnp.sum(
            grad.astype(jnp.float32) * attn.astype(jnp.float32), axis=-1, keepdims=True
        )
        score_grad = (prob * (product(grad, value, 1, 1) - delta)).astype(jnp.bfloat16)
        qn_grad = product(score_grad, k_norm, 1, 0) * SCALE
        kn_grad = product(score_grad, q_norm, 0, 0) * SCALE
        terms_ref[0:1, :] += jnp.sum(qn_grad * q_unit, axis=0, keepdims=True)
        terms_ref[1:2, :] += jnp.sum(kn_grad * k_unit, axis=0, keepdims=True)
        qg_ref[:, cols] = unnormalize(qn_grad, q_unit, q_inverse, q_gain).astype(jnp.bfloat16)
        kg_ref[:, cols] = unnormalize(kn_grad, k_unit, k_inverse, k_gain).astype(jnp.bfloat16)


def backward(queries_raw, keys_raw, values, part_one, part_two, norm_gains):
    tokens, width = queries_raw.shape
    block = pl.BlockSpec((PATCH, width), lambda i: (i, 0))
    gains = pl.BlockSpec((2, HD), lambda i: (0, 0))
    out = jax.ShapeDtypeStruct((tokens, width), jnp.bfloat16)
    return pl.pallas_call(
        backward_kernel,
        grid=(tokens // PATCH,),
        in_specs=[block] * 5 + [gains],
        out_specs=[block, block, block, gains],
        out_shape=[out, out, out, jax.ShapeDtypeStruct((2, HD), jnp.float32)],
        compiler_params=pltpu.CompilerParams(vmem_limit_bytes=VMEM_LIMIT),
    )(queries_raw, keys_raw, values, part_one, part_two, norm_gains)


def products_kernel(
    high_ref, grad_ref, weight_ref, same_ref, other_ref, part_same_ref, part_other_ref,
    wgrad_ref, total_same, total_other,
):
    step = pl.program_id(0)

    @pl.when(step == 0)
    def _():
        total_same[...] = jnp.zeros_like(total_same)
        total_other[...] = jnp.zeros_like(total_other)

    high = high_ref[0]
    weights = weight_ref[...].reshape(grad_ref.shape[3], weight_ref.shape[3])
    block = grad_ref[high, 0]
    flipped = product(same_ref[...], block, 1, 0)
    total_same[...] += product(block, weights, 1, 0)
    block = grad_ref[1 - high, 0]
    flipped += product(other_ref[...], block, 1, 0)
    total_other[...] += product(block, weights, 1, 0)
    wgrad_ref[...] = flipped.T.astype(wgrad_ref.dtype).reshape(wgrad_ref.shape)

    @pl.when(step == pl.num_programs(0) - 1)
    def _():
        part_same_ref[...] = total_same[...].astype(part_same_ref.dtype)
        part_other_ref[...] = total_other[...].astype(part_other_ref.dtype)


def products(high, grads, weights, attn_same, attn_other):
    _, blocks, tokens, width = grads.shape
    rows, heads = weights.shape[2:]
    pair = pl.BlockSpec((2, 1, rows, heads), lambda k, high: (k % 2, k // 2, 0, 0))
    attn = pl.BlockSpec((heads, tokens), lambda k, high: (0, 0))
    part = pl.BlockSpec((tokens, heads), lambda k, high: (0, 0))
    return pl.pallas_call(
        products_kernel,
        grid_spec=pltpu.PrefetchScalarGridSpec(
            num_scalar_prefetch=1,
            grid=(blocks,),
            in_specs=[
                pl.BlockSpec((2, 1, tokens, width), lambda k, high: (0, k, 0, 0)),
                pair,
                attn,
                attn,
            ],
            out_specs=[part, part, pair],
            scratch_shapes=[pltpu.VMEM((tokens, heads), jnp.float32)] * 2,
        ),
        out_shape=[
            jax.ShapeDtypeStruct((tokens, heads), jnp.bfloat16),
            jax.ShapeDtypeStruct((tokens, heads), jnp.bfloat16),
            jax.ShapeDtypeStruct(weights.shape, jnp.bfloat16),
        ],
        compiler_params=pltpu.CompilerParams(vmem_limit_bytes=VMEM_LIMIT),
        cost_estimate=pl.CostEstimate(
            flops=8 * blocks * tokens * width * heads,
            bytes_accessed=2 * (2 * blocks * tokens * width + 2 * blocks * width * heads),
            transcendentals=0,
        ),
    )(high, grads, weights, attn_same, attn_other)


def permute(array, target):
    pairs = []
    for low in range(2):
        for z in range(16):
            for high in range(2):
                to_low, to_z, to_high = target(low, z, high)
                pairs.append(((low * 16 + z) * 2 + high, (to_low * 16 + to_z % 16) * 2 + to_high))
    return lax.ppermute(array, ("yl", "z", "yh"), pairs)


def along(array, step):
    return permute(array, lambda low, z, high: (low, z + step, high))


def turned(array, step):
    return permute(array, lambda low, z, high: (high, z + step, low))


def pick(array, index):
    return lax.dynamic_index_in_dim(array, index, 0, keepdims=False)


def rolled(blocks, shift):
    return lax.dynamic_slice_in_dim(
        jnp.stack(blocks + blocks), (4 - shift) % 4, 4, axis=0
    )


def gather_rows(out_weight, z):
    column = rolled([turned(out_weight, -4 * step) for step in range(4)], z // 4)
    before = along(column, 1)
    after = along(column, -1)
    far = jnp.concatenate([along(column[:2], 2), along(column[2:], -2)])
    return rolled([column, after, far, before], z % 4)


def scatter_rows(wgrad, z):
    own = pick(wgrad, z % 4)
    before = along(pick(wgrad, (z + 1) % 4), 1)
    after = along(pick(wgrad, (z + 3) % 4), -1)
    far = pick(wgrad, (z + 2) % 4)
    far = jnp.concatenate([along(far[:2], 2), along(far[2:], -2)])
    column = sum(term.astype(jnp.float32) for term in (own, before, after, far))
    column = column.astype(jnp.bfloat16)
    terms = [turned(pick(column, (z // 4 + step) % 4), 4 * step) for step in range(4)]
    return sum(term.astype(jnp.float32) for term in terms)


def sum_over(array, axis, count):
    spread = lax.all_to_all(jnp.broadcast_to(array[None], (count,) + array.shape), axis, 0, 0)
    return jnp.sum(spread, axis=0)


def per_device(queries_raw, keys_raw, values, grad_out, out_weight, norm_gains):
    z = lax.axis_index("z")
    high = lax.axis_index("yh").reshape(1)
    grads = lax.all_gather(grad_out, ("yl", "x", "c"), axis=0)
    grads = grads.reshape((2, 8) + grad_out.shape)
    weights = gather_rows(out_weight, z)

    attn = forward(queries_raw, keys_raw, values, norm_gains)
    attn_same = turned(attn, 0)
    attn_other = permute(attn, lambda low, z, up: (up, z, 1 - low))

    part_same, part_other, wgrad = products(high, grads, weights, attn_same, attn_other)
    came_same = turned(part_same, 0)
    came_other = permute(part_other, lambda low, z, up: (1 - up, z, low))
    weight_grad = scatter_rows(wgrad, z)
    queries_grad, keys_grad, values_grad, terms = backward(
        queries_raw, keys_raw, values, came_same, came_other, norm_gains
    )
    gains_grad = sum_over(sum_over(terms, "z", 16), ("yl", "yh", "x", "c"), 32)
    return (queries_grad, keys_grad, values_grad, weight_grad, gains_grad)


def solution(mesh):
    fine = Mesh(mesh.devices.reshape(SIZES), AXES)
    spec = P(("yl", "z"), ("yh", "x", "c"))
    return jax.shard_map(
        per_device,
        mesh=fine,
        in_specs=(spec, spec, spec, spec, spec, P()),
        out_specs=(spec, spec, spec, spec, P()),
        check_vma=False,
    )
```

time: 419 us -> 210 us (0.50)
  the two profiles are of different devices: /device:TPU:2 before, /device:TPU:1 now
where the time goes in v2:
time: 210 us; the launch traced here: 209 us
  starting transfers between devices  92.7 us (44%)
  blocking collectives  38.6 us (18%)
  Pallas kernels  25 us (12%)
  waiting for transfers between devices  22.1 us (11%)
  between operations  14.6 us (7%)
  local copies, waits for them, and re-layouts  12.1 us (6%)
  other arithmetic  4.1 us (2%)
    ppermute x20, starting transfers between devices, permute(): return lax.ppermute(array, ('yl', 'z', 'yh'), pairs)  92.7 us
    all_to_all x2, blocking collectives, sum_over(): lax.all_to_all(jnp.broadcast_to(array[None], (count,) + array.shape), axi...  38.6 us
    ppermute x20, waiting for transfers between devices, permute(): return lax.ppermute(array, ('yl', 'z', 'yh'), pairs)  21.4 us
    pallas_call x1, Pallas kernels, products(): pl.pallas_call(products_kernel, grid_spec=pltpu.PrefetchScalarGridSpec(nu...  12.3 us
    pallas_call x1, Pallas kernels, backward(): pl.pallas_call(backward_kernel, grid=(tokens // PATCH,), in_specs=[block]...  7.36 us
    unnamed x20, local copies, waits for them, and re-layouts  5.59 us
    pallas_call x1, Pallas kernels, forward(): pl.pallas_call(forward_kernel, grid=(tokens // PATCH,), in_specs=[block,...  5.34 us
  transfers between devices with their start and end apart: 21, of which 5 were waited for; matrix products, arithmetic and copies ran while one was open for 6% of the time, Pallas kernels for 6%

profile of v2, /device:TPU:1, one launch (start us, length us, event | category | flops | bytes accessed | tf_op | source)
XLA Modules:
  0.0 209.1 jit_solution(15438198398129289594)
XLA Ops:
  7.2 0.7 all-gather.3.cloned.1.call-update
  7.9 1.6 collective-permute-start
  9.4 13.3 %collective-permute-start.1 = (bf16[192,256]{1,0:T(8,128)(2,1)}, bf16[192,256]{1,0:T(8,128)(2,1)S(1)}, u32[]{:S(2)}, u32[]{:S(2)}) collective-permute-start(bf16[192,256]{1,0:T(8,128)(2,1)} %param.10), channel_id=1, source_target_pairs={{0,192},{8,448},{16,208},{24,464},{32,224},{40,480},{48,240},{56,4... | collective-permute-start | bytes 294920 | tf_op jit(solution)/shard_map/ppermute | solution.py:180
  22.7 4.9 %collective-permute-start.2 = (bf16[192,256]{1,0:T(8,128)(2,1)}, bf16[192,256]{1,0:T(8,128)(2,1)S(1)}, u32[]{:S(2)}, u32[]{:S(2)}) collective-permute-start(bf16[192,256]{1,0:T(8,128)(2,1)} %param.10), channel_id=1, source_target_pairs={{0,128},{8,384},{16,144},{24,400},{32,160},{40,416},{48,176},{56,4... | collective-permute-start | bytes 294920 | tf_op jit(solution)/shard_map/ppermute | solution.py:180
  27.6 7.3 %collective-permute-start.3 = (bf16[192,256]{1,0:T(8,128)(2,1)}, bf16[192,256]{1,0:T(8,128)(2,1)S(1)}, u32[]{:S(2)}, u32[]{:S(2)}) collective-permute-start(bf16[192,256]{1,0:T(8,128)(2,1)} %param.10), channel_id=1, source_target_pairs={{0,64},{8,320},{16,80},{24,336},{32,96},{40,352},{48,112},{56,368}... | collective-permute-start | bytes 294920 | tf_op jit(solution)/shard_map/ppermute | solution.py:180
  35.0 2.5 %collective-permute-done.2 = bf16[192,256]{1,0:T(8,128)(2,1)S(1)} collective-permute-done((bf16[192,256]{1,0:T(8,128)(2,1)}, bf16[192,256]{1,0:T(8,128)(2,1)S(1)}, u32[]{:S(2)}, u32[]{:S(2)}) %collective-permute-start.2) | collective-permute-done | bytes 98336 | tf_op jit(solution)/shard_map/ppermute | solution.py:180
  37.5 5.6 %collective-permute-done.3 = bf16[192,256]{1,0:T(8,128)(2,1)S(1)} collective-permute-done((bf16[192,256]{1,0:T(8,128)(2,1)}, bf16[192,256]{1,0:T(8,128)(2,1)S(1)}, u32[]{:S(2)}, u32[]{:S(2)}) %collective-permute-start.3) | collective-permute-done | bytes 98336 | tf_op jit(solution)/shard_map/ppermute | solution.py:180
  43.2 0.8 bitcast_dynamic-update-slice_fusion.4
  44.0 11.2 %collective-permute-start.4 = (bf16[4,192,256]{2,1,0:T(8,128)(2,1)S(1)}, bf16[4,192,256]{2,1,0:T(8,128)(2,1)S(1)}, u32[]{:S(2)}, u32[]{:S(2)}) collective-permute-start(bf16[4,192,256]{2,1,0:T(8,128)(2,1)S(1)} %get-tuple-element.20), channel_id=1, source_target_pairs={{0,240},{8,248},{16,0},{24,8},{32,16},{40,24},{48,32},{56,40},{64,... | collective-permute-start | bytes 1179656 | tf_op jit(solution)/shard_map/ppermute | solution.py:180
  55.2 5.3 %shard_map.101 = bf16[256,768]{1,0:T(8,128)(2,1)} custom-call(bf16[768,256]{1,0:T(8,128)(2,1)} %q_ref.3, bf16[768,256]{1,0:T(8,128)(2,1)} %k_ref.3, bf16[768,256]{1,0:T(8,128)(2,1)} %v_ref.3, f32[2,128]{1,0:T(2,128)} %gains_ref.3), custom_call_target="tpu_custom_call" | custom-call | tf_op jit(solution)/shard_map/pallas_call | solution.py:56
  60.5 1.6 collective-permute-start.8
  62.2 7.6 %collective-permute-start.9 = (bf16[256,768]{1,0:T(8,128)(2,1)}, bf16[256,768]{1,0:T(8,128)(2,1)S(1)}, u32[]{:S(2)}, u32[]{:S(2)}) collective-permute-start(bf16[256,768]{1,0:T(8,128)(2,1)} %shard_map.101), channel_id=1, source_target_pairs={{0,8},{8,264},{16,24},{24,280},{32,40},{40,296},{48,56},{56,312},{... | collective-permute-start | bytes 1179656 | tf_op jit(solution)/shard_map/ppermute | solution.py:180
  69.9 1.9 collective-permute-start.7
  71.9 1.9 collective-permute-start.5
  73.8 5.5 %collective-permute-start.6 = (bf16[2,192,256]{2,1,0:T(8,128)(2,1)S(1)}, bf16[2,192,256]{2,1,0:T(8,128)(2,1)S(1)}, u32[]{:S(2)}, u32[]{:S(2)}) collective-permute-start(bf16[2,192,256]{2,1,0:T(8,128)(2,1)S(1)} %get-tuple-element.26), channel_id=1, source_target_pairs={{0,224},{8,232},{16,240},{24,248},{32,0},{40,8},{48,16},{56,24},{6... | collective-permute-start | bytes 589832 | tf_op jit(solution)/shard_map/ppermute | solution.py:180
  79.3 0.8 bitcast_dynamic-update-slice_fusion.2
  80.1 8.2 %collective-permute-done.5 = bf16[2,192,256]{2,1,0:T(8,128)(2,1)S(1)} collective-permute-done((bf16[2,192,256]{2,1,0:T(8,128)(2,1)S(1)}, bf16[2,192,256]{2,1,0:T(8,128)(2,1)S(1)}, u32[]{:S(2)}, u32[]{:S(2)}) %collective-permute-start.5) | collective-permute-done | bytes 196640 | tf_op jit(solution)/shard_map/ppermute | solution.py:180
  88.3 0.8 fusion.3
  89.1 0.8 bitcast_dynamic-update-slice_fusion
  89.8 0.8 bitcast_dynamic-update-slice_fusion.5
  90.6 0.8 bitcast_dynamic-update-slice_fusion.3
  91.4 0.8 fusion.4
  92.2 0.8 bitcast_dynamic-update-slice_fusion.1
  92.9 2.7 %constant_dynamic-slice_fusion.2.weight_ref = bf16[4,4,192,256]{3,2,1,0:T(8,128)(2,1)} fusion(bf16[8,4,192,256]{3,2,1,0:T(8,128)(2,1)} %bitcast_dynamic-update-slice_fusion.1, s32[]{:T(128)S(6)} %select_n.90), kind=kLoop, calls=%fused_computation.32 | loop fusion | bytes 3145732 | tf_op jit(solution)/shard_map/dynamic_slice | solution.py:196
  95.7 0.7 copy-done.2
  96.5 12.3 %shard_map.102 = (bf16[768,256]{1,0:T(8,128)(2,1)}, bf16[768,256]{1,0:T(8,128)(2,1)}, bf16[4,4,192,256]{3,2,1,0:T(8,128)(2,1)}) custom-call(s32[1]{0:T(128)} %bitcast.high_ref, bf16[2,8,768,384]{3,2,1,0:T(8,128)(2,1)} %bitcast.48, bf16[4,4,192,256]{3,2,1,0:T(8,128)(2,1)} %constant_dynamic-slice_fusion.2.weight_ref, bf16[256,768]{1,0:T(8,128)(2,1)} %copy-done.2, ...), custom_call_target="tpu_custom_call" | custom-call | flops 4831838208 | bytes 12582912 | tf_op jit(solution)/shard_map/pallas_call | solution.py:145
  108.8 1.2 dynamic-slice_bitcast_fusion.1
  110.0 5.1 %collective-permute-start.12 = (bf16[4,192,256]{2,1,0:T(8,128)(2,1)S(1)}, bf16[4,192,256]{2,1,0:T(8,128)(2,1)S(1)}, u32[]{:S(2)}, u32[]{:S(2)}) collective-permute-start(bf16[4,192,256]{2,1,0:T(8,128)(2,1)S(1)} %get-tuple-element.23), channel_id=1, source_target_pairs={{0,16},{8,24},{16,32},{24,40},{32,48},{40,56},{48,64},{56,72},{64,... | collective-permute-start | bytes 1179656 | tf_op jit(solution)/shard_map/ppermute | solution.py:180
  115.1 1.9 collective-permute-start.13
  117.0 1.1 dynamic-slice_bitcast_fusion.3
  118.1 3.1 %collective-permute-start.14 = (bf16[2,192,256]{2,1,0:T(8,128)(2,1)S(1)}, bf16[2,192,256]{2,1,0:T(8,128)(2,1)S(1)}, u32[]{:S(2)}, u32[]{:S(2)}) collective-permute-start(bf16[2,192,256]{2,1,0:T(8,128)(2,1)S(1)} %get-tuple-element.21), channel_id=1, source_target_pairs={{0,32},{8,40},{16,48},{24,56},{32,64},{40,72},{48,80},{56,88},{64,... | collective-permute-start | bytes 589832 | tf_op jit(solution)/shard_map/ppermute | solution.py:180
  121.2 4.3 %collective-permute-start.15 = (bf16[2,192,256]{2,1,0:T(8,128)(2,1)S(1)}, bf16[2,192,256]{2,1,0:T(8,128)(2,1)S(1)}, u32[]{:S(2)}, u32[]{:S(2)}) collective-permute-start(bf16[2,192,256]{2,1,0:T(8,128)(2,1)S(1)} %get-tuple-element.22), channel_id=1, source_target_pairs={{0,224},{8,232},{16,240},{24,248},{32,0},{40,8},{48,16},{56,24},{6... | collective-permute-start | bytes 589832 | tf_op jit(solution)/shard_map/ppermute | solution.py:180
  125.5 1.7 collective-permute-start.10
  127.1 0.8 collective-permute-done.14
  127.9 2.4 %collective-permute-start.11 = (bf16[768,256]{1,0:T(8,128)(2,1)}, bf16[768,256]{1,0:T(8,128)(2,1)S(1)}, u32[]{:S(2)}, u32[]{:S(2)}) collective-permute-start(bf16[768,256]{1,0:T(8,128)(2,1)} %get-tuple-element.13), channel_id=1, source_target_pairs={{0,256},{8,0},{16,272},{24,16},{32,288},{40,32},{48,304},{56,48},{... | collective-permute-start | bytes 1179656 | tf_op jit(solution)/shard_map/ppermute | solution.py:180
  130.4 4.4 %collective-permute-done.15 = bf16[2,192,256]{2,1,0:T(8,128)(2,1)S(1)} collective-permute-done((bf16[2,192,256]{2,1,0:T(8,128)(2,1)S(1)}, bf16[2,192,256]{2,1,0:T(8,128)(2,1)S(1)}, u32[]{:S(2)}, u32[]{:S(2)}) %collective-permute-start.15) | collective-permute-done | bytes 196640 | tf_op jit(solution)/shard_map/ppermute | solution.py:180
  134.8 1.2 fusion.2
  136.0 0.7 collective-permute-start.16
  136.7 3.3 %collective-permute-start.17 = (bf16[192,256]{1,0:T(8,128)(2,1)S(1)}, bf16[192,256]{1,0:T(8,128)(2,1)S(1)}, u32[]{:S(2)}, u32[]{:S(2)}) collective-permute-start(bf16[192,256]{1,0:T(8,128)(2,1)S(1)} %get-tuple-element.30), channel_id=1, source_target_pairs={{0,64},{8,320},{16,80},{24,336},{32,96},{40,352},{48,112},{56,368}... | collective-permute-start | bytes 294920 | tf_op jit(solution)/shard_map/ppermute | solution.py:180
  140.0 9.1 %collective-permute-start.18 = (bf16[192,256]{1,0:T(8,128)(2,1)S(1)}, bf16[192,256]{1,0:T(8,128)(2,1)S(1)}, u32[]{:S(2)}, u32[]{:S(2)}) collective-permute-start(bf16[192,256]{1,0:T(8,128)(2,1)S(1)} %get-tuple-element.29), channel_id=1, source_target_pairs={{0,128},{8,384},{16,144},{24,400},{32,160},{40,416},{48,176},{56,4... | collective-permute-start | bytes 294920 | tf_op jit(solution)/shard_map/ppermute | solution.py:180
  149.1 4.4 %collective-permute-start.19 = (bf16[192,256]{1,0:T(8,128)(2,1)S(1)}, bf16[192,256]{1,0:T(8,128)(2,1)S(1)}, u32[]{:S(2)}, u32[]{:S(2)}) collective-permute-start(bf16[192,256]{1,0:T(8,128)(2,1)S(1)} %get-tuple-element.28), channel_id=1, source_target_pairs={{0,192},{8,448},{16,208},{24,464},{32,224},{40,480},{48,240},{56,4... | collective-permute-start | bytes 294920 | tf_op jit(solution)/shard_map/ppermute | solution.py:180
  153.5 0.7 copy-done.1
  154.2 7.4 %shard_map.103 = (bf16[768,256]{1,0:T(8,128)(2,1)}, bf16[768,256]{1,0:T(8,128)(2,1)}, bf16[768,256]{1,0:T(8,128)(2,1)}, f32[2,128]{1,0:T(2,128)}) custom-call(bf16[768,256]{1,0:T(8,128)(2,1)} %q_ref.3, bf16[768,256]{1,0:T(8,128)(2,1)} %k_ref.3, bf16[768,256]{1,0:T(8,128)(2,1)} %v_ref.3, bf16[768,256]{1,0:T(8,128)(2,1)} %copy-done, ...), custom_call_target="tpu_custom_call" | custom-call | tf_op jit(solution)/shard_map/pallas_call | solution.py:102
  161.6 0.7 broadcast_in_dim.4
  162.3 17.1 %all_to_all.10 = f32[16,2,128]{2,1,0:T(2,128)S(1)} all-to-all(f32[16,2,128]{2,1,0:T(2,128)S(1)} %broadcast_in_dim.4), channel_id=1, replica_groups=mesh['yl'=2,'z'=16,'yh'=2,'x'=4,'c'=2] {'z'}, dimensions={0} | all-to-all | bytes 32768 | tf_op jit(solution)/shard_map/all_to_all | solution.py:222
  179.4 21.5 %all_to_all.11 = f32[32,2,128]{2,1,0:T(2,128)S(1)} all-to-all(f32[32,2,128]{2,1,0:T(2,128)S(1)} %broadcast_in_dim.5), channel_id=1, replica_groups=mesh['yl'=2,'z'=16,'yh'=2,'x'=4,'c'=2] {'yl','yh','x','c'}, dimensions={0} | all-to-all | bytes 65536 | tf_op jit(solution)/shard_map/all_to_all | solution.py:222
  200.9 0.6 reduce_sum.19
  201.6 0.7 convert_add_fusion.1
  (35 shorter events, 0.4 us)
Async XLA Ops:
  7.2 88.5 %all-gather.3.cloned.1.call-start = ((), (), s32[]{:S(2)}) async-start(), calls=%async_computation.2 | async-start | bytes 10027008 | tf_op jit(solution)/shard_map/all_gather | solution.py:229
  7.9 27.1 %collective-permute-start = (bf16[192,256]{1,0:T(8,128)(2,1)}, bf16[192,256]{1,0:T(8,128)(2,1)S(1)}, u32[]{:S(2)}, u32[]{:S(2)}) collective-permute-start(bf16[192,256]{1,0:T(8,128)(2,1)} %param.10), channel_id=1, source_target_pairs={{0,0},{8,256},{16,16},{24,272},{32,32},{40,288},{48,48},{56,304},{... | collective-permute-start | bytes 294920 | tf_op jit(solution)/shard_map/ppermute | solution.py:180
  9.4 25.5 %collective-permute-start.1 = (bf16[192,256]{1,0:T(8,128)(2,1)}, bf16[192,256]{1,0:T(8,128)(2,1)S(1)}, u32[]{:S(2)}, u32[]{:S(2)}) collective-permute-start(bf16[192,256]{1,0:T(8,128)(2,1)} %param.10), channel_id=1, source_target_pairs={{0,192},{8,448},{16,208},{24,464},{32,224},{40,480},{48,240},{56,4... | collective-permute-start | bytes 294920 | tf_op jit(solution)/shard_map/ppermute | solution.py:180
  22.7 14.8 %collective-permute-start.2 = (bf16[192,256]{1,0:T(8,128)(2,1)}, bf16[192,256]{1,0:T(8,128)(2,1)S(1)}, u32[]{:S(2)}, u32[]{:S(2)}) collective-permute-start(bf16[192,256]{1,0:T(8,128)(2,1)} %param.10), channel_id=1, source_target_pairs={{0,128},{8,384},{16,144},{24,400},{32,160},{40,416},{48,176},{56,4... | collective-permute-start | bytes 294920 | tf_op jit(solution)/shard_map/ppermute | solution.py:180
  27.6 15.4 %collective-permute-start.3 = (bf16[192,256]{1,0:T(8,128)(2,1)}, bf16[192,256]{1,0:T(8,128)(2,1)S(1)}, u32[]{:S(2)}, u32[]{:S(2)}) collective-permute-start(bf16[192,256]{1,0:T(8,128)(2,1)} %param.10), channel_id=1, source_target_pairs={{0,64},{8,320},{16,80},{24,336},{32,96},{40,352},{48,112},{56,368}... | collective-permute-start | bytes 294920 | tf_op jit(solution)/shard_map/ppermute | solution.py:180
  44.0 29.8 %collective-permute-start.4 = (bf16[4,192,256]{2,1,0:T(8,128)(2,1)S(1)}, bf16[4,192,256]{2,1,0:T(8,128)(2,1)S(1)}, u32[]{:S(2)}, u32[]{:S(2)}) collective-permute-start(bf16[4,192,256]{2,1,0:T(8,128)(2,1)S(1)} %get-tuple-element.20), channel_id=1, source_target_pairs={{0,240},{8,248},{16,0},{24,8},{32,16},{40,24},{48,32},{56,40},{64,... | collective-permute-start | bytes 1179656 | tf_op jit(solution)/shard_map/ppermute | solution.py:180
  60.5 35.1 %collective-permute-start.8 = (bf16[256,768]{1,0:T(8,128)(2,1)}, bf16[256,768]{1,0:T(8,128)(2,1)S(1)}, u32[]{:S(2)}, u32[]{:S(2)}) collective-permute-start(bf16[256,768]{1,0:T(8,128)(2,1)} %shard_map.101), channel_id=1, source_target_pairs={{0,0},{8,256},{16,16},{24,272},{32,32},{40,288},{48,48},{56,304},{... | collective-permute-start | bytes 1179656 | tf_op jit(solution)/shard_map/ppermute | solution.py:180
  62.2 33.5 %collective-permute-start.9 = (bf16[256,768]{1,0:T(8,128)(2,1)}, bf16[256,768]{1,0:T(8,128)(2,1)S(1)}, u32[]{:S(2)}, u32[]{:S(2)}) collective-permute-start(bf16[256,768]{1,0:T(8,128)(2,1)} %shard_map.101), channel_id=1, source_target_pairs={{0,8},{8,264},{16,24},{24,280},{32,40},{40,296},{48,56},{56,312},{... | collective-permute-start | bytes 1179656 | tf_op jit(solution)/shard_map/ppermute | solution.py:180
  69.9 19.1 %collective-permute-start.7 = (bf16[4,192,256]{2,1,0:T(8,128)(2,1)S(1)}, bf16[4,192,256]{2,1,0:T(8,128)(2,1)S(1)}, u32[]{:S(2)}, u32[]{:S(2)}) collective-permute-start(bf16[4,192,256]{2,1,0:T(8,128)(2,1)S(1)} %get-tuple-element.20), channel_id=1, source_target_pairs={{0,16},{8,24},{16,32},{24,40},{32,48},{40,56},{48,64},{56,72},{64,... | collective-permute-start | bytes 1179656 | tf_op jit(solution)/shard_map/ppermute | solution.py:180
  71.9 16.4 %collective-permute-start.5 = (bf16[2,192,256]{2,1,0:T(8,128)(2,1)S(1)}, bf16[2,192,256]{2,1,0:T(8,128)(2,1)S(1)}, u32[]{:S(2)}, u32[]{:S(2)}) collective-permute-start(bf16[2,192,256]{2,1,0:T(8,128)(2,1)S(1)} %get-tuple-element.25), channel_id=1, source_target_pairs={{0,32},{8,40},{16,48},{24,56},{32,64},{40,72},{48,80},{56,88},{64,... | collective-permute-start | bytes 589832 | tf_op jit(solution)/shard_map/ppermute | solution.py:180
  73.8 14.4 %collective-permute-start.6 = (bf16[2,192,256]{2,1,0:T(8,128)(2,1)S(1)}, bf16[2,192,256]{2,1,0:T(8,128)(2,1)S(1)}, u32[]{:S(2)}, u32[]{:S(2)}) collective-permute-start(bf16[2,192,256]{2,1,0:T(8,128)(2,1)S(1)} %get-tuple-element.26), channel_id=1, source_target_pairs={{0,224},{8,232},{16,240},{24,248},{32,0},{40,8},{48,16},{56,24},{6... | collective-permute-start | bytes 589832 | tf_op jit(solution)/shard_map/ppermute | solution.py:180
  95.7 0.7 copy-start.2
  95.7 0.9 copy-start.3
  110.0 24.8 %collective-permute-start.12 = (bf16[4,192,256]{2,1,0:T(8,128)(2,1)S(1)}, bf16[4,192,256]{2,1,0:T(8,128)(2,1)S(1)}, u32[]{:S(2)}, u32[]{:S(2)}) collective-permute-start(bf16[4,192,256]{2,1,0:T(8,128)(2,1)S(1)} %get-tuple-element.23), channel_id=1, source_target_pairs={{0,16},{8,24},{16,32},{24,40},{32,48},{40,56},{48,64},{56,72},{64,... | collective-permute-start | bytes 1179656 | tf_op jit(solution)/shard_map/ppermute | solution.py:180
  115.1 19.7 %collective-permute-start.13 = (bf16[4,192,256]{2,1,0:T(8,128)(2,1)S(1)}, bf16[4,192,256]{2,1,0:T(8,128)(2,1)S(1)}, u32[]{:S(2)}, u32[]{:S(2)}) collective-permute-start(bf16[4,192,256]{2,1,0:T(8,128)(2,1)S(1)} %get-tuple-element.24), channel_id=1, source_target_pairs={{0,240},{8,248},{16,0},{24,8},{32,16},{40,24},{48,32},{56,40},{64,... | collective-permute-start | bytes 1179656 | tf_op jit(solution)/shard_map/ppermute | solution.py:180
  118.1 9.9 %collective-permute-start.14 = (bf16[2,192,256]{2,1,0:T(8,128)(2,1)S(1)}, bf16[2,192,256]{2,1,0:T(8,128)(2,1)S(1)}, u32[]{:S(2)}, u32[]{:S(2)}) collective-permute-start(bf16[2,192,256]{2,1,0:T(8,128)(2,1)S(1)} %get-tuple-element.21), channel_id=1, source_target_pairs={{0,32},{8,40},{16,48},{24,56},{32,64},{40,72},{48,80},{56,88},{64,... | collective-permute-start | bytes 589832 | tf_op jit(solution)/shard_map/ppermute | solution.py:180
  121.2 13.6 %collective-permute-start.15 = (bf16[2,192,256]{2,1,0:T(8,128)(2,1)S(1)}, bf16[2,192,256]{2,1,0:T(8,128)(2,1)S(1)}, u32[]{:S(2)}, u32[]{:S(2)}) collective-permute-start(bf16[2,192,256]{2,1,0:T(8,128)(2,1)S(1)} %get-tuple-element.22), channel_id=1, source_target_pairs={{0,224},{8,232},{16,240},{24,248},{32,0},{40,8},{48,16},{56,24},{6... | collective-permute-start | bytes 589832 | tf_op jit(solution)/shard_map/ppermute | solution.py:180
  125.5 23.6 %collective-permute-start.10 = (bf16[768,256]{1,0:T(8,128)(2,1)}, bf16[768,256]{1,0:T(8,128)(2,1)S(1)}, u32[]{:S(2)}, u32[]{:S(2)}) collective-permute-start(bf16[768,256]{1,0:T(8,128)(2,1)} %get-tuple-element.12), channel_id=1, source_target_pairs={{0,0},{8,256},{16,16},{24,272},{32,32},{40,288},{48,48},{56,304},{... | collective-permute-start | bytes 1179656 | tf_op jit(solution)/shard_map/ppermute | solution.py:180
  127.9 25.6 %collective-permute-start.11 = (bf16[768,256]{1,0:T(8,128)(2,1)}, bf16[768,256]{1,0:T(8,128)(2,1)S(1)}, u32[]{:S(2)}, u32[]{:S(2)}) collective-permute-start(bf16[768,256]{1,0:T(8,128)(2,1)} %get-tuple-element.13), channel_id=1, source_target_pairs={{0,256},{8,0},{16,272},{24,16},{32,288},{40,32},{48,304},{56,48},{... | collective-permute-start | bytes 1179656 | tf_op jit(solution)/shard_map/ppermute | solution.py:180
  136.0 65.5 %collective-permute-start.16 = (bf16[192,256]{1,0:T(8,128)(2,1)S(1)}, bf16[192,256]{1,0:T(8,128)(2,1)S(1)}, u32[]{:S(2)}, u32[]{:S(2)}) collective-permute-start(bf16[192,256]{1,0:T(8,128)(2,1)S(1)} %get-tuple-element.27), channel_id=1, source_target_pairs={{0,0},{8,256},{16,16},{24,272},{32,32},{40,288},{48,48},{56,304},{... | collective-permute-start | bytes 294920 | tf_op jit(solution)/shard_map/ppermute | solution.py:180
  136.7 64.9 %collective-permute-start.17 = (bf16[192,256]{1,0:T(8,128)(2,1)S(1)}, bf16[192,256]{1,0:T(8,128)(2,1)S(1)}, u32[]{:S(2)}, u32[]{:S(2)}) collective-permute-start(bf16[192,256]{1,0:T(8,128)(2,1)S(1)} %get-tuple-element.30), channel_id=1, source_target_pairs={{0,64},{8,320},{16,80},{24,336},{32,96},{40,352},{48,112},{56,368}... | collective-permute-start | bytes 294920 | tf_op jit(solution)/shard_map/ppermute | solution.py:180
  140.0 61.6 %collective-permute-start.18 = (bf16[192,256]{1,0:T(8,128)(2,1)S(1)}, bf16[192,256]{1,0:T(8,128)(2,1)S(1)}, u32[]{:S(2)}, u32[]{:S(2)}) collective-permute-start(bf16[192,256]{1,0:T(8,128)(2,1)S(1)} %get-tuple-element.29), channel_id=1, source_target_pairs={{0,128},{8,384},{16,144},{24,400},{32,160},{40,416},{48,176},{56,4... | collective-permute-start | bytes 294920 | tf_op jit(solution)/shard_map/ppermute | solution.py:180
  149.1 4.4 %copy-start = (bf16[768,256]{1,0:T(8,128)(2,1)}, bf16[768,256]{1,0:T(8,128)(2,1)S(1)}, u32[]{:S(2)}) copy-start(bf16[768,256]{1,0:T(8,128)(2,1)S(1)} %collective-permute-done.10.one_ref) | copy-start | bytes 1179652
  149.1 52.5 %collective-permute-start.19 = (bf16[192,256]{1,0:T(8,128)(2,1)S(1)}, bf16[192,256]{1,0:T(8,128)(2,1)S(1)}, u32[]{:S(2)}, u32[]{:S(2)}) collective-permute-start(bf16[192,256]{1,0:T(8,128)(2,1)S(1)} %get-tuple-element.28), channel_id=1, source_target_pairs={{0,192},{8,448},{16,208},{24,464},{32,224},{40,480},{48,240},{56,4... | collective-permute-start | bytes 294920 | tf_op jit(solution)/shard_map/ppermute | solution.py:180
  153.5 0.8 copy-start.1
Sparse Core Ops, SparseCore 0:
  10.1 78.1 all-gather.2

commit v3 on v2

v3 whole, which is shorter than its diff:
```python
import jax
import jax.numpy as jnp
from jax import lax
from jax.experimental import pallas as pl
from jax.experimental.pallas import tpu as pltpu
from jax.sharding import Mesh, PartitionSpec as P

HD = 128
PATCH = 256
EPSILON = 1e-06
SCALE = HD ** (-0.5)
AXES = ("yl", "za", "zb", "yh", "x", "c")
SIZES = (2, 8, 2, 2, 4, 2)
VMEM_LIMIT = 56 * 1024 * 1024


def normalize(raw, gain):
    values32 = raw.astype(jnp.float32)
    center = values32 - jnp.mean(values32, axis=-1, keepdims=True)
    inverse = lax.rsqrt(jnp.mean(center * center, axis=-1, keepdims=True) + EPSILON)
    unit = center * inverse
    return (unit, inverse, (unit * gain).astype(jnp.bfloat16))


def unnormalize(grad, unit, inverse, gain):
    scaled = grad * gain
    centered = scaled - jnp.mean(scaled, axis=-1, keepdims=True)
    return (centered - unit * jnp.mean(scaled * unit, axis=-1, keepdims=True)) * inverse


def product(left, right, left_dim, right_dim):
    return lax.dot_general(
        left, right, (((left_dim,), (right_dim,)), ((), ())), preferred_element_type=jnp.float32
    )


def softmax(q_norm, k_norm):
    scores = product(q_norm, k_norm, 1, 1) * SCALE
    expo = jnp.exp(scores - jnp.max(scores, axis=-1, keepdims=True))
    return expo / jnp.sum(expo, axis=-1, keepdims=True)


def forward_kernel(q_ref, k_ref, v_ref, gains_ref, attn_ref):
    for head in range(q_ref.shape[1] // HD):
        cols = slice(head * HD, (head + 1) * HD)
        _, _, q_norm = normalize(q_ref[:, cols], gains_ref[0:1, :])
        _, _, k_norm = normalize(k_ref[:, cols], gains_ref[1:2, :])
        prob_low = softmax(q_norm, k_norm).astype(jnp.bfloat16)
        attn_ref[:, cols] = product(prob_low, v_ref[:, cols], 1, 0).astype(jnp.bfloat16)


def forward(queries_raw, keys_raw, values, norm_gains):
    tokens, width = queries_raw.shape
    block = pl.BlockSpec((PATCH, width), lambda i: (i, 0))
    return pl.pallas_call(
        forward_kernel,
        grid=(tokens // PATCH,),
        in_specs=[block, block, block, pl.BlockSpec((2, HD), lambda i: (0, 0))],
        out_specs=block,
        out_shape=jax.ShapeDtypeStruct((tokens, width), jnp.bfloat16),
        compiler_params=pltpu.CompilerParams(vmem_limit_bytes=VMEM_LIMIT),
    )(queries_raw, keys_raw, values, norm_gains)


def backward_kernel(
    q_ref, k_ref, v_ref, p0_ref, p1_ref, p2_ref, p3_ref, gains_ref,
    qg_ref, kg_ref, vg_ref, terms_ref,
):
    @pl.when(pl.program_id(0) == 0)
    def _():
        terms_ref[...] = jnp.zeros_like(terms_ref)

    q_gain, k_gain = gains_ref[0:1, :], gains_ref[1:2, :]
    for head in range(q_ref.shape[1] // HD):
        cols = slice(head * HD, (head + 1) * HD)
        value = v_ref[:, cols]
        q_unit, q_inverse, q_norm = normalize(q_ref[:, cols], q_gain)
        k_unit, k_inverse, k_norm = normalize(k_ref[:, cols], k_gain)
        prob = softmax(q_norm, k_norm)
        prob_low = prob.astype(jnp.bfloat16)
        attn = product(prob_low, value, 1, 0).astype(jnp.bfloat16)
        grad = sum(ref[cols, :].astype(jnp.float32) for ref in (p0_ref, p1_ref, p2_ref, p3_ref))
        grad = grad.T.astype(jnp.bfloat16)
        vg_ref[:, cols] = product(prob_low, grad, 0, 0).astype(jnp.bfloat16)
        delta = jnp.sum(
            grad.astype(jnp.float32) * attn.astype(jnp.float32), axis=-1, keepdims=True
        )
        score_grad = (prob * (product(grad, value, 1, 1) - delta)).astype(jnp.bfloat16)
        qn_grad = product(score_grad, k_norm, 1, 0) * SCALE
        kn_grad = product(score_grad, q_norm, 0, 0) * SCALE
        terms_ref[0:1, :] += jnp.sum(qn_grad * q_unit, axis=0, keepdims=True)
        terms_ref[1:2, :] += jnp.sum(kn_grad * k_unit, axis=0, keepdims=True)
        qg_ref[:, cols] = unnormalize(qn_grad, q_unit, q_inverse, q_gain).astype(jnp.bfloat16)
        kg_ref[:, cols] = unnormalize(kn_grad, k_unit, k_inverse, k_gain).astype(jnp.bfloat16)


def backward(queries_raw, keys_raw, values, parts, norm_gains):
    tokens, width = queries_raw.shape
    block = pl.BlockSpec((PATCH, width), lambda i: (i, 0))
    part = pl.BlockSpec((width, PATCH), lambda i: (0, i))
    gains = pl.BlockSpec((2, HD), lambda i: (0, 0))
    out = jax.ShapeDtypeStruct((tokens, width), jnp.bfloat16)
    return pl.pallas_call(
        backward_kernel,
        grid=(tokens // PATCH,),
        in_specs=[block] * 3 + [part] * 4 + [gains],
        out_specs=[block, block, block, gains],
        out_shape=[out, out, out, jax.ShapeDtypeStruct((2, HD), jnp.float32)],
        compiler_params=pltpu.CompilerParams(vmem_limit_bytes=VMEM_LIMIT),
    )(queries_raw, keys_raw, values, *parts, norm_gains)


def flip_kernel(parity_ref, grad_ref, keep_ref, give_ref, flipped):
    rows = keep_ref.shape[0]
    for half in range(2):
        block = grad_ref[...].T[half * rows : (half + 1) * rows]
        flipped[half] = block
    keep_ref[...] = flipped[parity_ref[0]]
    give_ref[...] = flipped[1 - parity_ref[0]]


def flip(parity, grad_out):
    tokens, width = grad_out.shape
    half = jax.ShapeDtypeStruct((width // 2, tokens), grad_out.dtype)
    return pl.pallas_call(
        flip_kernel,
        in_specs=[pl.BlockSpec(memory_space=pltpu.SMEM), pl.BlockSpec(memory_space=pltpu.VMEM)],
        out_specs=[pl.BlockSpec(memory_space=pltpu.VMEM)] * 2,
        out_shape=[half, half],
        scratch_shapes=[pltpu.VMEM((2, width // 2, tokens), grad_out.dtype)],
        compiler_params=pltpu.CompilerParams(vmem_limit_bytes=VMEM_LIMIT),
    )(parity, grad_out)


def products_kernel(
    high_ref, grad_ref, weight_ref, same_ref, other_ref, ps0_ref, ps1_ref, po0_ref, po1_ref,
    wgrad_ref, total,
):
    step = pl.program_id(0)

    @pl.when(step == 0)
    def _():
        total[...] = jnp.zeros_like(total)

    high = high_ref[0]
    weights = weight_ref[0].T
    wgrad = None
    for index, (low, attn_ref) in enumerate(((high, same_ref), (1 - high, other_ref))):
        for z in range(2):
            block = grad_ref[low, 0, z]
            term = product(block, attn_ref[z], 1, 0)
            wgrad = term if wgrad is None else wgrad + term
            total[index * 2 + z] += product(weights, block, 1, 0)
    wgrad_ref[0] = wgrad.astype(wgrad_ref.dtype)

    @pl.when(step == pl.num_programs(0) - 1)
    def _():
        for index, ref in enumerate((ps0_ref, ps1_ref, po0_ref, po1_ref)):
            ref[...] = total[index].astype(ref.dtype)


def products(high, grads, weights, attn_same, attn_other):
    _, blocks, _, rows, tokens = grads.shape
    heads = weights.shape[2]
    slab = pl.BlockSpec((1, rows, heads), lambda k, high: (k, 0, 0))
    attn = pl.BlockSpec((2, tokens, heads), lambda k, high: (0, 0, 0))
    part = pl.BlockSpec((heads, tokens), lambda k, high: (0, 0))
    return pl.pallas_call(
        products_kernel,
        grid_spec=pltpu.PrefetchScalarGridSpec(
            num_scalar_prefetch=1,
            grid=(blocks,),
            in_specs=[
                pl.BlockSpec((2, 1, 2, rows, tokens), lambda k, high: (0, k, 0, 0, 0)),
                slab,
                attn,
                attn,
            ],
            out_specs=[part] * 4 + [slab],
            scratch_shapes=[pltpu.VMEM((4, heads, tokens), jnp.float32)],
        ),
        out_shape=[jax.ShapeDtypeStruct((heads, tokens), jnp.bfloat16)] * 4
        + [jax.ShapeDtypeStruct(weights.shape, jnp.bfloat16)],
        compiler_params=pltpu.CompilerParams(vmem_limit_bytes=VMEM_LIMIT),
        cost_estimate=pl.CostEstimate(
            flops=16 * blocks * tokens * rows * heads,
            bytes_accessed=2 * (4 * blocks * tokens * rows + 2 * blocks * rows * heads),
            transcendentals=0,
        ),
    )(high, grads, weights, attn_same, attn_other)


def permute(array, target):
    pairs = []
    for low in range(2):
        for z in range(2):
            for high in range(2):
                to_low, to_z, to_high = target(low, z, high)
                pairs.append(((low * 2 + z) * 2 + high, (to_low * 2 + to_z) * 2 + to_high))
    return lax.ppermute(array, ("yl", "zb", "yh"), pairs)


def turned(array):
    return permute(array, lambda low, z, high: (high, z, low))


def beside(array):
    return permute(array, lambda low, z, high: (low, 1 - z, high))


def sum_over(array, axis, count):
    spread = lax.all_to_all(jnp.broadcast_to(array[None], (count,) + array.shape), axis, 0, 0)
    return jnp.sum(spread, axis=0)


def per_device(queries_raw, keys_raw, values, grad_out, out_weight, norm_gains):
    high = lax.axis_index("yh").reshape(1)
    parity = lax.axis_index("zb").reshape(1)
    keep, give = flip(parity, grad_out)
    mine = jnp.stack([keep, beside(give)])
    grads = lax.all_gather(mine, ("yl", "x", "c"), axis=0)
    grads = grads.reshape((2, 8) + mine.shape)
    own_rows, _ = lax.optimization_barrier((turned(out_weight), mine))
    weights = lax.all_gather(own_rows, "za", axis=0)

    attn = forward(queries_raw, keys_raw, values, norm_gains)
    attn = jnp.stack([attn, beside(attn)])
    attn_same = turned(attn)
    attn_other = permute(attn, lambda low, z, up: (up, z, 1 - low))

    ps0, ps1, po0, po1, wgrad = products(high, grads, weights, attn_same, attn_other)
    shard = lax.psum_scatter(wgrad, "za", scatter_dimension=0)
    parts = [
        turned(ps0),
        permute(ps1, lambda low, z, up: (up, 1 - z, low)),
        permute(po0, lambda low, z, up: (1 - up, z, low)),
        permute(po1, lambda low, z, up: (1 - up, 1 - z, low)),
    ]
    queries_grad, keys_grad, values_grad, terms = backward(
        queries_raw, keys_raw, values, parts, norm_gains
    )
    gains_grad = sum_over(sum_over(terms, ("yl", "yh", "x", "c"), 32), ("za", "zb"), 16)
    weight_grad = turned(shard).astype(jnp.float32)
    return (queries_grad, keys_grad, values_grad, weight_grad, gains_grad)


def solution(mesh):
    fine = Mesh(mesh.devices.reshape(SIZES), AXES)
    spec = P(("yl", "za", "zb"), ("yh", "x", "c"))
    return jax.shard_map(
        per_device,
        mesh=fine,
        in_specs=(spec, spec, spec, spec, spec, P()),
        out_specs=(spec, spec, spec, spec, P()),
        check_vma=False,
    )
```

time: 210 us -> 238 us (1.13)
  waiting for transfers between devices: 22.1 us -> 73.5 us
  starting transfers between devices: 92.7 us -> 42.3 us
  blocking collectives: 38.6 us -> 73.2 us
  local copies, waits for them, and re-layouts: 12.1 us -> 2.45 us
    ppermute x20 -> x10, starting transfers between devices: 92.7 us -> 42.2 us  [permute(): return lax.ppermute(array, ('yl', 'zb', 'yh'), pairs)]
    reduce_scatter x0 -> x1, waiting for transfers between devices: none -> 38.9 us  [per_device(): shard = lax.psum_scatter(wgrad, 'za', scatter_dimension=0)]
    all_gather x0 -> x1, blocking collectives: none -> 35.4 us  [per_device(): weights = lax.all_gather(own_rows, 'za', axis=0)]
    all_gather x1, waiting for transfers between devices: 0.02 us -> 24.9 us  [per_device(): grads = lax.all_gather(mine, ('yl', 'x', 'c'), axis=0)]
    ppermute x20 -> x10, waiting for transfers between devices: 21.4 us -> 9.69 us  [permute(): return lax.ppermute(array, ('yl', 'zb', 'yh'), pairs)]
    unnamed x20 -> x12, local copies, waits for them, and re-layouts: 5.59 us -> 1.75 us
    another operation x0 -> x2, other arithmetic: none -> 2.9 us  [the longest x1 1.83 us: per_device(): mine = jnp.stack([keep, beside(give)])]
    dynamic_slice x1 -> x0, local copies, waits for them, and re-layouts: 2.71 us -> none  [rolled(): lax.dynamic_slice_in_dim(jnp.stack(blocks + blocks), (4 - shift) % 4, 4,...]
  transfers between devices with their start and end apart: 21 -> 12, of which waited for: 5 -> 4; matrix products, arithmetic and copies ran while one was open for 6% -> 1% of each run, Pallas kernels for 6% -> 5%
where the time goes in v3:
time: 238 us; the launch traced here: 237 us
  waiting for transfers between devices  73.5 us (31%)
  blocking collectives  73.2 us (31%)
  starting transfers between devices  42.3 us (18%)
  Pallas kernels  27.3 us (11%)
  between operations  14.2 us (6%)
  other arithmetic  4.22 us (2%)
  local copies, waits for them, and re-layouts  2.45 us (1%)
    ppermute x10, starting transfers between devices, permute(): return lax.ppermute(array, ('yl', 'zb', 'yh'), pairs)  42.2 us
    reduce_scatter x1, waiting for transfers between devices, per_device(): shard = lax.psum_scatter(wgrad, 'za', scatter_dimension=0)  38.9 us
    all_to_all x2, blocking collectives, sum_over(): lax.all_to_all(jnp.broadcast_to(array[None], (count,) + array.shape), axi...  37.8 us
    all_gather x1, blocking collectives, per_device(): weights = lax.all_gather(own_rows, 'za', axis=0)  35.4 us
    all_gather x1, waiting for transfers between devices, per_device(): grads = lax.all_gather(mine, ('yl', 'x', 'c'), axis=0)  24.9 us
    pallas_call x1, Pallas kernels, products(): pl.pallas_call(products_kernel, grid_spec=pltpu.PrefetchScalarGridSpec(nu...  12.2 us
    ppermute x10, waiting for transfers between devices, permute(): return lax.ppermute(array, ('yl', 'zb', 'yh'), pairs)  9.69 us
    pallas_call x1, Pallas kernels, backward(): pl.pallas_call(backward_kernel, grid=(tokens // PATCH,), in_specs=[block]...  7.94 us
  transfers between devices with their start and end apart: 12, of which 4 were waited for; matrix products, arithmetic and copies ran while one was open for 1% of the time, Pallas kernels for 5%

profile of v3, /device:TPU:1, one launch (start us, length us, event | category | flops | bytes accessed | tf_op | source)
XLA Modules:
  0.0 237.2 jit_solution(9280113511448481547)
XLA Ops:
  7.2 0.0 all-gather.4.cloned.1.call-start
  7.2 2.2 shard_map.101
  9.4 4.4 %collective-permute-start = (bf16[192,768]{1,0:T(8,128)(2,1)}, bf16[192,768]{1,0:T(8,128)(2,1)S(1)}, u32[]{:S(2)}, u32[]{:S(2)}) collective-permute-start(bf16[192,768]{1,0:T(8,128)(2,1)} %get-tuple-element.18), channel_id=1, source_target_pairs={{0,16},{8,24},{16,0},{24,8},{256,272},{264,280},{272,256},{280,264... | collective-permute-start | bytes 884744 | tf_op jit(solution)/shard_map/ppermute | solution.py:200
  13.7 4.3 %collective-permute-done = bf16[192,768]{1,0:T(8,128)(2,1)S(1)} collective-permute-done((bf16[192,768]{1,0:T(8,128)(2,1)}, bf16[192,768]{1,0:T(8,128)(2,1)S(1)}, u32[]{:S(2)}, u32[]{:S(2)}) %collective-permute-start) | collective-permute-done | bytes 294944 | tf_op jit(solution)/shard_map/ppermute | solution.py:200
  18.0 1.8 pad_maximum_fusion.1
  19.9 0.0 all-gather.4.cloned.1.call-update
  19.9 0.0 reduce-scatter.2.cloned.1.call-start
  20.0 5.1 %shard_map.102 = bf16[768,256]{1,0:T(8,128)(2,1)} custom-call(bf16[768,256]{1,0:T(8,128)(2,1)} %q_ref.3, bf16[768,256]{1,0:T(8,128)(2,1)} %k_ref.3, bf16[768,256]{1,0:T(8,128)(2,1)} %v_ref.3, f32[2,128]{1,0:T(2,128)} %gains_ref.3), custom_call_target="tpu_custom_call" | custom-call | tf_op jit(solution)/shard_map/pallas_call | solution.py:55
  25.0 3.3 %collective-permute-start.2 = (bf16[768,256]{1,0:T(8,128)(2,1)}, bf16[768,256]{1,0:T(8,128)(2,1)S(1)}, u32[]{:S(2)}, u32[]{:S(2)}) collective-permute-start(bf16[768,256]{1,0:T(8,128)(2,1)} %shard_map.102), channel_id=1, source_target_pairs={{0,16},{8,24},{16,0},{24,8},{256,272},{264,280},{272,256},{280,264... | collective-permute-start | bytes 1179656 | tf_op jit(solution)/shard_map/ppermute | solution.py:200
  28.4 5.4 %collective-permute-done.2 = bf16[768,256]{1,0:T(8,128)(2,1)S(1)} collective-permute-done((bf16[768,256]{1,0:T(8,128)(2,1)}, bf16[768,256]{1,0:T(8,128)(2,1)S(1)}, u32[]{:S(2)}, u32[]{:S(2)}) %collective-permute-start.2) | collective-permute-done | bytes 393248 | tf_op jit(solution)/shard_map/ppermute | solution.py:200
  33.8 1.1 pad_maximum_fusion
  34.8 10.0 %collective-permute-start.4 = (bf16[2,768,256]{2,1,0:T(8,128)(2,1)S(1)}, bf16[2,768,256]{2,1,0:T(8,128)(2,1)S(1)}, u32[]{:S(2)}, u32[]{:S(2)}) collective-permute-start(bf16[2,768,256]{2,1,0:T(8,128)(2,1)S(1)} %pad_maximum_fusion), channel_id=1, source_target_pairs={{0,8},{8,264},{16,24},{24,280},{256,0},{264,256},{272,16},{280,272... | collective-permute-start | bytes 2359304 | tf_op jit(solution)/shard_map/ppermute | solution.py:200
  44.8 0.7 collective-permute-start.3
  45.5 1.6 collective-permute-start.1
  47.1 0.0 collective-permute-done.1
  47.1 35.4 %all-gather.1 = bf16[1536,256]{1,0:T(8,128)(2,1)} all-gather(bf16[192,256]{1,0:T(8,128)(2,1)S(1)} %collective-permute-done.1), channel_id=3, replica_groups=mesh['yl'=2,'za'=8,'zb'=2,'yh'=2,'x'=4,'c'=2] {'za'}, dimensions={0}, use_global_device_ids=true | all-gather | bytes 884736 | tf_op jit(solution)/shard_map/all_gather | solution.py:224
  82.5 0.0 collective-permute-done.4.other_ref
  82.5 0.0 copy-start.4
  82.5 0.0 collective-permute-done.3.same_ref
  82.5 0.0 copy-start.5
  82.5 24.9 %all-gather.4.cloned.1.call-done = bf16[32,192,768]{2,1,0:T(8,128)(2,1)} async-done(((bf16[2,192,768]{2,1,0:T(8,128)(2,1)}), bf16[32,192,768]{2,1,0:T(8,128)(2,1)}) %all-gather.4.cloned.1.call-update) | async-done | bytes 9437200 | tf_op jit(solution)/shard_map/all_gather | solution.py:221
  107.4 0.0 copy-done.4
  107.4 0.0 copy-done.5
  107.4 12.2 %shard_map.103 = (bf16[256,768]{1,0:T(8,128)(2,1)}, bf16[256,768]{1,0:T(8,128)(2,1)}, bf16[256,768]{1,0:T(8,128)(2,1)}, bf16[256,768]{1,0:T(8,128)(2,1)}, bf16[8,192,256]{2,1,0:T(8,128)(2,1)}) custom-call(s32[1]{0:T(128)} %bitcast.high_ref, bf16[2,8,2,192,768]{4,3,2,1,0:T(8,128)(2,1)} %bitcast.14, bf16[8,192,256]{2,1,0:T(8,128)(2,1)} %bitcast.10, ...), custom_call_target="tpu_custom_call" | custom-call | flops 4831838208 | bytes 11010048 | tf_op jit(solution)/shard_map/pallas_call | solution.py:168
  119.6 0.0 reduce-scatter.2.cloned.1.call-update
  119.6 1.7 collective-permute-start.5
  121.2 2.9 %collective-permute-start.6 = (bf16[256,768]{1,0:T(8,128)(2,1)}, bf16[256,768]{1,0:T(8,128)(2,1)S(1)}, u32[]{:S(2)}, u32[]{:S(2)}) collective-permute-start(bf16[256,768]{1,0:T(8,128)(2,1)} %get-tuple-element.21), channel_id=1, source_target_pairs={{0,16},{8,272},{16,0},{24,256},{256,24},{264,280},{272,8},{280,264... | collective-permute-start | bytes 1179656 | tf_op jit(solution)/shard_map/ppermute | solution.py:200
  124.2 13.5 %collective-permute-start.7 = (bf16[256,768]{1,0:T(8,128)(2,1)}, bf16[256,768]{1,0:T(8,128)(2,1)S(1)}, u32[]{:S(2)}, u32[]{:S(2)}) collective-permute-start(bf16[256,768]{1,0:T(8,128)(2,1)} %get-tuple-element.22), channel_id=1, source_target_pairs={{0,256},{8,0},{16,272},{24,16},{256,264},{264,8},{272,280},{280,24... | collective-permute-start | bytes 1179656 | tf_op jit(solution)/shard_map/ppermute | solution.py:200
  137.7 2.7 %collective-permute-start.8 = (bf16[256,768]{1,0:T(8,128)(2,1)}, bf16[256,768]{1,0:T(8,128)(2,1)S(1)}, u32[]{:S(2)}, u32[]{:S(2)}) collective-permute-start(bf16[256,768]{1,0:T(8,128)(2,1)} %get-tuple-element.23), channel_id=1, source_target_pairs={{0,272},{8,16},{16,256},{24,0},{256,280},{264,24},{272,264},{280,8... | collective-permute-start | bytes 1179656 | tf_op jit(solution)/shard_map/ppermute | solution.py:200
  140.4 38.9 %reduce-scatter.2.cloned.1.call-done = bf16[1,192,256]{2,1,0:T(8,128)(2,1)} async-done(((bf16[8,192,256]{2,1,0:T(8,128)(2,1)}), bf16[1,192,256]{2,1,0:T(8,128)(2,1)}) %reduce-scatter.2.cloned.1.call-update) | async-done | bytes 98320 | tf_op jit(solution)/shard_map/reduce_scatter | solution.py:232
  179.3 1.5 collective-permute-start.9
  180.8 0.0 collective-permute-done.5.p0_ref
  180.8 0.0 collective-permute-done.6.p1_ref
  180.8 0.0 copy-start.1
  180.8 0.0 collective-permute-done.7.p2_ref
  180.8 0.0 copy-start.2
  180.8 0.0 collective-permute-done.8.p3_ref
  180.8 0.7 copy-done
  181.6 0.1 copy-done.1
  181.7 0.1 copy-done.2
  181.8 0.8 copy-done.3
  182.6 7.9 %shard_map.104 = (bf16[768,256]{1,0:T(8,128)(2,1)}, bf16[768,256]{1,0:T(8,128)(2,1)}, bf16[768,256]{1,0:T(8,128)(2,1)}, f32[2,128]{1,0:T(2,128)}) custom-call(bf16[768,256]{1,0:T(8,128)(2,1)} %q_ref.3, bf16[768,256]{1,0:T(8,128)(2,1)} %k_ref.3, bf16[768,256]{1,0:T(8,128)(2,1)} %v_ref.3, bf16[256,768]{1,0:T(8,128)(2,1)} %copy-done, ...), custom_call_target="tpu_custom_call" | custom-call | tf_op jit(solution)/shard_map/pallas_call | solution.py:103
  190.5 0.7 broadcast_in_dim.4
  191.2 19.0 %all_to_all.10 = f32[32,2,128]{2,1,0:T(2,128)S(1)} all-to-all(f32[32,2,128]{2,1,0:T(2,128)S(1)} %broadcast_in_dim.4), channel_id=1, replica_groups=mesh['yl'=2,'za'=8,'zb'=2,'yh'=2,'x'=4,'c'=2] {'yl','yh','x','c'}, dimensions={0} | all-to-all | bytes 65536 | tf_op jit(solution)/shard_map/all_to_all | solution.py:212
  210.3 18.7 %all_to_all.11 = f32[16,2,128]{2,1,0:T(2,128)S(1)} all-to-all(f32[16,2,128]{2,1,0:T(2,128)S(1)} %broadcast_in_dim.5), channel_id=1, replica_groups=mesh['yl'=2,'za'=8,'zb'=2,'yh'=2,'x'=4,'c'=2] {'za','zb'}, dimensions={0} | all-to-all | bytes 32768 | tf_op jit(solution)/shard_map/all_to_all | solution.py:212
  229.1 0.6 reduce_sum.19
  229.6 0.0 collective-permute-done.9
  229.6 0.7 convert_element_type.3
  (4 shorter events, 0.1 us)
Async XLA Ops:
  7.2 100.2 %all-gather.4.cloned.1.call-start = ((), (), s32[]{:S(2)}) async-start(), calls=%async_computation.4 | async-start | bytes 10027008 | tf_op jit(solution)/shard_map/all_gather | solution.py:221
  9.4 8.7 %collective-permute-start = (bf16[192,768]{1,0:T(8,128)(2,1)}, bf16[192,768]{1,0:T(8,128)(2,1)S(1)}, u32[]{:S(2)}, u32[]{:S(2)}) collective-permute-start(bf16[192,768]{1,0:T(8,128)(2,1)} %get-tuple-element.18), channel_id=1, source_target_pairs={{0,16},{8,24},{16,0},{24,8},{256,272},{264,280},{272,256},{280,264... | collective-permute-start | bytes 884744 | tf_op jit(solution)/shard_map/ppermute | solution.py:200
  19.9 159.3 %reduce-scatter.2.cloned.1.call-start = ((), (), s32[]{:S(2)}) async-start(), calls=%async_computation.3 | async-start | bytes 884736 | tf_op jit(solution)/shard_map/reduce_scatter | solution.py:232
  25.0 8.7 %collective-permute-start.2 = (bf16[768,256]{1,0:T(8,128)(2,1)}, bf16[768,256]{1,0:T(8,128)(2,1)S(1)}, u32[]{:S(2)}, u32[]{:S(2)}) collective-permute-start(bf16[768,256]{1,0:T(8,128)(2,1)} %shard_map.102), channel_id=1, source_target_pairs={{0,16},{8,24},{16,0},{24,8},{256,272},{264,280},{272,256},{280,264... | collective-permute-start | bytes 1179656 | tf_op jit(solution)/shard_map/ppermute | solution.py:200
  34.8 47.6 %collective-permute-start.4 = (bf16[2,768,256]{2,1,0:T(8,128)(2,1)S(1)}, bf16[2,768,256]{2,1,0:T(8,128)(2,1)S(1)}, u32[]{:S(2)}, u32[]{:S(2)}) collective-permute-start(bf16[2,768,256]{2,1,0:T(8,128)(2,1)S(1)} %pad_maximum_fusion), channel_id=1, source_target_pairs={{0,8},{8,264},{16,24},{24,280},{256,0},{264,256},{272,16},{280,272... | collective-permute-start | bytes 2359304 | tf_op jit(solution)/shard_map/ppermute | solution.py:200
  44.8 37.7 %collective-permute-start.3 = (bf16[2,768,256]{2,1,0:T(8,128)(2,1)S(1)}, bf16[2,768,256]{2,1,0:T(8,128)(2,1)S(1)}, u32[]{:S(2)}, u32[]{:S(2)}) collective-permute-start(bf16[2,768,256]{2,1,0:T(8,128)(2,1)S(1)} %pad_maximum_fusion), channel_id=1, source_target_pairs={{0,0},{8,256},{16,16},{24,272},{256,8},{264,264},{272,24},{280,280... | collective-permute-start | bytes 2359304 | tf_op jit(solution)/shard_map/ppermute | solution.py:200
  45.5 1.6 collective-permute-start.1
  82.5 24.9 %copy-start.4 = (bf16[2,768,256]{2,1,0:T(8,128)(2,1)}, bf16[2,768,256]{2,1,0:T(8,128)(2,1)S(1)}, u32[]{:S(2)}) copy-start(bf16[2,768,256]{2,1,0:T(8,128)(2,1)S(1)} %collective-permute-done.4.other_ref) | copy-start | bytes 2359300
  82.5 24.9 %copy-start.5 = (bf16[2,768,256]{2,1,0:T(8,128)(2,1)}, bf16[2,768,256]{2,1,0:T(8,128)(2,1)S(1)}, u32[]{:S(2)}) copy-start(bf16[2,768,256]{2,1,0:T(8,128)(2,1)S(1)} %collective-permute-done.3.same_ref) | copy-start | bytes 2359300
  119.6 61.2 %collective-permute-start.5 = (bf16[256,768]{1,0:T(8,128)(2,1)}, bf16[256,768]{1,0:T(8,128)(2,1)S(1)}, u32[]{:S(2)}, u32[]{:S(2)}) collective-permute-start(bf16[256,768]{1,0:T(8,128)(2,1)} %get-tuple-element.20), channel_id=1, source_target_pairs={{0,0},{8,256},{16,16},{24,272},{256,8},{264,264},{272,24},{280,280... | collective-permute-start | bytes 1179656 | tf_op jit(solution)/shard_map/ppermute | solution.py:200
  121.2 59.5 %collective-permute-start.6 = (bf16[256,768]{1,0:T(8,128)(2,1)}, bf16[256,768]{1,0:T(8,128)(2,1)S(1)}, u32[]{:S(2)}, u32[]{:S(2)}) collective-permute-start(bf16[256,768]{1,0:T(8,128)(2,1)} %get-tuple-element.21), channel_id=1, source_target_pairs={{0,16},{8,272},{16,0},{24,256},{256,24},{264,280},{272,8},{280,264... | collective-permute-start | bytes 1179656 | tf_op jit(solution)/shard_map/ppermute | solution.py:200
  124.2 56.6 %collective-permute-start.7 = (bf16[256,768]{1,0:T(8,128)(2,1)}, bf16[256,768]{1,0:T(8,128)(2,1)S(1)}, u32[]{:S(2)}, u32[]{:S(2)}) collective-permute-start(bf16[256,768]{1,0:T(8,128)(2,1)} %get-tuple-element.22), channel_id=1, source_target_pairs={{0,256},{8,0},{16,272},{24,16},{256,264},{264,8},{272,280},{280,24... | collective-permute-start | bytes 1179656 | tf_op jit(solution)/shard_map/ppermute | solution.py:200
  137.7 43.1 %collective-permute-start.8 = (bf16[256,768]{1,0:T(8,128)(2,1)}, bf16[256,768]{1,0:T(8,128)(2,1)S(1)}, u32[]{:S(2)}, u32[]{:S(2)}) collective-permute-start(bf16[256,768]{1,0:T(8,128)(2,1)} %get-tuple-element.23), channel_id=1, source_target_pairs={{0,272},{8,16},{16,256},{24,0},{256,280},{264,24},{272,264},{280,8... | collective-permute-start | bytes 1179656 | tf_op jit(solution)/shard_map/ppermute | solution.py:200
  179.3 50.4 %collective-permute-start.9 = (bf16[192,256]{1,0:T(8,128)(2,1)}, bf16[192,256]{1,0:T(8,128)(2,1)S(1)}, u32[]{:S(2)}, u32[]{:S(2)}) collective-permute-start(bf16[192,256]{1,0:T(8,128)(2,1)} %bitcast.15), channel_id=1, source_target_pairs={{0,0},{8,256},{16,16},{24,272},{256,8},{264,264},{272,24},{280,280... | collective-permute-start | bytes 294920 | tf_op jit(solution)/shard_map/ppermute | solution.py:200
  180.8 0.8 copy-start
  180.8 0.9 copy-start.1
  180.8 1.0 copy-start.2
  181.8 0.8 copy-start.3
Sparse Core Ops, SparseCore 0:
  20.0 87.3 all-gather.3
  119.7 59.4 reduce-scatter.1

commit v4 on v2

--- a/solution.py
+++ b/solution.py
@@ -9,8 +9,9 @@
 PATCH = 256
 EPSILON = 1e-06
 SCALE = HD ** (-0.5)
-AXES = ("yl", "z", "yh", "x", "c")
-SIZES = (2, 16, 2, 4, 2)
+AXES = ("yl", "za", "zb", "yh", "x", "c")
+SIZES = (2, 4, 4, 2, 4, 2)
+Z = ("za", "zb")
 VMEM_LIMIT = 56 * 1024 * 1024
 
 
@@ -109,113 +110,114 @@
     )(queries_raw, keys_raw, values, part_one, part_two, norm_gains)
 
 
-def products_kernel(
-    high_ref, grad_ref, weight_ref, same_ref, other_ref, part_same_ref, part_other_ref,
-    wgrad_ref, total_same, total_other,
-):
+def weight_kernel(high_ref, grad_ref, same_ref, other_ref, wgrad_ref):
+    high = high_ref[0]
+    width = grad_ref.shape[4]
+    for core in range(2):
+        flipped = product(same_ref[...], grad_ref[high, 0, core], 1, 0)
+        flipped += product(other_ref[...], grad_ref[1 - high, 0, core], 1, 0)
+        wgrad_ref[core * width : (core + 1) * width] = flipped.T.astype(wgrad_ref.dtype)
+
+
+def grad_block(grads):
+    return pl.BlockSpec((2, 1) + grads.shape[2:], lambda x, high: (0, x, 0, 0, 0))
+
+
+def weight_product(high, grads, attn_same, attn_other):
+    _, blocks, cores, tokens, width = grads.shape
+    heads = attn_same.shape[0]
+    attn = pl.BlockSpec((heads, tokens), lambda x, high: (0, 0))
+    return pl.pallas_call(
+        weight_kernel,
+        grid_spec=pltpu.PrefetchScalarGridSpec(
+            num_scalar_prefetch=1,
+            grid=(blocks,),
+            in_specs=[grad_block(grads), attn, attn],
+            out_specs=pl.BlockSpec((cores * width, heads), lambda x, high: (x, 0)),
+        ),
+        out_shape=jax.ShapeDtypeStruct((blocks * cores * width, heads), jnp.bfloat16),
+        compiler_params=pltpu.CompilerParams(vmem_limit_bytes=VMEM_LIMIT),
+        cost_estimate=pl.CostEstimate(
+            flops=2 * grads.size * heads,
+            bytes_accessed=2 * (grads.size + blocks * cores * width * heads),
+            transcendentals=0,
+        ),
+    )(high, grads, attn_same, attn_other)
+
+
+def token_kernel(high_ref, grad_ref, weight_ref, same_ref, other_ref, total):
     step = pl.program_id(0)
-
-    @pl.when(step == 0)
-    def _():
-        total_same[...] = jnp.zeros_like(total_same)
-        total_other[...] = jnp.zeros_like(total_other)
-
     high = high_ref[0]
-    weights = weight_ref[...].reshape(grad_ref.shape[3], weight_ref.shape[3])
-    block = grad_ref[high, 0]
-    flipped = product(same_ref[...], block, 1, 0)
-    total_same[...] += product(block, weights, 1, 0)
-    block = grad_ref[1 - high, 0]
-    flipped += product(other_ref[...], block, 1, 0)
-    total_other[...] += product(block, weights, 1, 0)
-    wgrad_ref[...] = flipped.T.astype(wgrad_ref.dtype).reshape(wgrad_ref.shape)
+    weights = weight_ref[...].reshape(-1, weight_ref.shape[3])
+    for index, low in enumerate((high, 1 - high)):
+        block = jnp.concatenate([grad_ref[low, 0, 0], grad_ref[low, 0, 1]], axis=1)
+        term = product(block, weights, 1, 0)
+
+        @pl.when(step == 0)
+        def _():
+            total[index] = term
+
+        @pl.when(step > 0)
+        def _():
+            total[index] += term
 
     @pl.when(step == pl.num_programs(0) - 1)
     def _():
-        part_same_ref[...] = total_same[...].astype(part_same_ref.dtype)
-        part_other_ref[...] = total_other[...].astype(part_other_ref.dtype)
-
-
-def products(high, grads, weights, attn_same, attn_other):
-    _, blocks, tokens, width = grads.shape
-    rows, heads = weights.shape[2:]
-    pair = pl.BlockSpec((2, 1, rows, heads), lambda k, high: (k % 2, k // 2, 0, 0))
-    attn = pl.BlockSpec((heads, tokens), lambda k, high: (0, 0))
-    part = pl.BlockSpec((tokens, heads), lambda k, high: (0, 0))
-    return pl.pallas_call(
-        products_kernel,
+        same_ref[...] = total[0].astype(same_ref.dtype)
+        other_ref[...] = total[1].astype(other_ref.dtype)
+
+
+def token_product(high, grads, weights):
+    _, blocks, _, tokens, _ = grads.shape
+    fours, _, rows, heads = weights.shape
+    out = jax.ShapeDtypeStruct((tokens, heads), jnp.bfloat16)
+    return pl.pallas_call(
+        token_kernel,
         grid_spec=pltpu.PrefetchScalarGridSpec(
             num_scalar_prefetch=1,
             grid=(blocks,),
             in_specs=[
-                pl.BlockSpec((2, 1, tokens, width), lambda k, high: (0, k, 0, 0)),
-                pair,
-                attn,
-                attn,
+                grad_block(grads),
+                pl.BlockSpec((fours, 1, rows, heads), lambda x, high: (0, x, 0, 0)),
             ],
-            out_specs=[part, part, pair],
-            scratch_shapes=[pltpu.VMEM((tokens, heads), jnp.float32)] * 2,
-        ),
-        out_shape=[
-            jax.ShapeDtypeStruct((tokens, heads), jnp.bfloat16),
-            jax.ShapeDtypeStruct((tokens, heads), jnp.bfloat16),
-            jax.ShapeDtypeStruct(weights.shape, jnp.bfloat16),
-        ],
+            out_specs=[pl.BlockSpec((tokens, heads), lambda x, high: (0, 0))] * 2,
+            scratch_shapes=[pltpu.VMEM((2, tokens, heads), jnp.float32)],
+        ),
+        out_shape=[out, out],
         compiler_params=pltpu.CompilerParams(vmem_limit_bytes=VMEM_LIMIT),
         cost_estimate=pl.CostEstimate(
-            flops=8 * blocks * tokens * width * heads,
-            bytes_accessed=2 * (2 * blocks * tokens * width + 2 * blocks * width * heads),
+            flops=2 * grads.size * heads,
+            bytes_accessed=2 * (grads.size + weights.size),
             transcendentals=0,
         ),
-    )(high, grads, weights, attn_same, attn_other)
-
-
-def permute(array, target):
+    )(high, grads, weights)
+
+
+def swap_y(array, target):
     pairs = []
     for low in range(2):
-        for z in range(16):
-            for high in range(2):
-                to_low, to_z, to_high = target(low, z, high)
-                pairs.append(((low * 16 + z) * 2 + high, (to_low * 16 + to_z % 16) * 2 + to_high))
-    return lax.ppermute(array, ("yl", "z", "yh"), pairs)
+        for high in range(2):
+            to_low, to_high = target(low, high)
+            pairs.append((low * 2 + high, to_low * 2 + to_high))
+    return lax.ppermute(array, ("yl", "yh"), pairs)
+
+
+def turned(array):
+    return swap_y(array, lambda low, high: (high, low))
 
 
 def along(array, step):
-    return permute(array, lambda low, z, high: (low, z + step, high))
-
-
-def turned(array, step):
-    return permute(array, lambda low, z, high: (high, z + step, low))
-
-
-def pick(array, index):
-    return lax.dynamic_index_in_dim(array, index, 0, keepdims=False)
-
-
-def rolled(blocks, shift):
-    return lax.dynamic_slice_in_dim(
-        jnp.stack(blocks + blocks), (4 - shift) % 4, 4, axis=0
-    )
-
-
-def gather_rows(out_weight, z):
-    column = rolled([turned(out_weight, -4 * step) for step in range(4)], z // 4)
+    return lax.ppermute(array, Z, [(z, (z + step) % 16) for z in range(16)])
+
+
+def gather_rows(own_rows):
+    column = lax.all_gather(own_rows, "za", axis=0)
     before = along(column, 1)
     after = along(column, -1)
     far = jnp.concatenate([along(column[:2], 2), along(column[2:], -2)])
-    return rolled([column, after, far, before], z % 4)
-
-
-def scatter_rows(wgrad, z):
-    own = pick(wgrad, z % 4)
-    before = along(pick(wgrad, (z + 1) % 4), 1)
-    after = along(pick(wgrad, (z + 3) % 4), -1)
-    far = pick(wgrad, (z + 2) % 4)
-    far = jnp.concatenate([along(far[:2], 2), along(far[2:], -2)])
-    column = sum(term.astype(jnp.float32) for term in (own, before, after, far))
-    column = column.astype(jnp.bfloat16)
-    terms = [turned(pick(column, (z // 4 + step) % 4), 4 * step) for step in range(4)]
-    return sum(term.astype(jnp.float32) for term in terms)
+    blocks = [column, after, far, before]
+    shift = (4 - lax.axis_index("zb")) % 4
+    return lax.dynamic_slice_in_dim(jnp.stack(blocks + blocks), shift, 4, axis=0)
 
 
 def sum_over(array, axis, count):
@@ -224,30 +226,34 @@
 
 
 def per_device(queries_raw, keys_raw, values, grad_out, out_weight, norm_gains):
-    z = lax.axis_index("z")
     high = lax.axis_index("yh").reshape(1)
     grads = lax.all_gather(grad_out, ("yl", "x", "c"), axis=0)
-    grads = grads.reshape((2, 8) + grad_out.shape)
-    weights = gather_rows(out_weight, z)
+    grads = grads.reshape((2, 4, 2) + grad_out.shape)
 
     attn = forward(queries_raw, keys_raw, values, norm_gains)
-    attn_same = turned(attn, 0)
-    attn_other = permute(attn, lambda low, z, up: (up, z, 1 - low))
-
-    part_same, part_other, wgrad = products(high, grads, weights, attn_same, attn_other)
-    came_same = turned(part_same, 0)
-    came_other = permute(part_other, lambda low, z, up: (1 - up, z, low))
-    weight_grad = scatter_rows(wgrad, z)
+    attn_same = turned(attn)
+    attn_other = swap_y(attn, lambda low, up: (up, 1 - low))
+    weights = gather_rows(turned(out_weight))
+
+    wgrad = weight_product(high, grads, attn_same, attn_other)
+    shard = lax.psum_scatter(wgrad, Z, scatter_dimension=0, tiled=True)
+
+    weights, _ = lax.optimization_barrier((weights, wgrad))
+    part_same, part_other = token_product(high, grads, weights)
+    came_same = turned(part_same)
+    came_other = swap_y(part_other, lambda low, up: (1 - up, low))
     queries_grad, keys_grad, values_grad, terms = backward(
         queries_raw, keys_raw, values, came_same, came_other, norm_gains
     )
-    gains_grad = sum_over(sum_over(terms, "z", 16), ("yl", "yh", "x", "c"), 32)
+    gains_grad = sum_over(sum_over(terms, ("yl", "yh", "x", "c"), 32), Z, 16)
+    shard, gains_grad = lax.optimization_barrier((shard, gains_grad))
+    weight_grad = turned(shard).astype(jnp.float32)
     return (queries_grad, keys_grad, values_grad, weight_grad, gains_grad)
 
 
 def solution(mesh):
     fine = Mesh(mesh.devices.reshape(SIZES), AXES)
-    spec = P(("yl", "z"), ("yh", "x", "c"))
+    spec = P(("yl", "za", "zb"), ("yh", "x", "c"))
     return jax.shard_map(
         per_device,
         mesh=fine,

time: 210 us -> 233 us (1.11)
  the two profiles are of different devices: /device:TPU:1 before, /device:TPU:8 now
where the time goes in v4:
time: 233 us; the launch traced here: 232 us
  waiting for transfers between devices  85.1 us (37%)
  blocking collectives  65.2 us (28%)
  starting transfers between devices  33.8 us (15%)
  Pallas kernels  29.8 us (13%)
  between operations  14.2 us (6%)
  local copies, waits for them, and re-layouts  2.94 us (1%)
    all_gather x1, waiting for transfers between devices, per_device(): grads = lax.all_gather(grad_out, ('yl', 'x', 'c'), axis=0)  44.6 us
    all_to_all x2, blocking collectives, sum_over(): lax.all_to_all(jnp.broadcast_to(array[None], (count,) + array.shape), axi...  35.6 us
    all_gather x1, blocking collectives, gather_rows(): column = lax.all_gather(own_rows, 'za', axis=0)  29.6 us
    ppermute x6, waiting for transfers between devices, swap_y(): return lax.ppermute(array, ('yl', 'yh'), pairs)  27.7 us
    ppermute x6, starting transfers between devices, swap_y(): return lax.ppermute(array, ('yl', 'yh'), pairs)  19.9 us
    ppermute x4, starting transfers between devices, along(): return lax.ppermute(array, Z, [(z, (z + step) % 16) for z in range(16)])  13.8 us
    ppermute x4, waiting for transfers between devices, along(): return lax.ppermute(array, Z, [(z, (z + step) % 16) for z in range(16)])  12 us
    pallas_call x1, Pallas kernels, token_product(): pl.pallas_call(token_kernel, grid_spec=pltpu.PrefetchScalarGridSpec(num_s...  9.37 us
  transfers between devices with their start and end apart: 12, of which 9 were waited for; matrix products, arithmetic and copies ran while one was open for 1% of the time, Pallas kernels for 9%

profile of v4, /device:TPU:8, one launch (start us, length us, event | category | flops | bytes accessed | tf_op | source)
XLA Modules:
  0.0 232.5 jit_solution(8484773050803402734)
XLA Ops:
  7.2 0.0 all-gather.4.cloned.1.call-start
  7.2 0.7 all-gather.4.cloned.1.call-update
  7.9 0.0 reduce-scatter.2.cloned.1.call-start
  7.9 5.3 %shard_map.101 = bf16[256,768]{1,0:T(8,128)(2,1)} custom-call(bf16[768,256]{1,0:T(8,128)(2,1)} %q_ref.3, bf16[768,256]{1,0:T(8,128)(2,1)} %k_ref.3, bf16[768,256]{1,0:T(8,128)(2,1)} %v_ref.3, f32[2,128]{1,0:T(2,128)} %gains_ref.3), custom_call_target="tpu_custom_call" | custom-call | tf_op jit(solution)/shard_map/pallas_call | solution.py:57
  13.2 3.5 %collective-permute-start.5 = (bf16[256,768]{1,0:T(8,128)(2,1)}, bf16[256,768]{1,0:T(8,128)(2,1)S(1)}, u32[]{:S(2)}, u32[]{:S(2)}) collective-permute-start(bf16[256,768]{1,0:T(8,128)(2,1)} %shard_map.101), channel_id=1, source_target_pairs={{0,0},{8,256},{256,8},{264,264},{1,1},{9,257},{257,9},{265,265},{2... | collective-permute-start | bytes 1179656 | tf_op jit(solution)/shard_map/ppermute | solution.py:202
  16.7 5.9 %collective-permute-start.6 = (bf16[256,768]{1,0:T(8,128)(2,1)}, bf16[256,768]{1,0:T(8,128)(2,1)S(1)}, u32[]{:S(2)}, u32[]{:S(2)}) collective-permute-start(bf16[256,768]{1,0:T(8,128)(2,1)} %shard_map.101), channel_id=1, source_target_pairs={{0,8},{8,264},{256,0},{264,256},{1,9},{9,265},{257,1},{265,257},{2... | collective-permute-start | bytes 1179656 | tf_op jit(solution)/shard_map/ppermute | solution.py:202
  22.6 12.0 %collective-permute-done.5.same_ref = bf16[256,768]{1,0:T(8,128)(2,1)S(1)} collective-permute-done((bf16[256,768]{1,0:T(8,128)(2,1)}, bf16[256,768]{1,0:T(8,128)(2,1)S(1)}, u32[]{:S(2)}, u32[]{:S(2)}) %collective-permute-start.5) | collective-permute-done | bytes 393248 | tf_op jit(solution)/shard_map/ppermute | solution.py:202
  34.6 0.0 copy-start
  34.6 0.0 collective-permute-done.6.other_ref
  34.6 0.0 copy-start.1
  34.6 44.6 %all-gather.4.cloned.1.call-done = bf16[12288,384]{1,0:T(8,128)(2,1)} async-done(((bf16[768,384]{1,0:T(8,128)(2,1)}), bf16[12288,384]{1,0:T(8,128)(2,1)}) %all-gather.4.cloned.1.call-update) | async-done | bytes 9437200 | tf_op jit(solution)/shard_map/all_gather | solution.py:230
  79.3 0.0 copy-done
  79.3 0.0 copy-done.1
  79.3 0.0 copy-start.4
  79.3 7.8 %shard_map.102 = bf16[3072,256]{1,0:T(8,128)(2,1)} custom-call(s32[1]{0:T(128)} %bitcast.high_ref, bf16[2,4,2,768,384]{4,3,2,1,0:T(8,128)(2,1)} %bitcast.18, bf16[256,768]{1,0:T(8,128)(2,1)} %copy-done, bf16[256,768]{1,0:T(8,128)(2,1)} %copy-done.1), custom_call_target="tpu_custom_call" | custom-call | flops 2415919104 | bytes 11010048 | tf_op jit(solution)/shard_map/pallas_call | solution.py:130
  87.1 0.0 reduce-scatter.2.cloned.1.call-update
  87.1 0.0 copy-done.4
  87.1 3.3 %collective-permute-start = (bf16[192,256]{1,0:T(8,128)(2,1)S(1)}, bf16[192,256]{1,0:T(8,128)(2,1)S(1)}, u32[]{:S(2)}, u32[]{:S(2)}) collective-permute-start(bf16[192,256]{1,0:T(8,128)(2,1)S(1)} %copy-done.4), channel_id=1, source_target_pairs={{0,0},{8,256},{256,8},{264,264},{1,1},{9,257},{257,9},{265,265},{2... | collective-permute-start | bytes 294920 | tf_op jit(solution)/shard_map/ppermute | solution.py:202
  90.4 3.5 %collective-permute-done = bf16[192,256]{1,0:T(8,128)(2,1)S(1)} collective-permute-done((bf16[192,256]{1,0:T(8,128)(2,1)S(1)}, bf16[192,256]{1,0:T(8,128)(2,1)S(1)}, u32[]{:S(2)}, u32[]{:S(2)}) %collective-permute-start) | collective-permute-done | bytes 98336 | tf_op jit(solution)/shard_map/ppermute | solution.py:202
  94.0 29.6 %all-gather.1 = bf16[768,256]{1,0:T(8,128)(2,1)S(1)} all-gather(bf16[192,256]{1,0:T(8,128)(2,1)S(1)} %collective-permute-done), channel_id=3, replica_groups=mesh['yl'=2,'za'=4,'zb'=4,'yh'=2,'x'=4,'c'=2] {'za'}, dimensions={0}, use_global_device_ids=true | all-gather | bytes 491520 | tf_op jit(solution)/shard_map/all_gather | solution.py:214
  123.6 1.9 collective-permute-start.1
  125.5 3.9 %collective-permute-start.4 = (bf16[4,192,256]{2,1,0:T(8,128)(2,1)S(1)}, bf16[4,192,256]{2,1,0:T(8,128)(2,1)S(1)}, u32[]{:S(2)}, u32[]{:S(2)}) collective-permute-start(bf16[4,192,256]{2,1,0:T(8,128)(2,1)S(1)} %bitcast.21), channel_id=1, source_target_pairs={{0,16},{16,32},{32,48},{48,64},{64,80},{80,96},{96,112},{112,128},... | collective-permute-start | bytes 1179656 | tf_op jit(solution)/shard_map/ppermute | solution.py:210
  129.5 1.9 collective-permute-start.2
  131.5 6.0 %collective-permute-start.3 = (bf16[2,192,256]{2,1,0:T(8,128)(2,1)S(1)}, bf16[2,192,256]{2,1,0:T(8,128)(2,1)S(1)}, u32[]{:S(2)}, u32[]{:S(2)}) collective-permute-start(bf16[2,192,256]{2,1,0:T(8,128)(2,1)S(1)} %bitcast.24), channel_id=1, source_target_pairs={{0,224},{16,240},{32,0},{48,16},{64,32},{80,48},{96,64},{112,80},{... | collective-permute-start | bytes 589832 | tf_op jit(solution)/shard_map/ppermute | solution.py:210
  137.5 8.4 %collective-permute-done.1 = bf16[4,192,256]{2,1,0:T(8,128)(2,1)S(1)} collective-permute-done((bf16[4,192,256]{2,1,0:T(8,128)(2,1)S(1)}, bf16[4,192,256]{2,1,0:T(8,128)(2,1)S(1)}, u32[]{:S(2)}, u32[]{:S(2)}) %collective-permute-start.1) | collective-permute-done | bytes 393248 | tf_op jit(solution)/shard_map/ppermute | solution.py:210
  146.0 3.0 %collective-permute-done.2 = bf16[2,192,256]{2,1,0:T(8,128)(2,1)S(1)} collective-permute-done((bf16[2,192,256]{2,1,0:T(8,128)(2,1)S(1)}, bf16[2,192,256]{2,1,0:T(8,128)(2,1)S(1)}, u32[]{:S(2)}, u32[]{:S(2)}) %collective-permute-start.2) | collective-permute-done | bytes 196640 | tf_op jit(solution)/shard_map/ppermute | solution.py:210
  149.0 0.0 collective-permute-done.3
  149.0 0.6 collective-permute-done.4
  149.8 1.3 constant_dynamic-slice_fusion.weight_ref
  151.1 9.4 %shard_map.103 = (bf16[768,256]{1,0:T(8,128)(2,1)}, bf16[768,256]{1,0:T(8,128)(2,1)}) custom-call(s32[1]{0:T(128)} %bitcast.high_ref, bf16[2,4,2,768,384]{4,3,2,1,0:T(8,128)(2,1)} %bitcast.19, bf16[4,4,192,256]{3,2,1,0:T(8,128)(2,1)} %constant_dynamic-slice_fusion.weight_ref), custom_call_target="tpu_custom_call" | custom-call | flops 2415919104 | bytes 11010048 | tf_op jit(solution)/shard_map/pallas_call | solution.py:174
  160.4 2.9 %collective-permute-start.7 = (bf16[768,256]{1,0:T(8,128)(2,1)}, bf16[768,256]{1,0:T(8,128)(2,1)S(1)}, u32[]{:S(2)}, u32[]{:S(2)}) collective-permute-start(bf16[768,256]{1,0:T(8,128)(2,1)} %get-tuple-element.15), channel_id=1, source_target_pairs={{0,0},{8,256},{256,8},{264,264},{1,1},{9,257},{257,9},{265,265},{2... | collective-permute-start | bytes 1179656 | tf_op jit(solution)/shard_map/ppermute | solution.py:202
  163.4 1.9 collective-permute-start.8
  165.3 5.0 %collective-permute-done.7.one_ref = bf16[768,256]{1,0:T(8,128)(2,1)S(1)} collective-permute-done((bf16[768,256]{1,0:T(8,128)(2,1)}, bf16[768,256]{1,0:T(8,128)(2,1)S(1)}, u32[]{:S(2)}, u32[]{:S(2)}) %collective-permute-start.7) | collective-permute-done | bytes 393248 | tf_op jit(solution)/shard_map/ppermute | solution.py:202
  170.3 0.0 copy-start.2
  170.3 2.9 %collective-permute-done.8.two_ref = bf16[768,256]{1,0:T(8,128)(2,1)S(1)} collective-permute-done((bf16[768,256]{1,0:T(8,128)(2,1)}, bf16[768,256]{1,0:T(8,128)(2,1)S(1)}, u32[]{:S(2)}, u32[]{:S(2)}) %collective-permute-start.8) | collective-permute-done | bytes 393248 | tf_op jit(solution)/shard_map/ppermute | solution.py:202
  173.2 0.0 copy-done.2
  173.2 0.0 copy-start.3
  173.2 0.8 copy-done.3
  174.0 7.4 %shard_map.104 = (bf16[768,256]{1,0:T(8,128)(2,1)}, bf16[768,256]{1,0:T(8,128)(2,1)}, bf16[768,256]{1,0:T(8,128)(2,1)}, f32[2,128]{1,0:T(2,128)}) custom-call(bf16[768,256]{1,0:T(8,128)(2,1)} %q_ref.3, bf16[768,256]{1,0:T(8,128)(2,1)} %k_ref.3, bf16[768,256]{1,0:T(8,128)(2,1)} %v_ref.3, bf16[768,256]{1,0:T(8,128)(2,1)} %copy-done.2, ...), custom_call_target="tpu_custom_call" | custom-call | tf_op jit(solution)/shard_map/pallas_call | solution.py:103
  181.4 0.7 broadcast_in_dim.4
  182.1 14.8 %all_to_all.10 = f32[32,2,128]{2,1,0:T(2,128)S(1)} all-to-all(f32[32,2,128]{2,1,0:T(2,128)S(1)} %broadcast_in_dim.4), channel_id=1, replica_groups=mesh['yl'=2,'za'=4,'zb'=4,'yh'=2,'x'=4,'c'=2] {'yl','yh','x','c'}, dimensions={0} | all-to-all | bytes 65536 | tf_op jit(solution)/shard_map/all_to_all | solution.py:224
  196.9 20.8 %all_to_all.11 = f32[16,2,128]{2,1,0:T(2,128)S(1)} all-to-all(f32[16,2,128]{2,1,0:T(2,128)S(1)} %broadcast_in_dim.5), channel_id=1, replica_groups=mesh['yl'=2,'za'=4,'zb'=4,'yh'=2,'x'=4,'c'=2] {'za','zb'}, dimensions={0} | all-to-all | bytes 32768 | tf_op jit(solution)/shard_map/all_to_all | solution.py:224
  217.7 0.6 reduce_sum.19
  218.3 0.0 reduce-scatter.2.cloned.1.call-done
  218.3 2.4 %collective-permute-start.9 = (bf16[192,256]{1,0:T(8,128)(2,1)}, bf16[192,256]{1,0:T(8,128)(2,1)S(1)}, u32[]{:S(2)}, u32[]{:S(2)}) collective-permute-start(bf16[192,256]{1,0:T(8,128)(2,1)} %reduce-scatter.2.cloned.1.call-done), channel_id=1, source_target_pairs={{0,0},{8,256},{256,8},{264,264},{1,1},{9,257},{257,9},{265,265},{2... | collective-permute-start | bytes 294920 | tf_op jit(solution)/shard_map/ppermute | solution.py:202
  220.7 4.3 %collective-permute-done.9 = bf16[192,256]{1,0:T(8,128)(2,1)S(1)} collective-permute-done((bf16[192,256]{1,0:T(8,128)(2,1)}, bf16[192,256]{1,0:T(8,128)(2,1)S(1)}, u32[]{:S(2)}, u32[]{:S(2)}) %collective-permute-start.9) | collective-permute-done | bytes 98336 | tf_op jit(solution)/shard_map/ppermute | solution.py:202
  225.0 0.7 convert_element_type.3
  (11 shorter events, 0.3 us)
Async XLA Ops:
  7.2 72.1 %all-gather.4.cloned.1.call-start = ((), (), s32[]{:S(2)}) async-start(), calls=%async_computation.4 | async-start | bytes 10027008 | tf_op jit(solution)/shard_map/all_gather | solution.py:230
  7.9 210.4 %reduce-scatter.2.cloned.1.call-start = ((), (), s32[]{:S(2)}) async-start(), calls=%async_computation.3 | async-start | bytes 1671168 | tf_op jit(solution)/shard_map/reduce_scatter | solution.py:239
  13.2 21.4 %collective-permute-start.5 = (bf16[256,768]{1,0:T(8,128)(2,1)}, bf16[256,768]{1,0:T(8,128)(2,1)S(1)}, u32[]{:S(2)}, u32[]{:S(2)}) collective-permute-start(bf16[256,768]{1,0:T(8,128)(2,1)} %shard_map.101), channel_id=1, source_target_pairs={{0,0},{8,256},{256,8},{264,264},{1,1},{9,257},{257,9},{265,265},{2... | collective-permute-start | bytes 1179656 | tf_op jit(solution)/shard_map/ppermute | solution.py:202
  16.7 17.9 %collective-permute-start.6 = (bf16[256,768]{1,0:T(8,128)(2,1)}, bf16[256,768]{1,0:T(8,128)(2,1)S(1)}, u32[]{:S(2)}, u32[]{:S(2)}) collective-permute-start(bf16[256,768]{1,0:T(8,128)(2,1)} %shard_map.101), channel_id=1, source_target_pairs={{0,8},{8,264},{256,0},{264,256},{1,9},{9,265},{257,1},{265,257},{2... | collective-permute-start | bytes 1179656 | tf_op jit(solution)/shard_map/ppermute | solution.py:202
  34.6 44.7 %copy-start = (bf16[256,768]{1,0:T(8,128)(2,1)}, bf16[256,768]{1,0:T(8,128)(2,1)S(1)}, u32[]{:S(2)}) copy-start(bf16[256,768]{1,0:T(8,128)(2,1)S(1)} %collective-permute-done.5.same_ref) | copy-start | bytes 1179652
  34.6 44.7 %copy-start.1 = (bf16[256,768]{1,0:T(8,128)(2,1)}, bf16[256,768]{1,0:T(8,128)(2,1)S(1)}, u32[]{:S(2)}) copy-start(bf16[256,768]{1,0:T(8,128)(2,1)S(1)} %collective-permute-done.6.other_ref) | copy-start | bytes 1179652
  79.3 7.8 %copy-start.4 = (bf16[192,256]{1,0:T(8,128)(2,1)S(1)}, bf16[192,256]{1,0:T(8,128)(2,1)}, u32[]{:S(2)}) copy-start(bf16[192,256]{1,0:T(8,128)(2,1)} %param.10) | copy-start | bytes 294916
  87.1 6.8 %collective-permute-start = (bf16[192,256]{1,0:T(8,128)(2,1)S(1)}, bf16[192,256]{1,0:T(8,128)(2,1)S(1)}, u32[]{:S(2)}, u32[]{:S(2)}) collective-permute-start(bf16[192,256]{1,0:T(8,128)(2,1)S(1)} %copy-done.4), channel_id=1, source_target_pairs={{0,0},{8,256},{256,8},{264,264},{1,1},{9,257},{257,9},{265,265},{2... | collective-permute-start | bytes 294920 | tf_op jit(solution)/shard_map/ppermute | solution.py:202
  123.6 22.3 %collective-permute-start.1 = (bf16[4,192,256]{2,1,0:T(8,128)(2,1)S(1)}, bf16[4,192,256]{2,1,0:T(8,128)(2,1)S(1)}, u32[]{:S(2)}, u32[]{:S(2)}) collective-permute-start(bf16[4,192,256]{2,1,0:T(8,128)(2,1)S(1)} %bitcast.20), channel_id=1, source_target_pairs={{0,240},{16,0},{32,16},{48,32},{64,48},{80,64},{96,80},{112,96},{1... | collective-permute-start | bytes 1179656 | tf_op jit(solution)/shard_map/ppermute | solution.py:210
  125.5 24.1 %collective-permute-start.4 = (bf16[4,192,256]{2,1,0:T(8,128)(2,1)S(1)}, bf16[4,192,256]{2,1,0:T(8,128)(2,1)S(1)}, u32[]{:S(2)}, u32[]{:S(2)}) collective-permute-start(bf16[4,192,256]{2,1,0:T(8,128)(2,1)S(1)} %bitcast.21), channel_id=1, source_target_pairs={{0,16},{16,32},{32,48},{48,64},{64,80},{80,96},{96,112},{112,128},... | collective-permute-start | bytes 1179656 | tf_op jit(solution)/shard_map/ppermute | solution.py:210
  129.5 19.5 %collective-permute-start.2 = (bf16[2,192,256]{2,1,0:T(8,128)(2,1)S(1)}, bf16[2,192,256]{2,1,0:T(8,128)(2,1)S(1)}, u32[]{:S(2)}, u32[]{:S(2)}) collective-permute-start(bf16[2,192,256]{2,1,0:T(8,128)(2,1)S(1)} %bitcast.25), channel_id=1, source_target_pairs={{0,32},{16,48},{32,64},{48,80},{64,96},{80,112},{96,128},{112,144}... | collective-permute-start | bytes 589832 | tf_op jit(solution)/shard_map/ppermute | solution.py:210
  131.5 17.5 %collective-permute-start.3 = (bf16[2,192,256]{2,1,0:T(8,128)(2,1)S(1)}, bf16[2,192,256]{2,1,0:T(8,128)(2,1)S(1)}, u32[]{:S(2)}, u32[]{:S(2)}) collective-permute-start(bf16[2,192,256]{2,1,0:T(8,128)(2,1)S(1)} %bitcast.24), channel_id=1, source_target_pairs={{0,224},{16,240},{32,0},{48,16},{64,32},{80,48},{96,64},{112,80},{... | collective-permute-start | bytes 589832 | tf_op jit(solution)/shard_map/ppermute | solution.py:210
  160.4 9.9 %collective-permute-start.7 = (bf16[768,256]{1,0:T(8,128)(2,1)}, bf16[768,256]{1,0:T(8,128)(2,1)S(1)}, u32[]{:S(2)}, u32[]{:S(2)}) collective-permute-start(bf16[768,256]{1,0:T(8,128)(2,1)} %get-tuple-element.15), channel_id=1, source_target_pairs={{0,0},{8,256},{256,8},{264,264},{1,1},{9,257},{257,9},{265,265},{2... | collective-permute-start | bytes 1179656 | tf_op jit(solution)/shard_map/ppermute | solution.py:202
  163.4 9.9 %collective-permute-start.8 = (bf16[768,256]{1,0:T(8,128)(2,1)}, bf16[768,256]{1,0:T(8,128)(2,1)S(1)}, u32[]{:S(2)}, u32[]{:S(2)}) collective-permute-start(bf16[768,256]{1,0:T(8,128)(2,1)} %get-tuple-element.16), channel_id=1, source_target_pairs={{0,256},{8,0},{256,264},{264,8},{1,257},{9,1},{257,265},{265,9},{2... | collective-permute-start | bytes 1179656 | tf_op jit(solution)/shard_map/ppermute | solution.py:202
  170.3 2.9 %copy-start.2 = (bf16[768,256]{1,0:T(8,128)(2,1)}, bf16[768,256]{1,0:T(8,128)(2,1)S(1)}, u32[]{:S(2)}) copy-start(bf16[768,256]{1,0:T(8,128)(2,1)S(1)} %collective-permute-done.7.one_ref) | copy-start | bytes 1179652
  173.2 0.8 copy-start.3
  218.3 6.7 %collective-permute-start.9 = (bf16[192,256]{1,0:T(8,128)(2,1)}, bf16[192,256]{1,0:T(8,128)(2,1)S(1)}, u32[]{:S(2)}, u32[]{:S(2)}) collective-permute-start(bf16[192,256]{1,0:T(8,128)(2,1)} %reduce-scatter.2.cloned.1.call-done), channel_id=1, source_target_pairs={{0,0},{8,256},{256,8},{264,264},{1,1},{9,257},{257,9},{265,265},{2... | collective-permute-start | bytes 294920 | tf_op jit(solution)/shard_map/ppermute | solution.py:202
Sparse Core Ops, SparseCore 0:
  10.1 69.0 all-gather.3
  87.2 78.8 reduce-scatter.1

commit v5 on v4

--- a/solution.py
+++ b/solution.py
@@ -47,8 +47,7 @@
         _, _, q_norm = normalize(q_ref[:, cols], gains_ref[0:1, :])
         _, _, k_norm = normalize(k_ref[:, cols], gains_ref[1:2, :])
         prob_low = softmax(q_norm, k_norm).astype(jnp.bfloat16)
-        attn = product(prob_low, v_ref[:, cols], 1, 0)
-        attn_ref[cols, :] = attn.T.astype(jnp.bfloat16)
+        attn_ref[:, cols] = product(prob_low, v_ref[:, cols], 1, 0).astype(jnp.bfloat16)
 
 
 def forward(queries_raw, keys_raw, values, norm_gains):
@@ -58,8 +57,8 @@
         forward_kernel,
         grid=(tokens // PATCH,),
         in_specs=[block, block, block, pl.BlockSpec((2, HD), lambda i: (0, 0))],
-        out_specs=pl.BlockSpec((width, PATCH), lambda i: (0, i)),
-        out_shape=jax.ShapeDtypeStruct((width, tokens), jnp.bfloat16),
+        out_specs=block,
+        out_shape=jax.ShapeDtypeStruct((tokens, width), jnp.bfloat16),
         compiler_params=pltpu.CompilerParams(vmem_limit_bytes=VMEM_LIMIT),
     )(queries_raw, keys_raw, values, norm_gains)
 
@@ -114,9 +113,9 @@
     high = high_ref[0]
     width = grad_ref.shape[4]
     for core in range(2):
-        flipped = product(same_ref[...], grad_ref[high, 0, core], 1, 0)
-        flipped += product(other_ref[...], grad_ref[1 - high, 0, core], 1, 0)
-        wgrad_ref[core * width : (core + 1) * width] = flipped.T.astype(wgrad_ref.dtype)
+        term = product(grad_ref[high, 0, core], same_ref[...], 0, 0)
+        term += product(grad_ref[1 - high, 0, core], other_ref[...], 0, 0)
+        wgrad_ref[core * width : (core + 1) * width] = term.astype(wgrad_ref.dtype)
 
 
 def grad_block(grads):
@@ -125,8 +124,8 @@
 
 def weight_product(high, grads, attn_same, attn_other):
     _, blocks, cores, tokens, width = grads.shape
-    heads = attn_same.shape[0]
-    attn = pl.BlockSpec((heads, tokens), lambda x, high: (0, 0))
+    heads = attn_same.shape[1]
+    attn = pl.BlockSpec((tokens, heads), lambda x, high: (0, 0))
     return pl.pallas_call(
         weight_kernel,
         grid_spec=pltpu.PrefetchScalarGridSpec(
@@ -149,17 +148,15 @@
     step = pl.program_id(0)
     high = high_ref[0]
     weights = weight_ref[...].reshape(-1, weight_ref.shape[3])
+    width = grad_ref.shape[4]
+
+    @pl.when(step == 0)
+    def _():
+        total[...] = jnp.zeros_like(total)
+
     for index, low in enumerate((high, 1 - high)):
-        block = jnp.concatenate([grad_ref[low, 0, 0], grad_ref[low, 0, 1]], axis=1)
-        term = product(block, weights, 1, 0)
-
-        @pl.when(step == 0)
-        def _():
-            total[index] = term
-
-        @pl.when(step > 0)
-        def _():
-            total[index] += term
+        term = product(grad_ref[low, 0, 0], weights[:width], 1, 0)
+        total[index] += term + product(grad_ref[low, 0, 1], weights[width:], 1, 0)
 
     @pl.when(step == pl.num_programs(0) - 1)
     def _():
@@ -234,6 +231,7 @@
     attn_same = turned(attn)
     attn_other = swap_y(attn, lambda low, up: (up, 1 - low))
     weights = gather_rows(turned(out_weight))
+    grads, weights = lax.optimization_barrier((grads, weights))
 
     wgrad = weight_product(high, grads, attn_same, attn_other)
     shard = lax.psum_scatter(wgrad, Z, scatter_dimension=0, tiled=True)

time: 233 us -> 183 us (0.79)
  waiting for transfers between devices: 85.1 us -> 37.6 us
  Pallas kernels: 29.8 us -> 27.2 us
    all_gather x1, waiting for transfers between devices: 44.6 us -> 11.1 us  [per_device(): grads = lax.all_gather(grad_out, ('yl', 'x', 'c'), axis=0)]
    ppermute x6, waiting for transfers between devices: 27.7 us -> 17.9 us  [swap_y(): return lax.ppermute(array, ('yl', 'yh'), pairs)]
    ppermute x4, waiting for transfers between devices: 12 us -> 5.69 us  [along(): return lax.ppermute(array, Z, [(z, (z + step) % 16) for z in range(16)])]
  transfers between devices with their start and end apart: 12 -> 12, of which waited for: 9 -> 9; matrix products, arithmetic and copies ran while one was open for 1% -> 2% of each run, Pallas kernels for 9% -> 11%
where the time goes in v5:
time: 183 us
  blocking collectives  66.1 us (36%)
  waiting for transfers between devices  37.6 us (21%)
  starting transfers between devices  32.3 us (18%)
  Pallas kernels  27.2 us (15%)
  between operations  14.2 us (8%)
  local copies, waits for them, and re-layouts  3.8 us (2%)
    all_to_all x2, blocking collectives, sum_over(): lax.all_to_all(jnp.broadcast_to(array[None], (count,) + array.shape), axi...  37.1 us
    all_gather x1, blocking collectives, gather_rows(): column = lax.all_gather(own_rows, 'za', axis=0)  29 us
    ppermute x6, starting transfers between devices, swap_y(): return lax.ppermute(array, ('yl', 'yh'), pairs)  18.4 us
    ppermute x6, waiting for transfers between devices, swap_y(): return lax.ppermute(array, ('yl', 'yh'), pairs)  17.9 us
    ppermute x4, starting transfers between devices, along(): return lax.ppermute(array, Z, [(z, (z + step) % 16) for z in range(16)])  13.8 us
    all_gather x1, waiting for transfers between devices, per_device(): grads = lax.all_gather(grad_out, ('yl', 'x', 'c'), axis=0)  11.1 us
    pallas_call x1, Pallas kernels, token_product(): pl.pallas_call(token_kernel, grid_spec=pltpu.PrefetchScalarGridSpec(num_s...  7.69 us
    pallas_call x1, Pallas kernels, backward(): pl.pallas_call(backward_kernel, grid=(tokens // PATCH,), in_specs=[block]...  7.36 us
  transfers between devices with their start and end apart: 12, of which 9 were waited for; matrix products, arithmetic and copies ran while one was open for 2% of the time, Pallas kernels for 11%

profile of v5, /device:TPU:8, one launch (start us, length us, event | category | flops | bytes accessed | tf_op | source)
XLA Modules:
  0.0 182.7 jit_solution(14854941245696240567)
XLA Ops:
  7.2 0.0 all-gather.4.cloned.1.call-start
  7.2 0.7 all-gather.4.cloned.1.call-update
  7.9 0.0 reduce-scatter.2.cloned.1.call-start
  7.9 3.5 %collective-permute-start = (bf16[192,256]{1,0:T(8,128)(2,1)}, bf16[192,256]{1,0:T(8,128)(2,1)S(1)}, u32[]{:S(2)}, u32[]{:S(2)}) collective-permute-start(bf16[192,256]{1,0:T(8,128)(2,1)} %param.10), channel_id=1, source_target_pairs={{0,0},{8,256},{256,8},{264,264},{1,1},{9,257},{257,9},{265,265},{2... | collective-permute-start | bytes 294920 | tf_op jit(solution)/shard_map/ppermute | solution.py:199
  11.4 3.2 %collective-permute-done = bf16[192,256]{1,0:T(8,128)(2,1)S(1)} collective-permute-done((bf16[192,256]{1,0:T(8,128)(2,1)}, bf16[192,256]{1,0:T(8,128)(2,1)S(1)}, u32[]{:S(2)}, u32[]{:S(2)}) %collective-permute-start) | collective-permute-done | bytes 98336 | tf_op jit(solution)/shard_map/ppermute | solution.py:199
  14.7 29.0 %all-gather.1 = bf16[768,256]{1,0:T(8,128)(2,1)S(1)} all-gather(bf16[192,256]{1,0:T(8,128)(2,1)S(1)} %collective-permute-done), channel_id=3, replica_groups=mesh['yl'=2,'za'=4,'zb'=4,'yh'=2,'x'=4,'c'=2] {'za'}, dimensions={0}, use_global_device_ids=true | all-gather | bytes 491520 | tf_op jit(solution)/shard_map/all_gather | solution.py:211
  43.7 1.9 %collective-permute-start.1 = (bf16[4,192,256]{2,1,0:T(8,128)(2,1)S(1)}, bf16[4,192,256]{2,1,0:T(8,128)(2,1)S(1)}, u32[]{:S(2)}, u32[]{:S(2)}) collective-permute-start(bf16[4,192,256]{2,1,0:T(8,128)(2,1)S(1)} %bitcast.20), channel_id=1, source_target_pairs={{0,240},{16,0},{32,16},{48,32},{64,48},{80,64},{96,80},{112,96},{1... | collective-permute-start | bytes 1179656 | tf_op jit(solution)/shard_map/ppermute | solution.py:207
  45.6 5.1 %shard_map.101 = bf16[768,256]{1,0:T(8,128)(2,1)} custom-call(bf16[768,256]{1,0:T(8,128)(2,1)} %q_ref.3, bf16[768,256]{1,0:T(8,128)(2,1)} %k_ref.3, bf16[768,256]{1,0:T(8,128)(2,1)} %v_ref.3, f32[2,128]{1,0:T(2,128)} %gains_ref.3), custom_call_target="tpu_custom_call" | custom-call | tf_op jit(solution)/shard_map/pallas_call | solution.py:56
  50.7 3.5 %collective-permute-start.5 = (bf16[768,256]{1,0:T(8,128)(2,1)}, bf16[768,256]{1,0:T(8,128)(2,1)S(1)}, u32[]{:S(2)}, u32[]{:S(2)}) collective-permute-start(bf16[768,256]{1,0:T(8,128)(2,1)} %shard_map.101), channel_id=1, source_target_pairs={{0,0},{8,256},{256,8},{264,264},{1,1},{9,257},{257,9},{265,265},{2... | collective-permute-start | bytes 1179656 | tf_op jit(solution)/shard_map/ppermute | solution.py:199
  54.2 1.9 %collective-permute-start.6 = (bf16[768,256]{1,0:T(8,128)(2,1)}, bf16[768,256]{1,0:T(8,128)(2,1)S(1)}, u32[]{:S(2)}, u32[]{:S(2)}) collective-permute-start(bf16[768,256]{1,0:T(8,128)(2,1)} %shard_map.101), channel_id=1, source_target_pairs={{0,8},{8,264},{256,0},{264,256},{1,9},{9,265},{257,1},{265,257},{2... | collective-permute-start | bytes 1179656 | tf_op jit(solution)/shard_map/ppermute | solution.py:199
  56.1 3.9 %collective-permute-start.4 = (bf16[4,192,256]{2,1,0:T(8,128)(2,1)S(1)}, bf16[4,192,256]{2,1,0:T(8,128)(2,1)S(1)}, u32[]{:S(2)}, u32[]{:S(2)}) collective-permute-start(bf16[4,192,256]{2,1,0:T(8,128)(2,1)S(1)} %bitcast.21), channel_id=1, source_target_pairs={{0,16},{16,32},{32,48},{48,64},{64,80},{80,96},{96,112},{112,128},... | collective-permute-start | bytes 1179656 | tf_op jit(solution)/shard_map/ppermute | solution.py:207
  60.2 2.3 %collective-permute-start.2 = (bf16[2,192,256]{2,1,0:T(8,128)(2,1)S(1)}, bf16[2,192,256]{2,1,0:T(8,128)(2,1)S(1)}, u32[]{:S(2)}, u32[]{:S(2)}) collective-permute-start(bf16[2,192,256]{2,1,0:T(8,128)(2,1)S(1)} %bitcast.25), channel_id=1, source_target_pairs={{0,32},{16,48},{32,64},{48,80},{64,96},{80,112},{96,128},{112,144}... | collective-permute-start | bytes 589832 | tf_op jit(solution)/shard_map/ppermute | solution.py:207
  62.5 0.0 collective-permute-done.1
  62.5 5.6 %collective-permute-start.3 = (bf16[2,192,256]{2,1,0:T(8,128)(2,1)S(1)}, bf16[2,192,256]{2,1,0:T(8,128)(2,1)S(1)}, u32[]{:S(2)}, u32[]{:S(2)}) collective-permute-start(bf16[2,192,256]{2,1,0:T(8,128)(2,1)S(1)} %bitcast.24), channel_id=1, source_target_pairs={{0,224},{16,240},{32,0},{48,16},{64,32},{80,48},{96,64},{112,80},{... | collective-permute-start | bytes 589832 | tf_op jit(solution)/shard_map/ppermute | solution.py:207
  68.2 4.9 %collective-permute-done.2 = bf16[2,192,256]{2,1,0:T(8,128)(2,1)S(1)} collective-permute-done((bf16[2,192,256]{2,1,0:T(8,128)(2,1)S(1)}, bf16[2,192,256]{2,1,0:T(8,128)(2,1)S(1)}, u32[]{:S(2)}, u32[]{:S(2)}) %collective-permute-start.2) | collective-permute-done | bytes 196640 | tf_op jit(solution)/shard_map/ppermute | solution.py:207
  73.1 0.3 collective-permute-done.3
  73.4 0.5 collective-permute-done.4
  74.1 1.3 constant_dynamic-slice_fusion.weight_ref
  75.4 11.1 %all-gather.4.cloned.1.call-done = bf16[12288,384]{1,0:T(8,128)(2,1)} async-done(((bf16[768,384]{1,0:T(8,128)(2,1)}), bf16[12288,384]{1,0:T(8,128)(2,1)}) %all-gather.4.cloned.1.call-update) | async-done | bytes 9437200 | tf_op jit(solution)/shard_map/all_gather | solution.py:227
  86.4 0.0 collective-permute-done.5.same_ref
  86.4 0.0 copy-start
  86.4 0.0 collective-permute-done.6.other_ref
  86.4 0.0 copy-start.1
  86.4 0.7 copy-done
  87.2 0.1 copy-done.1
  87.3 7.1 %shard_map.102 = bf16[3072,256]{1,0:T(8,128)(2,1)} custom-call(s32[1]{0:T(128)} %bitcast.high_ref, bf16[2,4,2,768,384]{4,3,2,1,0:T(8,128)(2,1)} %bitcast.18, bf16[768,256]{1,0:T(8,128)(2,1)} %copy-done, bf16[768,256]{1,0:T(8,128)(2,1)} %copy-done.1), custom_call_target="tpu_custom_call" | custom-call | flops 2415919104 | bytes 11010048 | tf_op jit(solution)/shard_map/pallas_call | solution.py:129
  94.4 0.0 reduce-scatter.2.cloned.1.call-update
  94.4 7.7 %shard_map.103 = (bf16[768,256]{1,0:T(8,128)(2,1)}, bf16[768,256]{1,0:T(8,128)(2,1)}) custom-call(s32[1]{0:T(128)} %bitcast.high_ref, bf16[2,4,2,768,384]{4,3,2,1,0:T(8,128)(2,1)} %bitcast.19, bf16[4,4,192,256]{3,2,1,0:T(8,128)(2,1)} %constant_dynamic-slice_fusion.weight_ref), custom_call_target="tpu_custom_call" | custom-call | flops 2415919104 | bytes 11010048 | tf_op jit(solution)/shard_map/pallas_call | solution.py:171
  102.1 4.3 %collective-permute-start.7 = (bf16[768,256]{1,0:T(8,128)(2,1)}, bf16[768,256]{1,0:T(8,128)(2,1)S(1)}, u32[]{:S(2)}, u32[]{:S(2)}) collective-permute-start(bf16[768,256]{1,0:T(8,128)(2,1)} %get-tuple-element.19), channel_id=1, source_target_pairs={{0,0},{8,256},{256,8},{264,264},{1,1},{9,257},{257,9},{265,265},{2... | collective-permute-start | bytes 1179656 | tf_op jit(solution)/shard_map/ppermute | solution.py:199
  106.5 1.9 %collective-permute-start.8 = (bf16[768,256]{1,0:T(8,128)(2,1)}, bf16[768,256]{1,0:T(8,128)(2,1)S(1)}, u32[]{:S(2)}, u32[]{:S(2)}) collective-permute-start(bf16[768,256]{1,0:T(8,128)(2,1)} %get-tuple-element.20), channel_id=1, source_target_pairs={{0,256},{8,0},{256,264},{264,8},{1,257},{9,1},{257,265},{265,9},{2... | collective-permute-start | bytes 1179656 | tf_op jit(solution)/shard_map/ppermute | solution.py:199
  108.4 7.8 %collective-permute-done.7.one_ref = bf16[768,256]{1,0:T(8,128)(2,1)S(1)} collective-permute-done((bf16[768,256]{1,0:T(8,128)(2,1)}, bf16[768,256]{1,0:T(8,128)(2,1)S(1)}, u32[]{:S(2)}, u32[]{:S(2)}) %collective-permute-start.7) | collective-permute-done | bytes 393248 | tf_op jit(solution)/shard_map/ppermute | solution.py:199
  116.2 0.0 copy-start.2
  116.2 3.4 %collective-permute-done.8.two_ref = bf16[768,256]{1,0:T(8,128)(2,1)S(1)} collective-permute-done((bf16[768,256]{1,0:T(8,128)(2,1)}, bf16[768,256]{1,0:T(8,128)(2,1)S(1)}, u32[]{:S(2)}, u32[]{:S(2)}) %collective-permute-start.8) | collective-permute-done | bytes 393248 | tf_op jit(solution)/shard_map/ppermute | solution.py:199
  119.6 0.0 copy-done.2
  119.6 0.0 copy-start.3
  119.6 0.8 copy-done.3
  120.3 7.4 %shard_map.104 = (bf16[768,256]{1,0:T(8,128)(2,1)}, bf16[768,256]{1,0:T(8,128)(2,1)}, bf16[768,256]{1,0:T(8,128)(2,1)}, f32[2,128]{1,0:T(2,128)}) custom-call(bf16[768,256]{1,0:T(8,128)(2,1)} %q_ref.3, bf16[768,256]{1,0:T(8,128)(2,1)} %k_ref.3, bf16[768,256]{1,0:T(8,128)(2,1)} %v_ref.3, bf16[768,256]{1,0:T(8,128)(2,1)} %copy-done.2, ...), custom_call_target="tpu_custom_call" | custom-call | tf_op jit(solution)/shard_map/pallas_call | solution.py:102
  127.7 0.7 broadcast_in_dim.4
  128.4 12.6 %all_to_all.10 = f32[32,2,128]{2,1,0:T(2,128)S(1)} all-to-all(f32[32,2,128]{2,1,0:T(2,128)S(1)} %broadcast_in_dim.4), channel_id=1, replica_groups=mesh['yl'=2,'za'=4,'zb'=4,'yh'=2,'x'=4,'c'=2] {'yl','yh','x','c'}, dimensions={0} | all-to-all | bytes 65536 | tf_op jit(solution)/shard_map/all_to_all | solution.py:221
  141.0 24.5 %all_to_all.11 = f32[16,2,128]{2,1,0:T(2,128)S(1)} all-to-all(f32[16,2,128]{2,1,0:T(2,128)S(1)} %broadcast_in_dim.5), channel_id=1, replica_groups=mesh['yl'=2,'za'=4,'zb'=4,'yh'=2,'x'=4,'c'=2] {'za','zb'}, dimensions={0} | all-to-all | bytes 32768 | tf_op jit(solution)/shard_map/all_to_all | solution.py:221
  165.6 0.6 reduce_sum.19
  166.1 2.3 %reduce-scatter.2.cloned.1.call-done = bf16[192,256]{1,0:T(8,128)(2,1)} async-done(((bf16[3072,256]{1,0:T(8,128)(2,1)}), bf16[192,256]{1,0:T(8,128)(2,1)}) %reduce-scatter.2.cloned.1.call-update) | async-done | bytes 98320 | tf_op jit(solution)/shard_map/reduce_scatter | solution.py:237
  168.4 3.2 %collective-permute-start.9 = (bf16[192,256]{1,0:T(8,128)(2,1)}, bf16[192,256]{1,0:T(8,128)(2,1)S(1)}, u32[]{:S(2)}, u32[]{:S(2)}) collective-permute-start(bf16[192,256]{1,0:T(8,128)(2,1)} %reduce-scatter.2.cloned.1.call-done), channel_id=1, source_target_pairs={{0,0},{8,256},{256,8},{264,264},{1,1},{9,257},{257,9},{265,265},{2... | collective-permute-start | bytes 294920 | tf_op jit(solution)/shard_map/ppermute | solution.py:199
  171.7 3.5 %collective-permute-done.9 = bf16[192,256]{1,0:T(8,128)(2,1)S(1)} collective-permute-done((bf16[192,256]{1,0:T(8,128)(2,1)}, bf16[192,256]{1,0:T(8,128)(2,1)S(1)}, u32[]{:S(2)}, u32[]{:S(2)}) %collective-permute-start.9) | collective-permute-done | bytes 98336 | tf_op jit(solution)/shard_map/ppermute | solution.py:199
  175.1 0.7 convert_element_type.3
  (11 shorter events, 0.3 us)
Async XLA Ops:
  7.2 79.3 %all-gather.4.cloned.1.call-start = ((), (), s32[]{:S(2)}) async-start(), calls=%async_computation.4 | async-start | bytes 10027008 | tf_op jit(solution)/shard_map/all_gather | solution.py:227
  7.9 160.5 %reduce-scatter.2.cloned.1.call-start = ((), (), s32[]{:S(2)}) async-start(), calls=%async_computation.3 | async-start | bytes 1671168 | tf_op jit(solution)/shard_map/reduce_scatter | solution.py:237
  7.9 6.7 %collective-permute-start = (bf16[192,256]{1,0:T(8,128)(2,1)}, bf16[192,256]{1,0:T(8,128)(2,1)S(1)}, u32[]{:S(2)}, u32[]{:S(2)}) collective-permute-start(bf16[192,256]{1,0:T(8,128)(2,1)} %param.10), channel_id=1, source_target_pairs={{0,0},{8,256},{256,8},{264,264},{1,1},{9,257},{257,9},{265,265},{2... | collective-permute-start | bytes 294920 | tf_op jit(solution)/shard_map/ppermute | solution.py:199
  43.7 18.8 %collective-permute-start.1 = (bf16[4,192,256]{2,1,0:T(8,128)(2,1)S(1)}, bf16[4,192,256]{2,1,0:T(8,128)(2,1)S(1)}, u32[]{:S(2)}, u32[]{:S(2)}) collective-permute-start(bf16[4,192,256]{2,1,0:T(8,128)(2,1)S(1)} %bitcast.20), channel_id=1, source_target_pairs={{0,240},{16,0},{32,16},{48,32},{64,48},{80,64},{96,80},{112,96},{1... | collective-permute-start | bytes 1179656 | tf_op jit(solution)/shard_map/ppermute | solution.py:207
  50.7 35.7 %collective-permute-start.5 = (bf16[768,256]{1,0:T(8,128)(2,1)}, bf16[768,256]{1,0:T(8,128)(2,1)S(1)}, u32[]{:S(2)}, u32[]{:S(2)}) collective-permute-start(bf16[768,256]{1,0:T(8,128)(2,1)} %shard_map.101), channel_id=1, source_target_pairs={{0,0},{8,256},{256,8},{264,264},{1,1},{9,257},{257,9},{265,265},{2... | collective-permute-start | bytes 1179656 | tf_op jit(solution)/shard_map/ppermute | solution.py:199
  54.2 32.2 %collective-permute-start.6 = (bf16[768,256]{1,0:T(8,128)(2,1)}, bf16[768,256]{1,0:T(8,128)(2,1)S(1)}, u32[]{:S(2)}, u32[]{:S(2)}) collective-permute-start(bf16[768,256]{1,0:T(8,128)(2,1)} %shard_map.101), channel_id=1, source_target_pairs={{0,8},{8,264},{256,0},{264,256},{1,9},{9,265},{257,1},{265,257},{2... | collective-permute-start | bytes 1179656 | tf_op jit(solution)/shard_map/ppermute | solution.py:199
  56.1 17.8 %collective-permute-start.4 = (bf16[4,192,256]{2,1,0:T(8,128)(2,1)S(1)}, bf16[4,192,256]{2,1,0:T(8,128)(2,1)S(1)}, u32[]{:S(2)}, u32[]{:S(2)}) collective-permute-start(bf16[4,192,256]{2,1,0:T(8,128)(2,1)S(1)} %bitcast.21), channel_id=1, source_target_pairs={{0,16},{16,32},{32,48},{48,64},{64,80},{80,96},{96,112},{112,128},... | collective-permute-start | bytes 1179656 | tf_op jit(solution)/shard_map/ppermute | solution.py:207
  60.2 12.9 %collective-permute-start.2 = (bf16[2,192,256]{2,1,0:T(8,128)(2,1)S(1)}, bf16[2,192,256]{2,1,0:T(8,128)(2,1)S(1)}, u32[]{:S(2)}, u32[]{:S(2)}) collective-permute-start(bf16[2,192,256]{2,1,0:T(8,128)(2,1)S(1)} %bitcast.25), channel_id=1, source_target_pairs={{0,32},{16,48},{32,64},{48,80},{64,96},{80,112},{96,128},{112,144}... | collective-permute-start | bytes 589832 | tf_op jit(solution)/shard_map/ppermute | solution.py:207
  62.5 10.9 %collective-permute-start.3 = (bf16[2,192,256]{2,1,0:T(8,128)(2,1)S(1)}, bf16[2,192,256]{2,1,0:T(8,128)(2,1)S(1)}, u32[]{:S(2)}, u32[]{:S(2)}) collective-permute-start(bf16[2,192,256]{2,1,0:T(8,128)(2,1)S(1)} %bitcast.24), channel_id=1, source_target_pairs={{0,224},{16,240},{32,0},{48,16},{64,32},{80,48},{96,64},{112,80},{... | collective-permute-start | bytes 589832 | tf_op jit(solution)/shard_map/ppermute | solution.py:207
  86.4 0.7 copy-start
  86.4 0.9 copy-start.1
  102.1 14.1 %collective-permute-start.7 = (bf16[768,256]{1,0:T(8,128)(2,1)}, bf16[768,256]{1,0:T(8,128)(2,1)S(1)}, u32[]{:S(2)}, u32[]{:S(2)}) collective-permute-start(bf16[768,256]{1,0:T(8,128)(2,1)} %get-tuple-element.19), channel_id=1, source_target_pairs={{0,0},{8,256},{256,8},{264,264},{1,1},{9,257},{257,9},{265,265},{2... | collective-permute-start | bytes 1179656 | tf_op jit(solution)/shard_map/ppermute | solution.py:199
  106.5 13.1 %collective-permute-start.8 = (bf16[768,256]{1,0:T(8,128)(2,1)}, bf16[768,256]{1,0:T(8,128)(2,1)S(1)}, u32[]{:S(2)}, u32[]{:S(2)}) collective-permute-start(bf16[768,256]{1,0:T(8,128)(2,1)} %get-tuple-element.20), channel_id=1, source_target_pairs={{0,256},{8,0},{256,264},{264,8},{1,257},{9,1},{257,265},{265,9},{2... | collective-permute-start | bytes 1179656 | tf_op jit(solution)/shard_map/ppermute | solution.py:199
  116.2 3.4 %copy-start.2 = (bf16[768,256]{1,0:T(8,128)(2,1)}, bf16[768,256]{1,0:T(8,128)(2,1)S(1)}, u32[]{:S(2)}) copy-start(bf16[768,256]{1,0:T(8,128)(2,1)S(1)} %collective-permute-done.7.one_ref) | copy-start | bytes 1179652
  119.6 0.8 copy-start.3
  168.4 6.7 %collective-permute-start.9 = (bf16[192,256]{1,0:T(8,128)(2,1)}, bf16[192,256]{1,0:T(8,128)(2,1)S(1)}, u32[]{:S(2)}, u32[]{:S(2)}) collective-permute-start(bf16[192,256]{1,0:T(8,128)(2,1)} %reduce-scatter.2.cloned.1.call-done), channel_id=1, source_target_pairs={{0,0},{8,256},{256,8},{264,264},{1,1},{9,257},{257,9},{265,265},{2... | collective-permute-start | bytes 294920 | tf_op jit(solution)/shard_map/ppermute | solution.py:199
Sparse Core Ops, SparseCore 0:
  10.1 76.2 all-gather.3
  94.6 73.8 reduce-scatter.1

commit v6 on v5

v6 whole, which is shorter than its diff:
```python
import jax
import jax.numpy as jnp
from jax import lax
from jax.experimental import pallas as pl
from jax.experimental.pallas import tpu as pltpu
from jax.sharding import Mesh, PartitionSpec as P

HD = 128
PATCH = 256
EPSILON = 1e-06
SCALE = HD ** (-0.5)
AXES = ("yl", "z", "yh", "x", "c")
SIZES = (2, 16, 2, 4, 2)
VMEM_LIMIT = 56 * 1024 * 1024


def normalize(raw, gain):
    values32 = raw.astype(jnp.float32)
    center = values32 - jnp.mean(values32, axis=-1, keepdims=True)
    inverse = lax.rsqrt(jnp.mean(center * center, axis=-1, keepdims=True) + EPSILON)
    unit = center * inverse
    return (unit, inverse, (unit * gain).astype(jnp.bfloat16))


def unnormalize(grad, unit, inverse, gain):
    scaled = grad * gain
    centered = scaled - jnp.mean(scaled, axis=-1, keepdims=True)
    return (centered - unit * jnp.mean(scaled * unit, axis=-1, keepdims=True)) * inverse


def product(left, right, left_dim, right_dim):
    return lax.dot_general(
        left, right, (((left_dim,), (right_dim,)), ((), ())), preferred_element_type=jnp.float32
    )


def softmax(q_norm, k_norm):
    scores = product(q_norm, k_norm, 1, 1) * SCALE
    expo = jnp.exp(scores - jnp.max(scores, axis=-1, keepdims=True))
    return expo / jnp.sum(expo, axis=-1, keepdims=True)


def forward_kernel(q_ref, k_ref, v_ref, gains_ref, attn_ref):
    for head in range(q_ref.shape[1] // HD):
        cols = slice(head * HD, (head + 1) * HD)
        _, _, q_norm = normalize(q_ref[:, cols], gains_ref[0:1, :])
        _, _, k_norm = normalize(k_ref[:, cols], gains_ref[1:2, :])
        prob_low = softmax(q_norm, k_norm).astype(jnp.bfloat16)
        attn_ref[:, cols] = product(prob_low, v_ref[:, cols], 1, 0).astype(jnp.bfloat16)


def forward(queries_raw, keys_raw, values, norm_gains):
    tokens, width = queries_raw.shape
    block = pl.BlockSpec((PATCH, width), lambda i: (i, 0))
    return pl.pallas_call(
        forward_kernel,
        grid=(tokens // PATCH,),
        in_specs=[block, block, block, pl.BlockSpec((2, HD), lambda i: (0, 0))],
        out_specs=block,
        out_shape=jax.ShapeDtypeStruct((tokens, width), jnp.bfloat16),
        compiler_params=pltpu.CompilerParams(vmem_limit_bytes=VMEM_LIMIT),
    )(queries_raw, keys_raw, values, norm_gains)


def backward_kernel(
    q_ref, k_ref, v_ref, one_ref, two_ref, gains_ref, qg_ref, kg_ref, vg_ref, terms_ref
):
    @pl.when(pl.program_id(0) == 0)
    def _():
        terms_ref[...] = jnp.zeros_like(terms_ref)

    q_gain, k_gain = gains_ref[0:1, :], gains_ref[1:2, :]
    for head in range(q_ref.shape[1] // HD):
        cols = slice(head * HD, (head + 1) * HD)
        value = v_ref[:, cols]
        q_unit, q_inverse, q_norm = normalize(q_ref[:, cols], q_gain)
        k_unit, k_inverse, k_norm = normalize(k_ref[:, cols], k_gain)
        prob = softmax(q_norm, k_norm)
        prob_low = prob.astype(jnp.bfloat16)
        attn = product(prob_low, value, 1, 0).astype(jnp.bfloat16)
        grad = one_ref[:, cols].astype(jnp.float32) + two_ref[:, cols].astype(jnp.float32)
        grad = grad.astype(jnp.bfloat16)
        vg_ref[:, cols] = product(prob_low, grad, 0, 0).astype(jnp.bfloat16)
        delta = jnp.sum(
            grad.astype(jnp.float32) * attn.astype(jnp.float32), axis=-1, keepdims=True
        )
        score_grad = (prob * (product(grad, value, 1, 1) - delta)).astype(jnp.bfloat16)
        qn_grad = product(score_grad, k_norm, 1, 0) * SCALE
        kn_grad = product(score_grad, q_norm, 0, 0) * SCALE
        terms_ref[0:1, :] += jnp.sum(qn_grad * q_unit, axis=0, keepdims=True)
        terms_ref[1:2, :] += jnp.sum(kn_grad * k_unit, axis=0, keepdims=True)
        qg_ref[:, cols] = unnormalize(qn_grad, q_unit, q_inverse, q_gain).astype(jnp.bfloat16)
        kg_ref[:, cols] = unnormalize(kn_grad, k_unit, k_inverse, k_gain).astype(jnp.bfloat16)


def backward(queries_raw, keys_raw, values, part_one, part_two, norm_gains):
    tokens, width = queries_raw.shape
    block = pl.BlockSpec((PATCH, width), lambda i: (i, 0))
    gains = pl.BlockSpec((2, HD), lambda i: (0, 0))
    out = jax.ShapeDtypeStruct((tokens, width), jnp.bfloat16)
    return pl.pallas_call(
        backward_kernel,
        grid=(tokens // PATCH,),
        in_specs=[block] * 5 + [gains],
        out_specs=[block, block, block, gains],
        out_shape=[out, out, out, jax.ShapeDtypeStruct((2, HD), jnp.float32)],
        compiler_params=pltpu.CompilerParams(vmem_limit_bytes=VMEM_LIMIT),
    )(queries_raw, keys_raw, values, part_one, part_two, norm_gains)


STEPS = (0, 3, 1, 2)
CHUNK = 256


def row_block(place_ref, index):
    x = lax.rem(place_ref[0] + STEPS[index % 4], 4)
    core = place_ref[1] if index < 4 else 1 - place_ref[1]
    return 2 * x + core


def rows_of(place_ref, index, width):
    return pl.ds(pl.multiple_of(row_block(place_ref, index) * width, width), width)


def weight_kernel(place_ref, own_attn_ref, other_attn_ref, *refs):
    own_refs, other_refs, (wgrad_ref, total) = refs[:8], refs[8:16], refs[16:]
    step = pl.program_id(0)
    width = own_refs[0].shape[1]
    own_attn, other_attn = own_attn_ref[...], other_attn_ref[...]
    for index in range(8):
        rows = rows_of(place_ref, index, width)
        term = product(own_refs[index][...], own_attn, 0, 0)
        term += product(other_refs[index][...], other_attn, 0, 0)

        @pl.when(step == 0)
        def _():
            total[rows] = term

        @pl.when(step > 0)
        def _():
            total[rows] += term

    @pl.when(step == pl.num_programs(0) - 1)
    def _():
        wgrad_ref[...] = total[...].astype(wgrad_ref.dtype)


def weight_product(place, own, other, own_attn, other_attn):
    tokens, width = own[0].shape
    heads = own_attn.shape[1]
    rows = 8 * width
    block = pl.BlockSpec((CHUNK, width), lambda i, place: (i, 0))
    attn = pl.BlockSpec((CHUNK, heads), lambda i, place: (i, 0))
    return pl.pallas_call(
        weight_kernel,
        grid_spec=pltpu.PrefetchScalarGridSpec(
            num_scalar_prefetch=1,
            grid=(tokens // CHUNK,),
            in_specs=[attn, attn] + [block] * 16,
            out_specs=pl.BlockSpec((rows, heads), lambda i, place: (0, 0)),
            scratch_shapes=[pltpu.VMEM((rows, heads), jnp.float32)],
        ),
        out_shape=jax.ShapeDtypeStruct((rows, heads), jnp.bfloat16),
        compiler_params=pltpu.CompilerParams(vmem_limit_bytes=VMEM_LIMIT),
        cost_estimate=pl.CostEstimate(
            flops=4 * rows * tokens * heads,
            bytes_accessed=2 * (2 * rows * tokens + rows * heads),
            transcendentals=0,
        ),
    )(place, own_attn, other_attn, *own, *other)


def token_kernel(place_ref, weight_ref, *refs):
    blocks, part_ref = refs[:8], refs[8]
    width = blocks[0].shape[1]
    total = None
    for index in range(8):
        term = product(blocks[index][...], weight_ref[rows_of(place_ref, index, width)], 1, 0)
        total = term if total is None else total + term
    part_ref[...] = total.astype(part_ref.dtype)


def token_product(place, blocks, weights):
    tokens, width = blocks[0].shape
    rows, heads = weights.shape
    return pl.pallas_call(
        token_kernel,
        grid_spec=pltpu.PrefetchScalarGridSpec(
            num_scalar_prefetch=1,
            grid=(tokens // CHUNK,),
            in_specs=[pl.BlockSpec((rows, heads), lambda i, place: (0, 0))]
            + [pl.BlockSpec((CHUNK, width), lambda i, place: (i, 0))] * 8,
            out_specs=pl.BlockSpec((CHUNK, heads), lambda i, place: (i, 0)),
        ),
        out_shape=jax.ShapeDtypeStruct((tokens, heads), jnp.bfloat16),
        compiler_params=pltpu.CompilerParams(vmem_limit_bytes=VMEM_LIMIT),
        cost_estimate=pl.CostEstimate(
            flops=2 * rows * tokens * heads,
            bytes_accessed=2 * rows * (tokens + heads),
            transcendentals=0,
        ),
    )(place, weights, *blocks)


def swap_y(array, target):
    pairs = []
    for low in range(2):
        for high in range(2):
            place = target(low, high)
            if place is not None:
                pairs.append((low * 2 + high, place[0] * 2 + place[1]))
    return lax.ppermute(array, ("yl", "yh"), pairs)


def to_partner(array):
    return lax.ppermute(array, "yl", [(0, 1), (1, 0)])


def to_core(array):
    return lax.ppermute(array, "c", [(0, 1), (1, 0)])


def along_x(array, step):
    return lax.ppermute(array, "x", [(x, (x + step) % 4) for x in range(4)])


def halves_for(grad_out):
    near = swap_y(grad_out, lambda low, up: (up, up) if low != up else None)
    cross = swap_y(grad_out, lambda low, up: (up, 1 - up) if low != up else None)
    far = swap_y(grad_out, lambda low, up: (up, 1 - up) if low == up else None)
    stays = lax.axis_index("yl") == lax.axis_index("yh")
    return jnp.where(stays, grad_out, far), jnp.where(stays, near, cross)


def round_x(block):
    half = block.shape[0] // 2
    left, right = along_x(block, 1), along_x(block, -1)
    opposite = [along_x(left[:half], 1), along_x(right[half:], -1)]
    blocks = [block, left, right, jnp.concatenate(opposite)]
    return blocks + [to_core(piece) for piece in blocks]


def sum_over(array, axis, count):
    spread = lax.all_to_all(jnp.broadcast_to(array[None], (count,) + array.shape), axis, 0, 0)
    return jnp.sum(spread, axis=0)


def per_device(queries_raw, keys_raw, values, grad_out, out_weight, norm_gains):
    place = jnp.stack([lax.axis_index("x"), lax.axis_index("c")]).astype(jnp.int32)
    weights = lax.all_gather(out_weight, "z", axis=0, tiled=True)
    own, other = halves_for(grad_out)
    other, own = round_x(other), round_x(own)

    attn = forward(queries_raw, keys_raw, values, norm_gains)
    wgrad = weight_product(place, own, other, attn, to_partner(attn))
    shard = lax.psum_scatter(wgrad, "z", scatter_dimension=0, tiled=True)

    weights, _ = lax.optimization_barrier((weights, wgrad))
    part_other = token_product(place, other, weights)
    weights, _ = lax.optimization_barrier((weights, part_other))
    part_own = token_product(place, own, weights)
    queries_grad, keys_grad, values_grad, terms = backward(
        queries_raw, keys_raw, values, part_own, to_partner(part_other), norm_gains
    )
    gains_grad = sum_over(sum_over(terms, ("yl", "yh", "x", "c"), 32), "z", 16)
    shard, gains_grad = lax.optimization_barrier((shard, gains_grad))
    return (queries_grad, keys_grad, values_grad, shard.astype(jnp.float32), gains_grad)


def solution(mesh):
    fine = Mesh(mesh.devices.reshape(SIZES), AXES)
    spec = P(("yl", "z"), ("yh", "x", "c"))
    return jax.shard_map(
        per_device,
        mesh=fine,
        in_specs=(spec, spec, spec, spec, spec, P()),
        out_specs=(spec, spec, spec, spec, P()),
        check_vma=False,
    )
```

time: 183 us -> 215 us (1.17)
  the two profiles are of different devices: /device:TPU:8 before, /device:TPU:6 now
where the time goes in v6:
time: 215 us; the launch traced here: 214 us
  starting transfers between devices  71.8 us (33%)
  waiting for transfers between devices  40.3 us (19%)
  blocking collectives  39.4 us (18%)
  Pallas kernels  39.3 us (18%)
  between operations  14.5 us (7%)
  local copies, waits for them, and re-layouts  6.28 us (3%)
  other arithmetic  2.94 us (1%)
    all_to_all x2, blocking collectives, sum_over(): lax.all_to_all(jnp.broadcast_to(array[None], (count,) + array.shape), axi...  39.4 us
    ppermute x8, starting transfers between devices, along_x(): return lax.ppermute(array, 'x', [(x, (x + step) % 4) for x in range(4)])  23.6 us
    ppermute x2, starting transfers between devices, to_partner(): return lax.ppermute(array, 'yl', [(0, 1), (1, 0)])  20.9 us
    ppermute x8, waiting for transfers between devices, along_x(): return lax.ppermute(array, 'x', [(x, (x + step) % 4) for x in range(4)])  20.8 us
    ppermute x8, starting transfers between devices, to_core(): return lax.ppermute(array, 'c', [(0, 1), (1, 0)])  16.8 us
    pallas_call x1, Pallas kernels, weight_product(): pl.pallas_call(weight_kernel, grid_spec=pltpu.PrefetchScalarGridSpec(num_...  13.7 us
    pallas_call x2, Pallas kernels, token_product(): pl.pallas_call(token_kernel, grid_spec=pltpu.PrefetchScalarGridSpec(num_s...  13.1 us
    ppermute x3, starting transfers between devices, swap_y(): return lax.ppermute(array, ('yl', 'yh'), pairs)  10.4 us
  transfers between devices with their start and end apart: 23, of which 7 were waited for; matrix products, arithmetic and copies ran while one was open for 2% of the time, Pallas kernels for 18%

profile of v6, /device:TPU:6, one launch (start us, length us, event | category | flops | bytes accessed | tf_op | source)
XLA Modules:
  0.0 214.5 jit_solution(15220825197579084553)
XLA Ops:
  7.2 1.4 collective-permute-start.10
  8.7 0.7 collective-permute-start.11
  9.4 8.3 %collective-permute-start.1 = (bf16[768,384]{1,0:T(8,128)(2,1)}, bf16[768,384]{1,0:T(8,128)(2,1)S(1)}, u32[]{:S(2)}, u32[]{:S(2)}) collective-permute-start(bf16[768,384]{1,0:T(8,128)(2,1)} %param.9), channel_id=1, source_target_pairs={{0,8},{264,256},{1,9},{265,257},{2,10},{266,258},{3,11},{267,259},... | collective-permute-start | bytes 1769480 | tf_op jit(solution)/shard_map/ppermute | solution.py:212
  17.7 6.8 %collective-permute-done.10 = bf16[768,384]{1,0:T(8,128)(2,1)S(1)} collective-permute-done((bf16[768,384]{1,0:T(8,128)(2,1)}, bf16[768,384]{1,0:T(8,128)(2,1)S(1)}, u32[]{:S(2)}, u32[]{:S(2)}) %collective-permute-start.10) | collective-permute-done | bytes 589856 | tf_op jit(solution)/shard_map/ppermute | solution.py:212
  24.5 0.1 broadcast_select_fusion.refs_8_.refs_0_
  24.6 2.6 %collective-permute-start.12 = (bf16[768,384]{1,0:T(8,128)(2,1)S(1)}, bf16[768,384]{1,0:T(8,128)(2,1)S(1)}, u32[]{:S(2)}, u32[]{:S(2)}) collective-permute-start(bf16[768,384]{1,0:T(8,128)(2,1)S(1)} %broadcast_select_fusion.refs_8_.refs_0_), channel_id=1, source_target_pairs={{0,2},{2,4},{4,6},{6,0},{1,3},{3,5},{5,7},{7,1},{8,10},{10,12},{12... | collective-permute-start | bytes 1769480 | tf_op jit(solution)/shard_map/ppermute | solution.py:224
  27.2 3.3 %collective-permute-start.13 = (bf16[768,384]{1,0:T(8,128)(2,1)S(1)}, bf16[768,384]{1,0:T(8,128)(2,1)S(1)}, u32[]{:S(2)}, u32[]{:S(2)}) collective-permute-start(bf16[768,384]{1,0:T(8,128)(2,1)S(1)} %broadcast_select_fusion.refs_8_.refs_0_), channel_id=1, source_target_pairs={{0,6},{2,0},{4,2},{6,4},{1,7},{3,1},{5,3},{7,5},{8,14},{10,8},{12,... | collective-permute-start | bytes 1769480 | tf_op jit(solution)/shard_map/ppermute | solution.py:224
  30.5 0.1 broadcast_select_fusion.1.refs_0_
  30.6 3.8 %collective-permute-start.2 = (bf16[768,384]{1,0:T(8,128)(2,1)S(1)}, bf16[768,384]{1,0:T(8,128)(2,1)S(1)}, u32[]{:S(2)}, u32[]{:S(2)}) collective-permute-start(bf16[768,384]{1,0:T(8,128)(2,1)S(1)} %broadcast_select_fusion.1.refs_0_), channel_id=1, source_target_pairs={{0,2},{2,4},{4,6},{6,0},{1,3},{3,5},{5,7},{7,1},{8,10},{10,12},{12... | collective-permute-start | bytes 1769480 | tf_op jit(solution)/shard_map/ppermute | solution.py:224
  34.4 2.1 collective-permute-start.3
  36.4 6.3 %collective-permute-done.12.refs_9_.refs_1_ = bf16[768,384]{1,0:T(8,128)(2,1)S(1)} collective-permute-done((bf16[768,384]{1,0:T(8,128)(2,1)S(1)}, bf16[768,384]{1,0:T(8,128)(2,1)S(1)}, u32[]{:S(2)}, u32[]{:S(2)}) %collective-permute-start.12) | collective-permute-done | bytes 589856 | tf_op jit(solution)/shard_map/ppermute | solution.py:224
  42.8 3.8 %collective-permute-start.14 = (bf16[384,384]{1,0:T(8,128)(2,1)S(1)}, bf16[384,384]{1,0:T(8,128)(2,1)S(1)}, u32[]{:S(2)}, u32[]{:S(2)}) collective-permute-start(bf16[384,384]{1,0:T(8,128)(2,1)S(1)} %slice.18), channel_id=1, source_target_pairs={{0,2},{2,4},{4,6},{6,0},{1,3},{3,5},{5,7},{7,1},{8,10},{10,12},{12... | collective-permute-start | bytes 884744 | tf_op jit(solution)/shard_map/ppermute | solution.py:224
  46.7 2.1 collective-permute-start.15
  48.7 6.7 %collective-permute-done.2.refs_1_ = bf16[768,384]{1,0:T(8,128)(2,1)S(1)} collective-permute-done((bf16[768,384]{1,0:T(8,128)(2,1)S(1)}, bf16[768,384]{1,0:T(8,128)(2,1)S(1)}, u32[]{:S(2)}, u32[]{:S(2)}) %collective-permute-start.2) | collective-permute-done | bytes 589856 | tf_op jit(solution)/shard_map/ppermute | solution.py:224
  55.4 3.8 %collective-permute-start.4 = (bf16[384,384]{1,0:T(8,128)(2,1)S(1)}, bf16[384,384]{1,0:T(8,128)(2,1)S(1)}, u32[]{:S(2)}, u32[]{:S(2)}) collective-permute-start(bf16[384,384]{1,0:T(8,128)(2,1)S(1)} %slice.16), channel_id=1, source_target_pairs={{0,2},{2,4},{4,6},{6,0},{1,3},{3,5},{5,7},{7,1},{8,10},{10,12},{12... | collective-permute-start | bytes 884744 | tf_op jit(solution)/shard_map/ppermute | solution.py:224
  59.3 1.9 collective-permute-start.16
  61.2 2.4 %collective-permute-start.6 = (bf16[768,384]{1,0:T(8,128)(2,1)S(1)}, bf16[768,384]{1,0:T(8,128)(2,1)S(1)}, u32[]{:S(2)}, u32[]{:S(2)}) collective-permute-start(bf16[768,384]{1,0:T(8,128)(2,1)S(1)} %broadcast_select_fusion.1.refs_0_), channel_id=1, source_target_pairs={{0,1},{1,0},{2,3},{3,2},{4,5},{5,4},{6,7},{7,6},{8,9},{9,8},{10,11... | collective-permute-start | bytes 1769480 | tf_op jit(solution)/shard_map/ppermute | solution.py:220
  63.6 1.9 collective-permute-start.17
  65.6 5.1 %shard_map.101.own_attn_ref = bf16[768,256]{1,0:T(8,128)(2,1)} custom-call(bf16[768,256]{1,0:T(8,128)(2,1)} %q_ref.3, bf16[768,256]{1,0:T(8,128)(2,1)} %k_ref.3, bf16[768,256]{1,0:T(8,128)(2,1)} %v_ref.3, f32[2,128]{1,0:T(2,128)} %gains_ref.3), custom_call_target="tpu_custom_call" | custom-call | tf_op jit(solution)/shard_map/pallas_call | solution.py:55
  70.7 18.7 %collective-permute-start = (bf16[768,256]{1,0:T(8,128)(2,1)}, bf16[768,256]{1,0:T(8,128)(2,1)S(1)}, u32[]{:S(2)}, u32[]{:S(2)}) collective-permute-start(bf16[768,256]{1,0:T(8,128)(2,1)} %shard_map.101.own_attn_ref), channel_id=1, source_target_pairs={{0,256},{256,0},{1,257},{257,1},{2,258},{258,2},{3,259},{259,3},{4... | collective-permute-start | bytes 1179656 | tf_op jit(solution)/shard_map/ppermute | solution.py:216
  89.4 2.2 %collective-permute-start.5 = (bf16[384,384]{1,0:T(8,128)(2,1)S(1)}, bf16[384,384]{1,0:T(8,128)(2,1)S(1)}, u32[]{:S(2)}, u32[]{:S(2)}) collective-permute-start(bf16[384,384]{1,0:T(8,128)(2,1)S(1)} %slice.17), channel_id=1, source_target_pairs={{0,6},{2,0},{4,2},{6,4},{1,7},{3,1},{5,3},{7,5},{8,14},{10,8},{12,... | collective-permute-start | bytes 884744 | tf_op jit(solution)/shard_map/ppermute | solution.py:224
  91.7 0.7 constant_dynamic-update-slice_fusion.3
  92.4 0.7 constant_dynamic-update-slice_fusion.1
  93.2 0.8 constant_dynamic-update-slice_fusion.2.refs_11_.refs_3_
  93.9 7.7 %collective-permute-done.5 = bf16[384,384]{1,0:T(8,128)(2,1)S(1)} collective-permute-done((bf16[384,384]{1,0:T(8,128)(2,1)S(1)}, bf16[384,384]{1,0:T(8,128)(2,1)S(1)}, u32[]{:S(2)}, u32[]{:S(2)}) %collective-permute-start.5) | collective-permute-done | bytes 294944 | tf_op jit(solution)/shard_map/ppermute | solution.py:224
  101.7 1.9 collective-permute-start.18
  103.6 0.8 constant_dynamic-update-slice_fusion.refs_3_
  104.4 2.4 %collective-permute-start.7 = (bf16[768,384]{1,0:T(8,128)(2,1)S(1)}, bf16[768,384]{1,0:T(8,128)(2,1)}, u32[]{:S(2)}, u32[]{:S(2)}) collective-permute-start(bf16[768,384]{1,0:T(8,128)(2,1)S(1)} %collective-permute-done.2.refs_1_), channel_id=1, source_target_pairs={{0,1},{1,0},{2,3},{3,2},{4,5},{5,4},{6,7},{7,6},{8,9},{9,8},{10,11... | collective-permute-start | bytes 1769480 | tf_op jit(solution)/shard_map/ppermute | solution.py:220
  106.8 1.9 collective-permute-start.8
  108.7 2.4 %collective-permute-start.19 = (bf16[768,384]{1,0:T(8,128)(2,1)}, bf16[768,384]{1,0:T(8,128)(2,1)}, u32[]{:S(2)}, u32[]{:S(2)}) collective-permute-start(bf16[768,384]{1,0:T(8,128)(2,1)} %constant_dynamic-update-slice_fusion.2.refs_11_.refs_3_), channel_id=1, source_target_pairs={{0,1},{1,0},{2,3},{3,2},{4,5},{5,4},{6,7},{7,6},{8,9},{9,8},{10,11... | collective-permute-start | bytes 1769480 | tf_op jit(solution)/shard_map/ppermute | solution.py:220
  111.2 0.8 copy-done.8
  112.0 1.9 collective-permute-start.9
  113.9 0.6 pad_add_fusion.place_ref
  114.6 1.6 collective-permute-done.9.refs_7_
  116.1 0.9 copy-done.10
  117.0 13.7 %shard_map.102 = bf16[3072,256]{1,0:T(8,128)(2,1)} custom-call(s32[2]{0:T(128)} %pad_add_fusion.place_ref, bf16[768,256]{1,0:T(8,128)(2,1)} %shard_map.101.own_attn_ref, bf16[768,256]{1,0:T(8,128)(2,1)} %copy-done.12, bf16[768,384]{1,0:T(8,128)(2,1)} %copy-done.1, bf16[768,384]{1,0:T(8,128)(2,1)} %copy-done.3, bf16[768,384]{1,0:T(8,128)(2,1)} %copy-done.5, ...), custom_call_target="tpu_custom_call" | custom-call | flops 2415919104 | bytes 11010048 | tf_op jit(solution)/shard_map/pallas_call | solution.py:154
  130.7 6.6 %shard_map.103 = bf16[768,256]{1,0:T(8,128)(2,1)} custom-call(s32[2]{0:T(128)} %pad_add_fusion.place_ref, bf16[3072,256]{1,0:T(8,128)(2,1)} %all-gather.2.cloned.1.call-done.weight_ref, bf16[768,384]{1,0:T(8,128)(2,1)} %copy-done, bf16[768,384]{1,0:T(8,128)(2,1)} %copy-done.2, bf16[768,384]{1,0:T(8,128)(2,1)} %copy-done.4, ...), custom_call_target="tpu_custom_call" | custom-call | flops 1207959552 | bytes 6291456 | tf_op jit(solution)/shard_map/pallas_call | solution.py:186
  137.3 2.2 %collective-permute-start.20 = (bf16[768,256]{1,0:T(8,128)(2,1)}, bf16[768,256]{1,0:T(8,128)(2,1)S(1)}, u32[]{:S(2)}, u32[]{:S(2)}) collective-permute-start(bf16[768,256]{1,0:T(8,128)(2,1)} %shard_map.103), channel_id=1, source_target_pairs={{0,256},{256,0},{1,257},{257,1},{2,258},{258,2},{3,259},{259,3},{4... | collective-permute-start | bytes 1179656 | tf_op jit(solution)/shard_map/ppermute | solution.py:216
  139.5 6.6 %shard_map.104.one_ref = bf16[768,256]{1,0:T(8,128)(2,1)} custom-call(s32[2]{0:T(128)} %pad_add_fusion.place_ref, bf16[3072,256]{1,0:T(8,128)(2,1)} %all-gather.2.cloned.1.call-done.weight_ref, bf16[768,384]{1,0:T(8,128)(2,1)} %copy-done.1, bf16[768,384]{1,0:T(8,128)(2,1)} %copy-done.3, bf16[768,384]{1,0:T(8,128)(2,1)} %copy-done.5, ...), custom_call_target="tpu_custom_call" | custom-call | flops 1207959552 | bytes 6291456 | tf_op jit(solution)/shard_map/pallas_call | solution.py:186
  146.1 4.5 %collective-permute-done.20.two_ref = bf16[768,256]{1,0:T(8,128)(2,1)S(1)} collective-permute-done((bf16[768,256]{1,0:T(8,128)(2,1)}, bf16[768,256]{1,0:T(8,128)(2,1)S(1)}, u32[]{:S(2)}, u32[]{:S(2)}) %collective-permute-start.20) | collective-permute-done | bytes 393248 | tf_op jit(solution)/shard_map/ppermute | solution.py:216
  150.5 0.7 copy-done.13
  151.3 7.4 %shard_map.105 = (bf16[768,256]{1,0:T(8,128)(2,1)}, bf16[768,256]{1,0:T(8,128)(2,1)}, bf16[768,256]{1,0:T(8,128)(2,1)}, f32[2,128]{1,0:T(2,128)}) custom-call(bf16[768,256]{1,0:T(8,128)(2,1)} %q_ref.3, bf16[768,256]{1,0:T(8,128)(2,1)} %k_ref.3, bf16[768,256]{1,0:T(8,128)(2,1)} %v_ref.3, bf16[768,256]{1,0:T(8,128)(2,1)} %shard_map.104.one_ref, ...), custom_call_target="tpu_custom_call" | custom-call | tf_op jit(solution)/shard_map/pallas_call | solution.py:101
  158.7 0.7 broadcast_in_dim.4
  159.3 11.9 %all_to_all.10 = f32[32,2,128]{2,1,0:T(2,128)S(1)} all-to-all(f32[32,2,128]{2,1,0:T(2,128)S(1)} %broadcast_in_dim.4), channel_id=1, replica_groups=mesh['yl'=2,'z'=16,'yh'=2,'x'=4,'c'=2] {'yl','yh','x','c'}, dimensions={0} | all-to-all | bytes 65536 | tf_op jit(solution)/shard_map/all_to_all | solution.py:244
  171.3 27.5 %all_to_all.11 = f32[16,2,128]{2,1,0:T(2,128)S(1)} all-to-all(f32[16,2,128]{2,1,0:T(2,128)S(1)} %broadcast_in_dim.5), channel_id=1, replica_groups=mesh['yl'=2,'z'=16,'yh'=2,'x'=4,'c'=2] {'z'}, dimensions={0} | all-to-all | bytes 32768 | tf_op jit(solution)/shard_map/all_to_all | solution.py:244
  198.8 0.6 reduce_sum.19
  199.4 6.7 %reduce-scatter.2.cloned.1.call-done = bf16[192,256]{1,0:T(8,128)(2,1)} async-done(((bf16[3072,256]{1,0:T(8,128)(2,1)}), bf16[192,256]{1,0:T(8,128)(2,1)}) %reduce-scatter.2.cloned.1.call-update) | async-done | bytes 98320 | tf_op jit(solution)/shard_map/reduce_scatter | solution.py:256
  206.1 1.6 convert_element_type.3
  (51 shorter events, 0.4 us)
Async XLA Ops:
  7.2 23.3 %copy-start.11 = (bf16[768,384]{1,0:T(8,128)(2,1)S(1)}, bf16[768,384]{1,0:T(8,128)(2,1)}, u32[]{:S(2)}) copy-start(bf16[768,384]{1,0:T(8,128)(2,1)} %param.9) | copy-start | bytes 1769476
  7.2 123.6 %all-gather.2.cloned.1.call-start = ((), (), s32[]{:S(2)}) async-start(), calls=%async_computation.3 | async-start | bytes 1671168 | tf_op jit(solution)/shard_map/all_gather | solution.py:250
  7.2 17.3 %collective-permute-start.10 = (bf16[768,384]{1,0:T(8,128)(2,1)}, bf16[768,384]{1,0:T(8,128)(2,1)S(1)}, u32[]{:S(2)}, u32[]{:S(2)}) collective-permute-start(bf16[768,384]{1,0:T(8,128)(2,1)} %param.9), channel_id=1, source_target_pairs={{8,264},{256,0},{9,265},{257,1},{10,266},{258,2},{11,267},{259,3},... | collective-permute-start | bytes 1769480 | tf_op jit(solution)/shard_map/ppermute | solution.py:212
  8.7 15.9 %collective-permute-start.11 = (bf16[768,384]{1,0:T(8,128)(2,1)}, bf16[768,384]{1,0:T(8,128)(2,1)S(1)}, u32[]{:S(2)}, u32[]{:S(2)}) collective-permute-start(bf16[768,384]{1,0:T(8,128)(2,1)} %param.9), channel_id=1, source_target_pairs={{8,256},{256,8},{9,257},{257,9},{10,258},{258,10},{11,259},{259,11... | collective-permute-start | bytes 1769480 | tf_op jit(solution)/shard_map/ppermute | solution.py:212
  9.4 21.1 %collective-permute-start.1 = (bf16[768,384]{1,0:T(8,128)(2,1)}, bf16[768,384]{1,0:T(8,128)(2,1)S(1)}, u32[]{:S(2)}, u32[]{:S(2)}) collective-permute-start(bf16[768,384]{1,0:T(8,128)(2,1)} %param.9), channel_id=1, source_target_pairs={{0,8},{264,256},{1,9},{265,257},{2,10},{266,258},{3,11},{267,259},... | collective-permute-start | bytes 1769480 | tf_op jit(solution)/shard_map/ppermute | solution.py:212
  17.7 188.4 %reduce-scatter.2.cloned.1.call-start = ((), (), s32[]{:S(2)}) async-start(), calls=%async_computation.4 | async-start | bytes 1671168 | tf_op jit(solution)/shard_map/reduce_scatter | solution.py:256
  24.6 34.6 %copy-start = (bf16[768,384]{1,0:T(8,128)(2,1)}, bf16[768,384]{1,0:T(8,128)(2,1)S(1)}, u32[]{:S(2)}) copy-start(bf16[768,384]{1,0:T(8,128)(2,1)S(1)} %broadcast_select_fusion.refs_8_.refs_0_) | copy-start | bytes 1769476
  24.6 18.2 %collective-permute-start.12 = (bf16[768,384]{1,0:T(8,128)(2,1)S(1)}, bf16[768,384]{1,0:T(8,128)(2,1)S(1)}, u32[]{:S(2)}, u32[]{:S(2)}) collective-permute-start(bf16[768,384]{1,0:T(8,128)(2,1)S(1)} %broadcast_select_fusion.refs_8_.refs_0_), channel_id=1, source_target_pairs={{0,2},{2,4},{4,6},{6,0},{1,3},{3,5},{5,7},{7,1},{8,10},{10,12},{12... | collective-permute-start | bytes 1769480 | tf_op jit(solution)/shard_map/ppermute | solution.py:224
  27.2 19.4 %collective-permute-start.13 = (bf16[768,384]{1,0:T(8,128)(2,1)S(1)}, bf16[768,384]{1,0:T(8,128)(2,1)S(1)}, u32[]{:S(2)}, u32[]{:S(2)}) collective-permute-start(bf16[768,384]{1,0:T(8,128)(2,1)S(1)} %broadcast_select_fusion.refs_8_.refs_0_), channel_id=1, source_target_pairs={{0,6},{2,0},{4,2},{6,4},{1,7},{3,1},{5,3},{7,5},{8,14},{10,8},{12,... | collective-permute-start | bytes 1769480 | tf_op jit(solution)/shard_map/ppermute | solution.py:224
  30.6 40.1 %copy-start.1 = (bf16[768,384]{1,0:T(8,128)(2,1)}, bf16[768,384]{1,0:T(8,128)(2,1)S(1)}, u32[]{:S(2)}) copy-start(bf16[768,384]{1,0:T(8,128)(2,1)S(1)} %broadcast_select_fusion.1.refs_0_) | copy-start | bytes 1769476
  30.6 24.8 %collective-permute-start.2 = (bf16[768,384]{1,0:T(8,128)(2,1)S(1)}, bf16[768,384]{1,0:T(8,128)(2,1)S(1)}, u32[]{:S(2)}, u32[]{:S(2)}) collective-permute-start(bf16[768,384]{1,0:T(8,128)(2,1)S(1)} %broadcast_select_fusion.1.refs_0_), channel_id=1, source_target_pairs={{0,2},{2,4},{4,6},{6,0},{1,3},{3,5},{5,7},{7,1},{8,10},{10,12},{12... | collective-permute-start | bytes 1769480 | tf_op jit(solution)/shard_map/ppermute | solution.py:224
  34.4 26.8 %collective-permute-start.3 = (bf16[768,384]{1,0:T(8,128)(2,1)S(1)}, bf16[768,384]{1,0:T(8,128)(2,1)S(1)}, u32[]{:S(2)}, u32[]{:S(2)}) collective-permute-start(bf16[768,384]{1,0:T(8,128)(2,1)S(1)} %broadcast_select_fusion.1.refs_0_), channel_id=1, source_target_pairs={{0,6},{2,0},{4,2},{6,4},{1,7},{3,1},{5,3},{7,5},{8,14},{10,8},{12,... | collective-permute-start | bytes 1769480 | tf_op jit(solution)/shard_map/ppermute | solution.py:224
  42.8 27.9 %copy-start.2 = (bf16[768,384]{1,0:T(8,128)(2,1)}, bf16[768,384]{1,0:T(8,128)(2,1)S(1)}, u32[]{:S(2)}) copy-start(bf16[768,384]{1,0:T(8,128)(2,1)S(1)} %collective-permute-done.12.refs_9_.refs_1_) | copy-start | bytes 1769476
  42.8 20.8 %collective-permute-start.14 = (bf16[384,384]{1,0:T(8,128)(2,1)S(1)}, bf16[384,384]{1,0:T(8,128)(2,1)S(1)}, u32[]{:S(2)}, u32[]{:S(2)}) collective-permute-start(bf16[384,384]{1,0:T(8,128)(2,1)S(1)} %slice.18), channel_id=1, source_target_pairs={{0,2},{2,4},{4,6},{6,0},{1,3},{3,5},{5,7},{7,1},{8,10},{10,12},{12... | collective-permute-start | bytes 884744 | tf_op jit(solution)/shard_map/ppermute | solution.py:224
  46.6 55.1 %copy-start.4 = (bf16[768,384]{1,0:T(8,128)(2,1)}, bf16[768,384]{1,0:T(8,128)(2,1)S(1)}, u32[]{:S(2)}) copy-start(bf16[768,384]{1,0:T(8,128)(2,1)S(1)} %collective-permute-done.13.refs_10_.refs_2_) | copy-start | bytes 1769476
  46.7 24.0 %collective-permute-start.15 = (bf16[384,384]{1,0:T(8,128)(2,1)S(1)}, bf16[384,384]{1,0:T(8,128)(2,1)S(1)}, u32[]{:S(2)}, u32[]{:S(2)}) collective-permute-start(bf16[384,384]{1,0:T(8,128)(2,1)S(1)} %slice.19), channel_id=1, source_target_pairs={{0,6},{2,0},{4,2},{6,4},{1,7},{3,1},{5,3},{7,5},{8,14},{10,8},{12,... | collective-permute-start | bytes 884744 | tf_op jit(solution)/shard_map/ppermute | solution.py:224
  55.4 48.9 %copy-start.3 = (bf16[768,384]{1,0:T(8,128)(2,1)}, bf16[768,384]{1,0:T(8,128)(2,1)S(1)}, u32[]{:S(2)}) copy-start(bf16[768,384]{1,0:T(8,128)(2,1)S(1)} %collective-permute-done.2.refs_1_) | copy-start | bytes 1769476
  55.4 34.0 %collective-permute-start.4 = (bf16[384,384]{1,0:T(8,128)(2,1)S(1)}, bf16[384,384]{1,0:T(8,128)(2,1)S(1)}, u32[]{:S(2)}, u32[]{:S(2)}) collective-permute-start(bf16[384,384]{1,0:T(8,128)(2,1)S(1)} %slice.16), channel_id=1, source_target_pairs={{0,2},{2,4},{4,6},{6,0},{1,3},{3,5},{5,7},{7,1},{8,10},{10,12},{12... | collective-permute-start | bytes 884744 | tf_op jit(solution)/shard_map/ppermute | solution.py:224
  59.3 47.5 %collective-permute-start.16 = (bf16[768,384]{1,0:T(8,128)(2,1)S(1)}, bf16[768,384]{1,0:T(8,128)(2,1)S(1)}, u32[]{:S(2)}, u32[]{:S(2)}) collective-permute-start(bf16[768,384]{1,0:T(8,128)(2,1)S(1)} %broadcast_select_fusion.refs_8_.refs_0_), channel_id=1, source_target_pairs={{0,1},{1,0},{2,3},{3,2},{4,5},{5,4},{6,7},{7,6},{8,9},{9,8},{10,11... | collective-permute-start | bytes 1769480 | tf_op jit(solution)/shard_map/ppermute | solution.py:220
  61.2 45.6 %copy-start.5 = (bf16[768,384]{1,0:T(8,128)(2,1)}, bf16[768,384]{1,0:T(8,128)(2,1)S(1)}, u32[]{:S(2)}) copy-start(bf16[768,384]{1,0:T(8,128)(2,1)S(1)} %collective-permute-done.3.refs_2_) | copy-start | bytes 1769476
  61.2 47.5 %collective-permute-start.6 = (bf16[768,384]{1,0:T(8,128)(2,1)S(1)}, bf16[768,384]{1,0:T(8,128)(2,1)S(1)}, u32[]{:S(2)}, u32[]{:S(2)}) collective-permute-start(bf16[768,384]{1,0:T(8,128)(2,1)S(1)} %broadcast_select_fusion.1.refs_0_), channel_id=1, source_target_pairs={{0,1},{1,0},{2,3},{3,2},{4,5},{5,4},{6,7},{7,6},{8,9},{9,8},{10,11... | collective-permute-start | bytes 1769480 | tf_op jit(solution)/shard_map/ppermute | solution.py:220
  63.6 47.5 %collective-permute-start.17 = (bf16[768,384]{1,0:T(8,128)(2,1)S(1)}, bf16[768,384]{1,0:T(8,128)(2,1)S(1)}, u32[]{:S(2)}, u32[]{:S(2)}) collective-permute-start(bf16[768,384]{1,0:T(8,128)(2,1)S(1)} %collective-permute-done.12.refs_9_.refs_1_), channel_id=1, source_target_pairs={{0,1},{1,0},{2,3},{3,2},{4,5},{5,4},{6,7},{7,6},{8,9},{9,8},{10,11... | collective-permute-start | bytes 1769480 | tf_op jit(solution)/shard_map/ppermute | solution.py:220
  70.7 33.6 %collective-permute-start = (bf16[768,256]{1,0:T(8,128)(2,1)}, bf16[768,256]{1,0:T(8,128)(2,1)S(1)}, u32[]{:S(2)}, u32[]{:S(2)}) collective-permute-start(bf16[768,256]{1,0:T(8,128)(2,1)} %shard_map.101.own_attn_ref), channel_id=1, source_target_pairs={{0,256},{256,0},{1,257},{257,1},{2,258},{258,2},{3,259},{259,3},{4... | collective-permute-start | bytes 1179656 | tf_op jit(solution)/shard_map/ppermute | solution.py:216
  89.4 12.2 %collective-permute-start.5 = (bf16[384,384]{1,0:T(8,128)(2,1)S(1)}, bf16[384,384]{1,0:T(8,128)(2,1)S(1)}, u32[]{:S(2)}, u32[]{:S(2)}) collective-permute-start(bf16[384,384]{1,0:T(8,128)(2,1)S(1)} %slice.17), channel_id=1, source_target_pairs={{0,6},{2,0},{4,2},{6,4},{1,7},{3,1},{5,3},{7,5},{8,14},{10,8},{12,... | collective-permute-start | bytes 884744 | tf_op jit(solution)/shard_map/ppermute | solution.py:224
  101.7 12.9 %collective-permute-start.18 = (bf16[768,384]{1,0:T(8,128)(2,1)S(1)}, bf16[768,384]{1,0:T(8,128)(2,1)}, u32[]{:S(2)}, u32[]{:S(2)}) collective-permute-start(bf16[768,384]{1,0:T(8,128)(2,1)S(1)} %collective-permute-done.13.refs_10_.refs_2_), channel_id=1, source_target_pairs={{0,1},{1,0},{2,3},{3,2},{4,5},{5,4},{6,7},{7,6},{8,9},{9,8},{10,11... | collective-permute-start | bytes 1769480 | tf_op jit(solution)/shard_map/ppermute | solution.py:220
  104.3 6.8 %copy-start.12 = (bf16[768,256]{1,0:T(8,128)(2,1)}, bf16[768,256]{1,0:T(8,128)(2,1)S(1)}, u32[]{:S(2)}) copy-start(bf16[768,256]{1,0:T(8,128)(2,1)S(1)} %collective-permute-done.other_attn_ref) | copy-start | bytes 1179652
  104.4 10.2 %collective-permute-start.7 = (bf16[768,384]{1,0:T(8,128)(2,1)S(1)}, bf16[768,384]{1,0:T(8,128)(2,1)}, u32[]{:S(2)}, u32[]{:S(2)}) collective-permute-start(bf16[768,384]{1,0:T(8,128)(2,1)S(1)} %collective-permute-done.2.refs_1_), channel_id=1, source_target_pairs={{0,1},{1,0},{2,3},{3,2},{4,5},{5,4},{6,7},{7,6},{8,9},{9,8},{10,11... | collective-permute-start | bytes 1769480 | tf_op jit(solution)/shard_map/ppermute | solution.py:220
  106.8 4.4 %copy-start.7 = (bf16[768,384]{1,0:T(8,128)(2,1)}, bf16[768,384]{1,0:T(8,128)(2,1)S(1)}, u32[]{:S(2)}) copy-start(bf16[768,384]{1,0:T(8,128)(2,1)S(1)} %collective-permute-done.16.refs_12_.refs_4_) | copy-start | bytes 1769476
  106.8 7.7 %collective-permute-start.8 = (bf16[768,384]{1,0:T(8,128)(2,1)S(1)}, bf16[768,384]{1,0:T(8,128)(2,1)S(1)}, u32[]{:S(2)}, u32[]{:S(2)}) collective-permute-start(bf16[768,384]{1,0:T(8,128)(2,1)S(1)} %collective-permute-done.3.refs_2_), channel_id=1, source_target_pairs={{0,1},{1,0},{2,3},{3,2},{4,5},{5,4},{6,7},{7,6},{8,9},{9,8},{10,11... | collective-permute-start | bytes 1769480 | tf_op jit(solution)/shard_map/ppermute | solution.py:220
  108.7 2.5 %copy-start.6 = (bf16[768,384]{1,0:T(8,128)(2,1)}, bf16[768,384]{1,0:T(8,128)(2,1)S(1)}, u32[]{:S(2)}) copy-start(bf16[768,384]{1,0:T(8,128)(2,1)S(1)} %collective-permute-done.6.refs_4_) | copy-start | bytes 1769476
  108.7 5.8 %collective-permute-start.19 = (bf16[768,384]{1,0:T(8,128)(2,1)}, bf16[768,384]{1,0:T(8,128)(2,1)}, u32[]{:S(2)}, u32[]{:S(2)}) collective-permute-start(bf16[768,384]{1,0:T(8,128)(2,1)} %constant_dynamic-update-slice_fusion.2.refs_11_.refs_3_), channel_id=1, source_target_pairs={{0,1},{1,0},{2,3},{3,2},{4,5},{5,4},{6,7},{7,6},{8,9},{9,8},{10,11... | collective-permute-start | bytes 1769480 | tf_op jit(solution)/shard_map/ppermute | solution.py:220
  111.2 0.8 copy-start.8
  112.0 4.1 %collective-permute-start.9 = (bf16[768,384]{1,0:T(8,128)(2,1)}, bf16[768,384]{1,0:T(8,128)(2,1)S(1)}, u32[]{:S(2)}, u32[]{:S(2)}) collective-permute-start(bf16[768,384]{1,0:T(8,128)(2,1)} %constant_dynamic-update-slice_fusion.refs_3_), channel_id=1, source_target_pairs={{0,1},{1,0},{2,3},{3,2},{4,5},{5,4},{6,7},{7,6},{8,9},{9,8},{10,11... | collective-permute-start | bytes 1769480 | tf_op jit(solution)/shard_map/ppermute | solution.py:220
  114.5 1.6 copy-start.9
  116.1 0.9 copy-start.10
  137.3 13.2 %collective-permute-start.20 = (bf16[768,256]{1,0:T(8,128)(2,1)}, bf16[768,256]{1,0:T(8,128)(2,1)S(1)}, u32[]{:S(2)}, u32[]{:S(2)}) collective-permute-start(bf16[768,256]{1,0:T(8,128)(2,1)} %shard_map.103), channel_id=1, source_target_pairs={{0,256},{256,0},{1,257},{257,1},{2,258},{258,2},{3,259},{259,3},{4... | collective-permute-start | bytes 1179656 | tf_op jit(solution)/shard_map/ppermute | solution.py:216
  150.5 0.7 copy-start.13
Sparse Core Ops, SparseCore 0:
  17.8 75.9 all-gather.1
  130.8 75.1 reduce-scatter.1

commit v7 on v5

v7 whole, which is shorter than its diff:
```python
import jax
import jax.numpy as jnp
from jax import lax
from jax.experimental import pallas as pl
from jax.experimental.pallas import tpu as pltpu
from jax.sharding import Mesh, PartitionSpec as P

HD = 128
PATCH = 256
EPSILON = 1e-06
SCALE = HD ** (-0.5)
AXES = ("yl", "zp", "zq", "zb", "yh", "xp", "xq", "c")
SIZES = (2, 2, 2, 4, 2, 2, 2, 2)
Z = ("zp", "zq", "zb")
VMEM_LIMIT = 56 * 1024 * 1024


def normalize(raw, gain):
    values32 = raw.astype(jnp.float32)
    center = values32 - jnp.mean(values32, axis=-1, keepdims=True)
    inverse = lax.rsqrt(jnp.mean(center * center, axis=-1, keepdims=True) + EPSILON)
    unit = center * inverse
    return (unit, inverse, (unit * gain).astype(jnp.bfloat16))


def unnormalize(grad, unit, inverse, gain):
    scaled = grad * gain
    centered = scaled - jnp.mean(scaled, axis=-1, keepdims=True)
    return (centered - unit * jnp.mean(scaled * unit, axis=-1, keepdims=True)) * inverse


def product(left, right, left_dim, right_dim):
    return lax.dot_general(
        left, right, (((left_dim,), (right_dim,)), ((), ())), preferred_element_type=jnp.float32
    )


def softmax(q_norm, k_norm):
    scores = product(q_norm, k_norm, 1, 1) * SCALE
    expo = jnp.exp(scores - jnp.max(scores, axis=-1, keepdims=True))
    return expo / jnp.sum(expo, axis=-1, keepdims=True)


def forward_kernel(q_ref, k_ref, v_ref, gains_ref, attn_ref):
    for head in range(q_ref.shape[1] // HD):
        cols = slice(head * HD, (head + 1) * HD)
        _, _, q_norm = normalize(q_ref[:, cols], gains_ref[0:1, :])
        _, _, k_norm = normalize(k_ref[:, cols], gains_ref[1:2, :])
        prob_low = softmax(q_norm, k_norm).astype(jnp.bfloat16)
        attn_ref[:, cols] = product(prob_low, v_ref[:, cols], 1, 0).astype(jnp.bfloat16)


def forward(queries_raw, keys_raw, values, norm_gains):
    tokens, width = queries_raw.shape
    block = pl.BlockSpec((PATCH, width), lambda i: (i, 0))
    return pl.pallas_call(
        forward_kernel,
        grid=(tokens // PATCH,),
        in_specs=[block, block, block, pl.BlockSpec((2, HD), lambda i: (0, 0))],
        out_specs=block,
        out_shape=jax.ShapeDtypeStruct((tokens, width), jnp.bfloat16),
        compiler_params=pltpu.CompilerParams(vmem_limit_bytes=VMEM_LIMIT),
    )(queries_raw, keys_raw, values, norm_gains)


def backward_kernel(
    q_ref, k_ref, v_ref, p0_ref, p1_ref, p2_ref, p3_ref, gains_ref,
    qg_ref, kg_ref, vg_ref, terms_ref,
):
    @pl.when(pl.program_id(0) == 0)
    def _():
        terms_ref[...] = jnp.zeros_like(terms_ref)

    q_gain, k_gain = gains_ref[0:1, :], gains_ref[1:2, :]
    for head in range(q_ref.shape[1] // HD):
        cols = slice(head * HD, (head + 1) * HD)
        value = v_ref[:, cols]
        q_unit, q_inverse, q_norm = normalize(q_ref[:, cols], q_gain)
        k_unit, k_inverse, k_norm = normalize(k_ref[:, cols], k_gain)
        prob = softmax(q_norm, k_norm)
        prob_low = prob.astype(jnp.bfloat16)
        attn = product(prob_low, value, 1, 0).astype(jnp.bfloat16)
        grad = sum(ref[:, cols].astype(jnp.float32) for ref in (p0_ref, p1_ref, p2_ref, p3_ref))
        grad = grad.astype(jnp.bfloat16)
        vg_ref[:, cols] = product(prob_low, grad, 0, 0).astype(jnp.bfloat16)
        delta = jnp.sum(
            grad.astype(jnp.float32) * attn.astype(jnp.float32), axis=-1, keepdims=True
        )
        score_grad = (prob * (product(grad, value, 1, 1) - delta)).astype(jnp.bfloat16)
        qn_grad = product(score_grad, k_norm, 1, 0) * SCALE
        kn_grad = product(score_grad, q_norm, 0, 0) * SCALE
        terms_ref[0:1, :] += jnp.sum(qn_grad * q_unit, axis=0, keepdims=True)
        terms_ref[1:2, :] += jnp.sum(kn_grad * k_unit, axis=0, keepdims=True)
        qg_ref[:, cols] = unnormalize(qn_grad, q_unit, q_inverse, q_gain).astype(jnp.bfloat16)
        kg_ref[:, cols] = unnormalize(kn_grad, k_unit, k_inverse, k_gain).astype(jnp.bfloat16)


def backward(queries_raw, keys_raw, values, parts, norm_gains):
    tokens, width = queries_raw.shape
    block = pl.BlockSpec((PATCH, width), lambda i: (i, 0))
    gains = pl.BlockSpec((2, HD), lambda i: (0, 0))
    out = jax.ShapeDtypeStruct((tokens, width), jnp.bfloat16)
    return pl.pallas_call(
        backward_kernel,
        grid=(tokens // PATCH,),
        in_specs=[block] * 7 + [gains],
        out_specs=[block, block, block, gains],
        out_shape=[out, out, out, jax.ShapeDtypeStruct((2, HD), jnp.float32)],
        compiler_params=pltpu.CompilerParams(vmem_limit_bytes=VMEM_LIMIT),
    )(queries_raw, keys_raw, values, *parts, norm_gains)


def grad_block(grads):
    return pl.BlockSpec((2, 1, 1) + grads.shape[3:], lambda x, c, place: (0, x, c, 0, 0))


def weight_kernel(place_ref, grad_ref, same_ref, other_ref, wgrad_ref):
    high, mine = place_ref[0], place_ref[1]
    heads = wgrad_ref.shape[3]
    term = product(grad_ref[high, 0, 0], same_ref[...], 0, 0)
    term += product(grad_ref[1 - high, 0, 0], other_ref[...], 0, 0)
    term = term.astype(wgrad_ref.dtype)
    wgrad_ref[0, mine] = term[:, :heads]
    wgrad_ref[0, 1 - mine] = term[:, heads:]


def weight_product(place, grads, attn_same, attn_other):
    _, _, _, tokens, width = grads.shape
    heads = attn_same.shape[1] // 2
    attn = pl.BlockSpec((tokens, 2 * heads), lambda x, c, place: (0, 0))
    return pl.pallas_call(
        weight_kernel,
        grid_spec=pltpu.PrefetchScalarGridSpec(
            num_scalar_prefetch=1,
            grid=(2, 2),
            in_specs=[grad_block(grads), attn, attn],
            out_specs=pl.BlockSpec((1, 2, width, heads), lambda x, c, place: (x, 0, c, 0)),
        ),
        out_shape=jax.ShapeDtypeStruct((2, 2, 2 * width, heads), jnp.bfloat16),
        compiler_params=pltpu.CompilerParams(vmem_limit_bytes=VMEM_LIMIT),
        cost_estimate=pl.CostEstimate(
            flops=4 * grads.size * heads,
            bytes_accessed=2 * (grads.size + 8 * width * heads),
            transcendentals=0,
        ),
    )(place, grads, attn_same, attn_other)


def token_kernel(place_ref, grad_ref, weight_ref, *refs):
    parts, total = refs[:4], refs[4]
    step = 2 * pl.program_id(0) + pl.program_id(1)
    high, mine = place_ref[0], place_ref[1]

    @pl.when(step == 0)
    def _():
        total[...] = jnp.zeros_like(total)

    for side, column in enumerate((mine, 1 - mine)):
        weights = weight_ref[:, 0, column].reshape(-1, weight_ref.shape[4])
        for index, low in enumerate((high, 1 - high)):
            total[2 * index + side] += product(grad_ref[low, 0, 0], weights, 1, 0)

    @pl.when(step == 3)
    def _():
        for index in range(4):
            parts[index][...] = total[index].astype(parts[index].dtype)


def token_product(place, grads, weights):
    _, _, _, tokens, _ = grads.shape
    rows, heads = weights.shape[3:]
    return pl.pallas_call(
        token_kernel,
        grid_spec=pltpu.PrefetchScalarGridSpec(
            num_scalar_prefetch=1,
            grid=(2, 2),
            in_specs=[
                grad_block(grads),
                pl.BlockSpec((2, 1, 2, rows, heads), lambda x, c, place: (c, x, 0, 0, 0)),
            ],
            out_specs=[pl.BlockSpec((tokens, heads), lambda x, c, place: (0, 0))] * 4,
            scratch_shapes=[pltpu.VMEM((4, tokens, heads), jnp.float32)],
        ),
        out_shape=[jax.ShapeDtypeStruct((tokens, heads), jnp.bfloat16)] * 4,
        compiler_params=pltpu.CompilerParams(vmem_limit_bytes=VMEM_LIMIT),
        cost_estimate=pl.CostEstimate(
            flops=4 * grads.size * heads,
            bytes_accessed=2 * (grads.size + weights.size),
            transcendentals=0,
        ),
    )(place, grads, weights)


def permute(array, axes, target):
    count = len(axes)
    pairs = []
    for source in range(2**count):
        place = [(source >> (count - 1 - i)) & 1 for i in range(count)]
        goal = 0
        for value in target(*place):
            goal = 2 * goal + value % 2
        pairs.append((source, goal))
    return lax.ppermute(array, axes, pairs)


def exchanged(array):
    return permute(
        array,
        ("yl", "zq", "yh", "xq"),
        lambda low, zq, up, xq: (up, zq + (zq != xq), low, xq + (zq != xq)),
    )


def along(array, step):
    return lax.ppermute(array, Z, [(z, (z + step) % 16) for z in range(16)])


def gather_rows(own_rows):
    column = lax.all_gather(own_rows, ("zp", "zq"), axis=0)
    before = along(column, 1)
    after = along(column, -1)
    far = jnp.concatenate([along(column[:2], 2), along(column[2:], -2)])
    blocks = [column, after, far, before]
    shift = (4 - lax.axis_index("zb")) % 4
    rows = lax.dynamic_slice_in_dim(jnp.stack(blocks + blocks), shift, 4, axis=0)
    return rows.reshape((4, 2, 2) + own_rows.shape)


def sum_over(array, axis, count):
    spread = lax.all_to_all(jnp.broadcast_to(array[None], (count,) + array.shape), axis, 0, 0)
    return jnp.sum(spread, axis=0)


def per_device(queries_raw, keys_raw, values, grad_out, out_weight, norm_gains):
    place = jnp.stack([lax.axis_index("yh"), lax.axis_index("xq")]).astype(jnp.int32)
    grads = lax.all_gather(grad_out, ("yl", "xp", "c"), axis=0)
    grads = grads.reshape((2, 2, 2) + grad_out.shape)

    attn = forward(queries_raw, keys_raw, values, norm_gains)
    own_rows, attn = lax.optimization_barrier((exchanged(out_weight), attn))
    weights = gather_rows(own_rows)
    beside = permute(attn, ("xq",), lambda xq: (1 - xq,))
    attn = jnp.concatenate([attn, beside], axis=1)
    attn_same = permute(attn, ("yl", "yh"), lambda low, up: (up, low))
    attn_other = permute(attn, ("yl", "yh"), lambda low, up: (up, 1 - low))
    grads, weights = lax.optimization_barrier((grads, weights))

    wgrad = weight_product(place, grads, attn_same, attn_other)
    shard = lax.psum_scatter(
        wgrad.reshape(-1, wgrad.shape[3]), Z, scatter_dimension=0, tiled=True
    )

    weights, _ = lax.optimization_barrier((weights, wgrad))
    same, same_beside, other, other_beside = token_product(place, grads, weights)
    axes = ("yl", "yh", "xq")
    parts = [
        permute(same, axes, lambda low, up, xq: (up, low, xq)),
        permute(same_beside, axes, lambda low, up, xq: (up, low, 1 - xq)),
        permute(other, axes, lambda low, up, xq: (1 - up, low, xq)),
        permute(other_beside, axes, lambda low, up, xq: (1 - up, low, 1 - xq)),
    ]
    queries_grad, keys_grad, values_grad, terms = backward(
        queries_raw, keys_raw, values, parts, norm_gains
    )
    gains_grad = sum_over(sum_over(terms, ("yl", "yh", "xp", "xq", "c"), 32), Z, 16)
    shard, gains_grad = lax.optimization_barrier((shard, gains_grad))
    weight_grad = exchanged(shard).astype(jnp.float32)
    return (queries_grad, keys_grad, values_grad, weight_grad, gains_grad)


def solution(mesh):
    fine = Mesh(mesh.devices.reshape(SIZES), AXES)
    spec = P(("yl", "zp", "zq", "zb"), ("yh", "xp", "xq", "c"))
    return jax.shard_map(
        per_device,
        mesh=fine,
        in_specs=(spec, spec, spec, spec, spec, P()),
        out_specs=(spec, spec, spec, spec, P()),
        check_vma=False,
    )
```

time: 183 us -> 221 us (1.21)
  the two profiles are of different devices: /device:TPU:8 before, /device:TPU:3 now
where the time goes in v7:
time: 221 us; the launch traced here: 220 us
  blocking collectives  72.3 us (33%)
  starting transfers between devices  60.9 us (28%)
  waiting for transfers between devices  38.2 us (17%)
  Pallas kernels  27.8 us (13%)
  between operations  14.3 us (6%)
  local copies, waits for them, and re-layouts  4.9 us (2%)
    ppermute x9, starting transfers between devices, permute(): return lax.ppermute(array, axes, pairs)  49.6 us
    all_to_all x2, blocking collectives, sum_over(): lax.all_to_all(jnp.broadcast_to(array[None], (count,) + array.shape), axi...  37.5 us
    ppermute x9, waiting for transfers between devices, permute(): return lax.ppermute(array, axes, pairs)  37.5 us
    all_gather x1, blocking collectives, gather_rows(): column = lax.all_gather(own_rows, ('zp', 'zq'), axis=0)  34.8 us
    ppermute x4, starting transfers between devices, along(): return lax.ppermute(array, Z, [(z, (z + step) % 16) for z in range(16)])  11.2 us
    pallas_call x1, Pallas kernels, token_product(): pl.pallas_call(token_kernel, grid_spec=pltpu.PrefetchScalarGridSpec(num_s...  8.02 us
    pallas_call x1, Pallas kernels, backward(): pl.pallas_call(backward_kernel, grid=(tokens // PATCH,), in_specs=[block]...  7.47 us
    pallas_call x1, Pallas kernels, weight_product(): pl.pallas_call(weight_kernel, grid_spec=pltpu.PrefetchScalarGridSpec(num_...  7.2 us
  transfers between devices with their start and end apart: 15, of which 4 were waited for; matrix products, arithmetic and copies ran while one was open for 2% of the time, Pallas kernels for 9%

profile of v7, /device:TPU:3, one launch (start us, length us, event | category | flops | bytes accessed | tf_op | source)
XLA Modules:
  0.0 220.4 jit_solution(12429709962355411240)
XLA Ops:
  7.2 0.0 all-gather.4.cloned.1.call-start
  7.2 0.7 all-gather.4.cloned.1.call-update
  7.9 0.0 reduce-scatter.2.cloned.1.call-start
  7.9 8.8 %collective-permute-start = (bf16[192,256]{1,0:T(8,128)(2,1)}, bf16[192,256]{1,0:T(8,128)(2,1)S(1)}, u32[]{:S(2)}, u32[]{:S(2)}) collective-permute-start(bf16[192,256]{1,0:T(8,128)(2,1)} %param.10), channel_id=1, source_target_pairs={{0,0},{2,64},{8,256},{10,320},{64,2},{66,66},{72,258},{74,322},{25... | collective-permute-start | bytes 294920 | tf_op jit(solution)/shard_map/ppermute | solution.py:203
  16.8 5.1 %shard_map.101 = bf16[768,256]{1,0:T(8,128)(2,1)} custom-call(bf16[768,256]{1,0:T(8,128)(2,1)} %q_ref.3, bf16[768,256]{1,0:T(8,128)(2,1)} %k_ref.3, bf16[768,256]{1,0:T(8,128)(2,1)} %v_ref.3, f32[2,128]{1,0:T(2,128)} %gains_ref.3), custom_call_target="tpu_custom_call" | custom-call | tf_op jit(solution)/shard_map/pallas_call | solution.py:56
  21.8 0.7 pad_add_fusion.place_ref
  22.5 0.0 collective-permute-done
  22.5 34.8 %all-gather.1 = bf16[768,256]{1,0:T(8,128)(2,1)S(1)} all-gather(bf16[192,256]{1,0:T(8,128)(2,1)S(1)} %collective-permute-done), channel_id=3, replica_groups=mesh['yl'=2,'zp'=2,'zq'=2,'zb'=4,'yh'=2,'xp'=2,'xq'=2,'c'=2] {'zp','zq'}, dimensions={0}, use_global_device_ids=true | all-gather | bytes 491520 | tf_op jit(solution)/shard_map/all_gather | solution.py:219
  57.3 1.9 collective-permute-start.1
  59.2 4.8 %collective-permute-start.5 = (bf16[768,256]{1,0:T(8,128)(2,1)}, bf16[768,256]{1,0:T(8,128)(2,1)S(1)}, u32[]{:S(2)}, u32[]{:S(2)}) collective-permute-start(bf16[768,256]{1,0:T(8,128)(2,1)} %shard_map.101), channel_id=1, source_target_pairs={{0,2},{2,0},{1,3},{3,1},{4,6},{6,4},{5,7},{7,5},{8,10},{10,8},{9,1... | collective-permute-start | bytes 1179656 | tf_op jit(solution)/shard_map/ppermute | solution.py:203
  64.0 1.9 collective-permute-start.4
  66.0 1.9 collective-permute-start.2
  67.9 5.5 %collective-permute-start.3 = (bf16[2,192,256]{2,1,0:T(8,128)(2,1)S(1)}, bf16[2,192,256]{2,1,0:T(8,128)(2,1)S(1)}, u32[]{:S(2)}, u32[]{:S(2)}) collective-permute-start(bf16[2,192,256]{2,1,0:T(8,128)(2,1)S(1)} %bitcast.27), channel_id=1, source_target_pairs={{0,224},{16,240},{32,0},{48,16},{64,32},{80,48},{96,64},{112,80},{... | collective-permute-start | bytes 589832 | tf_op jit(solution)/shard_map/ppermute | solution.py:215
  73.4 1.0 constant_dynamic-update-slice_fusion.3
  74.4 0.0 collective-permute-done.5
  74.5 0.7 collective-permute-start.6
  75.2 0.0 collective-permute-done.1
  75.2 6.6 %collective-permute-start.7 = (bf16[768,512]{1,0:T(8,128)(2,1)S(1)}, bf16[768,512]{1,0:T(8,128)(2,1)S(1)}, u32[]{:S(2)}, u32[]{:S(2)}) collective-permute-start(bf16[768,512]{1,0:T(8,128)(2,1)S(1)} %constant_dynamic-update-slice_fusion.2), channel_id=1, source_target_pairs={{0,8},{8,264},{256,0},{264,256},{1,9},{9,265},{257,1},{265,257},{2... | collective-permute-start | bytes 2359304 | tf_op jit(solution)/shard_map/ppermute | solution.py:203
  81.9 0.0 collective-permute-done.2
  81.9 0.0 collective-permute-done.3
  82.0 0.0 collective-permute-done.4
  82.1 1.3 constant_dynamic-slice_fusion
  83.4 0.0 collective-permute-done.6.same_ref
  83.4 11.9 %collective-permute-done.7.other_ref = bf16[768,512]{1,0:T(8,128)(2,1)S(1)} collective-permute-done((bf16[768,512]{1,0:T(8,128)(2,1)S(1)}, bf16[768,512]{1,0:T(8,128)(2,1)S(1)}, u32[]{:S(2)}, u32[]{:S(2)}) %collective-permute-start.7) | collective-permute-done | bytes 786464 | tf_op jit(solution)/shard_map/ppermute | solution.py:203
  95.3 0.0 copy-done.4
  95.3 0.9 copy-done.5
  96.2 7.2 %shard_map.102 = bf16[2,2,768,256]{3,2,1,0:T(8,128)(2,1)} custom-call(s32[2]{0:T(128)} %pad_add_fusion.place_ref, bf16[2,2,2,768,384]{4,3,2,1,0:T(8,128)(2,1)} %bitcast.29, bf16[768,512]{1,0:T(8,128)(2,1)} %copy-done.4, bf16[768,512]{1,0:T(8,128)(2,1)} %copy-done.5), custom_call_target="tpu_custom_call" | custom-call | flops 2415919104 | bytes 6291456 | tf_op jit(solution)/shard_map/pallas_call | solution.py:131
  103.4 0.0 reduce-scatter.2.cloned.1.call-update
  103.5 8.0 %shard_map.103 = (bf16[768,256]{1,0:T(8,128)(2,1)}, bf16[768,256]{1,0:T(8,128)(2,1)}, bf16[768,256]{1,0:T(8,128)(2,1)}, bf16[768,256]{1,0:T(8,128)(2,1)}) custom-call(s32[2]{0:T(128)} %pad_add_fusion.place_ref, bf16[2,2,2,768,384]{4,3,2,1,0:T(8,128)(2,1)} %bitcast.30, bf16[4,2,2,192,256]{4,3,2,1,0:T(8,128)(2,1)} %bitcast.26), custom_call_target="tpu_custom_call" | custom-call | flops 2415919104 | bytes 6291456 | tf_op jit(solution)/shard_map/pallas_call | solution.py:172
  111.5 18.5 %collective-permute-start.10 = (bf16[768,256]{1,0:T(8,128)(2,1)}, bf16[768,256]{1,0:T(8,128)(2,1)S(1)}, u32[]{:S(2)}, u32[]{:S(2)}) collective-permute-start(bf16[768,256]{1,0:T(8,128)(2,1)} %get-tuple-element.27), channel_id=1, source_target_pairs={{0,256},{2,258},{8,0},{10,2},{256,264},{258,266},{264,8},{266,10},... | collective-permute-start | bytes 1179656 | tf_op jit(solution)/shard_map/ppermute | solution.py:203
  130.0 3.1 %collective-permute-start.11 = (bf16[768,256]{1,0:T(8,128)(2,1)}, bf16[768,256]{1,0:T(8,128)(2,1)S(1)}, u32[]{:S(2)}, u32[]{:S(2)}) collective-permute-start(bf16[768,256]{1,0:T(8,128)(2,1)} %get-tuple-element.28), channel_id=1, source_target_pairs={{0,258},{2,256},{8,2},{10,0},{256,266},{258,264},{264,10},{266,8},... | collective-permute-start | bytes 1179656 | tf_op jit(solution)/shard_map/ppermute | solution.py:203
  133.1 1.7 collective-permute-start.8
  134.7 2.2 collective-permute-start.9
  136.9 4.8 %collective-permute-done.10.p2_ref = bf16[768,256]{1,0:T(8,128)(2,1)S(1)} collective-permute-done((bf16[768,256]{1,0:T(8,128)(2,1)}, bf16[768,256]{1,0:T(8,128)(2,1)S(1)}, u32[]{:S(2)}, u32[]{:S(2)}) %collective-permute-start.10) | collective-permute-done | bytes 393248 | tf_op jit(solution)/shard_map/ppermute | solution.py:203
  141.7 0.0 collective-permute-done.11.p3_ref
  141.7 0.0 collective-permute-done.8.p0_ref
  141.8 0.0 copy-start.2
  141.8 6.3 %collective-permute-done.9.p1_ref = bf16[768,256]{1,0:T(8,128)(2,1)S(1)} collective-permute-done((bf16[768,256]{1,0:T(8,128)(2,1)}, bf16[768,256]{1,0:T(8,128)(2,1)S(1)}, u32[]{:S(2)}, u32[]{:S(2)}) %collective-permute-start.9) | collective-permute-done | bytes 393248 | tf_op jit(solution)/shard_map/ppermute | solution.py:203
  148.0 0.0 copy-done.1
  148.1 0.7 copy-done.3
  148.8 7.5 %shard_map.104 = (bf16[768,256]{1,0:T(8,128)(2,1)}, bf16[768,256]{1,0:T(8,128)(2,1)}, bf16[768,256]{1,0:T(8,128)(2,1)}, f32[2,128]{1,0:T(2,128)}) custom-call(bf16[768,256]{1,0:T(8,128)(2,1)} %q_ref.3, bf16[768,256]{1,0:T(8,128)(2,1)} %k_ref.3, bf16[768,256]{1,0:T(8,128)(2,1)} %v_ref.3, bf16[768,256]{1,0:T(8,128)(2,1)} %copy-done.2, ...), custom_call_target="tpu_custom_call" | custom-call | tf_op jit(solution)/shard_map/pallas_call | solution.py:103
  156.3 0.7 broadcast_in_dim.4
  157.0 21.8 %all_to_all.10 = f32[32,2,128]{2,1,0:T(2,128)S(1)} all-to-all(f32[32,2,128]{2,1,0:T(2,128)S(1)} %broadcast_in_dim.4), channel_id=1, replica_groups=mesh['yl'=2,'zp'=2,'zq'=2,'zb'=4,'yh'=2,'xp'=2,'xq'=2,'c'=2] {'yl','yh',..., dimensions={0} | all-to-all | bytes 65536 | tf_op jit(solution)/shard_map/all_to_all | solution.py:230
  178.8 15.7 %all_to_all.11 = f32[16,2,128]{2,1,0:T(2,128)S(1)} all-to-all(f32[16,2,128]{2,1,0:T(2,128)S(1)} %broadcast_in_dim.5), channel_id=1, replica_groups=mesh['yl'=2,'zp'=2,'zq'=2,'zb'=4,'yh'=2,'xp'=2,'xq'=2,'c'=2] {'zp','zq',..., dimensions={0} | all-to-all | bytes 32768 | tf_op jit(solution)/shard_map/all_to_all | solution.py:230
  194.5 0.6 reduce_sum.19
  195.1 3.4 %collective-permute-start.12 = (bf16[192,256]{1,0:T(8,128)(2,1)}, bf16[192,256]{1,0:T(8,128)(2,1)S(1)}, u32[]{:S(2)}, u32[]{:S(2)}) collective-permute-start(bf16[192,256]{1,0:T(8,128)(2,1)} %reduce-scatter.2.cloned.1.call-done), channel_id=1, source_target_pairs={{0,0},{2,64},{8,256},{10,320},{64,2},{66,66},{72,258},{74,322},{25... | collective-permute-start | bytes 294920 | tf_op jit(solution)/shard_map/ppermute | solution.py:203
  198.5 14.4 %collective-permute-done.12 = bf16[192,256]{1,0:T(8,128)(2,1)S(1)} collective-permute-done((bf16[192,256]{1,0:T(8,128)(2,1)}, bf16[192,256]{1,0:T(8,128)(2,1)S(1)}, u32[]{:S(2)}, u32[]{:S(2)}) %collective-permute-start.12) | collective-permute-done | bytes 98336 | tf_op jit(solution)/shard_map/ppermute | solution.py:203
  212.9 0.7 convert_element_type.3
  (21 shorter events, 0.3 us)
Async XLA Ops:
  7.2 76.3 %all-gather.4.cloned.1.call-start = ((), (), s32[]{:S(2)}) async-start(), calls=%async_computation.4 | async-start | bytes 5308416 | tf_op jit(solution)/shard_map/all_gather | solution.py:236
  7.9 187.2 %reduce-scatter.2.cloned.1.call-start = ((), (), s32[]{:S(2)}) async-start(), calls=%async_computation.3 | async-start | bytes 1671168 | tf_op jit(solution)/shard_map/reduce_scatter | solution.py:249
  7.9 14.6 %collective-permute-start = (bf16[192,256]{1,0:T(8,128)(2,1)}, bf16[192,256]{1,0:T(8,128)(2,1)S(1)}, u32[]{:S(2)}, u32[]{:S(2)}) collective-permute-start(bf16[192,256]{1,0:T(8,128)(2,1)} %param.10), channel_id=1, source_target_pairs={{0,0},{2,64},{8,256},{10,320},{64,2},{66,66},{72,258},{74,322},{25... | collective-permute-start | bytes 294920 | tf_op jit(solution)/shard_map/ppermute | solution.py:203
  57.3 17.9 %collective-permute-start.1 = (bf16[4,192,256]{2,1,0:T(8,128)(2,1)S(1)}, bf16[4,192,256]{2,1,0:T(8,128)(2,1)S(1)}, u32[]{:S(2)}, u32[]{:S(2)}) collective-permute-start(bf16[4,192,256]{2,1,0:T(8,128)(2,1)S(1)} %bitcast.21), channel_id=1, source_target_pairs={{0,240},{16,0},{32,16},{48,32},{64,48},{80,64},{96,80},{112,96},{1... | collective-permute-start | bytes 1179656 | tf_op jit(solution)/shard_map/ppermute | solution.py:215
  59.2 15.2 %collective-permute-start.5 = (bf16[768,256]{1,0:T(8,128)(2,1)}, bf16[768,256]{1,0:T(8,128)(2,1)S(1)}, u32[]{:S(2)}, u32[]{:S(2)}) collective-permute-start(bf16[768,256]{1,0:T(8,128)(2,1)} %shard_map.101), channel_id=1, source_target_pairs={{0,2},{2,0},{1,3},{3,1},{4,6},{6,4},{5,7},{7,5},{8,10},{10,8},{9,1... | collective-permute-start | bytes 1179656 | tf_op jit(solution)/shard_map/ppermute | solution.py:203
  64.0 17.9 %collective-permute-start.4 = (bf16[4,192,256]{2,1,0:T(8,128)(2,1)S(1)}, bf16[4,192,256]{2,1,0:T(8,128)(2,1)S(1)}, u32[]{:S(2)}, u32[]{:S(2)}) collective-permute-start(bf16[4,192,256]{2,1,0:T(8,128)(2,1)S(1)} %bitcast.22), channel_id=1, source_target_pairs={{0,16},{16,32},{32,48},{48,64},{64,80},{80,96},{96,112},{112,128},... | collective-permute-start | bytes 1179656 | tf_op jit(solution)/shard_map/ppermute | solution.py:215
  66.0 15.9 %collective-permute-start.2 = (bf16[2,192,256]{2,1,0:T(8,128)(2,1)S(1)}, bf16[2,192,256]{2,1,0:T(8,128)(2,1)S(1)}, u32[]{:S(2)}, u32[]{:S(2)}) collective-permute-start(bf16[2,192,256]{2,1,0:T(8,128)(2,1)S(1)} %bitcast.28), channel_id=1, source_target_pairs={{0,32},{16,48},{32,64},{48,80},{64,96},{80,112},{96,128},{112,144}... | collective-permute-start | bytes 589832 | tf_op jit(solution)/shard_map/ppermute | solution.py:215
  67.9 14.0 %collective-permute-start.3 = (bf16[2,192,256]{2,1,0:T(8,128)(2,1)S(1)}, bf16[2,192,256]{2,1,0:T(8,128)(2,1)S(1)}, u32[]{:S(2)}, u32[]{:S(2)}) collective-permute-start(bf16[2,192,256]{2,1,0:T(8,128)(2,1)S(1)} %bitcast.27), channel_id=1, source_target_pairs={{0,224},{16,240},{32,0},{48,16},{64,32},{80,48},{96,64},{112,80},{... | collective-permute-start | bytes 589832 | tf_op jit(solution)/shard_map/ppermute | solution.py:215
  74.5 8.9 %collective-permute-start.6 = (bf16[768,512]{1,0:T(8,128)(2,1)S(1)}, bf16[768,512]{1,0:T(8,128)(2,1)S(1)}, u32[]{:S(2)}, u32[]{:S(2)}) collective-permute-start(bf16[768,512]{1,0:T(8,128)(2,1)S(1)} %constant_dynamic-update-slice_fusion.2), channel_id=1, source_target_pairs={{0,0},{8,256},{256,8},{264,264},{1,1},{9,257},{257,9},{265,265},{2... | collective-permute-start | bytes 2359304 | tf_op jit(solution)/shard_map/ppermute | solution.py:203
  75.2 20.1 %collective-permute-start.7 = (bf16[768,512]{1,0:T(8,128)(2,1)S(1)}, bf16[768,512]{1,0:T(8,128)(2,1)S(1)}, u32[]{:S(2)}, u32[]{:S(2)}) collective-permute-start(bf16[768,512]{1,0:T(8,128)(2,1)S(1)} %constant_dynamic-update-slice_fusion.2), channel_id=1, source_target_pairs={{0,8},{8,264},{256,0},{264,256},{1,9},{9,265},{257,1},{265,257},{2... | collective-permute-start | bytes 2359304 | tf_op jit(solution)/shard_map/ppermute | solution.py:203
  83.4 11.9 %copy-start.4 = (bf16[768,512]{1,0:T(8,128)(2,1)}, bf16[768,512]{1,0:T(8,128)(2,1)S(1)}, u32[]{:S(2)}) copy-start(bf16[768,512]{1,0:T(8,128)(2,1)S(1)} %collective-permute-done.6.same_ref) | copy-start | bytes 2359300
  95.3 0.9 copy-start.5
  111.5 30.3 %collective-permute-start.10 = (bf16[768,256]{1,0:T(8,128)(2,1)}, bf16[768,256]{1,0:T(8,128)(2,1)S(1)}, u32[]{:S(2)}, u32[]{:S(2)}) collective-permute-start(bf16[768,256]{1,0:T(8,128)(2,1)} %get-tuple-element.27), channel_id=1, source_target_pairs={{0,256},{2,258},{8,0},{10,2},{256,264},{258,266},{264,8},{266,10},... | collective-permute-start | bytes 1179656 | tf_op jit(solution)/shard_map/ppermute | solution.py:203
  130.0 11.8 %collective-permute-start.11 = (bf16[768,256]{1,0:T(8,128)(2,1)}, bf16[768,256]{1,0:T(8,128)(2,1)S(1)}, u32[]{:S(2)}, u32[]{:S(2)}) collective-permute-start(bf16[768,256]{1,0:T(8,128)(2,1)} %get-tuple-element.28), channel_id=1, source_target_pairs={{0,258},{2,256},{8,2},{10,0},{256,266},{258,264},{264,10},{266,8},... | collective-permute-start | bytes 1179656 | tf_op jit(solution)/shard_map/ppermute | solution.py:203
  133.1 8.7 %collective-permute-start.8 = (bf16[768,256]{1,0:T(8,128)(2,1)}, bf16[768,256]{1,0:T(8,128)(2,1)S(1)}, u32[]{:S(2)}, u32[]{:S(2)}) collective-permute-start(bf16[768,256]{1,0:T(8,128)(2,1)} %get-tuple-element.25), channel_id=1, source_target_pairs={{0,0},{2,2},{8,256},{10,258},{256,8},{258,10},{264,264},{266,266},... | collective-permute-start | bytes 1179656 | tf_op jit(solution)/shard_map/ppermute | solution.py:203
  134.7 13.3 %collective-permute-start.9 = (bf16[768,256]{1,0:T(8,128)(2,1)}, bf16[768,256]{1,0:T(8,128)(2,1)S(1)}, u32[]{:S(2)}, u32[]{:S(2)}) collective-permute-start(bf16[768,256]{1,0:T(8,128)(2,1)} %get-tuple-element.26), channel_id=1, source_target_pairs={{0,2},{2,0},{8,258},{10,256},{256,10},{258,8},{264,266},{266,264},... | collective-permute-start | bytes 1179656 | tf_op jit(solution)/shard_map/ppermute | solution.py:203
  141.7 6.3 %copy-start = (bf16[768,256]{1,0:T(8,128)(2,1)}, bf16[768,256]{1,0:T(8,128)(2,1)S(1)}, u32[]{:S(2)}) copy-start(bf16[768,256]{1,0:T(8,128)(2,1)S(1)} %collective-permute-done.10.p2_ref) | copy-start | bytes 1179652
  141.7 6.3 %copy-start.1 = (bf16[768,256]{1,0:T(8,128)(2,1)}, bf16[768,256]{1,0:T(8,128)(2,1)S(1)}, u32[]{:S(2)}) copy-start(bf16[768,256]{1,0:T(8,128)(2,1)S(1)} %collective-permute-done.11.p3_ref) | copy-start | bytes 1179652
  141.8 6.3 %copy-start.2 = (bf16[768,256]{1,0:T(8,128)(2,1)}, bf16[768,256]{1,0:T(8,128)(2,1)S(1)}, u32[]{:S(2)}) copy-start(bf16[768,256]{1,0:T(8,128)(2,1)S(1)} %collective-permute-done.8.p0_ref) | copy-start | bytes 1179652
  148.1 0.7 copy-start.3
  195.1 17.8 %collective-permute-start.12 = (bf16[192,256]{1,0:T(8,128)(2,1)}, bf16[192,256]{1,0:T(8,128)(2,1)S(1)}, u32[]{:S(2)}, u32[]{:S(2)}) collective-permute-start(bf16[192,256]{1,0:T(8,128)(2,1)} %reduce-scatter.2.cloned.1.call-done), channel_id=1, source_target_pairs={{0,0},{2,64},{8,256},{10,320},{64,2},{66,66},{72,258},{74,322},{25... | collective-permute-start | bytes 294920 | tf_op jit(solution)/shard_map/ppermute | solution.py:203
Sparse Core Ops, SparseCore 0:
  10.2 47.0 all-gather.3
  103.6 75.1 reduce-scatter.1

commit v8 on v7

--- a/solution.py
+++ b/solution.py
@@ -203,11 +203,19 @@
     return lax.ppermute(array, axes, pairs)
 
 
-def exchanged(array):
+def rows_to_worker(array):
     return permute(
         array,
         ("yl", "zq", "yh", "xq"),
-        lambda low, zq, up, xq: (up, zq + (zq != xq), low, xq + (zq != xq)),
+        lambda low, zq, up, xq: (1 - up, zq + (zq != xq), low, xq + (zq != xq)),
+    )
+
+
+def rows_to_owner(array):
+    return permute(
+        array,
+        ("yl", "zq", "yh", "xq"),
+        lambda low, zq, up, xq: (up, zq + (zq != xq), 1 - low, xq + (zq != xq)),
     )
 
 
@@ -237,12 +245,12 @@
     grads = grads.reshape((2, 2, 2) + grad_out.shape)
 
     attn = forward(queries_raw, keys_raw, values, norm_gains)
-    own_rows, attn = lax.optimization_barrier((exchanged(out_weight), attn))
+    beside = permute(attn, ("xq",), lambda xq: (1 - xq,))
+    own_rows, beside = lax.optimization_barrier((rows_to_worker(out_weight), beside))
+    attn = jnp.concatenate([attn, beside], axis=1)
+    attn_same = permute(attn, ("yl", "yh"), lambda low, up: (1 - up, low))
+    attn_other = permute(attn, ("yl", "yh"), lambda low, up: (1 - up, 1 - low))
     weights = gather_rows(own_rows)
-    beside = permute(attn, ("xq",), lambda xq: (1 - xq,))
-    attn = jnp.concatenate([attn, beside], axis=1)
-    attn_same = permute(attn, ("yl", "yh"), lambda low, up: (up, low))
-    attn_other = permute(attn, ("yl", "yh"), lambda low, up: (up, 1 - low))
     grads, weights = lax.optimization_barrier((grads, weights))
 
     wgrad = weight_product(place, grads, attn_same, attn_other)
@@ -254,17 +262,17 @@
     same, same_beside, other, other_beside = token_product(place, grads, weights)
     axes = ("yl", "yh", "xq")
     parts = [
-        permute(same, axes, lambda low, up, xq: (up, low, xq)),
-        permute(same_beside, axes, lambda low, up, xq: (up, low, 1 - xq)),
-        permute(other, axes, lambda low, up, xq: (1 - up, low, xq)),
-        permute(other_beside, axes, lambda low, up, xq: (1 - up, low, 1 - xq)),
+        permute(same, axes, lambda low, up, xq: (up, 1 - low, xq)),
+        permute(same_beside, axes, lambda low, up, xq: (up, 1 - low, 1 - xq)),
+        permute(other, axes, lambda low, up, xq: (1 - up, 1 - low, xq)),
+        permute(other_beside, axes, lambda low, up, xq: (1 - up, 1 - low, 1 - xq)),
     ]
     queries_grad, keys_grad, values_grad, terms = backward(
         queries_raw, keys_raw, values, parts, norm_gains
     )
     gains_grad = sum_over(sum_over(terms, ("yl", "yh", "xp", "xq", "c"), 32), Z, 16)
     shard, gains_grad = lax.optimization_barrier((shard, gains_grad))
-    weight_grad = exchanged(shard).astype(jnp.float32)
+    weight_grad = rows_to_owner(shard).astype(jnp.float32)
     return (queries_grad, keys_grad, values_grad, weight_grad, gains_grad)
 
 

time: 221 us -> 226 us (1.023)
  the two profiles are of different devices: /device:TPU:3 before, /device:TPU:11 now
where the time goes in v8:
time: 226 us; the launch traced here: 225 us
  starting transfers between devices  71.4 us (32%)
  blocking collectives  63.9 us (28%)
  waiting for transfers between devices  39.1 us (17%)
  Pallas kernels  27.8 us (12%)
  between operations  14.3 us (6%)
  local copies, waits for them, and re-layouts  5.51 us (2%)
  other arithmetic  3.09 us (1%)
    ppermute x9, starting transfers between devices, permute(): return lax.ppermute(array, axes, pairs)  56.7 us
    all_gather x1, blocking collectives, gather_rows(): column = lax.all_gather(own_rows, ('zp', 'zq'), axis=0)  34.3 us
    ppermute x9, waiting for transfers between devices, permute(): return lax.ppermute(array, axes, pairs)  34.2 us
    all_to_all x2, blocking collectives, sum_over(): lax.all_to_all(jnp.broadcast_to(array[None], (count,) + array.shape), axi...  29.6 us
    ppermute x4, starting transfers between devices, along(): return lax.ppermute(array, Z, [(z, (z + step) % 16) for z in range(16)])  14.6 us
    pallas_call x1, Pallas kernels, token_product(): pl.pallas_call(token_kernel, grid_spec=pltpu.PrefetchScalarGridSpec(num_s...  8.01 us
    pallas_call x1, Pallas kernels, backward(): pl.pallas_call(backward_kernel, grid=(tokens // PATCH,), in_specs=[block]...  7.48 us
    pallas_call x1, Pallas kernels, weight_product(): pl.pallas_call(weight_kernel, grid_spec=pltpu.PrefetchScalarGridSpec(num_...  7.19 us
  transfers between devices with their start and end apart: 15, of which 5 were waited for; matrix products, arithmetic and copies ran while one was open for 2% of the time, Pallas kernels for 9%

profile of v8, /device:TPU:11, one launch (start us, length us, event | category | flops | bytes accessed | tf_op | source)
XLA Modules:
  0.0 225.1 jit_solution(15099628332468408952)
XLA Ops:
  7.2 0.0 all-gather.4.cloned.1.call-start
  7.2 0.7 all-gather.4.cloned.1.call-update
  7.9 0.0 reduce-scatter.2.cloned.1.call-start
  7.9 5.1 %shard_map.101 = bf16[768,256]{1,0:T(8,128)(2,1)} custom-call(bf16[768,256]{1,0:T(8,128)(2,1)} %q_ref.3, bf16[768,256]{1,0:T(8,128)(2,1)} %k_ref.3, bf16[768,256]{1,0:T(8,128)(2,1)} %v_ref.3, f32[2,128]{1,0:T(2,128)} %gains_ref.3), custom_call_target="tpu_custom_call" | custom-call | tf_op jit(solution)/shard_map/pallas_call | solution.py:56
  13.0 2.2 collective-permute-start.1
  15.2 11.5 %collective-permute-start = (bf16[192,256]{1,0:T(8,128)(2,1)}, bf16[192,256]{1,0:T(8,128)(2,1)S(1)}, u32[]{:S(2)}, u32[]{:S(2)}) collective-permute-start(bf16[192,256]{1,0:T(8,128)(2,1)} %param.10), channel_id=1, source_target_pairs={{0,256},{2,320},{8,0},{10,64},{64,258},{66,322},{72,2},{74,66},{25... | collective-permute-start | bytes 294920 | tf_op jit(solution)/shard_map/ppermute | solution.py:203
  26.7 0.7 pad_add_fusion.place_ref
  27.4 1.2 collective-permute-done
  28.6 0.0 collective-permute-done.1
  28.6 34.3 %all-gather.1 = bf16[768,256]{1,0:T(8,128)(2,1)S(1)} all-gather(bf16[192,256]{1,0:T(8,128)(2,1)S(1)} %collective-permute-done), channel_id=3, replica_groups=mesh['yl'=2,'zp'=2,'zq'=2,'zb'=4,'yh'=2,'xp'=2,'xq'=2,'c'=2] {'zp','zq'}, dimensions={0}, use_global_device_ids=true | all-gather | bytes 491520 | tf_op jit(solution)/shard_map/all_gather | solution.py:227
  62.9 1.9 collective-permute-start.2
  64.8 5.3 %collective-permute-start.5 = (bf16[4,192,256]{2,1,0:T(8,128)(2,1)S(1)}, bf16[4,192,256]{2,1,0:T(8,128)(2,1)S(1)}, u32[]{:S(2)}, u32[]{:S(2)}) collective-permute-start(bf16[4,192,256]{2,1,0:T(8,128)(2,1)S(1)} %bitcast.22), channel_id=1, source_target_pairs={{0,16},{16,32},{32,48},{48,64},{64,80},{80,96},{96,112},{112,128},... | collective-permute-start | bytes 1179656 | tf_op jit(solution)/shard_map/ppermute | solution.py:223
  70.1 1.1 pad_maximum_fusion
  71.2 3.1 %collective-permute-start.6 = (bf16[768,512]{1,0:T(8,128)(2,1)S(1)}, bf16[768,512]{1,0:T(8,128)(2,1)S(1)}, u32[]{:S(2)}, u32[]{:S(2)}) collective-permute-start(bf16[768,512]{1,0:T(8,128)(2,1)S(1)} %pad_maximum_fusion), channel_id=1, source_target_pairs={{0,256},{8,0},{256,264},{264,8},{1,257},{9,1},{257,265},{265,9},{2... | collective-permute-start | bytes 2359304 | tf_op jit(solution)/shard_map/ppermute | solution.py:203
  74.3 0.7 collective-permute-start.7
  75.1 1.9 collective-permute-start.3
  77.1 0.0 collective-permute-done.2
  77.1 5.5 %collective-permute-start.4 = (bf16[2,192,256]{2,1,0:T(8,128)(2,1)S(1)}, bf16[2,192,256]{2,1,0:T(8,128)(2,1)S(1)}, u32[]{:S(2)}, u32[]{:S(2)}) collective-permute-start(bf16[2,192,256]{2,1,0:T(8,128)(2,1)S(1)} %bitcast.27), channel_id=1, source_target_pairs={{0,224},{16,240},{32,0},{48,16},{64,32},{80,48},{96,64},{112,80},{... | collective-permute-start | bytes 589832 | tf_op jit(solution)/shard_map/ppermute | solution.py:223
  82.6 2.0 collective-permute-done.3
  84.6 2.3 %collective-permute-done.4 = bf16[2,192,256]{2,1,0:T(8,128)(2,1)S(1)} collective-permute-done((bf16[2,192,256]{2,1,0:T(8,128)(2,1)S(1)}, bf16[2,192,256]{2,1,0:T(8,128)(2,1)S(1)}, u32[]{:S(2)}, u32[]{:S(2)}) %collective-permute-start.4) | collective-permute-done | bytes 196640 | tf_op jit(solution)/shard_map/ppermute | solution.py:223
  86.8 0.0 collective-permute-done.5
  87.0 1.3 constant_dynamic-slice_fusion
  88.3 0.0 collective-permute-done.6.same_ref
  88.3 0.0 collective-permute-done.7.other_ref
  88.3 0.9 copy-done.4
  89.3 0.9 copy-done.5
  90.2 7.2 %shard_map.102 = bf16[2,2,768,256]{3,2,1,0:T(8,128)(2,1)} custom-call(s32[2]{0:T(128)} %pad_add_fusion.place_ref, bf16[2,2,2,768,384]{4,3,2,1,0:T(8,128)(2,1)} %bitcast.29, bf16[768,512]{1,0:T(8,128)(2,1)} %copy-done.4, bf16[768,512]{1,0:T(8,128)(2,1)} %copy-done.5), custom_call_target="tpu_custom_call" | custom-call | flops 2415919104 | bytes 6291456 | tf_op jit(solution)/shard_map/pallas_call | solution.py:131
  97.4 0.0 reduce-scatter.2.cloned.1.call-update
  97.4 8.0 %shard_map.103 = (bf16[768,256]{1,0:T(8,128)(2,1)}, bf16[768,256]{1,0:T(8,128)(2,1)}, bf16[768,256]{1,0:T(8,128)(2,1)}, bf16[768,256]{1,0:T(8,128)(2,1)}) custom-call(s32[2]{0:T(128)} %pad_add_fusion.place_ref, bf16[2,2,2,768,384]{4,3,2,1,0:T(8,128)(2,1)} %bitcast.30, bf16[4,2,2,192,256]{4,3,2,1,0:T(8,128)(2,1)} %bitcast.26), custom_call_target="tpu_custom_call" | custom-call | flops 2415919104 | bytes 6291456 | tf_op jit(solution)/shard_map/pallas_call | solution.py:172
  105.4 1.6 collective-permute-start.10
  107.1 8.2 %collective-permute-start.11 = (bf16[768,256]{1,0:T(8,128)(2,1)}, bf16[768,256]{1,0:T(8,128)(2,1)S(1)}, u32[]{:S(2)}, u32[]{:S(2)}) collective-permute-start(bf16[768,256]{1,0:T(8,128)(2,1)} %get-tuple-element.28), channel_id=1, source_target_pairs={{0,266},{2,264},{8,10},{10,8},{256,258},{258,256},{264,2},{266,0},... | collective-permute-start | bytes 1179656 | tf_op jit(solution)/shard_map/ppermute | solution.py:203
  115.3 23.3 %collective-permute-start.8 = (bf16[768,256]{1,0:T(8,128)(2,1)}, bf16[768,256]{1,0:T(8,128)(2,1)S(1)}, u32[]{:S(2)}, u32[]{:S(2)}) collective-permute-start(bf16[768,256]{1,0:T(8,128)(2,1)} %get-tuple-element.25), channel_id=1, source_target_pairs={{0,8},{2,10},{8,264},{10,266},{256,0},{258,2},{264,256},{266,258},... | collective-permute-start | bytes 1179656 | tf_op jit(solution)/shard_map/ppermute | solution.py:203
  138.6 1.9 collective-permute-start.9
  140.5 0.0 collective-permute-done.10.p2_ref
  140.5 0.0 copy-start
  140.5 0.0 collective-permute-done.11.p3_ref
  140.6 16.9 %collective-permute-done.8.p0_ref = bf16[768,256]{1,0:T(8,128)(2,1)S(1)} collective-permute-done((bf16[768,256]{1,0:T(8,128)(2,1)}, bf16[768,256]{1,0:T(8,128)(2,1)S(1)}, u32[]{:S(2)}, u32[]{:S(2)}) %collective-permute-start.8) | collective-permute-done | bytes 393248 | tf_op jit(solution)/shard_map/ppermute | solution.py:203
  157.4 0.0 collective-permute-done.9.p1_ref
  157.4 0.7 copy-done.2
  158.2 0.7 copy-done.3
  158.9 7.5 %shard_map.104 = (bf16[768,256]{1,0:T(8,128)(2,1)}, bf16[768,256]{1,0:T(8,128)(2,1)}, bf16[768,256]{1,0:T(8,128)(2,1)}, f32[2,128]{1,0:T(2,128)}) custom-call(bf16[768,256]{1,0:T(8,128)(2,1)} %q_ref.3, bf16[768,256]{1,0:T(8,128)(2,1)} %k_ref.3, bf16[768,256]{1,0:T(8,128)(2,1)} %v_ref.3, bf16[768,256]{1,0:T(8,128)(2,1)} %copy-done.2, ...), custom_call_target="tpu_custom_call" | custom-call | tf_op jit(solution)/shard_map/pallas_call | solution.py:103
  166.4 0.7 broadcast_in_dim.4
  167.1 13.3 %all_to_all.10 = f32[32,2,128]{2,1,0:T(2,128)S(1)} all-to-all(f32[32,2,128]{2,1,0:T(2,128)S(1)} %broadcast_in_dim.4), channel_id=1, replica_groups=mesh['yl'=2,'zp'=2,'zq'=2,'zb'=4,'yh'=2,'xp'=2,'xq'=2,'c'=2] {'yl','yh',..., dimensions={0} | all-to-all | bytes 65536 | tf_op jit(solution)/shard_map/all_to_all | solution.py:238
  180.4 16.3 %all_to_all.11 = f32[16,2,128]{2,1,0:T(2,128)S(1)} all-to-all(f32[16,2,128]{2,1,0:T(2,128)S(1)} %broadcast_in_dim.5), channel_id=1, replica_groups=mesh['yl'=2,'zp'=2,'zq'=2,'zb'=4,'yh'=2,'xp'=2,'xq'=2,'c'=2] {'zp','zq',..., dimensions={0} | all-to-all | bytes 32768 | tf_op jit(solution)/shard_map/all_to_all | solution.py:238
  196.7 0.6 reduce_sum.19
  197.3 4.2 %collective-permute-start.12 = (bf16[192,256]{1,0:T(8,128)(2,1)}, bf16[192,256]{1,0:T(8,128)(2,1)S(1)}, u32[]{:S(2)}, u32[]{:S(2)}) collective-permute-start(bf16[192,256]{1,0:T(8,128)(2,1)} %reduce-scatter.2.cloned.1.call-done), channel_id=1, source_target_pairs={{0,8},{2,72},{8,264},{10,328},{64,10},{66,74},{72,266},{74,330},{2... | collective-permute-start | bytes 294920 | tf_op jit(solution)/shard_map/ppermute | solution.py:203
  201.5 16.1 %collective-permute-done.12 = bf16[192,256]{1,0:T(8,128)(2,1)S(1)} collective-permute-done((bf16[192,256]{1,0:T(8,128)(2,1)}, bf16[192,256]{1,0:T(8,128)(2,1)S(1)}, u32[]{:S(2)}, u32[]{:S(2)}) %collective-permute-start.12) | collective-permute-done | bytes 98336 | tf_op jit(solution)/shard_map/ppermute | solution.py:203
  217.6 0.7 convert_element_type.3
  (20 shorter events, 0.3 us)
Async XLA Ops:
  7.2 81.1 %all-gather.4.cloned.1.call-start = ((), (), s32[]{:S(2)}) async-start(), calls=%async_computation.4 | async-start | bytes 5308416 | tf_op jit(solution)/shard_map/all_gather | solution.py:244
  7.9 189.4 %reduce-scatter.2.cloned.1.call-start = ((), (), s32[]{:S(2)}) async-start(), calls=%async_computation.3 | async-start | bytes 1671168 | tf_op jit(solution)/shard_map/reduce_scatter | solution.py:257
  13.0 15.6 %collective-permute-start.1 = (bf16[768,256]{1,0:T(8,128)(2,1)}, bf16[768,256]{1,0:T(8,128)(2,1)S(1)}, u32[]{:S(2)}, u32[]{:S(2)}) collective-permute-start(bf16[768,256]{1,0:T(8,128)(2,1)} %shard_map.101), channel_id=1, source_target_pairs={{0,2},{2,0},{1,3},{3,1},{4,6},{6,4},{5,7},{7,5},{8,10},{10,8},{9,1... | collective-permute-start | bytes 1179656 | tf_op jit(solution)/shard_map/ppermute | solution.py:203
  15.2 13.4 %collective-permute-start = (bf16[192,256]{1,0:T(8,128)(2,1)}, bf16[192,256]{1,0:T(8,128)(2,1)S(1)}, u32[]{:S(2)}, u32[]{:S(2)}) collective-permute-start(bf16[192,256]{1,0:T(8,128)(2,1)} %param.10), channel_id=1, source_target_pairs={{0,256},{2,320},{8,0},{10,64},{64,258},{66,322},{72,2},{74,66},{25... | collective-permute-start | bytes 294920 | tf_op jit(solution)/shard_map/ppermute | solution.py:203
  62.9 14.1 %collective-permute-start.2 = (bf16[4,192,256]{2,1,0:T(8,128)(2,1)S(1)}, bf16[4,192,256]{2,1,0:T(8,128)(2,1)S(1)}, u32[]{:S(2)}, u32[]{:S(2)}) collective-permute-start(bf16[4,192,256]{2,1,0:T(8,128)(2,1)S(1)} %bitcast.21), channel_id=1, source_target_pairs={{0,240},{16,0},{32,16},{48,32},{64,48},{80,64},{96,80},{112,96},{1... | collective-permute-start | bytes 1179656 | tf_op jit(solution)/shard_map/ppermute | solution.py:223
  64.8 22.0 %collective-permute-start.5 = (bf16[4,192,256]{2,1,0:T(8,128)(2,1)S(1)}, bf16[4,192,256]{2,1,0:T(8,128)(2,1)S(1)}, u32[]{:S(2)}, u32[]{:S(2)}) collective-permute-start(bf16[4,192,256]{2,1,0:T(8,128)(2,1)S(1)} %bitcast.22), channel_id=1, source_target_pairs={{0,16},{16,32},{32,48},{48,64},{64,80},{80,96},{96,112},{112,128},... | collective-permute-start | bytes 1179656 | tf_op jit(solution)/shard_map/ppermute | solution.py:223
  71.2 17.1 %collective-permute-start.6 = (bf16[768,512]{1,0:T(8,128)(2,1)S(1)}, bf16[768,512]{1,0:T(8,128)(2,1)S(1)}, u32[]{:S(2)}, u32[]{:S(2)}) collective-permute-start(bf16[768,512]{1,0:T(8,128)(2,1)S(1)} %pad_maximum_fusion), channel_id=1, source_target_pairs={{0,256},{8,0},{256,264},{264,8},{1,257},{9,1},{257,265},{265,9},{2... | collective-permute-start | bytes 2359304 | tf_op jit(solution)/shard_map/ppermute | solution.py:203
  74.3 14.0 %collective-permute-start.7 = (bf16[768,512]{1,0:T(8,128)(2,1)S(1)}, bf16[768,512]{1,0:T(8,128)(2,1)S(1)}, u32[]{:S(2)}, u32[]{:S(2)}) collective-permute-start(bf16[768,512]{1,0:T(8,128)(2,1)S(1)} %pad_maximum_fusion), channel_id=1, source_target_pairs={{0,264},{8,8},{256,256},{264,0},{1,265},{9,9},{257,257},{265,1},{2... | collective-permute-start | bytes 2359304 | tf_op jit(solution)/shard_map/ppermute | solution.py:203
  75.1 9.4 %collective-permute-start.3 = (bf16[2,192,256]{2,1,0:T(8,128)(2,1)S(1)}, bf16[2,192,256]{2,1,0:T(8,128)(2,1)S(1)}, u32[]{:S(2)}, u32[]{:S(2)}) collective-permute-start(bf16[2,192,256]{2,1,0:T(8,128)(2,1)S(1)} %bitcast.28), channel_id=1, source_target_pairs={{0,32},{16,48},{32,64},{48,80},{64,96},{80,112},{96,128},{112,144}... | collective-permute-start | bytes 589832 | tf_op jit(solution)/shard_map/ppermute | solution.py:223
  77.1 9.7 %collective-permute-start.4 = (bf16[2,192,256]{2,1,0:T(8,128)(2,1)S(1)}, bf16[2,192,256]{2,1,0:T(8,128)(2,1)S(1)}, u32[]{:S(2)}, u32[]{:S(2)}) collective-permute-start(bf16[2,192,256]{2,1,0:T(8,128)(2,1)S(1)} %bitcast.27), channel_id=1, source_target_pairs={{0,224},{16,240},{32,0},{48,16},{64,32},{80,48},{96,64},{112,80},{... | collective-permute-start | bytes 589832 | tf_op jit(solution)/shard_map/ppermute | solution.py:223
  88.3 0.9 copy-start.4
  89.3 0.9 copy-start.5
  105.4 35.1 %collective-permute-start.10 = (bf16[768,256]{1,0:T(8,128)(2,1)}, bf16[768,256]{1,0:T(8,128)(2,1)S(1)}, u32[]{:S(2)}, u32[]{:S(2)}) collective-permute-start(bf16[768,256]{1,0:T(8,128)(2,1)} %get-tuple-element.27), channel_id=1, source_target_pairs={{0,264},{2,266},{8,8},{10,10},{256,256},{258,258},{264,0},{266,2},... | collective-permute-start | bytes 1179656 | tf_op jit(solution)/shard_map/ppermute | solution.py:203
  107.1 33.5 %collective-permute-start.11 = (bf16[768,256]{1,0:T(8,128)(2,1)}, bf16[768,256]{1,0:T(8,128)(2,1)S(1)}, u32[]{:S(2)}, u32[]{:S(2)}) collective-permute-start(bf16[768,256]{1,0:T(8,128)(2,1)} %get-tuple-element.28), channel_id=1, source_target_pairs={{0,266},{2,264},{8,10},{10,8},{256,258},{258,256},{264,2},{266,0},... | collective-permute-start | bytes 1179656 | tf_op jit(solution)/shard_map/ppermute | solution.py:203
  115.3 42.1 %collective-permute-start.8 = (bf16[768,256]{1,0:T(8,128)(2,1)}, bf16[768,256]{1,0:T(8,128)(2,1)S(1)}, u32[]{:S(2)}, u32[]{:S(2)}) collective-permute-start(bf16[768,256]{1,0:T(8,128)(2,1)} %get-tuple-element.25), channel_id=1, source_target_pairs={{0,8},{2,10},{8,264},{10,266},{256,0},{258,2},{264,256},{266,258},... | collective-permute-start | bytes 1179656 | tf_op jit(solution)/shard_map/ppermute | solution.py:203
  138.6 18.8 %collective-permute-start.9 = (bf16[768,256]{1,0:T(8,128)(2,1)}, bf16[768,256]{1,0:T(8,128)(2,1)S(1)}, u32[]{:S(2)}, u32[]{:S(2)}) collective-permute-start(bf16[768,256]{1,0:T(8,128)(2,1)} %get-tuple-element.26), channel_id=1, source_target_pairs={{0,10},{2,8},{8,266},{10,264},{256,2},{258,0},{264,258},{266,256},... | collective-permute-start | bytes 1179656 | tf_op jit(solution)/shard_map/ppermute | solution.py:203
  140.5 16.9 %copy-start = (bf16[768,256]{1,0:T(8,128)(2,1)}, bf16[768,256]{1,0:T(8,128)(2,1)S(1)}, u32[]{:S(2)}) copy-start(bf16[768,256]{1,0:T(8,128)(2,1)S(1)} %collective-permute-done.10.p2_ref) | copy-start | bytes 1179652
  140.5 16.9 %copy-start.1 = (bf16[768,256]{1,0:T(8,128)(2,1)}, bf16[768,256]{1,0:T(8,128)(2,1)S(1)}, u32[]{:S(2)}) copy-start(bf16[768,256]{1,0:T(8,128)(2,1)S(1)} %collective-permute-done.11.p3_ref) | copy-start | bytes 1179652
  157.4 0.7 copy-start.2
  158.1 0.7 copy-start.3
  197.3 20.2 %collective-permute-start.12 = (bf16[192,256]{1,0:T(8,128)(2,1)}, bf16[192,256]{1,0:T(8,128)(2,1)S(1)}, u32[]{:S(2)}, u32[]{:S(2)}) collective-permute-start(bf16[192,256]{1,0:T(8,128)(2,1)} %reduce-scatter.2.cloned.1.call-done), channel_id=1, source_target_pairs={{0,8},{2,72},{8,264},{10,328},{64,10},{66,74},{72,266},{74,330},{2... | collective-permute-start | bytes 294920 | tf_op jit(solution)/shard_map/ppermute | solution.py:203
Sparse Core Ops, SparseCore 0:
  10.2 46.6 all-gather.3
  97.5 79.4 reduce-scatter.1

commit v9 on v6

--- a/solution.py
+++ b/solution.py
@@ -63,7 +63,8 @@
 
 
 def backward_kernel(
-    q_ref, k_ref, v_ref, one_ref, two_ref, gains_ref, qg_ref, kg_ref, vg_ref, terms_ref
+    stays_ref, q_ref, k_ref, v_ref, own_ref, p1_ref, p2_ref, p3_ref, gains_ref,
+    qg_ref, kg_ref, vg_ref, terms_ref,
 ):
     @pl.when(pl.program_id(0) == 0)
     def _():
@@ -78,8 +79,9 @@
         prob = softmax(q_norm, k_norm)
         prob_low = prob.astype(jnp.bfloat16)
         attn = product(prob_low, value, 1, 0).astype(jnp.bfloat16)
-        grad = one_ref[:, cols].astype(jnp.float32) + two_ref[:, cols].astype(jnp.float32)
-        grad = grad.astype(jnp.bfloat16)
+        grad = sum(ref[:, cols].astype(jnp.float32) for ref in (p1_ref, p2_ref, p3_ref))
+        own = jnp.where(stays_ref[0] == 1, own_ref[:, cols].astype(jnp.float32), 0.0)
+        grad = (grad + own).astype(jnp.bfloat16)
         vg_ref[:, cols] = product(prob_low, grad, 0, 0).astype(jnp.bfloat16)
         delta = jnp.sum(
             grad.astype(jnp.float32) * attn.astype(jnp.float32), axis=-1, keepdims=True
@@ -93,19 +95,22 @@
         kg_ref[:, cols] = unnormalize(kn_grad, k_unit, k_inverse, k_gain).astype(jnp.bfloat16)
 
 
-def backward(queries_raw, keys_raw, values, part_one, part_two, norm_gains):
+def backward(stays, queries_raw, keys_raw, values, parts, norm_gains):
     tokens, width = queries_raw.shape
-    block = pl.BlockSpec((PATCH, width), lambda i: (i, 0))
-    gains = pl.BlockSpec((2, HD), lambda i: (0, 0))
+    block = pl.BlockSpec((PATCH, width), lambda i, stays: (i, 0))
+    gains = pl.BlockSpec((2, HD), lambda i, stays: (0, 0))
     out = jax.ShapeDtypeStruct((tokens, width), jnp.bfloat16)
     return pl.pallas_call(
         backward_kernel,
-        grid=(tokens // PATCH,),
-        in_specs=[block] * 5 + [gains],
-        out_specs=[block, block, block, gains],
+        grid_spec=pltpu.PrefetchScalarGridSpec(
+            num_scalar_prefetch=1,
+            grid=(tokens // PATCH,),
+            in_specs=[block] * 7 + [gains],
+            out_specs=[block, block, block, gains],
+        ),
         out_shape=[out, out, out, jax.ShapeDtypeStruct((2, HD), jnp.float32)],
         compiler_params=pltpu.CompilerParams(vmem_limit_bytes=VMEM_LIMIT),
-    )(queries_raw, keys_raw, values, part_one, part_two, norm_gains)
+    )(stays, queries_raw, keys_raw, values, *parts, norm_gains)
 
 
 STEPS = (0, 3, 1, 2)
@@ -122,52 +127,60 @@
     return pl.ds(pl.multiple_of(row_block(place_ref, index) * width, width), width)
 
 
-def weight_kernel(place_ref, own_attn_ref, other_attn_ref, *refs):
-    own_refs, other_refs, (wgrad_ref, total) = refs[:8], refs[8:16], refs[16:]
-    step = pl.program_id(0)
-    width = own_refs[0].shape[1]
-    own_attn, other_attn = own_attn_ref[...], other_attn_ref[...]
+def add_blocks(place_ref, attn_ref, refs, total, start):
+    width = refs[0].shape[1]
+    attn = attn_ref[...]
     for index in range(8):
         rows = rows_of(place_ref, index, width)
-        term = product(own_refs[index][...], own_attn, 0, 0)
-        term += product(other_refs[index][...], other_attn, 0, 0)
-
-        @pl.when(step == 0)
+        term = product(refs[index][...], attn, 0, 0)
+
+        @pl.when(start)
         def _():
             total[rows] = term
 
-        @pl.when(step > 0)
+        @pl.when(jnp.logical_not(start))
         def _():
             total[rows] += term
 
-    @pl.when(step == pl.num_programs(0) - 1)
+
+def first_kernel(place_ref, attn_ref, *refs):
+    add_blocks(place_ref, attn_ref, refs[:8], refs[8], pl.program_id(0) == 0)
+
+
+def second_kernel(place_ref, attn_ref, *refs):
+    first_ref, wgrad_ref, total = refs[8:]
+    add_blocks(place_ref, attn_ref, refs[:8], total, pl.program_id(0) == 0)
+
+    @pl.when(pl.program_id(0) == pl.num_programs(0) - 1)
     def _():
-        wgrad_ref[...] = total[...].astype(wgrad_ref.dtype)
-
-
-def weight_product(place, own, other, own_attn, other_attn):
-    tokens, width = own[0].shape
-    heads = own_attn.shape[1]
+        wgrad_ref[...] = (total[...] + first_ref[...]).astype(wgrad_ref.dtype)
+
+
+def weight_product(place, attn, blocks, first=None):
+    tokens, width = blocks[0].shape
+    heads = attn.shape[1]
     rows = 8 * width
-    block = pl.BlockSpec((CHUNK, width), lambda i, place: (i, 0))
-    attn = pl.BlockSpec((CHUNK, heads), lambda i, place: (i, 0))
-    return pl.pallas_call(
-        weight_kernel,
+    whole = pl.BlockSpec((rows, heads), lambda i, place: (0, 0))
+    last = first is not None
+    return pl.pallas_call(
+        second_kernel if last else first_kernel,
         grid_spec=pltpu.PrefetchScalarGridSpec(
             num_scalar_prefetch=1,
             grid=(tokens // CHUNK,),
-            in_specs=[attn, attn] + [block] * 16,
-            out_specs=pl.BlockSpec((rows, heads), lambda i, place: (0, 0)),
-            scratch_shapes=[pltpu.VMEM((rows, heads), jnp.float32)],
-        ),
-        out_shape=jax.ShapeDtypeStruct((rows, heads), jnp.bfloat16),
+            in_specs=[pl.BlockSpec((CHUNK, heads), lambda i, place: (i, 0))]
+            + [pl.BlockSpec((CHUNK, width), lambda i, place: (i, 0))] * 8
+            + [whole] * last,
+            out_specs=whole,
+            scratch_shapes=[pltpu.VMEM((rows, heads), jnp.float32)] * last,
+        ),
+        out_shape=jax.ShapeDtypeStruct((rows, heads), jnp.bfloat16 if last else jnp.float32),
         compiler_params=pltpu.CompilerParams(vmem_limit_bytes=VMEM_LIMIT),
         cost_estimate=pl.CostEstimate(
-            flops=4 * rows * tokens * heads,
-            bytes_accessed=2 * (2 * rows * tokens + rows * heads),
+            flops=2 * rows * tokens * heads,
+            bytes_accessed=2 * rows * (tokens + 2 * heads),
             transcendentals=0,
         ),
-    )(place, own_attn, other_attn, *own, *other)
+    )(place, attn, *blocks, *([first] if last else []))
 
 
 def token_kernel(place_ref, weight_ref, *refs):
@@ -224,19 +237,8 @@
     return lax.ppermute(array, "x", [(x, (x + step) % 4) for x in range(4)])
 
 
-def halves_for(grad_out):
-    near = swap_y(grad_out, lambda low, up: (up, up) if low != up else None)
-    cross = swap_y(grad_out, lambda low, up: (up, 1 - up) if low != up else None)
-    far = swap_y(grad_out, lambda low, up: (up, 1 - up) if low == up else None)
-    stays = lax.axis_index("yl") == lax.axis_index("yh")
-    return jnp.where(stays, grad_out, far), jnp.where(stays, near, cross)
-
-
 def round_x(block):
-    half = block.shape[0] // 2
-    left, right = along_x(block, 1), along_x(block, -1)
-    opposite = [along_x(left[:half], 1), along_x(right[half:], -1)]
-    blocks = [block, left, right, jnp.concatenate(opposite)]
+    blocks = [block, along_x(block, 1), along_x(block, -1), along_x(block, 2)]
     return blocks + [to_core(piece) for piece in blocks]
 
 
@@ -247,24 +249,38 @@
 
 def per_device(queries_raw, keys_raw, values, grad_out, out_weight, norm_gains):
     place = jnp.stack([lax.axis_index("x"), lax.axis_index("c")]).astype(jnp.int32)
-    weights = lax.all_gather(out_weight, "z", axis=0, tiled=True)
-    own, other = halves_for(grad_out)
-    other, own = round_x(other), round_x(own)
+    stays = lax.axis_index("yl") == lax.axis_index("yh")
+    turn = lambda low, up: (up, low)
+    weights = lax.all_gather(swap_y(out_weight, turn), "z", axis=0, tiled=True)
+    own = round_x(grad_out)
+    other = round_x(to_partner(grad_out))
 
     attn = forward(queries_raw, keys_raw, values, norm_gains)
-    wgrad = weight_product(place, own, other, attn, to_partner(attn))
+    turned = swap_y(attn, turn)
+    crossed = swap_y(attn, lambda low, up: (up, 1 - low))
+    own_attn = jnp.where(stays, turned, crossed)
+    other_attn = jnp.where(stays, crossed, turned)
+    first = weight_product(place, own_attn, own)
+    wgrad = weight_product(place, other_attn, other, first)
     shard = lax.psum_scatter(wgrad, "z", scatter_dimension=0, tiled=True)
 
     weights, _ = lax.optimization_barrier((weights, wgrad))
     part_other = token_product(place, other, weights)
     weights, _ = lax.optimization_barrier((weights, part_other))
     part_own = token_product(place, own, weights)
+    parts = [
+        part_own,
+        swap_y(part_other, lambda low, up: (1 - low, low) if low == up else None),
+        swap_y(part_other, lambda low, up: (1 - low, low) if low != up else None),
+        swap_y(part_own, lambda low, up: (low, low) if low != up else None),
+    ]
     queries_grad, keys_grad, values_grad, terms = backward(
-        queries_raw, keys_raw, values, part_own, to_partner(part_other), norm_gains
+        stays.astype(jnp.int32).reshape(1), queries_raw, keys_raw, values, parts, norm_gains
     )
     gains_grad = sum_over(sum_over(terms, ("yl", "yh", "x", "c"), 32), "z", 16)
     shard, gains_grad = lax.optimization_barrier((shard, gains_grad))
-    return (queries_grad, keys_grad, values_grad, shard.astype(jnp.float32), gains_grad)
+    weight_grad = swap_y(shard, turn).astype(jnp.float32)
+    return (queries_grad, keys_grad, values_grad, weight_grad, gains_grad)
 
 
 def solution(mesh):

time: 215 us -> 219 us (1.019)
  the two profiles are of different devices: /device:TPU:6 before, /device:TPU:8 now
where the time goes in v9:
time: 219 us; the launch traced here: 218 us
  starting transfers between devices  67.1 us (31%)
  Pallas kernels  48.9 us (22%)
  waiting for transfers between devices  40.9 us (19%)
  blocking collectives  39.6 us (18%)
  between operations  14.5 us (7%)
  other arithmetic  3.95 us (2%)
  local copies, waits for them, and re-layouts  2.97 us (1%)
    all_to_all x2, blocking collectives, sum_over(): lax.all_to_all(jnp.broadcast_to(array[None], (count,) + array.shape), axi...  39.6 us
    ppermute x6, waiting for transfers between devices, along_x(): return lax.ppermute(array, 'x', [(x, (x + step) % 4) for x in range(4)])  24.1 us
    pallas_call x2, Pallas kernels, weight_product(): pl.pallas_call(second_kernel if last else first_kernel, grid_spec=pltpu.P...  23.2 us
    ppermute x7, starting transfers between devices, swap_y(): return lax.ppermute(array, ('yl', 'yh'), pairs)  22.7 us
    ppermute x6, starting transfers between devices, along_x(): return lax.ppermute(array, 'x', [(x, (x + step) % 4) for x in range(4)])  21 us
    ppermute x8, starting transfers between devices, to_core(): return lax.ppermute(array, 'c', [(0, 1), (1, 0)])  16.8 us
    ppermute x7, waiting for transfers between devices, swap_y(): return lax.ppermute(array, ('yl', 'yh'), pairs)  16.6 us
    pallas_call x2, Pallas kernels, token_product(): pl.pallas_call(token_kernel, grid_spec=pltpu.PrefetchScalarGridSpec(num_s...  13.2 us
  transfers between devices with their start and end apart: 24, of which 8 were waited for; matrix products, arithmetic and copies ran while one was open for 2% of the time, Pallas kernels for 22%

profile of v9, /device:TPU:8, one launch (start us, length us, event | category | flops | bytes accessed | tf_op | source)
XLA Modules:
  0.0 217.9 jit_solution(6251696790005504354)
XLA Ops:
  7.2 0.0 all-gather.2.cloned.1.call-start
  7.2 3.6 %collective-permute-start = (bf16[192,256]{1,0:T(8,128)(2,1)}, bf16[192,256]{1,0:T(8,128)(2,1)S(1)}, u32[]{:S(2)}, u32[]{:S(2)}) collective-permute-start(bf16[192,256]{1,0:T(8,128)(2,1)} %param.10), channel_id=1, source_target_pairs={{0,0},{8,256},{256,8},{264,264},{1,1},{9,257},{257,9},{265,265},{2... | collective-permute-start | bytes 294920 | tf_op jit(solution)/shard_map/ppermute | solution.py:225
  10.8 3.2 %collective-permute-done = bf16[192,256]{1,0:T(8,128)(2,1)S(1)} collective-permute-done((bf16[192,256]{1,0:T(8,128)(2,1)}, bf16[192,256]{1,0:T(8,128)(2,1)S(1)}, u32[]{:S(2)}, u32[]{:S(2)}) %collective-permute-start) | collective-permute-done | bytes 98336 | tf_op jit(solution)/shard_map/ppermute | solution.py:225
  14.1 0.6 copy-done.13
  14.7 0.0 reduce-scatter.2.cloned.1.call-start
  14.8 5.1 %shard_map.101 = bf16[768,256]{1,0:T(8,128)(2,1)} custom-call(bf16[768,256]{1,0:T(8,128)(2,1)} %q_ref.3, bf16[768,256]{1,0:T(8,128)(2,1)} %k_ref.3, bf16[768,256]{1,0:T(8,128)(2,1)} %v_ref.3, f32[2,128]{1,0:T(2,128)} %gains_ref.3), custom_call_target="tpu_custom_call" | custom-call | tf_op jit(solution)/shard_map/pallas_call | solution.py:55
  19.9 2.6 %collective-permute-start.1 = (bf16[768,256]{1,0:T(8,128)(2,1)}, bf16[768,256]{1,0:T(8,128)(2,1)}, u32[]{:S(2)}, u32[]{:S(2)}) collective-permute-start(bf16[768,256]{1,0:T(8,128)(2,1)} %shard_map.101), channel_id=1, source_target_pairs={{0,8},{8,264},{256,0},{264,256},{1,9},{9,265},{257,1},{265,257},{2... | collective-permute-start | bytes 1179656 | tf_op jit(solution)/shard_map/ppermute | solution.py:225
  22.4 2.8 %collective-permute-start.2 = (bf16[768,256]{1,0:T(8,128)(2,1)}, bf16[768,256]{1,0:T(8,128)(2,1)}, u32[]{:S(2)}, u32[]{:S(2)}) collective-permute-start(bf16[768,256]{1,0:T(8,128)(2,1)} %shard_map.101), channel_id=1, source_target_pairs={{0,0},{8,256},{256,8},{264,264},{1,1},{9,257},{257,9},{265,265},{2... | collective-permute-start | bytes 1179656 | tf_op jit(solution)/shard_map/ppermute | solution.py:225
  25.3 3.4 %collective-permute-start.11 = (bf16[768,384]{1,0:T(8,128)(2,1)S(1)}, bf16[768,384]{1,0:T(8,128)(2,1)S(1)}, u32[]{:S(2)}, u32[]{:S(2)}) collective-permute-start(bf16[768,384]{1,0:T(8,128)(2,1)S(1)} %copy-done), channel_id=1, source_target_pairs={{0,2},{2,4},{4,6},{6,0},{1,3},{3,5},{5,7},{7,1},{8,10},{10,12},{12... | collective-permute-start | bytes 1769480 | tf_op jit(solution)/shard_map/ppermute | solution.py:237
  28.7 3.7 %collective-permute-start.12 = (bf16[768,384]{1,0:T(8,128)(2,1)S(1)}, bf16[768,384]{1,0:T(8,128)(2,1)S(1)}, u32[]{:S(2)}, u32[]{:S(2)}) collective-permute-start(bf16[768,384]{1,0:T(8,128)(2,1)S(1)} %copy-done), channel_id=1, source_target_pairs={{0,6},{2,0},{4,2},{6,4},{1,7},{3,1},{5,3},{7,5},{8,14},{10,8},{12,... | collective-permute-start | bytes 1769480 | tf_op jit(solution)/shard_map/ppermute | solution.py:237
  32.4 6.5 %collective-permute-start.3 = (bf16[768,384]{1,0:T(8,128)(2,1)S(1)}, bf16[768,384]{1,0:T(8,128)(2,1)S(1)}, u32[]{:S(2)}, u32[]{:S(2)}) collective-permute-start(bf16[768,384]{1,0:T(8,128)(2,1)S(1)} %copy-done), channel_id=1, source_target_pairs={{0,256},{256,0},{1,257},{257,1},{2,258},{258,2},{3,259},{259,3},{4... | collective-permute-start | bytes 1769480 | tf_op jit(solution)/shard_map/ppermute | solution.py:229
  38.9 3.7 %collective-permute-start.13 = (bf16[768,384]{1,0:T(8,128)(2,1)S(1)}, bf16[768,384]{1,0:T(8,128)(2,1)S(1)}, u32[]{:S(2)}, u32[]{:S(2)}) collective-permute-start(bf16[768,384]{1,0:T(8,128)(2,1)S(1)} %copy-done), channel_id=1, source_target_pairs={{0,4},{2,6},{4,0},{6,2},{1,5},{3,7},{5,1},{7,3},{8,12},{10,14},{12... | collective-permute-start | bytes 1769480 | tf_op jit(solution)/shard_map/ppermute | solution.py:237
  42.6 1.9 collective-permute-start.14
  44.6 2.4 %collective-permute-start.15 = (bf16[768,384]{1,0:T(8,128)(2,1)S(1)}, bf16[768,384]{1,0:T(8,128)(2,1)S(1)}, u32[]{:S(2)}, u32[]{:S(2)}) collective-permute-start(bf16[768,384]{1,0:T(8,128)(2,1)S(1)} %collective-permute-done.11.refs_1_), channel_id=1, source_target_pairs={{0,1},{1,0},{2,3},{3,2},{4,5},{5,4},{6,7},{7,6},{8,9},{9,8},{10,11... | collective-permute-start | bytes 1769480 | tf_op jit(solution)/shard_map/ppermute | solution.py:233
  47.0 8.9 %collective-permute-done.12.refs_2_ = bf16[768,384]{1,0:T(8,128)(2,1)S(1)} collective-permute-done((bf16[768,384]{1,0:T(8,128)(2,1)S(1)}, bf16[768,384]{1,0:T(8,128)(2,1)S(1)}, u32[]{:S(2)}, u32[]{:S(2)}) %collective-permute-start.12) | collective-permute-done | bytes 589856 | tf_op jit(solution)/shard_map/ppermute | solution.py:237
  55.9 1.9 collective-permute-start.16
  57.8 1.9 collective-permute-start.6
  59.8 6.4 %collective-permute-start.4 = (bf16[768,384]{1,0:T(8,128)(2,1)S(1)}, bf16[768,384]{1,0:T(8,128)(2,1)}, u32[]{:S(2)}, u32[]{:S(2)}) collective-permute-start(bf16[768,384]{1,0:T(8,128)(2,1)S(1)} %collective-permute-done.3.refs_0_), channel_id=1, source_target_pairs={{0,2},{2,4},{4,6},{6,0},{1,3},{3,5},{5,7},{7,1},{8,10},{10,12},{12... | collective-permute-start | bytes 1769480 | tf_op jit(solution)/shard_map/ppermute | solution.py:237
  66.2 1.9 collective-permute-start.5
  68.2 1.9 collective-permute-start.17
  70.1 2.4 %collective-permute-start.7 = (bf16[768,384]{1,0:T(8,128)(2,1)S(1)}, bf16[768,384]{1,0:T(8,128)(2,1)}, u32[]{:S(2)}, u32[]{:S(2)}) collective-permute-start(bf16[768,384]{1,0:T(8,128)(2,1)S(1)} %collective-permute-done.3.refs_0_), channel_id=1, source_target_pairs={{0,1},{1,0},{2,3},{3,2},{4,5},{5,4},{6,7},{7,6},{8,9},{9,8},{10,11... | collective-permute-start | bytes 1769480 | tf_op jit(solution)/shard_map/ppermute | solution.py:233
  72.5 5.0 %collective-permute-done.6.refs_3_ = bf16[768,384]{1,0:T(8,128)(2,1)} collective-permute-done((bf16[768,384]{1,0:T(8,128)(2,1)S(1)}, bf16[768,384]{1,0:T(8,128)(2,1)}, u32[]{:S(2)}, u32[]{:S(2)}) %collective-permute-start.6) | collective-permute-done | bytes 589856 | tf_op jit(solution)/shard_map/ppermute | solution.py:237
  77.5 1.9 collective-permute-start.10
  79.4 10.3 %collective-permute-done.4.refs_1_ = bf16[768,384]{1,0:T(8,128)(2,1)} collective-permute-done((bf16[768,384]{1,0:T(8,128)(2,1)S(1)}, bf16[768,384]{1,0:T(8,128)(2,1)}, u32[]{:S(2)}, u32[]{:S(2)}) %collective-permute-start.4) | collective-permute-done | bytes 589856 | tf_op jit(solution)/shard_map/ppermute | solution.py:237
  89.7 2.0 collective-permute-start.8
  91.7 2.3 %collective-permute-start.9 = (bf16[768,384]{1,0:T(8,128)(2,1)}, bf16[768,384]{1,0:T(8,128)(2,1)}, u32[]{:S(2)}, u32[]{:S(2)}) collective-permute-start(bf16[768,384]{1,0:T(8,128)(2,1)} %collective-permute-done.5.refs_2_), channel_id=1, source_target_pairs={{0,1},{1,0},{2,3},{3,2},{4,5},{5,4},{6,7},{7,6},{8,9},{9,8},{10,11... | collective-permute-start | bytes 1769480 | tf_op jit(solution)/shard_map/ppermute | solution.py:233
  94.1 0.6 pad_add_fusion.place_ref
  94.7 2.0 broadcast_select_fusion
  96.7 0.8 copy-done.8
  97.6 11.0 %shard_map.102.refs_8_ = f32[3072,256]{1,0:T(8,128)} custom-call(s32[2]{0:T(128)} %pad_add_fusion.place_ref, bf16[768,256]{1,0:T(8,128)(2,1)} %get-tuple-element.21.attn_ref, bf16[768,384]{1,0:T(8,128)(2,1)} %refs_0_.3, bf16[768,384]{1,0:T(8,128)(2,1)} %copy-done.1, bf16[768,384]{1,0:T(8,128)(2,1)} %copy-done.2, bf16[768,384]{1,0:T(8,128)(2,1)} %copy-done.3, ...), custom_call_target="tpu_custom_call" | custom-call | flops 1207959552 | bytes 7864320 | tf_op jit(solution)/shard_map/pallas_call | solution.py:165
  108.6 12.2 %shard_map.103 = bf16[3072,256]{1,0:T(8,128)(2,1)} custom-call(s32[2]{0:T(128)} %pad_add_fusion.place_ref, bf16[768,256]{1,0:T(8,128)(2,1)} %get-tuple-element.22.attn_ref, bf16[768,384]{1,0:T(8,128)(2,1)} %copy-done.4, bf16[768,384]{1,0:T(8,128)(2,1)} %collective-permute-done.4.refs_1_, bf16[768,384]{1,0:T(8,128)(2,1)} %collective-permute-done.5.refs_2_, ...), custom_call_target="tpu_custom_call" | custom-call | flops 1207959552 | bytes 7864320 | tf_op jit(solution)/shard_map/pallas_call | solution.py:165
  120.8 6.6 %shard_map.104 = bf16[768,256]{1,0:T(8,128)(2,1)} custom-call(s32[2]{0:T(128)} %pad_add_fusion.place_ref, bf16[3072,256]{1,0:T(8,128)(2,1)} %all-gather.2.cloned.1.call-done.weight_ref, bf16[768,384]{1,0:T(8,128)(2,1)} %copy-done.4, bf16[768,384]{1,0:T(8,128)(2,1)} %collective-permute-done.4.refs_1_, bf16[768,384]{1,0:T(8,128)(2,1)} %collective-permute-done.5.refs_2_, ...), custom_call_target="tpu_custom_call" | custom-call | flops 1207959552 | bytes 6291456 | tf_op jit(solution)/shard_map/pallas_call | solution.py:199
  127.4 6.7 %shard_map.105.own_ref = bf16[768,256]{1,0:T(8,128)(2,1)} custom-call(s32[2]{0:T(128)} %pad_add_fusion.place_ref, bf16[3072,256]{1,0:T(8,128)(2,1)} %all-gather.2.cloned.1.call-done.weight_ref, bf16[768,384]{1,0:T(8,128)(2,1)} %refs_0_.3, bf16[768,384]{1,0:T(8,128)(2,1)} %copy-done.1, bf16[768,384]{1,0:T(8,128)(2,1)} %copy-done.2, ...), custom_call_target="tpu_custom_call" | custom-call | flops 1207959552 | bytes 6291456 | tf_op jit(solution)/shard_map/pallas_call | solution.py:199
  134.1 6.4 %collective-permute-start.20 = (bf16[768,256]{1,0:T(8,128)(2,1)}, bf16[768,256]{1,0:T(8,128)(2,1)S(1)}, u32[]{:S(2)}, u32[]{:S(2)}) collective-permute-start(bf16[768,256]{1,0:T(8,128)(2,1)} %shard_map.105.own_ref), channel_id=1, source_target_pairs={{8,0},{256,264},{9,1},{257,265},{10,2},{258,266},{11,3},{259,267},... | collective-permute-start | bytes 1179656 | tf_op jit(solution)/shard_map/ppermute | solution.py:225
  140.5 1.3 collective-permute-start.18
  141.8 3.5 %collective-permute-start.19 = (bf16[768,256]{1,0:T(8,128)(2,1)S(1)}, bf16[768,256]{1,0:T(8,128)(2,1)S(1)}, u32[]{:S(2)}, u32[]{:S(2)}) collective-permute-start(bf16[768,256]{1,0:T(8,128)(2,1)S(1)} %copy-done.12), channel_id=1, source_target_pairs={{8,256},{256,8},{9,257},{257,9},{10,258},{258,10},{11,259},{259,11... | collective-permute-start | bytes 1179656 | tf_op jit(solution)/shard_map/ppermute | solution.py:225
  145.3 4.1 %collective-permute-done.20.p3_ref = bf16[768,256]{1,0:T(8,128)(2,1)S(1)} collective-permute-done((bf16[768,256]{1,0:T(8,128)(2,1)}, bf16[768,256]{1,0:T(8,128)(2,1)S(1)}, u32[]{:S(2)}, u32[]{:S(2)}) %collective-permute-start.20) | collective-permute-done | bytes 393248 | tf_op jit(solution)/shard_map/ppermute | solution.py:225
  149.4 3.8 %collective-permute-done.18.p1_ref = bf16[768,256]{1,0:T(8,128)(2,1)S(1)} collective-permute-done((bf16[768,256]{1,0:T(8,128)(2,1)S(1)}, bf16[768,256]{1,0:T(8,128)(2,1)S(1)}, u32[]{:S(2)}, u32[]{:S(2)}) %collective-permute-start.18) | collective-permute-done | bytes 393248 | tf_op jit(solution)/shard_map/ppermute | solution.py:225
  153.2 1.3 collective-permute-done.19.p2_ref
  154.5 0.8 copy-done.11
  155.3 7.5 %shard_map.106 = (bf16[768,256]{1,0:T(8,128)(2,1)}, bf16[768,256]{1,0:T(8,128)(2,1)}, bf16[768,256]{1,0:T(8,128)(2,1)}, f32[2,128]{1,0:T(2,128)}) custom-call(s32[1]{0:T(128)} %bitcast.stays_ref, bf16[768,256]{1,0:T(8,128)(2,1)} %q_ref.3, bf16[768,256]{1,0:T(8,128)(2,1)} %k_ref.3, bf16[768,256]{1,0:T(8,128)(2,1)} %v_ref.3, ...), custom_call_target="tpu_custom_call" | custom-call | tf_op jit(solution)/shard_map/pallas_call | solution.py:103
  162.7 0.7 broadcast_in_dim.4
  163.4 12.2 %all_to_all.10 = f32[32,2,128]{2,1,0:T(2,128)S(1)} all-to-all(f32[32,2,128]{2,1,0:T(2,128)S(1)} %broadcast_in_dim.4), channel_id=1, replica_groups=mesh['yl'=2,'z'=16,'yh'=2,'x'=4,'c'=2] {'yl','yh','x','c'}, dimensions={0} | all-to-all | bytes 65536 | tf_op jit(solution)/shard_map/all_to_all | solution.py:246
  175.7 27.4 %all_to_all.11 = f32[16,2,128]{2,1,0:T(2,128)S(1)} all-to-all(f32[16,2,128]{2,1,0:T(2,128)S(1)} %broadcast_in_dim.5), channel_id=1, replica_groups=mesh['yl'=2,'z'=16,'yh'=2,'x'=4,'c'=2] {'z'}, dimensions={0} | all-to-all | bytes 32768 | tf_op jit(solution)/shard_map/all_to_all | solution.py:246
  203.1 0.6 reduce_sum.19
  203.7 2.5 %collective-permute-start.21 = (bf16[192,256]{1,0:T(8,128)(2,1)}, bf16[192,256]{1,0:T(8,128)(2,1)S(1)}, u32[]{:S(2)}, u32[]{:S(2)}) collective-permute-start(bf16[192,256]{1,0:T(8,128)(2,1)} %reduce-scatter.2.cloned.1.call-done), channel_id=1, source_target_pairs={{0,0},{8,256},{256,8},{264,264},{1,1},{9,257},{257,9},{265,265},{2... | collective-permute-start | bytes 294920 | tf_op jit(solution)/shard_map/ppermute | solution.py:225
  206.2 4.2 %collective-permute-done.21 = bf16[192,256]{1,0:T(8,128)(2,1)S(1)} collective-permute-done((bf16[192,256]{1,0:T(8,128)(2,1)}, bf16[192,256]{1,0:T(8,128)(2,1)S(1)}, u32[]{:S(2)}, u32[]{:S(2)}) %collective-permute-start.21) | collective-permute-done | bytes 98336 | tf_op jit(solution)/shard_map/ppermute | solution.py:225
  210.4 0.7 convert_element_type.4
  (45 shorter events, 0.2 us)
Async XLA Ops:
  7.2 18.1 %copy-start = (bf16[768,384]{1,0:T(8,128)(2,1)S(1)}, bf16[768,384]{1,0:T(8,128)(2,1)}, u32[]{:S(2)}) copy-start(bf16[768,384]{1,0:T(8,128)(2,1)} %refs_0_.3) | copy-start | bytes 1769476
  7.2 113.6 %all-gather.2.cloned.1.call-start = ((), (), s32[]{:S(2)}) async-start(), calls=%async_computation.3 | async-start | bytes 1671168 | tf_op jit(solution)/shard_map/all_gather | solution.py:254
  7.2 6.9 %collective-permute-start = (bf16[192,256]{1,0:T(8,128)(2,1)}, bf16[192,256]{1,0:T(8,128)(2,1)S(1)}, u32[]{:S(2)}, u32[]{:S(2)}) collective-permute-start(bf16[192,256]{1,0:T(8,128)(2,1)} %param.10), channel_id=1, source_target_pairs={{0,0},{8,256},{256,8},{264,264},{1,1},{9,257},{257,9},{265,265},{2... | collective-permute-start | bytes 294920 | tf_op jit(solution)/shard_map/ppermute | solution.py:225
  14.1 0.6 copy-start.13
  14.7 188.9 %reduce-scatter.2.cloned.1.call-start = ((), (), s32[]{:S(2)}) async-start(), calls=%async_computation.4 | async-start | bytes 1671168 | tf_op jit(solution)/shard_map/reduce_scatter | solution.py:265
  19.9 19.0 %collective-permute-start.1 = (bf16[768,256]{1,0:T(8,128)(2,1)}, bf16[768,256]{1,0:T(8,128)(2,1)}, u32[]{:S(2)}, u32[]{:S(2)}) collective-permute-start(bf16[768,256]{1,0:T(8,128)(2,1)} %shard_map.101), channel_id=1, source_target_pairs={{0,8},{8,264},{256,0},{264,256},{1,9},{9,265},{257,1},{265,257},{2... | collective-permute-start | bytes 1179656 | tf_op jit(solution)/shard_map/ppermute | solution.py:225
  22.4 20.2 %collective-permute-start.2 = (bf16[768,256]{1,0:T(8,128)(2,1)}, bf16[768,256]{1,0:T(8,128)(2,1)}, u32[]{:S(2)}, u32[]{:S(2)}) collective-permute-start(bf16[768,256]{1,0:T(8,128)(2,1)} %shard_map.101), channel_id=1, source_target_pairs={{0,0},{8,256},{256,8},{264,264},{1,1},{9,257},{257,9},{265,265},{2... | collective-permute-start | bytes 1179656 | tf_op jit(solution)/shard_map/ppermute | solution.py:225
  25.3 19.3 %collective-permute-start.11 = (bf16[768,384]{1,0:T(8,128)(2,1)S(1)}, bf16[768,384]{1,0:T(8,128)(2,1)S(1)}, u32[]{:S(2)}, u32[]{:S(2)}) collective-permute-start(bf16[768,384]{1,0:T(8,128)(2,1)S(1)} %copy-done), channel_id=1, source_target_pairs={{0,2},{2,4},{4,6},{6,0},{1,3},{3,5},{5,7},{7,1},{8,10},{10,12},{12... | collective-permute-start | bytes 1769480 | tf_op jit(solution)/shard_map/ppermute | solution.py:237
  28.7 27.2 %collective-permute-start.12 = (bf16[768,384]{1,0:T(8,128)(2,1)S(1)}, bf16[768,384]{1,0:T(8,128)(2,1)S(1)}, u32[]{:S(2)}, u32[]{:S(2)}) collective-permute-start(bf16[768,384]{1,0:T(8,128)(2,1)S(1)} %copy-done), channel_id=1, source_target_pairs={{0,6},{2,0},{4,2},{6,4},{1,7},{3,1},{5,3},{7,5},{8,14},{10,8},{12,... | collective-permute-start | bytes 1769480 | tf_op jit(solution)/shard_map/ppermute | solution.py:237
  32.4 25.4 %collective-permute-start.3 = (bf16[768,384]{1,0:T(8,128)(2,1)S(1)}, bf16[768,384]{1,0:T(8,128)(2,1)S(1)}, u32[]{:S(2)}, u32[]{:S(2)}) collective-permute-start(bf16[768,384]{1,0:T(8,128)(2,1)S(1)} %copy-done), channel_id=1, source_target_pairs={{0,256},{256,0},{1,257},{257,1},{2,258},{258,2},{3,259},{259,3},{4... | collective-permute-start | bytes 1769480 | tf_op jit(solution)/shard_map/ppermute | solution.py:229
  38.9 20.9 %collective-permute-start.13 = (bf16[768,384]{1,0:T(8,128)(2,1)S(1)}, bf16[768,384]{1,0:T(8,128)(2,1)S(1)}, u32[]{:S(2)}, u32[]{:S(2)}) collective-permute-start(bf16[768,384]{1,0:T(8,128)(2,1)S(1)} %copy-done), channel_id=1, source_target_pairs={{0,4},{2,6},{4,0},{6,2},{1,5},{3,7},{5,1},{7,3},{8,12},{10,14},{12... | collective-permute-start | bytes 1769480 | tf_op jit(solution)/shard_map/ppermute | solution.py:237
  42.6 23.6 %collective-permute-start.14 = (bf16[768,384]{1,0:T(8,128)(2,1)S(1)}, bf16[768,384]{1,0:T(8,128)(2,1)S(1)}, u32[]{:S(2)}, u32[]{:S(2)}) collective-permute-start(bf16[768,384]{1,0:T(8,128)(2,1)S(1)} %copy-done), channel_id=1, source_target_pairs={{0,1},{1,0},{2,3},{3,2},{4,5},{5,4},{6,7},{7,6},{8,9},{9,8},{10,11... | collective-permute-start | bytes 1769480 | tf_op jit(solution)/shard_map/ppermute | solution.py:233
  44.6 52.1 %copy-start.1 = (bf16[768,384]{1,0:T(8,128)(2,1)}, bf16[768,384]{1,0:T(8,128)(2,1)S(1)}, u32[]{:S(2)}) copy-start(bf16[768,384]{1,0:T(8,128)(2,1)S(1)} %collective-permute-done.11.refs_1_) | copy-start | bytes 1769476
  44.6 23.6 %collective-permute-start.15 = (bf16[768,384]{1,0:T(8,128)(2,1)S(1)}, bf16[768,384]{1,0:T(8,128)(2,1)S(1)}, u32[]{:S(2)}, u32[]{:S(2)}) collective-permute-start(bf16[768,384]{1,0:T(8,128)(2,1)S(1)} %collective-permute-done.11.refs_1_), channel_id=1, source_target_pairs={{0,1},{1,0},{2,3},{3,2},{4,5},{5,4},{6,7},{7,6},{8,9},{9,8},{10,11... | collective-permute-start | bytes 1769480 | tf_op jit(solution)/shard_map/ppermute | solution.py:233
  55.9 40.8 %copy-start.2 = (bf16[768,384]{1,0:T(8,128)(2,1)}, bf16[768,384]{1,0:T(8,128)(2,1)S(1)}, u32[]{:S(2)}) copy-start(bf16[768,384]{1,0:T(8,128)(2,1)S(1)} %collective-permute-done.12.refs_2_) | copy-start | bytes 1769476
  55.9 14.2 %collective-permute-start.16 = (bf16[768,384]{1,0:T(8,128)(2,1)S(1)}, bf16[768,384]{1,0:T(8,128)(2,1)S(1)}, u32[]{:S(2)}, u32[]{:S(2)}) collective-permute-start(bf16[768,384]{1,0:T(8,128)(2,1)S(1)} %collective-permute-done.12.refs_2_), channel_id=1, source_target_pairs={{0,1},{1,0},{2,3},{3,2},{4,5},{5,4},{6,7},{7,6},{8,9},{9,8},{10,11... | collective-permute-start | bytes 1769480 | tf_op jit(solution)/shard_map/ppermute | solution.py:233
  57.8 50.7 %copy-start.4 = (bf16[768,384]{1,0:T(8,128)(2,1)}, bf16[768,384]{1,0:T(8,128)(2,1)S(1)}, u32[]{:S(2)}) copy-start(bf16[768,384]{1,0:T(8,128)(2,1)S(1)} %collective-permute-done.3.refs_0_) | copy-start | bytes 1769476
  57.8 19.7 %collective-permute-start.6 = (bf16[768,384]{1,0:T(8,128)(2,1)S(1)}, bf16[768,384]{1,0:T(8,128)(2,1)}, u32[]{:S(2)}, u32[]{:S(2)}) collective-permute-start(bf16[768,384]{1,0:T(8,128)(2,1)S(1)} %collective-permute-done.3.refs_0_), channel_id=1, source_target_pairs={{0,4},{2,6},{4,0},{6,2},{1,5},{3,7},{5,1},{7,3},{8,12},{10,14},{12... | collective-permute-start | bytes 1769480 | tf_op jit(solution)/shard_map/ppermute | solution.py:237
  59.8 37.0 %copy-start.3 = (bf16[768,384]{1,0:T(8,128)(2,1)}, bf16[768,384]{1,0:T(8,128)(2,1)S(1)}, u32[]{:S(2)}) copy-start(bf16[768,384]{1,0:T(8,128)(2,1)S(1)} %collective-permute-done.13.refs_3_) | copy-start | bytes 1769476
  59.8 29.9 %collective-permute-start.4 = (bf16[768,384]{1,0:T(8,128)(2,1)S(1)}, bf16[768,384]{1,0:T(8,128)(2,1)}, u32[]{:S(2)}, u32[]{:S(2)}) collective-permute-start(bf16[768,384]{1,0:T(8,128)(2,1)S(1)} %collective-permute-done.3.refs_0_), channel_id=1, source_target_pairs={{0,2},{2,4},{4,6},{6,0},{1,3},{3,5},{5,7},{7,1},{8,10},{10,12},{12... | collective-permute-start | bytes 1769480 | tf_op jit(solution)/shard_map/ppermute | solution.py:237
  66.2 30.5 %copy-start.5 = (bf16[768,384]{1,0:T(8,128)(2,1)}, bf16[768,384]{1,0:T(8,128)(2,1)S(1)}, u32[]{:S(2)}) copy-start(bf16[768,384]{1,0:T(8,128)(2,1)S(1)} %collective-permute-done.14.refs_4_) | copy-start | bytes 1769476
  66.2 25.5 %collective-permute-start.5 = (bf16[768,384]{1,0:T(8,128)(2,1)S(1)}, bf16[768,384]{1,0:T(8,128)(2,1)}, u32[]{:S(2)}, u32[]{:S(2)}) collective-permute-start(bf16[768,384]{1,0:T(8,128)(2,1)S(1)} %collective-permute-done.3.refs_0_), channel_id=1, source_target_pairs={{0,6},{2,0},{4,2},{6,4},{1,7},{3,1},{5,3},{7,5},{8,14},{10,8},{12,... | collective-permute-start | bytes 1769480 | tf_op jit(solution)/shard_map/ppermute | solution.py:237
  68.2 23.6 %copy-start.6 = (bf16[768,384]{1,0:T(8,128)(2,1)}, bf16[768,384]{1,0:T(8,128)(2,1)S(1)}, u32[]{:S(2)}) copy-start(bf16[768,384]{1,0:T(8,128)(2,1)S(1)} %collective-permute-done.15.refs_5_) | copy-start | bytes 1769476
  68.2 28.5 %collective-permute-start.17 = (bf16[768,384]{1,0:T(8,128)(2,1)S(1)}, bf16[768,384]{1,0:T(8,128)(2,1)S(1)}, u32[]{:S(2)}, u32[]{:S(2)}) collective-permute-start(bf16[768,384]{1,0:T(8,128)(2,1)S(1)} %collective-permute-done.13.refs_3_), channel_id=1, source_target_pairs={{0,1},{1,0},{2,3},{3,2},{4,5},{5,4},{6,7},{7,6},{8,9},{9,8},{10,11... | collective-permute-start | bytes 1769480 | tf_op jit(solution)/shard_map/ppermute | solution.py:233
  70.1 23.9 %copy-start.7 = (bf16[768,384]{1,0:T(8,128)(2,1)}, bf16[768,384]{1,0:T(8,128)(2,1)S(1)}, u32[]{:S(2)}) copy-start(bf16[768,384]{1,0:T(8,128)(2,1)S(1)} %collective-permute-done.16.refs_6_) | copy-start | bytes 1769476
  70.1 38.4 %collective-permute-start.7 = (bf16[768,384]{1,0:T(8,128)(2,1)S(1)}, bf16[768,384]{1,0:T(8,128)(2,1)}, u32[]{:S(2)}, u32[]{:S(2)}) collective-permute-start(bf16[768,384]{1,0:T(8,128)(2,1)S(1)} %collective-permute-done.3.refs_0_), channel_id=1, source_target_pairs={{0,1},{1,0},{2,3},{3,2},{4,5},{5,4},{6,7},{7,6},{8,9},{9,8},{10,11... | collective-permute-start | bytes 1769480 | tf_op jit(solution)/shard_map/ppermute | solution.py:233
  77.5 31.1 %collective-permute-start.10 = (bf16[768,384]{1,0:T(8,128)(2,1)}, bf16[768,384]{1,0:T(8,128)(2,1)}, u32[]{:S(2)}, u32[]{:S(2)}) collective-permute-start(bf16[768,384]{1,0:T(8,128)(2,1)} %collective-permute-done.6.refs_3_), channel_id=1, source_target_pairs={{0,1},{1,0},{2,3},{3,2},{4,5},{5,4},{6,7},{7,6},{8,9},{9,8},{10,11... | collective-permute-start | bytes 1769480 | tf_op jit(solution)/shard_map/ppermute | solution.py:233
  89.7 18.9 %collective-permute-start.8 = (bf16[768,384]{1,0:T(8,128)(2,1)}, bf16[768,384]{1,0:T(8,128)(2,1)}, u32[]{:S(2)}, u32[]{:S(2)}) collective-permute-start(bf16[768,384]{1,0:T(8,128)(2,1)} %collective-permute-done.4.refs_1_), channel_id=1, source_target_pairs={{0,1},{1,0},{2,3},{3,2},{4,5},{5,4},{6,7},{7,6},{8,9},{9,8},{10,11... | collective-permute-start | bytes 1769480 | tf_op jit(solution)/shard_map/ppermute | solution.py:233
  91.7 16.9 %collective-permute-start.9 = (bf16[768,384]{1,0:T(8,128)(2,1)}, bf16[768,384]{1,0:T(8,128)(2,1)}, u32[]{:S(2)}, u32[]{:S(2)}) collective-permute-start(bf16[768,384]{1,0:T(8,128)(2,1)} %collective-permute-done.5.refs_2_), channel_id=1, source_target_pairs={{0,1},{1,0},{2,3},{3,2},{4,5},{5,4},{6,7},{7,6},{8,9},{9,8},{10,11... | collective-permute-start | bytes 1769480 | tf_op jit(solution)/shard_map/ppermute | solution.py:233
  96.7 0.9 copy-start.8
  127.4 13.1 %copy-start.12 = (bf16[768,256]{1,0:T(8,128)(2,1)S(1)}, bf16[768,256]{1,0:T(8,128)(2,1)}, u32[]{:S(2)}) copy-start(bf16[768,256]{1,0:T(8,128)(2,1)} %shard_map.104) | copy-start | bytes 1179652
  134.1 15.3 %collective-permute-start.20 = (bf16[768,256]{1,0:T(8,128)(2,1)}, bf16[768,256]{1,0:T(8,128)(2,1)S(1)}, u32[]{:S(2)}, u32[]{:S(2)}) collective-permute-start(bf16[768,256]{1,0:T(8,128)(2,1)} %shard_map.105.own_ref), channel_id=1, source_target_pairs={{8,0},{256,264},{9,1},{257,265},{10,2},{258,266},{11,3},{259,267},... | collective-permute-start | bytes 1179656 | tf_op jit(solution)/shard_map/ppermute | solution.py:225
  140.5 12.7 %collective-permute-start.18 = (bf16[768,256]{1,0:T(8,128)(2,1)S(1)}, bf16[768,256]{1,0:T(8,128)(2,1)S(1)}, u32[]{:S(2)}, u32[]{:S(2)}) collective-permute-start(bf16[768,256]{1,0:T(8,128)(2,1)S(1)} %copy-done.12), channel_id=1, source_target_pairs={{0,256},{264,8},{1,257},{265,9},{2,258},{266,10},{3,259},{267,11},... | collective-permute-start | bytes 1179656 | tf_op jit(solution)/shard_map/ppermute | solution.py:225
  141.8 12.7 %collective-permute-start.19 = (bf16[768,256]{1,0:T(8,128)(2,1)S(1)}, bf16[768,256]{1,0:T(8,128)(2,1)S(1)}, u32[]{:S(2)}, u32[]{:S(2)}) collective-permute-start(bf16[768,256]{1,0:T(8,128)(2,1)S(1)} %copy-done.12), channel_id=1, source_target_pairs={{8,256},{256,8},{9,257},{257,9},{10,258},{258,10},{11,259},{259,11... | collective-permute-start | bytes 1179656 | tf_op jit(solution)/shard_map/ppermute | solution.py:225
  149.4 5.1 %copy-start.9 = (bf16[768,256]{1,0:T(8,128)(2,1)}, bf16[768,256]{1,0:T(8,128)(2,1)S(1)}, u32[]{:S(2)}) copy-start(bf16[768,256]{1,0:T(8,128)(2,1)S(1)} %collective-permute-done.20.p3_ref) | copy-start | bytes 1179652
  153.2 1.3 copy-start.10
  154.5 0.8 copy-start.11
  203.7 6.7 %collective-permute-start.21 = (bf16[192,256]{1,0:T(8,128)(2,1)}, bf16[192,256]{1,0:T(8,128)(2,1)S(1)}, u32[]{:S(2)}, u32[]{:S(2)}) collective-permute-start(bf16[192,256]{1,0:T(8,128)(2,1)} %reduce-scatter.2.cloned.1.call-done), channel_id=1, source_target_pairs={{0,0},{8,256},{256,8},{264,264},{1,1},{9,257},{257,9},{265,265},{2... | collective-permute-start | bytes 294920 | tf_op jit(solution)/shard_map/ppermute | solution.py:225
Sparse Core Ops, SparseCore 0:
  14.9 76.7 all-gather.1
  120.9 76.5 reduce-scatter.1

commit v10 on v5

--- a/solution.py
+++ b/solution.py
@@ -9,9 +9,9 @@
 PATCH = 256
 EPSILON = 1e-06
 SCALE = HD ** (-0.5)
-AXES = ("yl", "za", "zb", "yh", "x", "c")
-SIZES = (2, 4, 4, 2, 4, 2)
-Z = ("za", "zb")
+AXES = ("yl", "za", "zm", "zl", "yh", "x", "c")
+SIZES = (2, 4, 2, 2, 2, 4, 2)
+Z = ("za", "zm", "zl")
 VMEM_LIMIT = 56 * 1024 * 1024
 
 
@@ -109,85 +109,89 @@
     )(queries_raw, keys_raw, values, part_one, part_two, norm_gains)
 
 
-def weight_kernel(high_ref, grad_ref, same_ref, other_ref, wgrad_ref):
-    high = high_ref[0]
-    width = grad_ref.shape[4]
+def weight_kernel(place_ref, grad_ref, same_ref, other_ref, keep_ref, give_ref):
+    high, parity = place_ref[0], place_ref[1]
+    rows = keep_ref.shape[1]
     for core in range(2):
         term = product(grad_ref[high, 0, core], same_ref[...], 0, 0)
         term += product(grad_ref[1 - high, 0, core], other_ref[...], 0, 0)
-        wgrad_ref[core * width : (core + 1) * width] = term.astype(wgrad_ref.dtype)
-
-
-def grad_block(grads):
-    return pl.BlockSpec((2, 1) + grads.shape[2:], lambda x, high: (0, x, 0, 0, 0))
-
-
-def weight_product(high, grads, attn_same, attn_other):
+        term = term.astype(keep_ref.dtype)
+        even, odd = term[:rows], term[rows:]
+        keep_ref[core] = jnp.where(parity == 0, even, odd)
+        give_ref[core] = jnp.where(parity == 0, odd, even)
+
+
+def weight_product(place, grads, attn_same, attn_other):
     _, blocks, cores, tokens, width = grads.shape
     heads = attn_same.shape[1]
-    attn = pl.BlockSpec((tokens, heads), lambda x, high: (0, 0))
+    attn = pl.BlockSpec((tokens, heads), lambda x, place: (0, 0))
+    slab = pl.BlockSpec((cores, width // 2, heads), lambda x, place: (x, 0, 0))
+    out = jax.ShapeDtypeStruct((blocks * cores, width // 2, heads), jnp.bfloat16)
     return pl.pallas_call(
         weight_kernel,
         grid_spec=pltpu.PrefetchScalarGridSpec(
             num_scalar_prefetch=1,
             grid=(blocks,),
-            in_specs=[grad_block(grads), attn, attn],
-            out_specs=pl.BlockSpec((cores * width, heads), lambda x, high: (x, 0)),
-        ),
-        out_shape=jax.ShapeDtypeStruct((blocks * cores * width, heads), jnp.bfloat16),
+            in_specs=[
+                pl.BlockSpec((2, 1) + grads.shape[2:], lambda x, place: (0, x, 0, 0, 0)),
+                attn,
+                attn,
+            ],
+            out_specs=[slab, slab],
+        ),
+        out_shape=[out, out],
         compiler_params=pltpu.CompilerParams(vmem_limit_bytes=VMEM_LIMIT),
         cost_estimate=pl.CostEstimate(
             flops=2 * grads.size * heads,
             bytes_accessed=2 * (grads.size + blocks * cores * width * heads),
             transcendentals=0,
         ),
-    )(high, grads, attn_same, attn_other)
-
-
-def token_kernel(high_ref, grad_ref, weight_ref, same_ref, other_ref, total):
+    )(place, grads, attn_same, attn_other)
+
+
+def token_kernel(low_ref, grad_ref, weight_ref, part_ref, total):
     step = pl.program_id(0)
-    high = high_ref[0]
     weights = weight_ref[...].reshape(-1, weight_ref.shape[3])
     width = grad_ref.shape[4]
+    term = product(grad_ref[0, 0, 0], weights[:width], 1, 0)
+    term += product(grad_ref[0, 0, 1], weights[width:], 1, 0)
 
     @pl.when(step == 0)
     def _():
-        total[...] = jnp.zeros_like(total)
-
-    for index, low in enumerate((high, 1 - high)):
-        term = product(grad_ref[low, 0, 0], weights[:width], 1, 0)
-        total[index] += term + product(grad_ref[low, 0, 1], weights[width:], 1, 0)
+        total[...] = term
+
+    @pl.when(step > 0)
+    def _():
+        total[...] += term
 
     @pl.when(step == pl.num_programs(0) - 1)
     def _():
-        same_ref[...] = total[0].astype(same_ref.dtype)
-        other_ref[...] = total[1].astype(other_ref.dtype)
-
-
-def token_product(high, grads, weights):
+        part_ref[...] = total[...].astype(part_ref.dtype)
+
+
+def token_product(low, grads, weights):
     _, blocks, _, tokens, _ = grads.shape
     fours, _, rows, heads = weights.shape
-    out = jax.ShapeDtypeStruct((tokens, heads), jnp.bfloat16)
     return pl.pallas_call(
         token_kernel,
         grid_spec=pltpu.PrefetchScalarGridSpec(
             num_scalar_prefetch=1,
             grid=(blocks,),
             in_specs=[
-                grad_block(grads),
-                pl.BlockSpec((fours, 1, rows, heads), lambda x, high: (0, x, 0, 0)),
+                pl.BlockSpec((1, 1) + grads.shape[2:], lambda x, low: (low[0], x, 0, 0, 0)),
+                pl.BlockSpec((fours, 1, rows, heads), lambda x, low: (0, x, 0, 0)),
             ],
-            out_specs=[pl.BlockSpec((tokens, heads), lambda x, high: (0, 0))] * 2,
-            scratch_shapes=[pltpu.VMEM((2, tokens, heads), jnp.float32)],
-        ),
-        out_shape=[out, out],
+            out_specs=pl.BlockSpec((tokens, heads), lambda x, low: (0, 0)),
+            scratch_shapes=[pltpu.VMEM((tokens, heads), jnp.float32)],
+        ),
+        out_shape=jax.ShapeDtypeStruct((tokens, heads), jnp.bfloat16),
         compiler_params=pltpu.CompilerParams(vmem_limit_bytes=VMEM_LIMIT),
         cost_estimate=pl.CostEstimate(
-            flops=2 * grads.size * heads,
-            bytes_accessed=2 * (grads.size + weights.size),
+            flops=grads.size * heads,
+            bytes_accessed=grads.size + 2 * weights.size,
             transcendentals=0,
         ),
-    )(high, grads, weights)
+    )(low, grads, weights)
 
 
 def swap_y(array, target):
@@ -213,8 +217,13 @@
     after = along(column, -1)
     far = jnp.concatenate([along(column[:2], 2), along(column[2:], -2)])
     blocks = [column, after, far, before]
-    shift = (4 - lax.axis_index("zb")) % 4
+    shift = (4 - lax.axis_index(("zm", "zl"))) % 4
     return lax.dynamic_slice_in_dim(jnp.stack(blocks + blocks), shift, 4, axis=0)
+
+
+def pair_terms(give):
+    half = give.shape[0] // 2
+    return along(give[:half], 1), along(give[half:], -1)
 
 
 def sum_over(array, axis, count):
@@ -223,7 +232,8 @@
 
 
 def per_device(queries_raw, keys_raw, values, grad_out, out_weight, norm_gains):
-    high = lax.axis_index("yh").reshape(1)
+    high = lax.axis_index("yh").astype(jnp.int32).reshape(1)
+    place = jnp.concatenate([high, lax.axis_index("zl").astype(jnp.int32).reshape(1)])
     grads = lax.all_gather(grad_out, ("yl", "x", "c"), axis=0)
     grads = grads.reshape((2, 4, 2) + grad_out.shape)
 
@@ -233,13 +243,20 @@
     weights = gather_rows(turned(out_weight))
     grads, weights = lax.optimization_barrier((grads, weights))
 
-    wgrad = weight_product(high, grads, attn_same, attn_other)
-    shard = lax.psum_scatter(wgrad, Z, scatter_dimension=0, tiled=True)
-
-    weights, _ = lax.optimization_barrier((weights, wgrad))
-    part_same, part_other = token_product(high, grads, weights)
+    keep, give = weight_product(place, grads, attn_same, attn_other)
+    before, after = pair_terms(give)
+    weights, _ = lax.optimization_barrier((weights, give))
+    part_other = token_product(1 - high, grads, weights)
+
+    before, after, part_other = lax.optimization_barrier((before, after, part_other))
+    came = jnp.concatenate([before, after]).astype(jnp.float32)
+    column = (keep.astype(jnp.float32) + came).astype(keep.dtype)
+    shard = lax.psum_scatter(column, ("za", "zm"), scatter_dimension=0)
+
+    weights, _ = lax.optimization_barrier((weights, column))
+    part_same = token_product(high, grads, weights)
+    came_other = swap_y(part_other, lambda low, up: (1 - up, low))
     came_same = turned(part_same)
-    came_other = swap_y(part_other, lambda low, up: (1 - up, low))
     queries_grad, keys_grad, values_grad, terms = backward(
         queries_raw, keys_raw, values, came_same, came_other, norm_gains
     )
@@ -251,7 +268,7 @@
 
 def solution(mesh):
     fine = Mesh(mesh.devices.reshape(SIZES), AXES)
-    spec = P(("yl", "za", "zb"), ("yh", "x", "c"))
+    spec = P(("yl", "za", "zm", "zl"), ("yh", "x", "c"))
     return jax.shard_map(
         per_device,
         mesh=fine,

time: 183 us -> 192 us (1.049)
  starting transfers between devices: 32.3 us -> 44.6 us
  waiting for transfers between devices: 37.6 us -> 30.9 us
  blocking collectives: 66.1 us -> 61.5 us
  Pallas kernels: 27.2 us -> 31.4 us
    ppermute x4 -> x6, starting transfers between devices: 13.8 us -> 26.8 us  [along(): return lax.ppermute(array, Z, [(z, (z + step) % 16) for z in range(16)])]
    all_gather x1, waiting for transfers between devices: 11.1 us -> 6.21 us  [per_device(): grads = lax.all_gather(grad_out, ('yl', 'x', 'c'), axis=0)]
    ppermute x4 -> x6, waiting for transfers between devices: 5.69 us -> 9.56 us  [along(): return lax.ppermute(array, Z, [(z, (z + step) % 16) for z in range(16)])]
    pallas_call x1 -> x2, Pallas kernels: 7.69 us -> 11.2 us  [token_product(): pl.pallas_call(token_kernel, grid_spec=pltpu.PrefetchScalarGridSpec(num_s...]
    ppermute x6, waiting for transfers between devices: 17.9 us -> 14.4 us  [swap_y(): return lax.ppermute(array, ('yl', 'yh'), pairs)]
    all_gather x1, blocking collectives: 29 us -> 26.5 us  [gather_rows(): column = lax.all_gather(own_rows, 'za', axis=0)]
    reduce_scatter x1, waiting for transfers between devices: 2.29 us -> 0.01 us  [per_device(): shard = lax.psum_scatter(column, ('za', 'zm'), scatter_dimension=0)]
    all_to_all x2, blocking collectives: 37.1 us -> 34.9 us  [sum_over(): lax.all_to_all(jnp.broadcast_to(array[None], (count,) + array.shape), axi...]
  transfers between devices with their start and end apart: 12 -> 14, of which waited for: 9 -> 7; matrix products, arithmetic and copies ran while one was open for 2% -> 2% of each run, Pallas kernels for 11% -> 12%
where the time goes in v10:
time: 192 us; the launch traced here: 191 us
  blocking collectives  61.5 us (32%)
  starting transfers between devices  44.6 us (23%)
  Pallas kernels  31.4 us (16%)
  waiting for transfers between devices  30.9 us (16%)
  between operations  14.3 us (7%)
  local copies, waits for them, and re-layouts  5.55 us (3%)
  other arithmetic  3.02 us (2%)
    all_to_all x2, blocking collectives, sum_over(): lax.all_to_all(jnp.broadcast_to(array[None], (count,) + array.shape), axi...  34.9 us
    ppermute x6, starting transfers between devices, along(): return lax.ppermute(array, Z, [(z, (z + step) % 16) for z in range(16)])  26.8 us
    all_gather x1, blocking collectives, gather_rows(): column = lax.all_gather(own_rows, 'za', axis=0)  26.5 us
    ppermute x6, starting transfers between devices, swap_y(): return lax.ppermute(array, ('yl', 'yh'), pairs)  17.7 us
    ppermute x6, waiting for transfers between devices, swap_y(): return lax.ppermute(array, ('yl', 'yh'), pairs)  14.4 us
    pallas_call x2, Pallas kernels, token_product(): pl.pallas_call(token_kernel, grid_spec=pltpu.PrefetchScalarGridSpec(num_s...  11.2 us
    ppermute x6, waiting for transfers between devices, along(): return lax.ppermute(array, Z, [(z, (z + step) % 16) for z in range(16)])  9.56 us
    pallas_call x1, Pallas kernels, weight_product(): pl.pallas_call(weight_kernel, grid_spec=pltpu.PrefetchScalarGridSpec(num_...  7.8 us
  transfers between devices with their start and end apart: 14, of which 7 were waited for; matrix products, arithmetic and copies ran while one was open for 2% of the time, Pallas kernels for 12%

profile of v10, /device:TPU:8, one launch (start us, length us, event | category | flops | bytes accessed | tf_op | source)
XLA Modules:
  0.0 191.2 jit_solution(17922330789467388399)
XLA Ops:
  7.2 0.0 all-gather.4.cloned.1.call-start
  7.2 0.7 all-gather.4.cloned.1.call-update
  7.9 0.0 reduce-scatter.2.cloned.1.call-start
  7.9 3.5 %collective-permute-start = (bf16[192,256]{1,0:T(8,128)(2,1)}, bf16[192,256]{1,0:T(8,128)(2,1)S(1)}, u32[]{:S(2)}, u32[]{:S(2)}) collective-permute-start(bf16[192,256]{1,0:T(8,128)(2,1)} %param.10), channel_id=1, source_target_pairs={{0,0},{8,256},{256,8},{264,264},{1,1},{9,257},{257,9},{265,265},{2... | collective-permute-start | bytes 294920 | tf_op jit(solution)/shard_map/ppermute | solution.py:203
  11.4 5.1 %shard_map.101 = bf16[768,256]{1,0:T(8,128)(2,1)} custom-call(bf16[768,256]{1,0:T(8,128)(2,1)} %q_ref.3, bf16[768,256]{1,0:T(8,128)(2,1)} %k_ref.3, bf16[768,256]{1,0:T(8,128)(2,1)} %v_ref.3, f32[2,128]{1,0:T(2,128)} %gains_ref.3), custom_call_target="tpu_custom_call" | custom-call | tf_op jit(solution)/shard_map/pallas_call | solution.py:56
  16.5 2.3 %collective-permute-start.5 = (bf16[768,256]{1,0:T(8,128)(2,1)}, bf16[768,256]{1,0:T(8,128)(2,1)S(1)}, u32[]{:S(2)}, u32[]{:S(2)}) collective-permute-start(bf16[768,256]{1,0:T(8,128)(2,1)} %shard_map.101), channel_id=1, source_target_pairs={{0,0},{8,256},{256,8},{264,264},{1,1},{9,257},{257,9},{265,265},{2... | collective-permute-start | bytes 1179656 | tf_op jit(solution)/shard_map/ppermute | solution.py:203
  18.9 5.1 %collective-permute-start.6 = (bf16[768,256]{1,0:T(8,128)(2,1)}, bf16[768,256]{1,0:T(8,128)(2,1)S(1)}, u32[]{:S(2)}, u32[]{:S(2)}) collective-permute-start(bf16[768,256]{1,0:T(8,128)(2,1)} %shard_map.101), channel_id=1, source_target_pairs={{0,8},{8,264},{256,0},{264,256},{1,9},{9,265},{257,1},{265,257},{2... | collective-permute-start | bytes 1179656 | tf_op jit(solution)/shard_map/ppermute | solution.py:203
  23.9 0.0 collective-permute-done
  23.9 26.5 %all-gather.1 = bf16[768,256]{1,0:T(8,128)(2,1)S(1)} all-gather(bf16[192,256]{1,0:T(8,128)(2,1)S(1)} %collective-permute-done), channel_id=3, replica_groups=mesh['yl'=2,'za'=4,'zm'=2,'zl'=2,'yh'=2,'x'=4,'c'=2] {'za'}, dimensions={0}, use_global_device_ids=true | all-gather | bytes 491520 | tf_op jit(solution)/shard_map/all_gather | solution.py:215
  50.5 2.9 %collective-permute-start.1 = (bf16[4,192,256]{2,1,0:T(8,128)(2,1)S(1)}, bf16[4,192,256]{2,1,0:T(8,128)(2,1)S(1)}, u32[]{:S(2)}, u32[]{:S(2)}) collective-permute-start(bf16[4,192,256]{2,1,0:T(8,128)(2,1)S(1)} %bitcast.23), channel_id=1, source_target_pairs={{0,240},{16,0},{32,16},{48,32},{64,48},{80,64},{96,80},{112,96},{1... | collective-permute-start | bytes 1179656 | tf_op jit(solution)/shard_map/ppermute | solution.py:211
  53.4 0.6 pad_add_fusion.place_ref
  54.0 3.0 %collective-permute-start.4 = (bf16[4,192,256]{2,1,0:T(8,128)(2,1)S(1)}, bf16[4,192,256]{2,1,0:T(8,128)(2,1)S(1)}, u32[]{:S(2)}, u32[]{:S(2)}) collective-permute-start(bf16[4,192,256]{2,1,0:T(8,128)(2,1)S(1)} %bitcast.24), channel_id=1, source_target_pairs={{0,16},{16,32},{32,48},{48,64},{64,80},{80,96},{96,112},{112,128},... | collective-permute-start | bytes 1179656 | tf_op jit(solution)/shard_map/ppermute | solution.py:211
  57.1 3.7 %collective-permute-start.2 = (bf16[2,192,256]{2,1,0:T(8,128)(2,1)S(1)}, bf16[2,192,256]{2,1,0:T(8,128)(2,1)S(1)}, u32[]{:S(2)}, u32[]{:S(2)}) collective-permute-start(bf16[2,192,256]{2,1,0:T(8,128)(2,1)S(1)} %bitcast.28), channel_id=1, source_target_pairs={{0,32},{16,48},{32,64},{48,80},{64,96},{80,112},{96,128},{112,144}... | collective-permute-start | bytes 589832 | tf_op jit(solution)/shard_map/ppermute | solution.py:211
  60.8 0.0 collective-permute-done.1
  60.8 4.3 %collective-permute-start.3 = (bf16[2,192,256]{2,1,0:T(8,128)(2,1)S(1)}, bf16[2,192,256]{2,1,0:T(8,128)(2,1)S(1)}, u32[]{:S(2)}, u32[]{:S(2)}) collective-permute-start(bf16[2,192,256]{2,1,0:T(8,128)(2,1)S(1)} %bitcast.27), channel_id=1, source_target_pairs={{0,224},{16,240},{32,0},{48,16},{64,32},{80,48},{96,64},{112,80},{... | collective-permute-start | bytes 589832 | tf_op jit(solution)/shard_map/ppermute | solution.py:211
  65.1 6.4 %collective-permute-done.2 = bf16[2,192,256]{2,1,0:T(8,128)(2,1)S(1)} collective-permute-done((bf16[2,192,256]{2,1,0:T(8,128)(2,1)S(1)}, bf16[2,192,256]{2,1,0:T(8,128)(2,1)S(1)}, u32[]{:S(2)}, u32[]{:S(2)}) %collective-permute-start.2) | collective-permute-done | bytes 196640 | tf_op jit(solution)/shard_map/ppermute | solution.py:211
  71.6 0.0 collective-permute-done.3
  71.6 0.0 collective-permute-done.4
  71.8 1.3 constant_dynamic-slice_fusion.weight_ref
  73.0 6.2 %all-gather.4.cloned.1.call-done = bf16[12288,384]{1,0:T(8,128)(2,1)} async-done(((bf16[768,384]{1,0:T(8,128)(2,1)}), bf16[12288,384]{1,0:T(8,128)(2,1)}) %all-gather.4.cloned.1.call-update) | async-done | bytes 9437200 | tf_op jit(solution)/shard_map/all_gather | solution.py:237
  79.3 0.0 collective-permute-done.5.same_ref
  79.3 0.0 collective-permute-done.6.other_ref
  79.3 0.7 copy-done.1
  80.0 0.7 copy-done.2
  80.8 7.8 %shard_map.102 = (bf16[8,192,256]{2,1,0:T(8,128)(2,1)}, bf16[8,192,256]{2,1,0:T(8,128)(2,1)}) custom-call(s32[2]{0:T(128)} %pad_add_fusion.place_ref, bf16[2,4,2,768,384]{4,3,2,1,0:T(8,128)(2,1)} %bitcast.20, bf16[768,256]{1,0:T(8,128)(2,1)} %copy-done.1, bf16[768,256]{1,0:T(8,128)(2,1)} %copy-done.2), custom_call_target="tpu_custom_call" | custom-call | flops 2415919104 | bytes 11010048 | tf_op jit(solution)/shard_map/pallas_call | solution.py:130
  88.5 1.2 fusion.2
  89.7 3.5 %collective-permute-start.7 = (bf16[4,192,256]{2,1,0:T(8,128)(2,1)S(1)}, bf16[4,192,256]{2,1,0:T(8,128)(2,1)S(1)}, u32[]{:S(2)}, u32[]{:S(2)}) collective-permute-start(bf16[4,192,256]{2,1,0:T(8,128)(2,1)S(1)} %get-tuple-element.36), channel_id=1, source_target_pairs={{0,16},{16,32},{32,48},{48,64},{64,80},{80,96},{96,112},{112,128},... | collective-permute-start | bytes 1179656 | tf_op jit(solution)/shard_map/ppermute | solution.py:211
  93.2 9.4 %collective-permute-start.8 = (bf16[4,192,256]{2,1,0:T(8,128)(2,1)S(1)}, bf16[4,192,256]{2,1,0:T(8,128)(2,1)S(1)}, u32[]{:S(2)}, u32[]{:S(2)}) collective-permute-start(bf16[4,192,256]{2,1,0:T(8,128)(2,1)S(1)} %get-tuple-element.35), channel_id=1, source_target_pairs={{0,240},{16,0},{32,16},{48,32},{64,48},{80,64},{96,80},{112,96},{1... | collective-permute-start | bytes 1179656 | tf_op jit(solution)/shard_map/ppermute | solution.py:211
  102.6 5.6 %shard_map.103 = bf16[768,256]{1,0:T(8,128)(2,1)} custom-call(s32[1]{0:T(128)S(6)} %sub.7.low_ref, bf16[2,4,2,768,384]{4,3,2,1,0:T(8,128)(2,1)} %bitcast.21, bf16[4,4,192,256]{3,2,1,0:T(8,128)(2,1)} %constant_dynamic-slice_fusion.weight_ref), custom_call_target="tpu_custom_call" | custom-call | flops 1207959552 | bytes 6291456 | tf_op jit(solution)/shard_map/pallas_call | solution.py:175
  108.2 2.0 %collective-permute-done.7 = bf16[4,192,256]{2,1,0:T(8,128)(2,1)S(1)} collective-permute-done((bf16[4,192,256]{2,1,0:T(8,128)(2,1)S(1)}, bf16[4,192,256]{2,1,0:T(8,128)(2,1)S(1)}, u32[]{:S(2)}, u32[]{:S(2)}) %collective-permute-start.7) | collective-permute-done | bytes 393248 | tf_op jit(solution)/shard_map/ppermute | solution.py:211
  110.2 1.2 collective-permute-done.8
  111.4 1.1 add_convert_fusion
  112.4 0.0 reduce-scatter.2.cloned.1.call-update
  112.5 0.0 copy-start.3
  112.5 5.6 %shard_map.104 = bf16[768,256]{1,0:T(8,128)(2,1)} custom-call(s32[1]{0:T(128)} %bitcast.low_ref, bf16[2,4,2,768,384]{4,3,2,1,0:T(8,128)(2,1)} %bitcast.22, bf16[4,4,192,256]{3,2,1,0:T(8,128)(2,1)} %constant_dynamic-slice_fusion.weight_ref), custom_call_target="tpu_custom_call" | custom-call | flops 1207959552 | bytes 6291456 | tf_op jit(solution)/shard_map/pallas_call | solution.py:175
  118.1 2.5 %collective-permute-start.9 = (bf16[768,256]{1,0:T(8,128)(2,1)}, bf16[768,256]{1,0:T(8,128)(2,1)S(1)}, u32[]{:S(2)}, u32[]{:S(2)}) collective-permute-start(bf16[768,256]{1,0:T(8,128)(2,1)} %shard_map.104), channel_id=1, source_target_pairs={{0,0},{8,256},{256,8},{264,264},{1,1},{9,257},{257,9},{265,265},{2... | collective-permute-start | bytes 1179656 | tf_op jit(solution)/shard_map/ppermute | solution.py:203
  120.5 1.9 %collective-permute-start.10 = (bf16[768,256]{1,0:T(8,128)(2,1)S(1)}, bf16[768,256]{1,0:T(8,128)(2,1)S(1)}, u32[]{:S(2)}, u32[]{:S(2)}) collective-permute-start(bf16[768,256]{1,0:T(8,128)(2,1)S(1)} %copy-done.3), channel_id=1, source_target_pairs={{0,256},{8,0},{256,264},{264,8},{1,257},{9,1},{257,265},{265,9},{2... | collective-permute-start | bytes 1179656 | tf_op jit(solution)/shard_map/ppermute | solution.py:203
  122.5 8.1 %collective-permute-done.9.one_ref = bf16[768,256]{1,0:T(8,128)(2,1)S(1)} collective-permute-done((bf16[768,256]{1,0:T(8,128)(2,1)}, bf16[768,256]{1,0:T(8,128)(2,1)S(1)}, u32[]{:S(2)}, u32[]{:S(2)}) %collective-permute-start.9) | collective-permute-done | bytes 393248 | tf_op jit(solution)/shard_map/ppermute | solution.py:203
  130.6 2.0 %collective-permute-done.10.two_ref = bf16[768,256]{1,0:T(8,128)(2,1)S(1)} collective-permute-done((bf16[768,256]{1,0:T(8,128)(2,1)S(1)}, bf16[768,256]{1,0:T(8,128)(2,1)S(1)}, u32[]{:S(2)}, u32[]{:S(2)}) %collective-permute-start.10) | collective-permute-done | bytes 393248 | tf_op jit(solution)/shard_map/ppermute | solution.py:203
  132.6 0.7 copy-done.5
  133.3 7.4 %shard_map.105 = (bf16[768,256]{1,0:T(8,128)(2,1)}, bf16[768,256]{1,0:T(8,128)(2,1)}, bf16[768,256]{1,0:T(8,128)(2,1)}, f32[2,128]{1,0:T(2,128)}) custom-call(bf16[768,256]{1,0:T(8,128)(2,1)} %q_ref.3, bf16[768,256]{1,0:T(8,128)(2,1)} %k_ref.3, bf16[768,256]{1,0:T(8,128)(2,1)} %v_ref.3, bf16[768,256]{1,0:T(8,128)(2,1)} %copy-done.4, ...), custom_call_target="tpu_custom_call" | custom-call | tf_op jit(solution)/shard_map/pallas_call | solution.py:102
  140.7 0.7 broadcast_in_dim.4
  141.4 13.3 %all_to_all.10 = f32[32,2,128]{2,1,0:T(2,128)S(1)} all-to-all(f32[32,2,128]{2,1,0:T(2,128)S(1)} %broadcast_in_dim.4), channel_id=1, replica_groups=mesh['yl'=2,'za'=4,'zm'=2,'zl'=2,'yh'=2,'x'=4,'c'=2] {'yl','yh','x','c'}, dimensions={0} | all-to-all | bytes 65536 | tf_op jit(solution)/shard_map/all_to_all | solution.py:230
  154.8 21.6 %all_to_all.11 = f32[16,2,128]{2,1,0:T(2,128)S(1)} all-to-all(f32[16,2,128]{2,1,0:T(2,128)S(1)} %broadcast_in_dim.5), channel_id=1, replica_groups=mesh['yl'=2,'za'=4,'zm'=2,'zl'=2,'yh'=2,'x'=4,'c'=2] {'za','zm','zl'}, dimensions={0} | all-to-all | bytes 32768 | tf_op jit(solution)/shard_map/all_to_all | solution.py:230
  176.4 0.6 reduce_sum.19
  177.0 2.4 %collective-permute-start.11 = (bf16[192,256]{1,0:T(8,128)(2,1)}, bf16[192,256]{1,0:T(8,128)(2,1)S(1)}, u32[]{:S(2)}, u32[]{:S(2)}) collective-permute-start(bf16[192,256]{1,0:T(8,128)(2,1)} %bitcast.29), channel_id=1, source_target_pairs={{0,0},{8,256},{256,8},{264,264},{1,1},{9,257},{257,9},{265,265},{2... | collective-permute-start | bytes 294920 | tf_op jit(solution)/shard_map/ppermute | solution.py:203
  179.5 4.3 %collective-permute-done.11 = bf16[192,256]{1,0:T(8,128)(2,1)S(1)} collective-permute-done((bf16[192,256]{1,0:T(8,128)(2,1)}, bf16[192,256]{1,0:T(8,128)(2,1)S(1)}, u32[]{:S(2)}, u32[]{:S(2)}) %collective-permute-start.11) | collective-permute-done | bytes 98336 | tf_op jit(solution)/shard_map/ppermute | solution.py:203
  183.7 0.7 convert_element_type.15
  (20 shorter events, 0.3 us)
Async XLA Ops:
  7.2 72.1 %all-gather.4.cloned.1.call-start = ((), (), s32[]{:S(2)}) async-start(), calls=%async_computation.4 | async-start | bytes 10027008 | tf_op jit(solution)/shard_map/all_gather | solution.py:237
  7.9 169.1 %reduce-scatter.2.cloned.1.call-start = ((), (), s32[]{:S(2)}) async-start(), calls=%async_computation.3 | async-start | bytes 884736 | tf_op jit(solution)/shard_map/reduce_scatter | solution.py:254
  7.9 16.0 %collective-permute-start = (bf16[192,256]{1,0:T(8,128)(2,1)}, bf16[192,256]{1,0:T(8,128)(2,1)S(1)}, u32[]{:S(2)}, u32[]{:S(2)}) collective-permute-start(bf16[192,256]{1,0:T(8,128)(2,1)} %param.10), channel_id=1, source_target_pairs={{0,0},{8,256},{256,8},{264,264},{1,1},{9,257},{257,9},{265,265},{2... | collective-permute-start | bytes 294920 | tf_op jit(solution)/shard_map/ppermute | solution.py:203
  16.5 62.7 %collective-permute-start.5 = (bf16[768,256]{1,0:T(8,128)(2,1)}, bf16[768,256]{1,0:T(8,128)(2,1)S(1)}, u32[]{:S(2)}, u32[]{:S(2)}) collective-permute-start(bf16[768,256]{1,0:T(8,128)(2,1)} %shard_map.101), channel_id=1, source_target_pairs={{0,0},{8,256},{256,8},{264,264},{1,1},{9,257},{257,9},{265,265},{2... | collective-permute-start | bytes 1179656 | tf_op jit(solution)/shard_map/ppermute | solution.py:203
  18.9 60.4 %collective-permute-start.6 = (bf16[768,256]{1,0:T(8,128)(2,1)}, bf16[768,256]{1,0:T(8,128)(2,1)S(1)}, u32[]{:S(2)}, u32[]{:S(2)}) collective-permute-start(bf16[768,256]{1,0:T(8,128)(2,1)} %shard_map.101), channel_id=1, source_target_pairs={{0,8},{8,264},{256,0},{264,256},{1,9},{9,265},{257,1},{265,257},{2... | collective-permute-start | bytes 1179656 | tf_op jit(solution)/shard_map/ppermute | solution.py:203
  50.5 10.3 %collective-permute-start.1 = (bf16[4,192,256]{2,1,0:T(8,128)(2,1)S(1)}, bf16[4,192,256]{2,1,0:T(8,128)(2,1)S(1)}, u32[]{:S(2)}, u32[]{:S(2)}) collective-permute-start(bf16[4,192,256]{2,1,0:T(8,128)(2,1)S(1)} %bitcast.23), channel_id=1, source_target_pairs={{0,240},{16,0},{32,16},{48,32},{64,48},{80,64},{96,80},{112,96},{1... | collective-permute-start | bytes 1179656 | tf_op jit(solution)/shard_map/ppermute | solution.py:211
  54.0 17.6 %collective-permute-start.4 = (bf16[4,192,256]{2,1,0:T(8,128)(2,1)S(1)}, bf16[4,192,256]{2,1,0:T(8,128)(2,1)S(1)}, u32[]{:S(2)}, u32[]{:S(2)}) collective-permute-start(bf16[4,192,256]{2,1,0:T(8,128)(2,1)S(1)} %bitcast.24), channel_id=1, source_target_pairs={{0,16},{16,32},{32,48},{48,64},{64,80},{80,96},{96,112},{112,128},... | collective-permute-start | bytes 1179656 | tf_op jit(solution)/shard_map/ppermute | solution.py:211
  57.1 14.4 %collective-permute-start.2 = (bf16[2,192,256]{2,1,0:T(8,128)(2,1)S(1)}, bf16[2,192,256]{2,1,0:T(8,128)(2,1)S(1)}, u32[]{:S(2)}, u32[]{:S(2)}) collective-permute-start(bf16[2,192,256]{2,1,0:T(8,128)(2,1)S(1)} %bitcast.28), channel_id=1, source_target_pairs={{0,32},{16,48},{32,64},{48,80},{64,96},{80,112},{96,128},{112,144}... | collective-permute-start | bytes 589832 | tf_op jit(solution)/shard_map/ppermute | solution.py:211
  60.8 10.8 %collective-permute-start.3 = (bf16[2,192,256]{2,1,0:T(8,128)(2,1)S(1)}, bf16[2,192,256]{2,1,0:T(8,128)(2,1)S(1)}, u32[]{:S(2)}, u32[]{:S(2)}) collective-permute-start(bf16[2,192,256]{2,1,0:T(8,128)(2,1)S(1)} %bitcast.27), channel_id=1, source_target_pairs={{0,224},{16,240},{32,0},{48,16},{64,32},{80,48},{96,64},{112,80},{... | collective-permute-start | bytes 589832 | tf_op jit(solution)/shard_map/ppermute | solution.py:211
  79.3 0.7 copy-start.1
  80.0 0.7 copy-start.2
  89.7 20.5 %collective-permute-start.7 = (bf16[4,192,256]{2,1,0:T(8,128)(2,1)S(1)}, bf16[4,192,256]{2,1,0:T(8,128)(2,1)S(1)}, u32[]{:S(2)}, u32[]{:S(2)}) collective-permute-start(bf16[4,192,256]{2,1,0:T(8,128)(2,1)S(1)} %get-tuple-element.36), channel_id=1, source_target_pairs={{0,16},{16,32},{32,48},{48,64},{64,80},{80,96},{96,112},{112,128},... | collective-permute-start | bytes 1179656 | tf_op jit(solution)/shard_map/ppermute | solution.py:211
  93.2 18.2 %collective-permute-start.8 = (bf16[4,192,256]{2,1,0:T(8,128)(2,1)S(1)}, bf16[4,192,256]{2,1,0:T(8,128)(2,1)S(1)}, u32[]{:S(2)}, u32[]{:S(2)}) collective-permute-start(bf16[4,192,256]{2,1,0:T(8,128)(2,1)S(1)} %get-tuple-element.35), channel_id=1, source_target_pairs={{0,240},{16,0},{32,16},{48,32},{64,48},{80,64},{96,80},{112,96},{1... | collective-permute-start | bytes 1179656 | tf_op jit(solution)/shard_map/ppermute | solution.py:211
  102.6 8.8 %copy-start = (bf16[8,192,256]{2,1,0:T(8,128)(2,1)S(1)}, bf16[8,192,256]{2,1,0:T(8,128)(2,1)}, u32[]{:S(2)}) copy-start(bf16[8,192,256]{2,1,0:T(8,128)(2,1)} %get-tuple-element.24) | copy-start | bytes 2359300
  112.5 8.1 %copy-start.3 = (bf16[768,256]{1,0:T(8,128)(2,1)S(1)}, bf16[768,256]{1,0:T(8,128)(2,1)}, u32[]{:S(2)}) copy-start(bf16[768,256]{1,0:T(8,128)(2,1)} %shard_map.103) | copy-start | bytes 1179652
  118.1 12.5 %collective-permute-start.9 = (bf16[768,256]{1,0:T(8,128)(2,1)}, bf16[768,256]{1,0:T(8,128)(2,1)S(1)}, u32[]{:S(2)}, u32[]{:S(2)}) collective-permute-start(bf16[768,256]{1,0:T(8,128)(2,1)} %shard_map.104), channel_id=1, source_target_pairs={{0,0},{8,256},{256,8},{264,264},{1,1},{9,257},{257,9},{265,265},{2... | collective-permute-start | bytes 1179656 | tf_op jit(solution)/shard_map/ppermute | solution.py:203
  120.5 12.1 %collective-permute-start.10 = (bf16[768,256]{1,0:T(8,128)(2,1)S(1)}, bf16[768,256]{1,0:T(8,128)(2,1)S(1)}, u32[]{:S(2)}, u32[]{:S(2)}) collective-permute-start(bf16[768,256]{1,0:T(8,128)(2,1)S(1)} %copy-done.3), channel_id=1, source_target_pairs={{0,256},{8,0},{256,264},{264,8},{1,257},{9,1},{257,265},{265,9},{2... | collective-permute-start | bytes 1179656 | tf_op jit(solution)/shard_map/ppermute | solution.py:203
  130.6 2.0 %copy-start.4 = (bf16[768,256]{1,0:T(8,128)(2,1)}, bf16[768,256]{1,0:T(8,128)(2,1)S(1)}, u32[]{:S(2)}) copy-start(bf16[768,256]{1,0:T(8,128)(2,1)S(1)} %collective-permute-done.9.one_ref) | copy-start | bytes 1179652
  132.6 0.7 copy-start.5
  177.0 6.7 %collective-permute-start.11 = (bf16[192,256]{1,0:T(8,128)(2,1)}, bf16[192,256]{1,0:T(8,128)(2,1)S(1)}, u32[]{:S(2)}, u32[]{:S(2)}) collective-permute-start(bf16[192,256]{1,0:T(8,128)(2,1)} %bitcast.29), channel_id=1, source_target_pairs={{0,0},{8,256},{256,8},{264,264},{1,1},{9,257},{257,9},{265,265},{2... | collective-permute-start | bytes 294920 | tf_op jit(solution)/shard_map/ppermute | solution.py:203
Sparse Core Ops, SparseCore 0:
  10.1 69.0 all-gather.3
  112.6 48.0 reduce-scatter.1

commit v11 on v5

--- a/solution.py
+++ b/solution.py
@@ -230,7 +230,8 @@
     attn = forward(queries_raw, keys_raw, values, norm_gains)
     attn_same = turned(attn)
     attn_other = swap_y(attn, lambda low, up: (up, 1 - low))
-    weights = gather_rows(turned(out_weight))
+    own_rows, _ = lax.optimization_barrier((turned(out_weight), attn))
+    weights = gather_rows(own_rows)
     grads, weights = lax.optimization_barrier((grads, weights))
 
     wgrad = weight_product(high, grads, attn_same, attn_other)

time: 183 us -> 184 us (level)
  the two profiles are of different devices: /device:TPU:8 before, /device:TPU:10 now
where the time goes in v11:
time: 184 us; the launch traced here: 183 us
  blocking collectives  69.2 us (38%)
  waiting for transfers between devices  37.4 us (20%)
  starting transfers between devices  29.6 us (16%)
  Pallas kernels  27.2 us (15%)
  between operations  14.2 us (8%)
  local copies, waits for them, and re-layouts  3.81 us (2%)
    all_to_all x2, blocking collectives, sum_over(): lax.all_to_all(jnp.broadcast_to(array[None], (count,) + array.shape), axi...  39.3 us
    all_gather x1, blocking collectives, gather_rows(): column = lax.all_gather(own_rows, 'za', axis=0)  30 us
    ppermute x6, starting transfers between devices, swap_y(): return lax.ppermute(array, ('yl', 'yh'), pairs)  15.9 us
    ppermute x6, waiting for transfers between devices, swap_y(): return lax.ppermute(array, ('yl', 'yh'), pairs)  14.7 us
    ppermute x4, starting transfers between devices, along(): return lax.ppermute(array, Z, [(z, (z + step) % 16) for z in range(16)])  13.6 us
    all_gather x1, waiting for transfers between devices, per_device(): grads = lax.all_gather(grad_out, ('yl', 'x', 'c'), axis=0)  12.9 us
    pallas_call x1, Pallas kernels, token_product(): pl.pallas_call(token_kernel, grid_spec=pltpu.PrefetchScalarGridSpec(num_s...  7.68 us
    pallas_call x1, Pallas kernels, backward(): pl.pallas_call(backward_kernel, grid=(tokens // PATCH,), in_specs=[block]...  7.37 us
  transfers between devices with their start and end apart: 12, of which 6 were waited for; matrix products, arithmetic and copies ran while one was open for 2% of the time, Pallas kernels for 11%

profile of v11, /device:TPU:10, one launch (start us, length us, event | category | flops | bytes accessed | tf_op | source)
XLA Modules:
  0.0 182.8 jit_solution(4842685233546424652)
XLA Ops:
  7.2 0.0 all-gather.4.cloned.1.call-start
  7.2 0.7 all-gather.4.cloned.1.call-update
  7.9 0.0 reduce-scatter.2.cloned.1.call-start
  7.9 3.5 %collective-permute-start = (bf16[192,256]{1,0:T(8,128)(2,1)}, bf16[192,256]{1,0:T(8,128)(2,1)S(1)}, u32[]{:S(2)}, u32[]{:S(2)}) collective-permute-start(bf16[192,256]{1,0:T(8,128)(2,1)} %param.10), channel_id=1, source_target_pairs={{0,0},{8,256},{256,8},{264,264},{1,1},{9,257},{257,9},{265,265},{2... | collective-permute-start | bytes 294920 | tf_op jit(solution)/shard_map/ppermute | solution.py:199
  11.4 5.1 %shard_map.101 = bf16[768,256]{1,0:T(8,128)(2,1)} custom-call(bf16[768,256]{1,0:T(8,128)(2,1)} %q_ref.3, bf16[768,256]{1,0:T(8,128)(2,1)} %k_ref.3, bf16[768,256]{1,0:T(8,128)(2,1)} %v_ref.3, f32[2,128]{1,0:T(2,128)} %gains_ref.3), custom_call_target="tpu_custom_call" | custom-call | tf_op jit(solution)/shard_map/pallas_call | solution.py:56
  16.5 0.0 collective-permute-done
  16.5 30.0 %all-gather.1 = bf16[768,256]{1,0:T(8,128)(2,1)S(1)} all-gather(bf16[192,256]{1,0:T(8,128)(2,1)S(1)} %collective-permute-done), channel_id=3, replica_groups=mesh['yl'=2,'za'=4,'zb'=4,'yh'=2,'x'=4,'c'=2] {'za'}, dimensions={0}, use_global_device_ids=true | all-gather | bytes 491520 | tf_op jit(solution)/shard_map/all_gather | solution.py:211
  46.5 2.9 %collective-permute-start.1 = (bf16[4,192,256]{2,1,0:T(8,128)(2,1)S(1)}, bf16[4,192,256]{2,1,0:T(8,128)(2,1)S(1)}, u32[]{:S(2)}, u32[]{:S(2)}) collective-permute-start(bf16[4,192,256]{2,1,0:T(8,128)(2,1)S(1)} %bitcast.20), channel_id=1, source_target_pairs={{0,240},{16,0},{32,16},{48,32},{64,48},{80,64},{96,80},{112,96},{1... | collective-permute-start | bytes 1179656 | tf_op jit(solution)/shard_map/ppermute | solution.py:207
  49.4 2.4 %collective-permute-start.5 = (bf16[768,256]{1,0:T(8,128)(2,1)}, bf16[768,256]{1,0:T(8,128)(2,1)S(1)}, u32[]{:S(2)}, u32[]{:S(2)}) collective-permute-start(bf16[768,256]{1,0:T(8,128)(2,1)} %shard_map.101), channel_id=1, source_target_pairs={{0,0},{8,256},{256,8},{264,264},{1,1},{9,257},{257,9},{265,265},{2... | collective-permute-start | bytes 1179656 | tf_op jit(solution)/shard_map/ppermute | solution.py:199
  51.8 1.9 %collective-permute-start.6 = (bf16[768,256]{1,0:T(8,128)(2,1)}, bf16[768,256]{1,0:T(8,128)(2,1)S(1)}, u32[]{:S(2)}, u32[]{:S(2)}) collective-permute-start(bf16[768,256]{1,0:T(8,128)(2,1)} %shard_map.101), channel_id=1, source_target_pairs={{0,8},{8,264},{256,0},{264,256},{1,9},{9,265},{257,1},{265,257},{2... | collective-permute-start | bytes 1179656 | tf_op jit(solution)/shard_map/ppermute | solution.py:199
  53.7 2.8 %collective-permute-start.4 = (bf16[4,192,256]{2,1,0:T(8,128)(2,1)S(1)}, bf16[4,192,256]{2,1,0:T(8,128)(2,1)S(1)}, u32[]{:S(2)}, u32[]{:S(2)}) collective-permute-start(bf16[4,192,256]{2,1,0:T(8,128)(2,1)S(1)} %bitcast.21), channel_id=1, source_target_pairs={{0,16},{16,32},{32,48},{48,64},{64,80},{80,96},{96,112},{112,128},... | collective-permute-start | bytes 1179656 | tf_op jit(solution)/shard_map/ppermute | solution.py:207
  56.6 3.1 %collective-permute-start.2 = (bf16[2,192,256]{2,1,0:T(8,128)(2,1)S(1)}, bf16[2,192,256]{2,1,0:T(8,128)(2,1)S(1)}, u32[]{:S(2)}, u32[]{:S(2)}) collective-permute-start(bf16[2,192,256]{2,1,0:T(8,128)(2,1)S(1)} %bitcast.25), channel_id=1, source_target_pairs={{0,32},{16,48},{32,64},{48,80},{64,96},{80,112},{96,128},{112,144}... | collective-permute-start | bytes 589832 | tf_op jit(solution)/shard_map/ppermute | solution.py:207
  59.7 0.0 collective-permute-done.1
  59.7 4.9 %collective-permute-start.3 = (bf16[2,192,256]{2,1,0:T(8,128)(2,1)S(1)}, bf16[2,192,256]{2,1,0:T(8,128)(2,1)S(1)}, u32[]{:S(2)}, u32[]{:S(2)}) collective-permute-start(bf16[2,192,256]{2,1,0:T(8,128)(2,1)S(1)} %bitcast.24), channel_id=1, source_target_pairs={{0,224},{16,240},{32,0},{48,16},{64,32},{80,48},{96,64},{112,80},{... | collective-permute-start | bytes 589832 | tf_op jit(solution)/shard_map/ppermute | solution.py:207
  64.6 5.9 %collective-permute-done.2 = bf16[2,192,256]{2,1,0:T(8,128)(2,1)S(1)} collective-permute-done((bf16[2,192,256]{2,1,0:T(8,128)(2,1)S(1)}, bf16[2,192,256]{2,1,0:T(8,128)(2,1)S(1)}, u32[]{:S(2)}, u32[]{:S(2)}) %collective-permute-start.2) | collective-permute-done | bytes 196640 | tf_op jit(solution)/shard_map/ppermute | solution.py:207
  70.5 0.0 collective-permute-done.3
  70.6 0.0 collective-permute-done.4
  70.8 1.3 constant_dynamic-slice_fusion.weight_ref
  72.0 12.9 %all-gather.4.cloned.1.call-done = bf16[12288,384]{1,0:T(8,128)(2,1)} async-done(((bf16[768,384]{1,0:T(8,128)(2,1)}), bf16[12288,384]{1,0:T(8,128)(2,1)}) %all-gather.4.cloned.1.call-update) | async-done | bytes 9437200 | tf_op jit(solution)/shard_map/all_gather | solution.py:227
  84.9 0.0 collective-permute-done.5.same_ref
  84.9 0.0 copy-start
  84.9 0.0 collective-permute-done.6.other_ref
  85.0 0.0 copy-start.1
  85.0 0.7 copy-done
  85.7 0.1 copy-done.1
  85.8 7.1 %shard_map.102 = bf16[3072,256]{1,0:T(8,128)(2,1)} custom-call(s32[1]{0:T(128)} %bitcast.high_ref, bf16[2,4,2,768,384]{4,3,2,1,0:T(8,128)(2,1)} %bitcast.18, bf16[768,256]{1,0:T(8,128)(2,1)} %copy-done, bf16[768,256]{1,0:T(8,128)(2,1)} %copy-done.1), custom_call_target="tpu_custom_call" | custom-call | flops 2415919104 | bytes 11010048 | tf_op jit(solution)/shard_map/pallas_call | solution.py:129
  92.9 0.0 reduce-scatter.2.cloned.1.call-update
  92.9 7.7 %shard_map.103 = (bf16[768,256]{1,0:T(8,128)(2,1)}, bf16[768,256]{1,0:T(8,128)(2,1)}) custom-call(s32[1]{0:T(128)} %bitcast.high_ref, bf16[2,4,2,768,384]{4,3,2,1,0:T(8,128)(2,1)} %bitcast.19, bf16[4,4,192,256]{3,2,1,0:T(8,128)(2,1)} %constant_dynamic-slice_fusion.weight_ref), custom_call_target="tpu_custom_call" | custom-call | flops 2415919104 | bytes 11010048 | tf_op jit(solution)/shard_map/pallas_call | solution.py:171
  100.6 3.0 %collective-permute-start.7 = (bf16[768,256]{1,0:T(8,128)(2,1)}, bf16[768,256]{1,0:T(8,128)(2,1)S(1)}, u32[]{:S(2)}, u32[]{:S(2)}) collective-permute-start(bf16[768,256]{1,0:T(8,128)(2,1)} %get-tuple-element.21), channel_id=1, source_target_pairs={{0,0},{8,256},{256,8},{264,264},{1,1},{9,257},{257,9},{265,265},{2... | collective-permute-start | bytes 1179656 | tf_op jit(solution)/shard_map/ppermute | solution.py:199
  103.6 1.9 %collective-permute-start.8 = (bf16[768,256]{1,0:T(8,128)(2,1)}, bf16[768,256]{1,0:T(8,128)(2,1)S(1)}, u32[]{:S(2)}, u32[]{:S(2)}) collective-permute-start(bf16[768,256]{1,0:T(8,128)(2,1)} %get-tuple-element.22), channel_id=1, source_target_pairs={{0,256},{8,0},{256,264},{264,8},{1,257},{9,1},{257,265},{265,9},{2... | collective-permute-start | bytes 1179656 | tf_op jit(solution)/shard_map/ppermute | solution.py:199
  105.5 8.4 %collective-permute-done.7.one_ref = bf16[768,256]{1,0:T(8,128)(2,1)S(1)} collective-permute-done((bf16[768,256]{1,0:T(8,128)(2,1)}, bf16[768,256]{1,0:T(8,128)(2,1)S(1)}, u32[]{:S(2)}, u32[]{:S(2)}) %collective-permute-start.7) | collective-permute-done | bytes 393248 | tf_op jit(solution)/shard_map/ppermute | solution.py:199
  114.0 0.0 copy-start.2
  114.0 2.7 %collective-permute-done.8.two_ref = bf16[768,256]{1,0:T(8,128)(2,1)S(1)} collective-permute-done((bf16[768,256]{1,0:T(8,128)(2,1)}, bf16[768,256]{1,0:T(8,128)(2,1)S(1)}, u32[]{:S(2)}, u32[]{:S(2)}) %collective-permute-start.8) | collective-permute-done | bytes 393248 | tf_op jit(solution)/shard_map/ppermute | solution.py:199
  116.7 0.0 copy-done.2
  116.7 0.0 copy-start.3
  116.7 0.8 copy-done.3
  117.4 7.4 %shard_map.104 = (bf16[768,256]{1,0:T(8,128)(2,1)}, bf16[768,256]{1,0:T(8,128)(2,1)}, bf16[768,256]{1,0:T(8,128)(2,1)}, f32[2,128]{1,0:T(2,128)}) custom-call(bf16[768,256]{1,0:T(8,128)(2,1)} %q_ref.3, bf16[768,256]{1,0:T(8,128)(2,1)} %k_ref.3, bf16[768,256]{1,0:T(8,128)(2,1)} %v_ref.3, bf16[768,256]{1,0:T(8,128)(2,1)} %copy-done.2, ...), custom_call_target="tpu_custom_call" | custom-call | tf_op jit(solution)/shard_map/pallas_call | solution.py:102
  124.8 0.7 broadcast_in_dim.4
  125.5 14.6 %all_to_all.10 = f32[32,2,128]{2,1,0:T(2,128)S(1)} all-to-all(f32[32,2,128]{2,1,0:T(2,128)S(1)} %broadcast_in_dim.4), channel_id=1, replica_groups=mesh['yl'=2,'za'=4,'zb'=4,'yh'=2,'x'=4,'c'=2] {'yl','yh','x','c'}, dimensions={0} | all-to-all | bytes 65536 | tf_op jit(solution)/shard_map/all_to_all | solution.py:221
  140.1 24.7 %all_to_all.11 = f32[16,2,128]{2,1,0:T(2,128)S(1)} all-to-all(f32[16,2,128]{2,1,0:T(2,128)S(1)} %broadcast_in_dim.5), channel_id=1, replica_groups=mesh['yl'=2,'za'=4,'zb'=4,'yh'=2,'x'=4,'c'=2] {'za','zb'}, dimensions={0} | all-to-all | bytes 32768 | tf_op jit(solution)/shard_map/all_to_all | solution.py:221
  164.8 0.6 reduce_sum.19
  165.4 3.2 %reduce-scatter.2.cloned.1.call-done = bf16[192,256]{1,0:T(8,128)(2,1)} async-done(((bf16[3072,256]{1,0:T(8,128)(2,1)}), bf16[192,256]{1,0:T(8,128)(2,1)}) %reduce-scatter.2.cloned.1.call-update) | async-done | bytes 98320 | tf_op jit(solution)/shard_map/reduce_scatter | solution.py:238
  168.6 3.2 %collective-permute-start.9 = (bf16[192,256]{1,0:T(8,128)(2,1)}, bf16[192,256]{1,0:T(8,128)(2,1)S(1)}, u32[]{:S(2)}, u32[]{:S(2)}) collective-permute-start(bf16[192,256]{1,0:T(8,128)(2,1)} %reduce-scatter.2.cloned.1.call-done), channel_id=1, source_target_pairs={{0,0},{8,256},{256,8},{264,264},{1,1},{9,257},{257,9},{265,265},{2... | collective-permute-start | bytes 294920 | tf_op jit(solution)/shard_map/ppermute | solution.py:199
  171.8 3.5 %collective-permute-done.9 = bf16[192,256]{1,0:T(8,128)(2,1)S(1)} collective-permute-done((bf16[192,256]{1,0:T(8,128)(2,1)}, bf16[192,256]{1,0:T(8,128)(2,1)S(1)}, u32[]{:S(2)}, u32[]{:S(2)}) %collective-permute-start.9) | collective-permute-done | bytes 98336 | tf_op jit(solution)/shard_map/ppermute | solution.py:199
  175.3 0.7 convert_element_type.3
  (11 shorter events, 0.3 us)
Async XLA Ops:
  7.2 77.8 %all-gather.4.cloned.1.call-start = ((), (), s32[]{:S(2)}) async-start(), calls=%async_computation.4 | async-start | bytes 10027008 | tf_op jit(solution)/shard_map/all_gather | solution.py:227
  7.9 160.7 %reduce-scatter.2.cloned.1.call-start = ((), (), s32[]{:S(2)}) async-start(), calls=%async_computation.3 | async-start | bytes 1671168 | tf_op jit(solution)/shard_map/reduce_scatter | solution.py:238
  7.9 8.6 %collective-permute-start = (bf16[192,256]{1,0:T(8,128)(2,1)}, bf16[192,256]{1,0:T(8,128)(2,1)S(1)}, u32[]{:S(2)}, u32[]{:S(2)}) collective-permute-start(bf16[192,256]{1,0:T(8,128)(2,1)} %param.10), channel_id=1, source_target_pairs={{0,0},{8,256},{256,8},{264,264},{1,1},{9,257},{257,9},{265,265},{2... | collective-permute-start | bytes 294920 | tf_op jit(solution)/shard_map/ppermute | solution.py:199
  46.5 13.2 %collective-permute-start.1 = (bf16[4,192,256]{2,1,0:T(8,128)(2,1)S(1)}, bf16[4,192,256]{2,1,0:T(8,128)(2,1)S(1)}, u32[]{:S(2)}, u32[]{:S(2)}) collective-permute-start(bf16[4,192,256]{2,1,0:T(8,128)(2,1)S(1)} %bitcast.20), channel_id=1, source_target_pairs={{0,240},{16,0},{32,16},{48,32},{64,48},{80,64},{96,80},{112,96},{1... | collective-permute-start | bytes 1179656 | tf_op jit(solution)/shard_map/ppermute | solution.py:207
  49.4 35.6 %collective-permute-start.5 = (bf16[768,256]{1,0:T(8,128)(2,1)}, bf16[768,256]{1,0:T(8,128)(2,1)S(1)}, u32[]{:S(2)}, u32[]{:S(2)}) collective-permute-start(bf16[768,256]{1,0:T(8,128)(2,1)} %shard_map.101), channel_id=1, source_target_pairs={{0,0},{8,256},{256,8},{264,264},{1,1},{9,257},{257,9},{265,265},{2... | collective-permute-start | bytes 1179656 | tf_op jit(solution)/shard_map/ppermute | solution.py:199
  51.8 33.2 %collective-permute-start.6 = (bf16[768,256]{1,0:T(8,128)(2,1)}, bf16[768,256]{1,0:T(8,128)(2,1)S(1)}, u32[]{:S(2)}, u32[]{:S(2)}) collective-permute-start(bf16[768,256]{1,0:T(8,128)(2,1)} %shard_map.101), channel_id=1, source_target_pairs={{0,8},{8,264},{256,0},{264,256},{1,9},{9,265},{257,1},{265,257},{2... | collective-permute-start | bytes 1179656 | tf_op jit(solution)/shard_map/ppermute | solution.py:199
  53.7 16.8 %collective-permute-start.4 = (bf16[4,192,256]{2,1,0:T(8,128)(2,1)S(1)}, bf16[4,192,256]{2,1,0:T(8,128)(2,1)S(1)}, u32[]{:S(2)}, u32[]{:S(2)}) collective-permute-start(bf16[4,192,256]{2,1,0:T(8,128)(2,1)S(1)} %bitcast.21), channel_id=1, source_target_pairs={{0,16},{16,32},{32,48},{48,64},{64,80},{80,96},{96,112},{112,128},... | collective-permute-start | bytes 1179656 | tf_op jit(solution)/shard_map/ppermute | solution.py:207
  56.6 13.9 %collective-permute-start.2 = (bf16[2,192,256]{2,1,0:T(8,128)(2,1)S(1)}, bf16[2,192,256]{2,1,0:T(8,128)(2,1)S(1)}, u32[]{:S(2)}, u32[]{:S(2)}) collective-permute-start(bf16[2,192,256]{2,1,0:T(8,128)(2,1)S(1)} %bitcast.25), channel_id=1, source_target_pairs={{0,32},{16,48},{32,64},{48,80},{64,96},{80,112},{96,128},{112,144}... | collective-permute-start | bytes 589832 | tf_op jit(solution)/shard_map/ppermute | solution.py:207
  59.7 10.8 %collective-permute-start.3 = (bf16[2,192,256]{2,1,0:T(8,128)(2,1)S(1)}, bf16[2,192,256]{2,1,0:T(8,128)(2,1)S(1)}, u32[]{:S(2)}, u32[]{:S(2)}) collective-permute-start(bf16[2,192,256]{2,1,0:T(8,128)(2,1)S(1)} %bitcast.24), channel_id=1, source_target_pairs={{0,224},{16,240},{32,0},{48,16},{64,32},{80,48},{96,64},{112,80},{... | collective-permute-start | bytes 589832 | tf_op jit(solution)/shard_map/ppermute | solution.py:207
  84.9 0.7 copy-start
  85.0 0.9 copy-start.1
  100.6 13.4 %collective-permute-start.7 = (bf16[768,256]{1,0:T(8,128)(2,1)}, bf16[768,256]{1,0:T(8,128)(2,1)S(1)}, u32[]{:S(2)}, u32[]{:S(2)}) collective-permute-start(bf16[768,256]{1,0:T(8,128)(2,1)} %get-tuple-element.21), channel_id=1, source_target_pairs={{0,0},{8,256},{256,8},{264,264},{1,1},{9,257},{257,9},{265,265},{2... | collective-permute-start | bytes 1179656 | tf_op jit(solution)/shard_map/ppermute | solution.py:199
  103.6 13.1 %collective-permute-start.8 = (bf16[768,256]{1,0:T(8,128)(2,1)}, bf16[768,256]{1,0:T(8,128)(2,1)S(1)}, u32[]{:S(2)}, u32[]{:S(2)}) collective-permute-start(bf16[768,256]{1,0:T(8,128)(2,1)} %get-tuple-element.22), channel_id=1, source_target_pairs={{0,256},{8,0},{256,264},{264,8},{1,257},{9,1},{257,265},{265,9},{2... | collective-permute-start | bytes 1179656 | tf_op jit(solution)/shard_map/ppermute | solution.py:199
  114.0 2.7 %copy-start.2 = (bf16[768,256]{1,0:T(8,128)(2,1)}, bf16[768,256]{1,0:T(8,128)(2,1)S(1)}, u32[]{:S(2)}) copy-start(bf16[768,256]{1,0:T(8,128)(2,1)S(1)} %collective-permute-done.7.one_ref) | copy-start | bytes 1179652
  116.7 0.8 copy-start.3
  168.6 6.7 %collective-permute-start.9 = (bf16[192,256]{1,0:T(8,128)(2,1)}, bf16[192,256]{1,0:T(8,128)(2,1)S(1)}, u32[]{:S(2)}, u32[]{:S(2)}) collective-permute-start(bf16[192,256]{1,0:T(8,128)(2,1)} %reduce-scatter.2.cloned.1.call-done), channel_id=1, source_target_pairs={{0,0},{8,256},{256,8},{264,264},{1,1},{9,257},{257,9},{265,265},{2... | collective-permute-start | bytes 294920 | tf_op jit(solution)/shard_map/ppermute | solution.py:199
Sparse Core Ops, SparseCore 0:
  10.1 74.7 all-gather.3
  93.1 75.4 reduce-scatter.1

commit v12 on v11

--- a/solution.py
+++ b/solution.py
@@ -230,7 +230,7 @@
     attn = forward(queries_raw, keys_raw, values, norm_gains)
     attn_same = turned(attn)
     attn_other = swap_y(attn, lambda low, up: (up, 1 - low))
-    own_rows, _ = lax.optimization_barrier((turned(out_weight), attn))
+    own_rows, attn_same = lax.optimization_barrier((turned(out_weight), attn_same))
     weights = gather_rows(own_rows)
     grads, weights = lax.optimization_barrier((grads, weights))
 

time: 184 us -> 183 us (level)
  the two profiles are of different devices: /device:TPU:10 before, /device:TPU:8 now
where the time goes in v12:
time: 183 us
  blocking collectives  66.3 us (36%)
  waiting for transfers between devices  38.6 us (21%)
  starting transfers between devices  31.2 us (17%)
  Pallas kernels  27.2 us (15%)
  between operations  14.2 us (8%)
  local copies, waits for them, and re-layouts  3.69 us (2%)
    all_to_all x2, blocking collectives, sum_over(): lax.all_to_all(jnp.broadcast_to(array[None], (count,) + array.shape), axi...  37.1 us
    all_gather x1, blocking collectives, gather_rows(): column = lax.all_gather(own_rows, 'za', axis=0)  29.1 us
    ppermute x6, waiting for transfers between devices, swap_y(): return lax.ppermute(array, ('yl', 'yh'), pairs)  23.8 us
    ppermute x6, starting transfers between devices, swap_y(): return lax.ppermute(array, ('yl', 'yh'), pairs)  17.4 us
    ppermute x4, starting transfers between devices, along(): return lax.ppermute(array, Z, [(z, (z + step) % 16) for z in range(16)])  13.8 us
    pallas_call x1, Pallas kernels, token_product(): pl.pallas_call(token_kernel, grid_spec=pltpu.PrefetchScalarGridSpec(num_s...  7.68 us
    pallas_call x1, Pallas kernels, backward(): pl.pallas_call(backward_kernel, grid=(tokens // PATCH,), in_specs=[block]...  7.36 us
    pallas_call x1, Pallas kernels, weight_product(): pl.pallas_call(weight_kernel, grid_spec=pltpu.PrefetchScalarGridSpec(num_...  7.1 us
  transfers between devices with their start and end apart: 12, of which 8 were waited for; matrix products, arithmetic and copies ran while one was open for 2% of the time, Pallas kernels for 11%

profile of v12, /device:TPU:8, one launch (start us, length us, event | category | flops | bytes accessed | tf_op | source)
XLA Modules:
  0.0 182.5 jit_solution(3810404193403395416)
XLA Ops:
  7.2 0.0 all-gather.4.cloned.1.call-start
  7.2 0.7 all-gather.4.cloned.1.call-update
  7.9 0.0 reduce-scatter.2.cloned.1.call-start
  7.9 5.1 %shard_map.101 = bf16[768,256]{1,0:T(8,128)(2,1)} custom-call(bf16[768,256]{1,0:T(8,128)(2,1)} %q_ref.3, bf16[768,256]{1,0:T(8,128)(2,1)} %k_ref.3, bf16[768,256]{1,0:T(8,128)(2,1)} %v_ref.3, f32[2,128]{1,0:T(2,128)} %gains_ref.3), custom_call_target="tpu_custom_call" | custom-call | tf_op jit(solution)/shard_map/pallas_call | solution.py:56
  13.0 3.5 %collective-permute-start.1 = (bf16[768,256]{1,0:T(8,128)(2,1)}, bf16[768,256]{1,0:T(8,128)(2,1)S(1)}, u32[]{:S(2)}, u32[]{:S(2)}) collective-permute-start(bf16[768,256]{1,0:T(8,128)(2,1)} %shard_map.101), channel_id=1, source_target_pairs={{0,0},{8,256},{256,8},{264,264},{1,1},{9,257},{257,9},{265,265},{2... | collective-permute-start | bytes 1179656 | tf_op jit(solution)/shard_map/ppermute | solution.py:199
  16.5 2.4 %collective-permute-start = (bf16[192,256]{1,0:T(8,128)(2,1)}, bf16[192,256]{1,0:T(8,128)(2,1)S(1)}, u32[]{:S(2)}, u32[]{:S(2)}) collective-permute-start(bf16[192,256]{1,0:T(8,128)(2,1)} %param.10), channel_id=1, source_target_pairs={{0,0},{8,256},{256,8},{264,264},{1,1},{9,257},{257,9},{265,265},{2... | collective-permute-start | bytes 294920 | tf_op jit(solution)/shard_map/ppermute | solution.py:199
  18.9 9.2 %collective-permute-done = bf16[192,256]{1,0:T(8,128)(2,1)S(1)} collective-permute-done((bf16[192,256]{1,0:T(8,128)(2,1)}, bf16[192,256]{1,0:T(8,128)(2,1)S(1)}, u32[]{:S(2)}, u32[]{:S(2)}) %collective-permute-start) | collective-permute-done | bytes 98336 | tf_op jit(solution)/shard_map/ppermute | solution.py:199
  28.1 0.0 collective-permute-done.1.same_ref
  28.1 0.0 copy-start
  28.1 29.1 %all-gather.1 = bf16[768,256]{1,0:T(8,128)(2,1)S(1)} all-gather(bf16[192,256]{1,0:T(8,128)(2,1)S(1)} %collective-permute-done), channel_id=3, replica_groups=mesh['yl'=2,'za'=4,'zb'=4,'yh'=2,'x'=4,'c'=2] {'za'}, dimensions={0}, use_global_device_ids=true | all-gather | bytes 491520 | tf_op jit(solution)/shard_map/all_gather | solution.py:211
  57.2 3.5 %collective-permute-start.2 = (bf16[4,192,256]{2,1,0:T(8,128)(2,1)S(1)}, bf16[4,192,256]{2,1,0:T(8,128)(2,1)S(1)}, u32[]{:S(2)}, u32[]{:S(2)}) collective-permute-start(bf16[4,192,256]{2,1,0:T(8,128)(2,1)S(1)} %bitcast.20), channel_id=1, source_target_pairs={{0,240},{16,0},{32,16},{48,32},{64,48},{80,64},{96,80},{112,96},{1... | collective-permute-start | bytes 1179656 | tf_op jit(solution)/shard_map/ppermute | solution.py:207
  60.8 1.9 %collective-permute-start.6 = (bf16[768,256]{1,0:T(8,128)(2,1)}, bf16[768,256]{1,0:T(8,128)(2,1)S(1)}, u32[]{:S(2)}, u32[]{:S(2)}) collective-permute-start(bf16[768,256]{1,0:T(8,128)(2,1)} %shard_map.101), channel_id=1, source_target_pairs={{0,8},{8,264},{256,0},{264,256},{1,9},{9,265},{257,1},{265,257},{2... | collective-permute-start | bytes 1179656 | tf_op jit(solution)/shard_map/ppermute | solution.py:199
  62.7 2.3 %collective-permute-start.5 = (bf16[4,192,256]{2,1,0:T(8,128)(2,1)S(1)}, bf16[4,192,256]{2,1,0:T(8,128)(2,1)S(1)}, u32[]{:S(2)}, u32[]{:S(2)}) collective-permute-start(bf16[4,192,256]{2,1,0:T(8,128)(2,1)S(1)} %bitcast.21), channel_id=1, source_target_pairs={{0,16},{16,32},{32,48},{48,64},{64,80},{80,96},{96,112},{112,128},... | collective-permute-start | bytes 1179656 | tf_op jit(solution)/shard_map/ppermute | solution.py:207
  65.1 2.8 %collective-permute-start.3 = (bf16[2,192,256]{2,1,0:T(8,128)(2,1)S(1)}, bf16[2,192,256]{2,1,0:T(8,128)(2,1)S(1)}, u32[]{:S(2)}, u32[]{:S(2)}) collective-permute-start(bf16[2,192,256]{2,1,0:T(8,128)(2,1)S(1)} %bitcast.25), channel_id=1, source_target_pairs={{0,32},{16,48},{32,64},{48,80},{64,96},{80,112},{96,128},{112,144}... | collective-permute-start | bytes 589832 | tf_op jit(solution)/shard_map/ppermute | solution.py:207
  67.9 5.1 %collective-permute-start.4 = (bf16[2,192,256]{2,1,0:T(8,128)(2,1)S(1)}, bf16[2,192,256]{2,1,0:T(8,128)(2,1)S(1)}, u32[]{:S(2)}, u32[]{:S(2)}) collective-permute-start(bf16[2,192,256]{2,1,0:T(8,128)(2,1)S(1)} %bitcast.24), channel_id=1, source_target_pairs={{0,224},{16,240},{32,0},{48,16},{64,32},{80,48},{96,64},{112,80},{... | collective-permute-start | bytes 589832 | tf_op jit(solution)/shard_map/ppermute | solution.py:207
  73.1 0.0 collective-permute-done.2
  73.1 5.7 %collective-permute-done.3 = bf16[2,192,256]{2,1,0:T(8,128)(2,1)S(1)} collective-permute-done((bf16[2,192,256]{2,1,0:T(8,128)(2,1)S(1)}, bf16[2,192,256]{2,1,0:T(8,128)(2,1)S(1)}, u32[]{:S(2)}, u32[]{:S(2)}) %collective-permute-start.3) | collective-permute-done | bytes 196640 | tf_op jit(solution)/shard_map/ppermute | solution.py:207
  78.8 0.0 collective-permute-done.4
  78.8 0.3 collective-permute-done.5
  79.2 0.0 copy-done
  79.3 1.3 constant_dynamic-slice_fusion.weight_ref
  80.6 5.9 %all-gather.4.cloned.1.call-done = bf16[12288,384]{1,0:T(8,128)(2,1)} async-done(((bf16[768,384]{1,0:T(8,128)(2,1)}), bf16[12288,384]{1,0:T(8,128)(2,1)}) %all-gather.4.cloned.1.call-update) | async-done | bytes 9437200 | tf_op jit(solution)/shard_map/all_gather | solution.py:227
  86.4 0.0 collective-permute-done.6.other_ref
  86.4 0.0 copy-start.1
  86.4 0.7 copy-done.1
  87.2 7.1 %shard_map.102 = bf16[3072,256]{1,0:T(8,128)(2,1)} custom-call(s32[1]{0:T(128)} %bitcast.high_ref, bf16[2,4,2,768,384]{4,3,2,1,0:T(8,128)(2,1)} %bitcast.18, bf16[768,256]{1,0:T(8,128)(2,1)} %copy-done, bf16[768,256]{1,0:T(8,128)(2,1)} %copy-done.1), custom_call_target="tpu_custom_call" | custom-call | flops 2415919104 | bytes 11010048 | tf_op jit(solution)/shard_map/pallas_call | solution.py:129
  94.3 0.0 reduce-scatter.2.cloned.1.call-update
  94.3 7.7 %shard_map.103 = (bf16[768,256]{1,0:T(8,128)(2,1)}, bf16[768,256]{1,0:T(8,128)(2,1)}) custom-call(s32[1]{0:T(128)} %bitcast.high_ref, bf16[2,4,2,768,384]{4,3,2,1,0:T(8,128)(2,1)} %bitcast.19, bf16[4,4,192,256]{3,2,1,0:T(8,128)(2,1)} %constant_dynamic-slice_fusion.weight_ref), custom_call_target="tpu_custom_call" | custom-call | flops 2415919104 | bytes 11010048 | tf_op jit(solution)/shard_map/pallas_call | solution.py:171
  102.0 4.4 %collective-permute-start.7 = (bf16[768,256]{1,0:T(8,128)(2,1)}, bf16[768,256]{1,0:T(8,128)(2,1)S(1)}, u32[]{:S(2)}, u32[]{:S(2)}) collective-permute-start(bf16[768,256]{1,0:T(8,128)(2,1)} %get-tuple-element.23), channel_id=1, source_target_pairs={{0,0},{8,256},{256,8},{264,264},{1,1},{9,257},{257,9},{265,265},{2... | collective-permute-start | bytes 1179656 | tf_op jit(solution)/shard_map/ppermute | solution.py:199
  106.4 1.9 %collective-permute-start.8 = (bf16[768,256]{1,0:T(8,128)(2,1)}, bf16[768,256]{1,0:T(8,128)(2,1)S(1)}, u32[]{:S(2)}, u32[]{:S(2)}) collective-permute-start(bf16[768,256]{1,0:T(8,128)(2,1)} %get-tuple-element.24), channel_id=1, source_target_pairs={{0,256},{8,0},{256,264},{264,8},{1,257},{9,1},{257,265},{265,9},{2... | collective-permute-start | bytes 1179656 | tf_op jit(solution)/shard_map/ppermute | solution.py:199
  108.3 7.8 %collective-permute-done.7.one_ref = bf16[768,256]{1,0:T(8,128)(2,1)S(1)} collective-permute-done((bf16[768,256]{1,0:T(8,128)(2,1)}, bf16[768,256]{1,0:T(8,128)(2,1)S(1)}, u32[]{:S(2)}, u32[]{:S(2)}) %collective-permute-start.7) | collective-permute-done | bytes 393248 | tf_op jit(solution)/shard_map/ppermute | solution.py:199
  116.1 0.0 copy-start.2
  116.1 3.4 %collective-permute-done.8.two_ref = bf16[768,256]{1,0:T(8,128)(2,1)S(1)} collective-permute-done((bf16[768,256]{1,0:T(8,128)(2,1)}, bf16[768,256]{1,0:T(8,128)(2,1)S(1)}, u32[]{:S(2)}, u32[]{:S(2)}) %collective-permute-start.8) | collective-permute-done | bytes 393248 | tf_op jit(solution)/shard_map/ppermute | solution.py:199
  119.4 0.0 copy-done.2
  119.5 0.0 copy-start.3
  119.5 0.8 copy-done.3
  120.2 7.4 %shard_map.104 = (bf16[768,256]{1,0:T(8,128)(2,1)}, bf16[768,256]{1,0:T(8,128)(2,1)}, bf16[768,256]{1,0:T(8,128)(2,1)}, f32[2,128]{1,0:T(2,128)}) custom-call(bf16[768,256]{1,0:T(8,128)(2,1)} %q_ref.3, bf16[768,256]{1,0:T(8,128)(2,1)} %k_ref.3, bf16[768,256]{1,0:T(8,128)(2,1)} %v_ref.3, bf16[768,256]{1,0:T(8,128)(2,1)} %copy-done.2, ...), custom_call_target="tpu_custom_call" | custom-call | tf_op jit(solution)/shard_map/pallas_call | solution.py:102
  127.6 0.7 broadcast_in_dim.4
  128.3 12.6 %all_to_all.10 = f32[32,2,128]{2,1,0:T(2,128)S(1)} all-to-all(f32[32,2,128]{2,1,0:T(2,128)S(1)} %broadcast_in_dim.4), channel_id=1, replica_groups=mesh['yl'=2,'za'=4,'zb'=4,'yh'=2,'x'=4,'c'=2] {'yl','yh','x','c'}, dimensions={0} | all-to-all | bytes 65536 | tf_op jit(solution)/shard_map/all_to_all | solution.py:221
  140.9 24.6 %all_to_all.11 = f32[16,2,128]{2,1,0:T(2,128)S(1)} all-to-all(f32[16,2,128]{2,1,0:T(2,128)S(1)} %broadcast_in_dim.5), channel_id=1, replica_groups=mesh['yl'=2,'za'=4,'zb'=4,'yh'=2,'x'=4,'c'=2] {'za','zb'}, dimensions={0} | all-to-all | bytes 32768 | tf_op jit(solution)/shard_map/all_to_all | solution.py:221
  165.4 0.6 reduce_sum.19
  166.0 2.3 %reduce-scatter.2.cloned.1.call-done = bf16[192,256]{1,0:T(8,128)(2,1)} async-done(((bf16[3072,256]{1,0:T(8,128)(2,1)}), bf16[192,256]{1,0:T(8,128)(2,1)}) %reduce-scatter.2.cloned.1.call-update) | async-done | bytes 98320 | tf_op jit(solution)/shard_map/reduce_scatter | solution.py:238
  168.3 3.3 %collective-permute-start.9 = (bf16[192,256]{1,0:T(8,128)(2,1)}, bf16[192,256]{1,0:T(8,128)(2,1)S(1)}, u32[]{:S(2)}, u32[]{:S(2)}) collective-permute-start(bf16[192,256]{1,0:T(8,128)(2,1)} %reduce-scatter.2.cloned.1.call-done), channel_id=1, source_target_pairs={{0,0},{8,256},{256,8},{264,264},{1,1},{9,257},{257,9},{265,265},{2... | collective-permute-start | bytes 294920 | tf_op jit(solution)/shard_map/ppermute | solution.py:199
  171.6 3.4 %collective-permute-done.9 = bf16[192,256]{1,0:T(8,128)(2,1)S(1)} collective-permute-done((bf16[192,256]{1,0:T(8,128)(2,1)}, bf16[192,256]{1,0:T(8,128)(2,1)S(1)}, u32[]{:S(2)}, u32[]{:S(2)}) %collective-permute-start.9) | collective-permute-done | bytes 98336 | tf_op jit(solution)/shard_map/ppermute | solution.py:199
  175.0 0.7 convert_element_type.3
  (11 shorter events, 0.3 us)
Async XLA Ops:
  7.2 79.3 %all-gather.4.cloned.1.call-start = ((), (), s32[]{:S(2)}) async-start(), calls=%async_computation.4 | async-start | bytes 10027008 | tf_op jit(solution)/shard_map/all_gather | solution.py:227
  7.9 160.4 %reduce-scatter.2.cloned.1.call-start = ((), (), s32[]{:S(2)}) async-start(), calls=%async_computation.3 | async-start | bytes 1671168 | tf_op jit(solution)/shard_map/reduce_scatter | solution.py:238
  13.0 15.1 %collective-permute-start.1 = (bf16[768,256]{1,0:T(8,128)(2,1)}, bf16[768,256]{1,0:T(8,128)(2,1)S(1)}, u32[]{:S(2)}, u32[]{:S(2)}) collective-permute-start(bf16[768,256]{1,0:T(8,128)(2,1)} %shard_map.101), channel_id=1, source_target_pairs={{0,0},{8,256},{256,8},{264,264},{1,1},{9,257},{257,9},{265,265},{2... | collective-permute-start | bytes 1179656 | tf_op jit(solution)/shard_map/ppermute | solution.py:199
  16.5 11.6 %collective-permute-start = (bf16[192,256]{1,0:T(8,128)(2,1)}, bf16[192,256]{1,0:T(8,128)(2,1)S(1)}, u32[]{:S(2)}, u32[]{:S(2)}) collective-permute-start(bf16[192,256]{1,0:T(8,128)(2,1)} %param.10), channel_id=1, source_target_pairs={{0,0},{8,256},{256,8},{264,264},{1,1},{9,257},{257,9},{265,265},{2... | collective-permute-start | bytes 294920 | tf_op jit(solution)/shard_map/ppermute | solution.py:199
  28.1 51.2 %copy-start = (bf16[768,256]{1,0:T(8,128)(2,1)}, bf16[768,256]{1,0:T(8,128)(2,1)S(1)}, u32[]{:S(2)}) copy-start(bf16[768,256]{1,0:T(8,128)(2,1)S(1)} %collective-permute-done.1.same_ref) | copy-start | bytes 1179652
  57.2 15.8 %collective-permute-start.2 = (bf16[4,192,256]{2,1,0:T(8,128)(2,1)S(1)}, bf16[4,192,256]{2,1,0:T(8,128)(2,1)S(1)}, u32[]{:S(2)}, u32[]{:S(2)}) collective-permute-start(bf16[4,192,256]{2,1,0:T(8,128)(2,1)S(1)} %bitcast.20), channel_id=1, source_target_pairs={{0,240},{16,0},{32,16},{48,32},{64,48},{80,64},{96,80},{112,96},{1... | collective-permute-start | bytes 1179656 | tf_op jit(solution)/shard_map/ppermute | solution.py:207
  60.8 25.7 %collective-permute-start.6 = (bf16[768,256]{1,0:T(8,128)(2,1)}, bf16[768,256]{1,0:T(8,128)(2,1)S(1)}, u32[]{:S(2)}, u32[]{:S(2)}) collective-permute-start(bf16[768,256]{1,0:T(8,128)(2,1)} %shard_map.101), channel_id=1, source_target_pairs={{0,8},{8,264},{256,0},{264,256},{1,9},{9,265},{257,1},{265,257},{2... | collective-permute-start | bytes 1179656 | tf_op jit(solution)/shard_map/ppermute | solution.py:199
  62.7 16.4 %collective-permute-start.5 = (bf16[4,192,256]{2,1,0:T(8,128)(2,1)S(1)}, bf16[4,192,256]{2,1,0:T(8,128)(2,1)S(1)}, u32[]{:S(2)}, u32[]{:S(2)}) collective-permute-start(bf16[4,192,256]{2,1,0:T(8,128)(2,1)S(1)} %bitcast.21), channel_id=1, source_target_pairs={{0,16},{16,32},{32,48},{48,64},{64,80},{80,96},{96,112},{112,128},... | collective-permute-start | bytes 1179656 | tf_op jit(solution)/shard_map/ppermute | solution.py:207
  65.1 13.7 %collective-permute-start.3 = (bf16[2,192,256]{2,1,0:T(8,128)(2,1)S(1)}, bf16[2,192,256]{2,1,0:T(8,128)(2,1)S(1)}, u32[]{:S(2)}, u32[]{:S(2)}) collective-permute-start(bf16[2,192,256]{2,1,0:T(8,128)(2,1)S(1)} %bitcast.25), channel_id=1, source_target_pairs={{0,32},{16,48},{32,64},{48,80},{64,96},{80,112},{96,128},{112,144}... | collective-permute-start | bytes 589832 | tf_op jit(solution)/shard_map/ppermute | solution.py:207
  67.9 10.8 %collective-permute-start.4 = (bf16[2,192,256]{2,1,0:T(8,128)(2,1)S(1)}, bf16[2,192,256]{2,1,0:T(8,128)(2,1)S(1)}, u32[]{:S(2)}, u32[]{:S(2)}) collective-permute-start(bf16[2,192,256]{2,1,0:T(8,128)(2,1)S(1)} %bitcast.24), channel_id=1, source_target_pairs={{0,224},{16,240},{32,0},{48,16},{64,32},{80,48},{96,64},{112,80},{... | collective-permute-start | bytes 589832 | tf_op jit(solution)/shard_map/ppermute | solution.py:207
  86.4 0.7 copy-start.1
  102.0 14.1 %collective-permute-start.7 = (bf16[768,256]{1,0:T(8,128)(2,1)}, bf16[768,256]{1,0:T(8,128)(2,1)S(1)}, u32[]{:S(2)}, u32[]{:S(2)}) collective-permute-start(bf16[768,256]{1,0:T(8,128)(2,1)} %get-tuple-element.23), channel_id=1, source_target_pairs={{0,0},{8,256},{256,8},{264,264},{1,1},{9,257},{257,9},{265,265},{2... | collective-permute-start | bytes 1179656 | tf_op jit(solution)/shard_map/ppermute | solution.py:199
  106.4 13.1 %collective-permute-start.8 = (bf16[768,256]{1,0:T(8,128)(2,1)}, bf16[768,256]{1,0:T(8,128)(2,1)S(1)}, u32[]{:S(2)}, u32[]{:S(2)}) collective-permute-start(bf16[768,256]{1,0:T(8,128)(2,1)} %get-tuple-element.24), channel_id=1, source_target_pairs={{0,256},{8,0},{256,264},{264,8},{1,257},{9,1},{257,265},{265,9},{2... | collective-permute-start | bytes 1179656 | tf_op jit(solution)/shard_map/ppermute | solution.py:199
  116.1 3.4 %copy-start.2 = (bf16[768,256]{1,0:T(8,128)(2,1)}, bf16[768,256]{1,0:T(8,128)(2,1)S(1)}, u32[]{:S(2)}) copy-start(bf16[768,256]{1,0:T(8,128)(2,1)S(1)} %collective-permute-done.7.one_ref) | copy-start | bytes 1179652
  119.5 0.8 copy-start.3
  168.3 6.7 %collective-permute-start.9 = (bf16[192,256]{1,0:T(8,128)(2,1)}, bf16[192,256]{1,0:T(8,128)(2,1)S(1)}, u32[]{:S(2)}, u32[]{:S(2)}) collective-permute-start(bf16[192,256]{1,0:T(8,128)(2,1)} %reduce-scatter.2.cloned.1.call-done), channel_id=1, source_target_pairs={{0,0},{8,256},{256,8},{264,264},{1,1},{9,257},{257,9},{265,265},{2... | collective-permute-start | bytes 294920 | tf_op jit(solution)/shard_map/ppermute | solution.py:199
Sparse Core Ops, SparseCore 0:
  10.1 76.2 all-gather.3
  94.4 73.8 reduce-scatter.1

commit v13 on v12

--- a/solution.py
+++ b/solution.py
@@ -230,7 +230,7 @@
     attn = forward(queries_raw, keys_raw, values, norm_gains)
     attn_same = turned(attn)
     attn_other = swap_y(attn, lambda low, up: (up, 1 - low))
-    own_rows, attn_same = lax.optimization_barrier((turned(out_weight), attn_same))
+    own_rows, attn_other = lax.optimization_barrier((turned(out_weight), attn_other))
     weights = gather_rows(own_rows)
     grads, weights = lax.optimization_barrier((grads, weights))
 

time: 183 us -> 177 us (0.967)
  waiting for transfers between devices: 38.6 us -> 28.8 us
  starting transfers between devices: 31.2 us -> 35.1 us
    all_gather x1, waiting for transfers between devices: 5.85 us -> 0.01 us  [per_device(): grads = lax.all_gather(grad_out, ('yl', 'x', 'c'), axis=0)]
    ppermute x6, waiting for transfers between devices: 23.8 us -> 18.2 us  [swap_y(): return lax.ppermute(array, ('yl', 'yh'), pairs)]
    ppermute x6, starting transfers between devices: 17.4 us -> 20.4 us  [swap_y(): return lax.ppermute(array, ('yl', 'yh'), pairs)]
  transfers between devices with their start and end apart: 12 -> 12, of which waited for: 8 -> 6; matrix products, arithmetic and copies ran while one was open for 2% -> 2% of each run, Pallas kernels for 11% -> 11%
where the time goes in v13:
time: 177 us; the launch traced here: 176 us
  blocking collectives  65.8 us (37%)
  starting transfers between devices  35.1 us (20%)
  waiting for transfers between devices  28.8 us (16%)
  Pallas kernels  27.2 us (15%)
  between operations  14.2 us (8%)
  local copies, waits for them, and re-layouts  3.69 us (2%)
    all_to_all x2, blocking collectives, sum_over(): lax.all_to_all(jnp.broadcast_to(array[None], (count,) + array.shape), axi...  35.4 us
    all_gather x1, blocking collectives, gather_rows(): column = lax.all_gather(own_rows, 'za', axis=0)  30.4 us
    ppermute x6, starting transfers between devices, swap_y(): return lax.ppermute(array, ('yl', 'yh'), pairs)  20.4 us
    ppermute x6, waiting for transfers between devices, swap_y(): return lax.ppermute(array, ('yl', 'yh'), pairs)  18.2 us
    ppermute x4, starting transfers between devices, along(): return lax.ppermute(array, Z, [(z, (z + step) % 16) for z in range(16)])  14.7 us
    pallas_call x1, Pallas kernels, token_product(): pl.pallas_call(token_kernel, grid_spec=pltpu.PrefetchScalarGridSpec(num_s...  7.69 us
    pallas_call x1, Pallas kernels, backward(): pl.pallas_call(backward_kernel, grid=(tokens // PATCH,), in_specs=[block]...  7.37 us
    pallas_call x1, Pallas kernels, weight_product(): pl.pallas_call(weight_kernel, grid_spec=pltpu.PrefetchScalarGridSpec(num_...  7.1 us
  transfers between devices with their start and end apart: 12, of which 6 were waited for; matrix products, arithmetic and copies ran while one was open for 2% of the time, Pallas kernels for 11%

profile of v13, /device:TPU:8, one launch (start us, length us, event | category | flops | bytes accessed | tf_op | source)
XLA Modules:
  0.0 176.3 jit_solution(14291842658874919937)
XLA Ops:
  7.2 0.0 all-gather.4.cloned.1.call-start
  7.2 0.7 all-gather.4.cloned.1.call-update
  7.9 0.0 reduce-scatter.2.cloned.1.call-start
  7.9 5.1 %shard_map.101 = bf16[768,256]{1,0:T(8,128)(2,1)} custom-call(bf16[768,256]{1,0:T(8,128)(2,1)} %q_ref.3, bf16[768,256]{1,0:T(8,128)(2,1)} %k_ref.3, bf16[768,256]{1,0:T(8,128)(2,1)} %v_ref.3, f32[2,128]{1,0:T(2,128)} %gains_ref.3), custom_call_target="tpu_custom_call" | custom-call | tf_op jit(solution)/shard_map/pallas_call | solution.py:56
  13.0 7.7 %collective-permute-start.1 = (bf16[768,256]{1,0:T(8,128)(2,1)}, bf16[768,256]{1,0:T(8,128)(2,1)S(1)}, u32[]{:S(2)}, u32[]{:S(2)}) collective-permute-start(bf16[768,256]{1,0:T(8,128)(2,1)} %shard_map.101), channel_id=1, source_target_pairs={{0,8},{8,264},{256,0},{264,256},{1,9},{9,265},{257,1},{265,257},{2... | collective-permute-start | bytes 1179656 | tf_op jit(solution)/shard_map/ppermute | solution.py:199
  20.8 1.9 %collective-permute-start = (bf16[192,256]{1,0:T(8,128)(2,1)}, bf16[192,256]{1,0:T(8,128)(2,1)S(1)}, u32[]{:S(2)}, u32[]{:S(2)}) collective-permute-start(bf16[192,256]{1,0:T(8,128)(2,1)} %param.10), channel_id=1, source_target_pairs={{0,0},{8,256},{256,8},{264,264},{1,1},{9,257},{257,9},{265,265},{2... | collective-permute-start | bytes 294920 | tf_op jit(solution)/shard_map/ppermute | solution.py:199
  22.7 6.9 %collective-permute-done = bf16[192,256]{1,0:T(8,128)(2,1)S(1)} collective-permute-done((bf16[192,256]{1,0:T(8,128)(2,1)}, bf16[192,256]{1,0:T(8,128)(2,1)S(1)}, u32[]{:S(2)}, u32[]{:S(2)}) %collective-permute-start) | collective-permute-done | bytes 98336 | tf_op jit(solution)/shard_map/ppermute | solution.py:199
  29.6 0.0 collective-permute-done.1.other_ref
  29.6 0.0 copy-start
  29.6 30.4 %all-gather.1 = bf16[768,256]{1,0:T(8,128)(2,1)S(1)} all-gather(bf16[192,256]{1,0:T(8,128)(2,1)S(1)} %collective-permute-done), channel_id=3, replica_groups=mesh['yl'=2,'za'=4,'zb'=4,'yh'=2,'x'=4,'c'=2] {'za'}, dimensions={0}, use_global_device_ids=true | all-gather | bytes 491520 | tf_op jit(solution)/shard_map/all_gather | solution.py:211
  60.0 3.1 %collective-permute-start.2 = (bf16[4,192,256]{2,1,0:T(8,128)(2,1)S(1)}, bf16[4,192,256]{2,1,0:T(8,128)(2,1)S(1)}, u32[]{:S(2)}, u32[]{:S(2)}) collective-permute-start(bf16[4,192,256]{2,1,0:T(8,128)(2,1)S(1)} %bitcast.20), channel_id=1, source_target_pairs={{0,240},{16,0},{32,16},{48,32},{64,48},{80,64},{96,80},{112,96},{1... | collective-permute-start | bytes 1179656 | tf_op jit(solution)/shard_map/ppermute | solution.py:207
  63.1 3.3 %collective-permute-start.6 = (bf16[768,256]{1,0:T(8,128)(2,1)}, bf16[768,256]{1,0:T(8,128)(2,1)S(1)}, u32[]{:S(2)}, u32[]{:S(2)}) collective-permute-start(bf16[768,256]{1,0:T(8,128)(2,1)} %shard_map.101), channel_id=1, source_target_pairs={{0,0},{8,256},{256,8},{264,264},{1,1},{9,257},{257,9},{265,265},{2... | collective-permute-start | bytes 1179656 | tf_op jit(solution)/shard_map/ppermute | solution.py:199
  66.4 3.6 %collective-permute-start.5 = (bf16[4,192,256]{2,1,0:T(8,128)(2,1)S(1)}, bf16[4,192,256]{2,1,0:T(8,128)(2,1)S(1)}, u32[]{:S(2)}, u32[]{:S(2)}) collective-permute-start(bf16[4,192,256]{2,1,0:T(8,128)(2,1)S(1)} %bitcast.21), channel_id=1, source_target_pairs={{0,16},{16,32},{32,48},{48,64},{64,80},{80,96},{96,112},{112,128},... | collective-permute-start | bytes 1179656 | tf_op jit(solution)/shard_map/ppermute | solution.py:207
  70.1 2.7 %collective-permute-start.3 = (bf16[2,192,256]{2,1,0:T(8,128)(2,1)S(1)}, bf16[2,192,256]{2,1,0:T(8,128)(2,1)S(1)}, u32[]{:S(2)}, u32[]{:S(2)}) collective-permute-start(bf16[2,192,256]{2,1,0:T(8,128)(2,1)S(1)} %bitcast.25), channel_id=1, source_target_pairs={{0,32},{16,48},{32,64},{48,80},{64,96},{80,112},{96,128},{112,144}... | collective-permute-start | bytes 589832 | tf_op jit(solution)/shard_map/ppermute | solution.py:207
  72.8 5.2 %collective-permute-start.4 = (bf16[2,192,256]{2,1,0:T(8,128)(2,1)S(1)}, bf16[2,192,256]{2,1,0:T(8,128)(2,1)S(1)}, u32[]{:S(2)}, u32[]{:S(2)}) collective-permute-start(bf16[2,192,256]{2,1,0:T(8,128)(2,1)S(1)} %bitcast.24), channel_id=1, source_target_pairs={{0,224},{16,240},{32,0},{48,16},{64,32},{80,48},{96,64},{112,80},{... | collective-permute-start | bytes 589832 | tf_op jit(solution)/shard_map/ppermute | solution.py:207
  78.1 0.0 collective-permute-done.2
  78.1 6.2 %collective-permute-done.3 = bf16[2,192,256]{2,1,0:T(8,128)(2,1)S(1)} collective-permute-done((bf16[2,192,256]{2,1,0:T(8,128)(2,1)S(1)}, bf16[2,192,256]{2,1,0:T(8,128)(2,1)S(1)}, u32[]{:S(2)}, u32[]{:S(2)}) %collective-permute-start.3) | collective-permute-done | bytes 196640 | tf_op jit(solution)/shard_map/ppermute | solution.py:207
  84.3 0.0 collective-permute-done.4
  84.4 0.0 collective-permute-done.5
  84.5 0.0 copy-done
  84.6 1.3 constant_dynamic-slice_fusion.weight_ref
  85.8 0.0 all-gather.4.cloned.1.call-done
  85.9 0.0 collective-permute-done.6.same_ref
  85.9 0.0 copy-start.1
  85.9 0.7 copy-done.1
  86.6 7.1 %shard_map.102 = bf16[3072,256]{1,0:T(8,128)(2,1)} custom-call(s32[1]{0:T(128)} %bitcast.high_ref, bf16[2,4,2,768,384]{4,3,2,1,0:T(8,128)(2,1)} %bitcast.18, bf16[768,256]{1,0:T(8,128)(2,1)} %copy-done.1, bf16[768,256]{1,0:T(8,128)(2,1)} %copy-done), custom_call_target="tpu_custom_call" | custom-call | flops 2415919104 | bytes 11010048 | tf_op jit(solution)/shard_map/pallas_call | solution.py:129
  93.7 0.0 reduce-scatter.2.cloned.1.call-update
  93.7 7.7 %shard_map.103 = (bf16[768,256]{1,0:T(8,128)(2,1)}, bf16[768,256]{1,0:T(8,128)(2,1)}) custom-call(s32[1]{0:T(128)} %bitcast.high_ref, bf16[2,4,2,768,384]{4,3,2,1,0:T(8,128)(2,1)} %bitcast.19, bf16[4,4,192,256]{3,2,1,0:T(8,128)(2,1)} %constant_dynamic-slice_fusion.weight_ref), custom_call_target="tpu_custom_call" | custom-call | flops 2415919104 | bytes 11010048 | tf_op jit(solution)/shard_map/pallas_call | solution.py:171
  101.4 2.2 %collective-permute-start.7 = (bf16[768,256]{1,0:T(8,128)(2,1)}, bf16[768,256]{1,0:T(8,128)(2,1)S(1)}, u32[]{:S(2)}, u32[]{:S(2)}) collective-permute-start(bf16[768,256]{1,0:T(8,128)(2,1)} %get-tuple-element.23), channel_id=1, source_target_pairs={{0,0},{8,256},{256,8},{264,264},{1,1},{9,257},{257,9},{265,265},{2... | collective-permute-start | bytes 1179656 | tf_op jit(solution)/shard_map/ppermute | solution.py:199
  103.6 1.9 %collective-permute-start.8 = (bf16[768,256]{1,0:T(8,128)(2,1)}, bf16[768,256]{1,0:T(8,128)(2,1)S(1)}, u32[]{:S(2)}, u32[]{:S(2)}) collective-permute-start(bf16[768,256]{1,0:T(8,128)(2,1)} %get-tuple-element.24), channel_id=1, source_target_pairs={{0,256},{8,0},{256,264},{264,8},{1,257},{9,1},{257,265},{265,9},{2... | collective-permute-start | bytes 1179656 | tf_op jit(solution)/shard_map/ppermute | solution.py:199
  105.5 5.8 %collective-permute-done.7.one_ref = bf16[768,256]{1,0:T(8,128)(2,1)S(1)} collective-permute-done((bf16[768,256]{1,0:T(8,128)(2,1)}, bf16[768,256]{1,0:T(8,128)(2,1)S(1)}, u32[]{:S(2)}, u32[]{:S(2)}) %collective-permute-start.7) | collective-permute-done | bytes 393248 | tf_op jit(solution)/shard_map/ppermute | solution.py:199
  111.3 0.0 copy-start.2
  111.3 2.2 %collective-permute-done.8.two_ref = bf16[768,256]{1,0:T(8,128)(2,1)S(1)} collective-permute-done((bf16[768,256]{1,0:T(8,128)(2,1)}, bf16[768,256]{1,0:T(8,128)(2,1)S(1)}, u32[]{:S(2)}, u32[]{:S(2)}) %collective-permute-start.8) | collective-permute-done | bytes 393248 | tf_op jit(solution)/shard_map/ppermute | solution.py:199
  113.5 0.0 copy-done.2
  113.5 0.0 copy-start.3
  113.5 0.8 copy-done.3
  114.2 7.4 %shard_map.104 = (bf16[768,256]{1,0:T(8,128)(2,1)}, bf16[768,256]{1,0:T(8,128)(2,1)}, bf16[768,256]{1,0:T(8,128)(2,1)}, f32[2,128]{1,0:T(2,128)}) custom-call(bf16[768,256]{1,0:T(8,128)(2,1)} %q_ref.3, bf16[768,256]{1,0:T(8,128)(2,1)} %k_ref.3, bf16[768,256]{1,0:T(8,128)(2,1)} %v_ref.3, bf16[768,256]{1,0:T(8,128)(2,1)} %copy-done.2, ...), custom_call_target="tpu_custom_call" | custom-call | tf_op jit(solution)/shard_map/pallas_call | solution.py:102
  121.6 0.7 broadcast_in_dim.4
  122.3 14.8 %all_to_all.10 = f32[32,2,128]{2,1,0:T(2,128)S(1)} all-to-all(f32[32,2,128]{2,1,0:T(2,128)S(1)} %broadcast_in_dim.4), channel_id=1, replica_groups=mesh['yl'=2,'za'=4,'zb'=4,'yh'=2,'x'=4,'c'=2] {'yl','yh','x','c'}, dimensions={0} | all-to-all | bytes 65536 | tf_op jit(solution)/shard_map/all_to_all | solution.py:221
  137.2 20.6 %all_to_all.11 = f32[16,2,128]{2,1,0:T(2,128)S(1)} all-to-all(f32[16,2,128]{2,1,0:T(2,128)S(1)} %broadcast_in_dim.5), channel_id=1, replica_groups=mesh['yl'=2,'za'=4,'zb'=4,'yh'=2,'x'=4,'c'=2] {'za','zb'}, dimensions={0} | all-to-all | bytes 32768 | tf_op jit(solution)/shard_map/all_to_all | solution.py:221
  157.8 0.6 reduce_sum.19
  158.3 3.7 %reduce-scatter.2.cloned.1.call-done = bf16[192,256]{1,0:T(8,128)(2,1)} async-done(((bf16[3072,256]{1,0:T(8,128)(2,1)}), bf16[192,256]{1,0:T(8,128)(2,1)}) %reduce-scatter.2.cloned.1.call-update) | async-done | bytes 98320 | tf_op jit(solution)/shard_map/reduce_scatter | solution.py:238
  162.1 3.4 %collective-permute-start.9 = (bf16[192,256]{1,0:T(8,128)(2,1)}, bf16[192,256]{1,0:T(8,128)(2,1)S(1)}, u32[]{:S(2)}, u32[]{:S(2)}) collective-permute-start(bf16[192,256]{1,0:T(8,128)(2,1)} %reduce-scatter.2.cloned.1.call-done), channel_id=1, source_target_pairs={{0,0},{8,256},{256,8},{264,264},{1,1},{9,257},{257,9},{265,265},{2... | collective-permute-start | bytes 294920 | tf_op jit(solution)/shard_map/ppermute | solution.py:199
  165.5 3.3 %collective-permute-done.9 = bf16[192,256]{1,0:T(8,128)(2,1)S(1)} collective-permute-done((bf16[192,256]{1,0:T(8,128)(2,1)}, bf16[192,256]{1,0:T(8,128)(2,1)S(1)}, u32[]{:S(2)}, u32[]{:S(2)}) %collective-permute-start.9) | collective-permute-done | bytes 98336 | tf_op jit(solution)/shard_map/ppermute | solution.py:199
  168.8 0.7 convert_element_type.3
  (11 shorter events, 0.3 us)
Async XLA Ops:
  7.2 78.7 %all-gather.4.cloned.1.call-start = ((), (), s32[]{:S(2)}) async-start(), calls=%async_computation.4 | async-start | bytes 10027008 | tf_op jit(solution)/shard_map/all_gather | solution.py:227
  7.9 154.2 %reduce-scatter.2.cloned.1.call-start = ((), (), s32[]{:S(2)}) async-start(), calls=%async_computation.3 | async-start | bytes 1671168 | tf_op jit(solution)/shard_map/reduce_scatter | solution.py:238
  13.0 16.6 %collective-permute-start.1 = (bf16[768,256]{1,0:T(8,128)(2,1)}, bf16[768,256]{1,0:T(8,128)(2,1)S(1)}, u32[]{:S(2)}, u32[]{:S(2)}) collective-permute-start(bf16[768,256]{1,0:T(8,128)(2,1)} %shard_map.101), channel_id=1, source_target_pairs={{0,8},{8,264},{256,0},{264,256},{1,9},{9,265},{257,1},{265,257},{2... | collective-permute-start | bytes 1179656 | tf_op jit(solution)/shard_map/ppermute | solution.py:199
  20.8 8.8 %collective-permute-start = (bf16[192,256]{1,0:T(8,128)(2,1)}, bf16[192,256]{1,0:T(8,128)(2,1)S(1)}, u32[]{:S(2)}, u32[]{:S(2)}) collective-permute-start(bf16[192,256]{1,0:T(8,128)(2,1)} %param.10), channel_id=1, source_target_pairs={{0,0},{8,256},{256,8},{264,264},{1,1},{9,257},{257,9},{265,265},{2... | collective-permute-start | bytes 294920 | tf_op jit(solution)/shard_map/ppermute | solution.py:199
  29.6 54.9 %copy-start = (bf16[768,256]{1,0:T(8,128)(2,1)}, bf16[768,256]{1,0:T(8,128)(2,1)S(1)}, u32[]{:S(2)}) copy-start(bf16[768,256]{1,0:T(8,128)(2,1)S(1)} %collective-permute-done.1.other_ref) | copy-start | bytes 1179652
  60.0 18.1 %collective-permute-start.2 = (bf16[4,192,256]{2,1,0:T(8,128)(2,1)S(1)}, bf16[4,192,256]{2,1,0:T(8,128)(2,1)S(1)}, u32[]{:S(2)}, u32[]{:S(2)}) collective-permute-start(bf16[4,192,256]{2,1,0:T(8,128)(2,1)S(1)} %bitcast.20), channel_id=1, source_target_pairs={{0,240},{16,0},{32,16},{48,32},{64,48},{80,64},{96,80},{112,96},{1... | collective-permute-start | bytes 1179656 | tf_op jit(solution)/shard_map/ppermute | solution.py:207
  63.1 22.7 %collective-permute-start.6 = (bf16[768,256]{1,0:T(8,128)(2,1)}, bf16[768,256]{1,0:T(8,128)(2,1)S(1)}, u32[]{:S(2)}, u32[]{:S(2)}) collective-permute-start(bf16[768,256]{1,0:T(8,128)(2,1)} %shard_map.101), channel_id=1, source_target_pairs={{0,0},{8,256},{256,8},{264,264},{1,1},{9,257},{257,9},{265,265},{2... | collective-permute-start | bytes 1179656 | tf_op jit(solution)/shard_map/ppermute | solution.py:199
  66.4 17.9 %collective-permute-start.5 = (bf16[4,192,256]{2,1,0:T(8,128)(2,1)S(1)}, bf16[4,192,256]{2,1,0:T(8,128)(2,1)S(1)}, u32[]{:S(2)}, u32[]{:S(2)}) collective-permute-start(bf16[4,192,256]{2,1,0:T(8,128)(2,1)S(1)} %bitcast.21), channel_id=1, source_target_pairs={{0,16},{16,32},{32,48},{48,64},{64,80},{80,96},{96,112},{112,128},... | collective-permute-start | bytes 1179656 | tf_op jit(solution)/shard_map/ppermute | solution.py:207
  70.1 14.2 %collective-permute-start.3 = (bf16[2,192,256]{2,1,0:T(8,128)(2,1)S(1)}, bf16[2,192,256]{2,1,0:T(8,128)(2,1)S(1)}, u32[]{:S(2)}, u32[]{:S(2)}) collective-permute-start(bf16[2,192,256]{2,1,0:T(8,128)(2,1)S(1)} %bitcast.25), channel_id=1, source_target_pairs={{0,32},{16,48},{32,64},{48,80},{64,96},{80,112},{96,128},{112,144}... | collective-permute-start | bytes 589832 | tf_op jit(solution)/shard_map/ppermute | solution.py:207
  72.8 11.5 %collective-permute-start.4 = (bf16[2,192,256]{2,1,0:T(8,128)(2,1)S(1)}, bf16[2,192,256]{2,1,0:T(8,128)(2,1)S(1)}, u32[]{:S(2)}, u32[]{:S(2)}) collective-permute-start(bf16[2,192,256]{2,1,0:T(8,128)(2,1)S(1)} %bitcast.24), channel_id=1, source_target_pairs={{0,224},{16,240},{32,0},{48,16},{64,32},{80,48},{96,64},{112,80},{... | collective-permute-start | bytes 589832 | tf_op jit(solution)/shard_map/ppermute | solution.py:207
  85.9 0.7 copy-start.1
  101.4 9.9 %collective-permute-start.7 = (bf16[768,256]{1,0:T(8,128)(2,1)}, bf16[768,256]{1,0:T(8,128)(2,1)S(1)}, u32[]{:S(2)}, u32[]{:S(2)}) collective-permute-start(bf16[768,256]{1,0:T(8,128)(2,1)} %get-tuple-element.23), channel_id=1, source_target_pairs={{0,0},{8,256},{256,8},{264,264},{1,1},{9,257},{257,9},{265,265},{2... | collective-permute-start | bytes 1179656 | tf_op jit(solution)/shard_map/ppermute | solution.py:199
  103.6 9.9 %collective-permute-start.8 = (bf16[768,256]{1,0:T(8,128)(2,1)}, bf16[768,256]{1,0:T(8,128)(2,1)S(1)}, u32[]{:S(2)}, u32[]{:S(2)}) collective-permute-start(bf16[768,256]{1,0:T(8,128)(2,1)} %get-tuple-element.24), channel_id=1, source_target_pairs={{0,256},{8,0},{256,264},{264,8},{1,257},{9,1},{257,265},{265,9},{2... | collective-permute-start | bytes 1179656 | tf_op jit(solution)/shard_map/ppermute | solution.py:199
  111.3 2.2 %copy-start.2 = (bf16[768,256]{1,0:T(8,128)(2,1)}, bf16[768,256]{1,0:T(8,128)(2,1)S(1)}, u32[]{:S(2)}) copy-start(bf16[768,256]{1,0:T(8,128)(2,1)S(1)} %collective-permute-done.7.one_ref) | copy-start | bytes 1179652
  113.5 0.8 copy-start.3
  162.1 6.7 %collective-permute-start.9 = (bf16[192,256]{1,0:T(8,128)(2,1)}, bf16[192,256]{1,0:T(8,128)(2,1)S(1)}, u32[]{:S(2)}, u32[]{:S(2)}) collective-permute-start(bf16[192,256]{1,0:T(8,128)(2,1)} %reduce-scatter.2.cloned.1.call-done), channel_id=1, source_target_pairs={{0,0},{8,256},{256,8},{264,264},{1,1},{9,257},{257,9},{265,265},{2... | collective-permute-start | bytes 294920 | tf_op jit(solution)/shard_map/ppermute | solution.py:199
Sparse Core Ops, SparseCore 0:
  10.1 69.0 all-gather.3
  93.8 68.1 reduce-scatter.1

commit v14 on v13

--- a/solution.py
+++ b/solution.py
@@ -214,7 +214,8 @@
     far = jnp.concatenate([along(column[:2], 2), along(column[2:], -2)])
     blocks = [column, after, far, before]
     shift = (4 - lax.axis_index("zb")) % 4
-    return lax.dynamic_slice_in_dim(jnp.stack(blocks + blocks), shift, 4, axis=0)
+    rows = lax.dynamic_slice_in_dim(jnp.stack(blocks + blocks), shift, 4, axis=0)
+    return rows, before, after
 
 
 def sum_over(array, axis, count):
@@ -231,8 +232,8 @@
     attn_same = turned(attn)
     attn_other = swap_y(attn, lambda low, up: (up, 1 - low))
     own_rows, attn_other = lax.optimization_barrier((turned(out_weight), attn_other))
-    weights = gather_rows(own_rows)
-    grads, weights = lax.optimization_barrier((grads, weights))
+    weights, before, after = gather_rows(own_rows)
+    grads, _, _ = lax.optimization_barrier((grads, before, after))
 
     wgrad = weight_product(high, grads, attn_same, attn_other)
     shard = lax.psum_scatter(wgrad, Z, scatter_dimension=0, tiled=True)

time: 177 us -> 191 us (1.079)
  waiting for transfers between devices: 28.8 us -> 41.6 us
    ppermute x4, waiting for transfers between devices: 6.2 us -> 14.8 us  [along(): return lax.ppermute(array, Z, [(z, (z + step) % 16) for z in range(16)])]
    all_gather x1, waiting for transfers between devices: 0.01 us -> 5.04 us  [per_device(): grads = lax.all_gather(grad_out, ('yl', 'x', 'c'), axis=0)]
    reduce_scatter x1, waiting for transfers between devices: 3.73 us -> 0.01 us  [per_device(): shard = lax.psum_scatter(wgrad, Z, scatter_dimension=0, tiled=True)]
    ppermute x6, waiting for transfers between devices: 18.2 us -> 21.1 us  [swap_y(): return lax.ppermute(array, ('yl', 'yh'), pairs)]
  transfers between devices with their start and end apart: 12 -> 12, of which waited for: 6 -> 8; matrix products, arithmetic and copies ran while one was open for 2% -> 2% of each run, Pallas kernels for 11% -> 11%
where the time goes in v14:
time: 191 us; the launch traced here: 190 us
  blocking collectives  65.7 us (34%)
  waiting for transfers between devices  41.6 us (22%)
  starting transfers between devices  36.5 us (19%)
  Pallas kernels  27.2 us (14%)
  between operations  14.2 us (7%)
  local copies, waits for them, and re-layouts  3.69 us (2%)
    all_to_all x2, blocking collectives, sum_over(): lax.all_to_all(jnp.broadcast_to(array[None], (count,) + array.shape), axi...  35.3 us
    all_gather x1, blocking collectives, gather_rows(): column = lax.all_gather(own_rows, 'za', axis=0)  30.4 us
    ppermute x6, starting transfers between devices, swap_y(): return lax.ppermute(array, ('yl', 'yh'), pairs)  21.9 us
    ppermute x6, waiting for transfers between devices, swap_y(): return lax.ppermute(array, ('yl', 'yh'), pairs)  21.1 us
    ppermute x4, waiting for transfers between devices, along(): return lax.ppermute(array, Z, [(z, (z + step) % 16) for z in range(16)])  14.8 us
    ppermute x4, starting transfers between devices, along(): return lax.ppermute(array, Z, [(z, (z + step) % 16) for z in range(16)])  14.5 us
    pallas_call x1, Pallas kernels, token_product(): pl.pallas_call(token_kernel, grid_spec=pltpu.PrefetchScalarGridSpec(num_s...  7.66 us
    pallas_call x1, Pallas kernels, backward(): pl.pallas_call(backward_kernel, grid=(tokens // PATCH,), in_specs=[block]...  7.37 us
  transfers between devices with their start and end apart: 12, of which 8 were waited for; matrix products, arithmetic and copies ran while one was open for 2% of the time, Pallas kernels for 11%

profile of v14, /device:TPU:8, one launch (start us, length us, event | category | flops | bytes accessed | tf_op | source)
XLA Modules:
  0.0 190.4 jit_solution(2384010269935102981)
XLA Ops:
  7.2 0.0 all-gather.4.cloned.1.call-start
  7.2 0.7 all-gather.4.cloned.1.call-update
  7.9 0.0 reduce-scatter.2.cloned.1.call-start
  7.9 5.1 %shard_map.101 = bf16[768,256]{1,0:T(8,128)(2,1)} custom-call(bf16[768,256]{1,0:T(8,128)(2,1)} %q_ref.3, bf16[768,256]{1,0:T(8,128)(2,1)} %k_ref.3, bf16[768,256]{1,0:T(8,128)(2,1)} %v_ref.3, f32[2,128]{1,0:T(2,128)} %gains_ref.3), custom_call_target="tpu_custom_call" | custom-call | tf_op jit(solution)/shard_map/pallas_call | solution.py:56
  13.0 7.7 %collective-permute-start.1 = (bf16[768,256]{1,0:T(8,128)(2,1)}, bf16[768,256]{1,0:T(8,128)(2,1)S(1)}, u32[]{:S(2)}, u32[]{:S(2)}) collective-permute-start(bf16[768,256]{1,0:T(8,128)(2,1)} %shard_map.101), channel_id=1, source_target_pairs={{0,8},{8,264},{256,0},{264,256},{1,9},{9,265},{257,1},{265,257},{2... | collective-permute-start | bytes 1179656 | tf_op jit(solution)/shard_map/ppermute | solution.py:199
  20.8 1.9 %collective-permute-start = (bf16[192,256]{1,0:T(8,128)(2,1)}, bf16[192,256]{1,0:T(8,128)(2,1)S(1)}, u32[]{:S(2)}, u32[]{:S(2)}) collective-permute-start(bf16[192,256]{1,0:T(8,128)(2,1)} %param.10), channel_id=1, source_target_pairs={{0,0},{8,256},{256,8},{264,264},{1,1},{9,257},{257,9},{265,265},{2... | collective-permute-start | bytes 294920 | tf_op jit(solution)/shard_map/ppermute | solution.py:199
  22.7 6.9 %collective-permute-done = bf16[192,256]{1,0:T(8,128)(2,1)S(1)} collective-permute-done((bf16[192,256]{1,0:T(8,128)(2,1)}, bf16[192,256]{1,0:T(8,128)(2,1)S(1)}, u32[]{:S(2)}, u32[]{:S(2)}) %collective-permute-start) | collective-permute-done | bytes 98336 | tf_op jit(solution)/shard_map/ppermute | solution.py:199
  29.6 0.0 collective-permute-done.1.other_ref
  29.6 0.0 copy-start
  29.6 30.4 %all-gather.1 = bf16[768,256]{1,0:T(8,128)(2,1)S(1)} all-gather(bf16[192,256]{1,0:T(8,128)(2,1)S(1)} %collective-permute-done), channel_id=3, replica_groups=mesh['yl'=2,'za'=4,'zb'=4,'yh'=2,'x'=4,'c'=2] {'za'}, dimensions={0}, use_global_device_ids=true | all-gather | bytes 491520 | tf_op jit(solution)/shard_map/all_gather | solution.py:211
  60.0 3.1 %collective-permute-start.3 = (bf16[4,192,256]{2,1,0:T(8,128)(2,1)S(1)}, bf16[4,192,256]{2,1,0:T(8,128)(2,1)S(1)}, u32[]{:S(2)}, u32[]{:S(2)}) collective-permute-start(bf16[4,192,256]{2,1,0:T(8,128)(2,1)S(1)} %bitcast.20), channel_id=1, source_target_pairs={{0,240},{16,0},{32,16},{48,32},{64,48},{80,64},{96,80},{112,96},{1... | collective-permute-start | bytes 1179656 | tf_op jit(solution)/shard_map/ppermute | solution.py:207
  63.1 2.7 %collective-permute-start.2 = (bf16[4,192,256]{2,1,0:T(8,128)(2,1)S(1)}, bf16[4,192,256]{2,1,0:T(8,128)(2,1)S(1)}, u32[]{:S(2)}, u32[]{:S(2)}) collective-permute-start(bf16[4,192,256]{2,1,0:T(8,128)(2,1)S(1)} %bitcast.21), channel_id=1, source_target_pairs={{0,16},{16,32},{32,48},{48,64},{64,80},{80,96},{96,112},{112,128},... | collective-permute-start | bytes 1179656 | tf_op jit(solution)/shard_map/ppermute | solution.py:207
  65.9 4.2 %collective-permute-start.6 = (bf16[768,256]{1,0:T(8,128)(2,1)}, bf16[768,256]{1,0:T(8,128)(2,1)S(1)}, u32[]{:S(2)}, u32[]{:S(2)}) collective-permute-start(bf16[768,256]{1,0:T(8,128)(2,1)} %shard_map.101), channel_id=1, source_target_pairs={{0,0},{8,256},{256,8},{264,264},{1,1},{9,257},{257,9},{265,265},{2... | collective-permute-start | bytes 1179656 | tf_op jit(solution)/shard_map/ppermute | solution.py:199
  70.0 0.0 collective-permute-done.3
  70.1 4.2 %collective-permute-done.2 = bf16[4,192,256]{2,1,0:T(8,128)(2,1)S(1)} collective-permute-done((bf16[4,192,256]{2,1,0:T(8,128)(2,1)S(1)}, bf16[4,192,256]{2,1,0:T(8,128)(2,1)S(1)}, u32[]{:S(2)}, u32[]{:S(2)}) %collective-permute-start.2) | collective-permute-done | bytes 393248 | tf_op jit(solution)/shard_map/ppermute | solution.py:207
  74.2 5.0 %all-gather.4.cloned.1.call-done = bf16[12288,384]{1,0:T(8,128)(2,1)} async-done(((bf16[768,384]{1,0:T(8,128)(2,1)}), bf16[12288,384]{1,0:T(8,128)(2,1)}) %all-gather.4.cloned.1.call-update) | async-done | bytes 9437200 | tf_op jit(solution)/shard_map/all_gather | solution.py:228
  79.3 0.0 collective-permute-done.6.same_ref
  79.3 0.0 copy-start.1
  79.3 0.0 copy-done
  79.3 0.7 copy-done.1
  80.0 7.1 %shard_map.102 = bf16[3072,256]{1,0:T(8,128)(2,1)} custom-call(s32[1]{0:T(128)} %bitcast.high_ref, bf16[2,4,2,768,384]{4,3,2,1,0:T(8,128)(2,1)} %bitcast.18, bf16[768,256]{1,0:T(8,128)(2,1)} %copy-done.1, bf16[768,256]{1,0:T(8,128)(2,1)} %copy-done), custom_call_target="tpu_custom_call" | custom-call | flops 2415919104 | bytes 11010048 | tf_op jit(solution)/shard_map/pallas_call | solution.py:129
  87.1 0.0 reduce-scatter.2.cloned.1.call-update
  87.2 4.5 %collective-permute-start.4 = (bf16[2,192,256]{2,1,0:T(8,128)(2,1)S(1)}, bf16[2,192,256]{2,1,0:T(8,128)(2,1)S(1)}, u32[]{:S(2)}, u32[]{:S(2)}) collective-permute-start(bf16[2,192,256]{2,1,0:T(8,128)(2,1)S(1)} %bitcast.25), channel_id=1, source_target_pairs={{0,32},{16,48},{32,64},{48,80},{64,96},{80,112},{96,128},{112,144}... | collective-permute-start | bytes 589832 | tf_op jit(solution)/shard_map/ppermute | solution.py:207
  91.6 4.2 %collective-permute-start.5 = (bf16[2,192,256]{2,1,0:T(8,128)(2,1)S(1)}, bf16[2,192,256]{2,1,0:T(8,128)(2,1)S(1)}, u32[]{:S(2)}, u32[]{:S(2)}) collective-permute-start(bf16[2,192,256]{2,1,0:T(8,128)(2,1)S(1)} %bitcast.24), channel_id=1, source_target_pairs={{0,224},{16,240},{32,0},{48,16},{64,32},{80,48},{96,64},{112,80},{... | collective-permute-start | bytes 589832 | tf_op jit(solution)/shard_map/ppermute | solution.py:207
  95.9 5.2 %collective-permute-done.4 = bf16[2,192,256]{2,1,0:T(8,128)(2,1)S(1)} collective-permute-done((bf16[2,192,256]{2,1,0:T(8,128)(2,1)S(1)}, bf16[2,192,256]{2,1,0:T(8,128)(2,1)S(1)}, u32[]{:S(2)}, u32[]{:S(2)}) %collective-permute-start.4) | collective-permute-done | bytes 196640 | tf_op jit(solution)/shard_map/ppermute | solution.py:207
  101.2 5.5 %collective-permute-done.5 = bf16[2,192,256]{2,1,0:T(8,128)(2,1)S(1)} collective-permute-done((bf16[2,192,256]{2,1,0:T(8,128)(2,1)S(1)}, bf16[2,192,256]{2,1,0:T(8,128)(2,1)S(1)}, u32[]{:S(2)}, u32[]{:S(2)}) %collective-permute-start.5) | collective-permute-done | bytes 196640 | tf_op jit(solution)/shard_map/ppermute | solution.py:207
  106.8 1.3 constant_dynamic-slice_fusion.weight_ref
  108.1 7.7 %shard_map.103 = (bf16[768,256]{1,0:T(8,128)(2,1)}, bf16[768,256]{1,0:T(8,128)(2,1)}) custom-call(s32[1]{0:T(128)} %bitcast.high_ref, bf16[2,4,2,768,384]{4,3,2,1,0:T(8,128)(2,1)} %bitcast.19, bf16[4,4,192,256]{3,2,1,0:T(8,128)(2,1)} %constant_dynamic-slice_fusion.weight_ref), custom_call_target="tpu_custom_call" | custom-call | flops 2415919104 | bytes 11010048 | tf_op jit(solution)/shard_map/pallas_call | solution.py:171
  115.8 3.3 %collective-permute-start.7 = (bf16[768,256]{1,0:T(8,128)(2,1)}, bf16[768,256]{1,0:T(8,128)(2,1)S(1)}, u32[]{:S(2)}, u32[]{:S(2)}) collective-permute-start(bf16[768,256]{1,0:T(8,128)(2,1)} %get-tuple-element.21), channel_id=1, source_target_pairs={{0,0},{8,256},{256,8},{264,264},{1,1},{9,257},{257,9},{265,265},{2... | collective-permute-start | bytes 1179656 | tf_op jit(solution)/shard_map/ppermute | solution.py:199
  119.1 2.4 %collective-permute-start.8 = (bf16[768,256]{1,0:T(8,128)(2,1)}, bf16[768,256]{1,0:T(8,128)(2,1)S(1)}, u32[]{:S(2)}, u32[]{:S(2)}) collective-permute-start(bf16[768,256]{1,0:T(8,128)(2,1)} %get-tuple-element.22), channel_id=1, source_target_pairs={{0,256},{8,0},{256,264},{264,8},{1,257},{9,1},{257,265},{265,9},{2... | collective-permute-start | bytes 1179656 | tf_op jit(solution)/shard_map/ppermute | solution.py:199
  121.5 6.9 %collective-permute-done.7.one_ref = bf16[768,256]{1,0:T(8,128)(2,1)S(1)} collective-permute-done((bf16[768,256]{1,0:T(8,128)(2,1)}, bf16[768,256]{1,0:T(8,128)(2,1)S(1)}, u32[]{:S(2)}, u32[]{:S(2)}) %collective-permute-start.7) | collective-permute-done | bytes 393248 | tf_op jit(solution)/shard_map/ppermute | solution.py:199
  128.4 0.0 copy-start.2
  128.4 3.0 %collective-permute-done.8.two_ref = bf16[768,256]{1,0:T(8,128)(2,1)S(1)} collective-permute-done((bf16[768,256]{1,0:T(8,128)(2,1)}, bf16[768,256]{1,0:T(8,128)(2,1)S(1)}, u32[]{:S(2)}, u32[]{:S(2)}) %collective-permute-start.8) | collective-permute-done | bytes 393248 | tf_op jit(solution)/shard_map/ppermute | solution.py:199
  131.4 0.0 copy-done.2
  131.4 0.0 copy-start.3
  131.4 0.8 copy-done.3
  132.1 7.4 %shard_map.104 = (bf16[768,256]{1,0:T(8,128)(2,1)}, bf16[768,256]{1,0:T(8,128)(2,1)}, bf16[768,256]{1,0:T(8,128)(2,1)}, f32[2,128]{1,0:T(2,128)}) custom-call(bf16[768,256]{1,0:T(8,128)(2,1)} %q_ref.3, bf16[768,256]{1,0:T(8,128)(2,1)} %k_ref.3, bf16[768,256]{1,0:T(8,128)(2,1)} %v_ref.3, bf16[768,256]{1,0:T(8,128)(2,1)} %copy-done.2, ...), custom_call_target="tpu_custom_call" | custom-call | tf_op jit(solution)/shard_map/pallas_call | solution.py:102
  139.5 0.7 broadcast_in_dim.4
  140.2 13.0 %all_to_all.10 = f32[32,2,128]{2,1,0:T(2,128)S(1)} all-to-all(f32[32,2,128]{2,1,0:T(2,128)S(1)} %broadcast_in_dim.4), channel_id=1, replica_groups=mesh['yl'=2,'za'=4,'zb'=4,'yh'=2,'x'=4,'c'=2] {'yl','yh','x','c'}, dimensions={0} | all-to-all | bytes 65536 | tf_op jit(solution)/shard_map/all_to_all | solution.py:222
  153.3 22.3 %all_to_all.11 = f32[16,2,128]{2,1,0:T(2,128)S(1)} all-to-all(f32[16,2,128]{2,1,0:T(2,128)S(1)} %broadcast_in_dim.5), channel_id=1, replica_groups=mesh['yl'=2,'za'=4,'zb'=4,'yh'=2,'x'=4,'c'=2] {'za','zb'}, dimensions={0} | all-to-all | bytes 32768 | tf_op jit(solution)/shard_map/all_to_all | solution.py:222
  175.5 0.6 reduce_sum.19
  176.1 0.0 reduce-scatter.2.cloned.1.call-done
  176.1 2.4 %collective-permute-start.9 = (bf16[192,256]{1,0:T(8,128)(2,1)}, bf16[192,256]{1,0:T(8,128)(2,1)S(1)}, u32[]{:S(2)}, u32[]{:S(2)}) collective-permute-start(bf16[192,256]{1,0:T(8,128)(2,1)} %reduce-scatter.2.cloned.1.call-done), channel_id=1, source_target_pairs={{0,0},{8,256},{256,8},{264,264},{1,1},{9,257},{257,9},{265,265},{2... | collective-permute-start | bytes 294920 | tf_op jit(solution)/shard_map/ppermute | solution.py:199
  178.6 4.3 %collective-permute-done.9 = bf16[192,256]{1,0:T(8,128)(2,1)S(1)} collective-permute-done((bf16[192,256]{1,0:T(8,128)(2,1)}, bf16[192,256]{1,0:T(8,128)(2,1)S(1)}, u32[]{:S(2)}, u32[]{:S(2)}) %collective-permute-start.9) | collective-permute-done | bytes 98336 | tf_op jit(solution)/shard_map/ppermute | solution.py:199
  182.8 0.7 convert_element_type.3
  (11 shorter events, 0.3 us)
Async XLA Ops:
  7.2 72.1 %all-gather.4.cloned.1.call-start = ((), (), s32[]{:S(2)}) async-start(), calls=%async_computation.4 | async-start | bytes 10027008 | tf_op jit(solution)/shard_map/all_gather | solution.py:228
  7.9 168.2 %reduce-scatter.2.cloned.1.call-start = ((), (), s32[]{:S(2)}) async-start(), calls=%async_computation.3 | async-start | bytes 1671168 | tf_op jit(solution)/shard_map/reduce_scatter | solution.py:239
  13.0 16.6 %collective-permute-start.1 = (bf16[768,256]{1,0:T(8,128)(2,1)}, bf16[768,256]{1,0:T(8,128)(2,1)S(1)}, u32[]{:S(2)}, u32[]{:S(2)}) collective-permute-start(bf16[768,256]{1,0:T(8,128)(2,1)} %shard_map.101), channel_id=1, source_target_pairs={{0,8},{8,264},{256,0},{264,256},{1,9},{9,265},{257,1},{265,257},{2... | collective-permute-start | bytes 1179656 | tf_op jit(solution)/shard_map/ppermute | solution.py:199
  20.8 8.8 %collective-permute-start = (bf16[192,256]{1,0:T(8,128)(2,1)}, bf16[192,256]{1,0:T(8,128)(2,1)S(1)}, u32[]{:S(2)}, u32[]{:S(2)}) collective-permute-start(bf16[192,256]{1,0:T(8,128)(2,1)} %param.10), channel_id=1, source_target_pairs={{0,0},{8,256},{256,8},{264,264},{1,1},{9,257},{257,9},{265,265},{2... | collective-permute-start | bytes 294920 | tf_op jit(solution)/shard_map/ppermute | solution.py:199
  29.6 49.7 %copy-start = (bf16[768,256]{1,0:T(8,128)(2,1)}, bf16[768,256]{1,0:T(8,128)(2,1)S(1)}, u32[]{:S(2)}) copy-start(bf16[768,256]{1,0:T(8,128)(2,1)S(1)} %collective-permute-done.1.other_ref) | copy-start | bytes 1179652
  60.0 10.0 %collective-permute-start.3 = (bf16[4,192,256]{2,1,0:T(8,128)(2,1)S(1)}, bf16[4,192,256]{2,1,0:T(8,128)(2,1)S(1)}, u32[]{:S(2)}, u32[]{:S(2)}) collective-permute-start(bf16[4,192,256]{2,1,0:T(8,128)(2,1)S(1)} %bitcast.20), channel_id=1, source_target_pairs={{0,240},{16,0},{32,16},{48,32},{64,48},{80,64},{96,80},{112,96},{1... | collective-permute-start | bytes 1179656 | tf_op jit(solution)/shard_map/ppermute | solution.py:207
  63.1 11.1 %collective-permute-start.2 = (bf16[4,192,256]{2,1,0:T(8,128)(2,1)S(1)}, bf16[4,192,256]{2,1,0:T(8,128)(2,1)S(1)}, u32[]{:S(2)}, u32[]{:S(2)}) collective-permute-start(bf16[4,192,256]{2,1,0:T(8,128)(2,1)S(1)} %bitcast.21), channel_id=1, source_target_pairs={{0,16},{16,32},{32,48},{48,64},{64,80},{80,96},{96,112},{112,128},... | collective-permute-start | bytes 1179656 | tf_op jit(solution)/shard_map/ppermute | solution.py:207
  65.9 13.4 %collective-permute-start.6 = (bf16[768,256]{1,0:T(8,128)(2,1)}, bf16[768,256]{1,0:T(8,128)(2,1)S(1)}, u32[]{:S(2)}, u32[]{:S(2)}) collective-permute-start(bf16[768,256]{1,0:T(8,128)(2,1)} %shard_map.101), channel_id=1, source_target_pairs={{0,0},{8,256},{256,8},{264,264},{1,1},{9,257},{257,9},{265,265},{2... | collective-permute-start | bytes 1179656 | tf_op jit(solution)/shard_map/ppermute | solution.py:199
  79.3 0.7 copy-start.1
  87.2 14.0 %collective-permute-start.4 = (bf16[2,192,256]{2,1,0:T(8,128)(2,1)S(1)}, bf16[2,192,256]{2,1,0:T(8,128)(2,1)S(1)}, u32[]{:S(2)}, u32[]{:S(2)}) collective-permute-start(bf16[2,192,256]{2,1,0:T(8,128)(2,1)S(1)} %bitcast.25), channel_id=1, source_target_pairs={{0,32},{16,48},{32,64},{48,80},{64,96},{80,112},{96,128},{112,144}... | collective-permute-start | bytes 589832 | tf_op jit(solution)/shard_map/ppermute | solution.py:207
  91.6 15.0 %collective-permute-start.5 = (bf16[2,192,256]{2,1,0:T(8,128)(2,1)S(1)}, bf16[2,192,256]{2,1,0:T(8,128)(2,1)S(1)}, u32[]{:S(2)}, u32[]{:S(2)}) collective-permute-start(bf16[2,192,256]{2,1,0:T(8,128)(2,1)S(1)} %bitcast.24), channel_id=1, source_target_pairs={{0,224},{16,240},{32,0},{48,16},{64,32},{80,48},{96,64},{112,80},{... | collective-permute-start | bytes 589832 | tf_op jit(solution)/shard_map/ppermute | solution.py:207
  115.8 12.6 %collective-permute-start.7 = (bf16[768,256]{1,0:T(8,128)(2,1)}, bf16[768,256]{1,0:T(8,128)(2,1)S(1)}, u32[]{:S(2)}, u32[]{:S(2)}) collective-permute-start(bf16[768,256]{1,0:T(8,128)(2,1)} %get-tuple-element.21), channel_id=1, source_target_pairs={{0,0},{8,256},{256,8},{264,264},{1,1},{9,257},{257,9},{265,265},{2... | collective-permute-start | bytes 1179656 | tf_op jit(solution)/shard_map/ppermute | solution.py:199
  119.1 12.3 %collective-permute-start.8 = (bf16[768,256]{1,0:T(8,128)(2,1)}, bf16[768,256]{1,0:T(8,128)(2,1)S(1)}, u32[]{:S(2)}, u32[]{:S(2)}) collective-permute-start(bf16[768,256]{1,0:T(8,128)(2,1)} %get-tuple-element.22), channel_id=1, source_target_pairs={{0,256},{8,0},{256,264},{264,8},{1,257},{9,1},{257,265},{265,9},{2... | collective-permute-start | bytes 1179656 | tf_op jit(solution)/shard_map/ppermute | solution.py:199
  128.4 3.0 %copy-start.2 = (bf16[768,256]{1,0:T(8,128)(2,1)}, bf16[768,256]{1,0:T(8,128)(2,1)S(1)}, u32[]{:S(2)}) copy-start(bf16[768,256]{1,0:T(8,128)(2,1)S(1)} %collective-permute-done.7.one_ref) | copy-start | bytes 1179652
  131.4 0.8 copy-start.3
  176.1 6.7 %collective-permute-start.9 = (bf16[192,256]{1,0:T(8,128)(2,1)}, bf16[192,256]{1,0:T(8,128)(2,1)S(1)}, u32[]{:S(2)}, u32[]{:S(2)}) collective-permute-start(bf16[192,256]{1,0:T(8,128)(2,1)} %reduce-scatter.2.cloned.1.call-done), channel_id=1, source_target_pairs={{0,0},{8,256},{256,8},{264,264},{1,1},{9,257},{257,9},{265,265},{2... | collective-permute-start | bytes 294920 | tf_op jit(solution)/shard_map/ppermute | solution.py:199
Sparse Core Ops, SparseCore 0:
  10.1 69.0 all-gather.3
  87.2 72.8 reduce-scatter.1

commit v15 on v13

--- a/solution.py
+++ b/solution.py
@@ -9,9 +9,9 @@
 PATCH = 256
 EPSILON = 1e-06
 SCALE = HD ** (-0.5)
-AXES = ("yl", "za", "zb", "yh", "x", "c")
-SIZES = (2, 4, 4, 2, 4, 2)
-Z = ("za", "zb")
+AXES = ("yl", "za", "zm", "zl", "yh", "x", "c")
+SIZES = (2, 4, 2, 2, 2, 4, 2)
+Z = ("za", "zm", "zl")
 VMEM_LIMIT = 56 * 1024 * 1024
 
 
@@ -147,7 +147,6 @@
 def token_kernel(high_ref, grad_ref, weight_ref, same_ref, other_ref, total):
     step = pl.program_id(0)
     high = high_ref[0]
-    weights = weight_ref[...].reshape(-1, weight_ref.shape[3])
     width = grad_ref.shape[4]
 
     @pl.when(step == 0)
@@ -155,8 +154,9 @@
         total[...] = jnp.zeros_like(total)
 
     for index, low in enumerate((high, 1 - high)):
-        term = product(grad_ref[low, 0, 0], weights[:width], 1, 0)
-        total[index] += term + product(grad_ref[low, 0, 1], weights[width:], 1, 0)
+        term = product(grad_ref[low, 0, 0], weight_ref[:, 0].reshape(width, -1), 1, 0)
+        term += product(grad_ref[low, 0, 1], weight_ref[:, 1].reshape(width, -1), 1, 0)
+        total[index] += term
 
     @pl.when(step == pl.num_programs(0) - 1)
     def _():
@@ -166,7 +166,7 @@
 
 def token_product(high, grads, weights):
     _, blocks, _, tokens, _ = grads.shape
-    fours, _, rows, heads = weights.shape
+    _, _, rows, heads = weights.shape
     out = jax.ShapeDtypeStruct((tokens, heads), jnp.bfloat16)
     return pl.pallas_call(
         token_kernel,
@@ -175,7 +175,7 @@
             grid=(blocks,),
             in_specs=[
                 grad_block(grads),
-                pl.BlockSpec((fours, 1, rows, heads), lambda x, high: (0, x, 0, 0)),
+                pl.BlockSpec((2, 2, rows, heads), lambda x, high: (0, x, 0, 0)),
             ],
             out_specs=[pl.BlockSpec((tokens, heads), lambda x, high: (0, 0))] * 2,
             scratch_shapes=[pltpu.VMEM((2, tokens, heads), jnp.float32)],
@@ -208,13 +208,10 @@
 
 
 def gather_rows(own_rows):
-    column = lax.all_gather(own_rows, "za", axis=0)
-    before = along(column, 1)
-    after = along(column, -1)
-    far = jnp.concatenate([along(column[:2], 2), along(column[2:], -2)])
-    blocks = [column, after, far, before]
-    shift = (4 - lax.axis_index("zb")) % 4
-    return lax.dynamic_slice_in_dim(jnp.stack(blocks + blocks), shift, 4, axis=0)
+    same = lax.all_gather(own_rows, ("za", "zm"), axis=0)
+    other = jnp.concatenate([along(same[:4], 1), along(same[4:], -1)])
+    blocks = jnp.stack([same, other, same])
+    return lax.dynamic_slice_in_dim(blocks, lax.axis_index("zl"), 2, axis=0)
 
 
 def sum_over(array, axis, count):
@@ -252,7 +249,7 @@
 
 def solution(mesh):
     fine = Mesh(mesh.devices.reshape(SIZES), AXES)
-    spec = P(("yl", "za", "zb"), ("yh", "x", "c"))
+    spec = P(("yl", "za", "zm", "zl"), ("yh", "x", "c"))
     return jax.shard_map(
         per_device,
         mesh=fine,

time: 177 us -> 177 us (level)
  blocking collectives: 65.8 us -> 73.1 us
  starting transfers between devices: 35.1 us -> 29.4 us
  waiting for transfers between devices: 28.8 us -> 26.6 us
  other arithmetic: 1.38 us -> 3.42 us
    all_gather x1, blocking collectives: 30.4 us -> 38.1 us  [gather_rows(): same = lax.all_gather(own_rows, ('za', 'zm'), axis=0)]
    ppermute x4 -> x2, starting transfers between devices: 14.7 us -> 7.05 us  [along(): return lax.ppermute(array, Z, [(z, (z + step) % 16) for z in range(16)])]
    ppermute x4 -> x2, waiting for transfers between devices: 6.2 us -> 3.21 us  [along(): return lax.ppermute(array, Z, [(z, (z + step) % 16) for z in range(16)])]
    another operation x0 -> x2, other arithmetic: none -> 2.1 us  [gather_rows(): blocks = jnp.stack([same, other, same])]
    ppermute x6, starting transfers between devices: 20.4 us -> 22.2 us  [swap_y(): return lax.ppermute(array, ('yl', 'yh'), pairs)]
  transfers between devices with their start and end apart: 12 -> 10, of which waited for: 6 -> 8; matrix products, arithmetic and copies ran while one was open for 2% -> 2% of each run, Pallas kernels for 11% -> 11%
where the time goes in v15:
time: 177 us; the launch traced here: 176 us
  blocking collectives  73.1 us (41%)
  starting transfers between devices  29.4 us (17%)
  Pallas kernels  27.2 us (15%)
  waiting for transfers between devices  26.6 us (15%)
  between operations  14.2 us (8%)
  other arithmetic  3.42 us (2%)
  local copies, waits for them, and re-layouts  2.27 us (1%)
    all_gather x1, blocking collectives, gather_rows(): same = lax.all_gather(own_rows, ('za', 'zm'), axis=0)  38.1 us
    all_to_all x2, blocking collectives, sum_over(): lax.all_to_all(jnp.broadcast_to(array[None], (count,) + array.shape), axi...  35 us
    ppermute x6, starting transfers between devices, swap_y(): return lax.ppermute(array, ('yl', 'yh'), pairs)  22.2 us
    ppermute x6, waiting for transfers between devices, swap_y(): return lax.ppermute(array, ('yl', 'yh'), pairs)  18.9 us
    pallas_call x1, Pallas kernels, token_product(): pl.pallas_call(token_kernel, grid_spec=pltpu.PrefetchScalarGridSpec(num_s...  7.64 us
    pallas_call x1, Pallas kernels, backward(): pl.pallas_call(backward_kernel, grid=(tokens // PATCH,), in_specs=[block]...  7.37 us
    pallas_call x1, Pallas kernels, weight_product(): pl.pallas_call(weight_kernel, grid_spec=pltpu.PrefetchScalarGridSpec(num_...  7.1 us
    ppermute x2, starting transfers between devices, along(): return lax.ppermute(array, Z, [(z, (z + step) % 16) for z in range(16)])  7.05 us
  transfers between devices with their start and end apart: 10, of which 8 were waited for; matrix products, arithmetic and copies ran while one was open for 2% of the time, Pallas kernels for 11%

profile of v15, /device:TPU:8, one launch (start us, length us, event | category | flops | bytes accessed | tf_op | source)
XLA Modules:
  0.0 176.1 jit_solution(6120173593159695968)
XLA Ops:
  7.2 0.0 copy-start.5
  7.2 0.0 all-gather.4.cloned.1.call-start
  7.2 0.7 all-gather.4.cloned.1.call-update
  7.9 0.0 reduce-scatter.2.cloned.1.call-start
  8.0 5.1 %shard_map.101 = bf16[768,256]{1,0:T(8,128)(2,1)} custom-call(bf16[768,256]{1,0:T(8,128)(2,1)} %q_ref.3, bf16[768,256]{1,0:T(8,128)(2,1)} %k_ref.3, bf16[768,256]{1,0:T(8,128)(2,1)} %v_ref.3, f32[2,128]{1,0:T(2,128)} %gains_ref.3), custom_call_target="tpu_custom_call" | custom-call | tf_op jit(solution)/shard_map/pallas_call | solution.py:56
  13.0 0.0 copy-start.4
  13.0 7.9 %collective-permute-start.1 = (bf16[768,256]{1,0:T(8,128)(2,1)}, bf16[768,256]{1,0:T(8,128)(2,1)S(1)}, u32[]{:S(2)}, u32[]{:S(2)}) collective-permute-start(bf16[768,256]{1,0:T(8,128)(2,1)} %shard_map.101), channel_id=1, source_target_pairs={{0,8},{8,264},{256,0},{264,256},{1,9},{9,265},{257,1},{265,257},{2... | collective-permute-start | bytes 1179656 | tf_op jit(solution)/shard_map/ppermute | solution.py:199
  20.9 0.0 copy-done.5
  20.9 1.9 %collective-permute-start = (bf16[192,256]{1,0:T(8,128)(2,1)S(1)}, bf16[192,256]{1,0:T(8,128)(2,1)S(1)}, u32[]{:S(2)}, u32[]{:S(2)}) collective-permute-start(bf16[192,256]{1,0:T(8,128)(2,1)S(1)} %copy-done.5), channel_id=1, source_target_pairs={{0,0},{8,256},{256,8},{264,264},{1,1},{9,257},{257,9},{265,265},{2... | collective-permute-start | bytes 294920 | tf_op jit(solution)/shard_map/ppermute | solution.py:199
  22.8 6.9 %collective-permute-done = bf16[192,256]{1,0:T(8,128)(2,1)S(1)} collective-permute-done((bf16[192,256]{1,0:T(8,128)(2,1)S(1)}, bf16[192,256]{1,0:T(8,128)(2,1)S(1)}, u32[]{:S(2)}, u32[]{:S(2)}) %collective-permute-start) | collective-permute-done | bytes 98336 | tf_op jit(solution)/shard_map/ppermute | solution.py:199
  29.7 0.0 collective-permute-done.1.other_ref
  29.7 0.0 copy-start
  29.7 38.1 %all-gather.1 = bf16[1536,256]{1,0:T(8,128)(2,1)S(1)} all-gather(bf16[192,256]{1,0:T(8,128)(2,1)S(1)} %collective-permute-done), channel_id=3, replica_groups=mesh['yl'=2,'za'=4,'zm'=2,'zl'=2,'yh'=2,'x'=4,'c'=2] {'za','zm'}, dimensions={0}, use_global_device_ids=true | all-gather | bytes 884736 | tf_op jit(solution)/shard_map/all_gather | solution.py:211
  67.9 0.1 fusion.2
  67.9 4.3 %collective-permute-start.2 = (bf16[4,192,256]{2,1,0:T(8,128)(2,1)S(1)}, bf16[4,192,256]{2,1,0:T(8,128)(2,1)S(1)}, u32[]{:S(2)}, u32[]{:S(2)}) collective-permute-start(bf16[4,192,256]{2,1,0:T(8,128)(2,1)S(1)} %bitcast.11), channel_id=1, source_target_pairs={{0,16},{16,32},{32,48},{48,64},{64,80},{80,96},{96,112},{112,128},... | collective-permute-start | bytes 1179656 | tf_op jit(solution)/shard_map/ppermute | solution.py:207
  72.2 2.8 %collective-permute-start.3 = (bf16[4,192,256]{2,1,0:T(8,128)(2,1)S(1)}, bf16[4,192,256]{2,1,0:T(8,128)(2,1)S(1)}, u32[]{:S(2)}, u32[]{:S(2)}) collective-permute-start(bf16[4,192,256]{2,1,0:T(8,128)(2,1)S(1)} %bitcast.10), channel_id=1, source_target_pairs={{0,240},{16,0},{32,16},{48,32},{64,48},{80,64},{96,80},{112,96},{1... | collective-permute-start | bytes 1179656 | tf_op jit(solution)/shard_map/ppermute | solution.py:207
  75.0 0.0 copy-done.4
  75.0 3.6 %collective-permute-start.4 = (bf16[768,256]{1,0:T(8,128)(2,1)S(1)}, bf16[768,256]{1,0:T(8,128)(2,1)S(1)}, u32[]{:S(2)}, u32[]{:S(2)}) collective-permute-start(bf16[768,256]{1,0:T(8,128)(2,1)S(1)} %copy-done.4), channel_id=1, source_target_pairs={{0,0},{8,256},{256,8},{264,264},{1,1},{9,257},{257,9},{265,265},{2... | collective-permute-start | bytes 1179656 | tf_op jit(solution)/shard_map/ppermute | solution.py:199
  78.6 0.2 collective-permute-done.2
  78.8 3.0 %collective-permute-done.3 = bf16[4,192,256]{2,1,0:T(8,128)(2,1)S(1)} collective-permute-done((bf16[4,192,256]{2,1,0:T(8,128)(2,1)S(1)}, bf16[4,192,256]{2,1,0:T(8,128)(2,1)S(1)}, u32[]{:S(2)}, u32[]{:S(2)}) %collective-permute-start.3) | collective-permute-done | bytes 393248 | tf_op jit(solution)/shard_map/ppermute | solution.py:207
  81.9 0.1 maximum_bitcast_fusion
  81.9 0.0 copy-done
  81.9 2.0 %fusion.1.weight_ref = bf16[2,8,192,256]{3,2,1,0:T(8,128)(2,1)} fusion(s32[]{:T(128)S(6)} %select_n.3, bf16[1,8,192,256]{3,2,1,0:T(8,128)(2,1)S(1)} %bitcast.9, bf16[1,8,192,256]{3,2,1,0:T(8,128)(2,1)S(1)} %maximum_bitcast_fusion), kind=kLoop, calls=%fused_computation.4 | loop fusion | flops 1572864 | bytes 3145732 | tf_op jit(solution)/shard_map/stack | solution.py:213
  84.0 0.0 all-gather.4.cloned.1.call-done
  84.0 0.7 collective-permute-done.4.same_ref
  84.7 0.0 copy-start.1
  84.7 0.7 copy-done.1
  85.4 7.1 %shard_map.102 = bf16[3072,256]{1,0:T(8,128)(2,1)} custom-call(s32[1]{0:T(128)} %bitcast.high_ref, bf16[2,4,2,768,384]{4,3,2,1,0:T(8,128)(2,1)} %bitcast.7, bf16[768,256]{1,0:T(8,128)(2,1)} %copy-done.1, bf16[768,256]{1,0:T(8,128)(2,1)} %copy-done), custom_call_target="tpu_custom_call" | custom-call | flops 2415919104 | bytes 11010048 | tf_op jit(solution)/shard_map/pallas_call | solution.py:129
  92.5 0.0 reduce-scatter.2.cloned.1.call-update
  92.5 7.6 %shard_map.103 = (bf16[768,256]{1,0:T(8,128)(2,1)}, bf16[768,256]{1,0:T(8,128)(2,1)}) custom-call(s32[1]{0:T(128)} %bitcast.high_ref, bf16[2,4,2,768,384]{4,3,2,1,0:T(8,128)(2,1)} %bitcast.8, bf16[2,8,192,256]{3,2,1,0:T(8,128)(2,1)} %fusion.1.weight_ref), custom_call_target="tpu_custom_call" | custom-call | flops 2415919104 | bytes 11010048 | tf_op jit(solution)/shard_map/pallas_call | solution.py:171
  100.2 3.6 %collective-permute-start.5 = (bf16[768,256]{1,0:T(8,128)(2,1)}, bf16[768,256]{1,0:T(8,128)(2,1)S(1)}, u32[]{:S(2)}, u32[]{:S(2)}) collective-permute-start(bf16[768,256]{1,0:T(8,128)(2,1)} %get-tuple-element.23), channel_id=1, source_target_pairs={{0,0},{8,256},{256,8},{264,264},{1,1},{9,257},{257,9},{265,265},{2... | collective-permute-start | bytes 1179656 | tf_op jit(solution)/shard_map/ppermute | solution.py:199
  103.8 1.9 %collective-permute-start.6 = (bf16[768,256]{1,0:T(8,128)(2,1)}, bf16[768,256]{1,0:T(8,128)(2,1)S(1)}, u32[]{:S(2)}, u32[]{:S(2)}) collective-permute-start(bf16[768,256]{1,0:T(8,128)(2,1)} %get-tuple-element.24), channel_id=1, source_target_pairs={{0,256},{8,0},{256,264},{264,8},{1,257},{9,1},{257,265},{265,9},{2... | collective-permute-start | bytes 1179656 | tf_op jit(solution)/shard_map/ppermute | solution.py:199
  105.7 4.3 %collective-permute-done.5.one_ref = bf16[768,256]{1,0:T(8,128)(2,1)S(1)} collective-permute-done((bf16[768,256]{1,0:T(8,128)(2,1)}, bf16[768,256]{1,0:T(8,128)(2,1)S(1)}, u32[]{:S(2)}, u32[]{:S(2)}) %collective-permute-start.5) | collective-permute-done | bytes 393248 | tf_op jit(solution)/shard_map/ppermute | solution.py:199
  110.0 0.0 copy-start.2
  110.1 3.6 %collective-permute-done.6.two_ref = bf16[768,256]{1,0:T(8,128)(2,1)S(1)} collective-permute-done((bf16[768,256]{1,0:T(8,128)(2,1)}, bf16[768,256]{1,0:T(8,128)(2,1)S(1)}, u32[]{:S(2)}, u32[]{:S(2)}) %collective-permute-start.6) | collective-permute-done | bytes 393248 | tf_op jit(solution)/shard_map/ppermute | solution.py:199
  113.7 0.0 copy-done.2
  113.7 0.0 copy-start.3
  113.7 0.8 copy-done.3
  114.4 7.4 %shard_map.104 = (bf16[768,256]{1,0:T(8,128)(2,1)}, bf16[768,256]{1,0:T(8,128)(2,1)}, bf16[768,256]{1,0:T(8,128)(2,1)}, f32[2,128]{1,0:T(2,128)}) custom-call(bf16[768,256]{1,0:T(8,128)(2,1)} %q_ref.3, bf16[768,256]{1,0:T(8,128)(2,1)} %k_ref.3, bf16[768,256]{1,0:T(8,128)(2,1)} %v_ref.3, bf16[768,256]{1,0:T(8,128)(2,1)} %copy-done.2, ...), custom_call_target="tpu_custom_call" | custom-call | tf_op jit(solution)/shard_map/pallas_call | solution.py:102
  121.8 0.7 broadcast_in_dim.4
  122.5 12.8 %all_to_all.10 = f32[32,2,128]{2,1,0:T(2,128)S(1)} all-to-all(f32[32,2,128]{2,1,0:T(2,128)S(1)} %broadcast_in_dim.4), channel_id=1, replica_groups=mesh['yl'=2,'za'=4,'zm'=2,'zl'=2,'yh'=2,'x'=4,'c'=2] {'yl','yh','x','c'}, dimensions={0} | all-to-all | bytes 65536 | tf_op jit(solution)/shard_map/all_to_all | solution.py:218
  135.4 22.2 %all_to_all.11 = f32[16,2,128]{2,1,0:T(2,128)S(1)} all-to-all(f32[16,2,128]{2,1,0:T(2,128)S(1)} %broadcast_in_dim.5), channel_id=1, replica_groups=mesh['yl'=2,'za'=4,'zm'=2,'zl'=2,'yh'=2,'x'=4,'c'=2] {'za','zm','zl'}, dimensions={0} | all-to-all | bytes 32768 | tf_op jit(solution)/shard_map/all_to_all | solution.py:218
  157.5 0.6 reduce_sum.19
  158.1 3.8 %reduce-scatter.2.cloned.1.call-done = bf16[192,256]{1,0:T(8,128)(2,1)} async-done(((bf16[3072,256]{1,0:T(8,128)(2,1)}), bf16[192,256]{1,0:T(8,128)(2,1)}) %reduce-scatter.2.cloned.1.call-update) | async-done | bytes 98320 | tf_op jit(solution)/shard_map/reduce_scatter | solution.py:235
  161.9 3.3 %collective-permute-start.7 = (bf16[192,256]{1,0:T(8,128)(2,1)}, bf16[192,256]{1,0:T(8,128)(2,1)S(1)}, u32[]{:S(2)}, u32[]{:S(2)}) collective-permute-start(bf16[192,256]{1,0:T(8,128)(2,1)} %reduce-scatter.2.cloned.1.call-done), channel_id=1, source_target_pairs={{0,0},{8,256},{256,8},{264,264},{1,1},{9,257},{257,9},{265,265},{2... | collective-permute-start | bytes 294920 | tf_op jit(solution)/shard_map/ppermute | solution.py:199
  165.2 3.4 %collective-permute-done.7 = bf16[192,256]{1,0:T(8,128)(2,1)S(1)} collective-permute-done((bf16[192,256]{1,0:T(8,128)(2,1)}, bf16[192,256]{1,0:T(8,128)(2,1)S(1)}, u32[]{:S(2)}, u32[]{:S(2)}) %collective-permute-start.7) | collective-permute-done | bytes 98336 | tf_op jit(solution)/shard_map/ppermute | solution.py:199
  168.6 0.7 convert_element_type.3
  (2 shorter events, 0.1 us)
Async XLA Ops:
  7.2 13.7 %copy-start.5 = (bf16[192,256]{1,0:T(8,128)(2,1)S(1)}, bf16[192,256]{1,0:T(8,128)(2,1)}, u32[]{:S(2)}) copy-start(bf16[192,256]{1,0:T(8,128)(2,1)} %param.10) | copy-start | bytes 294916
  7.2 76.8 %all-gather.4.cloned.1.call-start = ((), (), s32[]{:S(2)}) async-start(), calls=%async_computation.4 | async-start | bytes 10027008 | tf_op jit(solution)/shard_map/all_gather | solution.py:224
  7.9 154.0 %reduce-scatter.2.cloned.1.call-start = ((), (), s32[]{:S(2)}) async-start(), calls=%async_computation.3 | async-start | bytes 1671168 | tf_op jit(solution)/shard_map/reduce_scatter | solution.py:235
  13.0 62.0 %copy-start.4 = (bf16[768,256]{1,0:T(8,128)(2,1)S(1)}, bf16[768,256]{1,0:T(8,128)(2,1)}, u32[]{:S(2)}) copy-start(bf16[768,256]{1,0:T(8,128)(2,1)} %shard_map.101) | copy-start | bytes 1179652
  13.0 16.7 %collective-permute-start.1 = (bf16[768,256]{1,0:T(8,128)(2,1)}, bf16[768,256]{1,0:T(8,128)(2,1)S(1)}, u32[]{:S(2)}, u32[]{:S(2)}) collective-permute-start(bf16[768,256]{1,0:T(8,128)(2,1)} %shard_map.101), channel_id=1, source_target_pairs={{0,8},{8,264},{256,0},{264,256},{1,9},{9,265},{257,1},{265,257},{2... | collective-permute-start | bytes 1179656 | tf_op jit(solution)/shard_map/ppermute | solution.py:199
  20.9 8.8 %collective-permute-start = (bf16[192,256]{1,0:T(8,128)(2,1)S(1)}, bf16[192,256]{1,0:T(8,128)(2,1)S(1)}, u32[]{:S(2)}, u32[]{:S(2)}) collective-permute-start(bf16[192,256]{1,0:T(8,128)(2,1)S(1)} %copy-done.5), channel_id=1, source_target_pairs={{0,0},{8,256},{256,8},{264,264},{1,1},{9,257},{257,9},{265,265},{2... | collective-permute-start | bytes 294920 | tf_op jit(solution)/shard_map/ppermute | solution.py:199
  29.7 52.2 %copy-start = (bf16[768,256]{1,0:T(8,128)(2,1)}, bf16[768,256]{1,0:T(8,128)(2,1)S(1)}, u32[]{:S(2)}) copy-start(bf16[768,256]{1,0:T(8,128)(2,1)S(1)} %collective-permute-done.1.other_ref) | copy-start | bytes 1179652
  67.9 10.9 %collective-permute-start.2 = (bf16[4,192,256]{2,1,0:T(8,128)(2,1)S(1)}, bf16[4,192,256]{2,1,0:T(8,128)(2,1)S(1)}, u32[]{:S(2)}, u32[]{:S(2)}) collective-permute-start(bf16[4,192,256]{2,1,0:T(8,128)(2,1)S(1)} %bitcast.11), channel_id=1, source_target_pairs={{0,16},{16,32},{32,48},{48,64},{64,80},{80,96},{96,112},{112,128},... | collective-permute-start | bytes 1179656 | tf_op jit(solution)/shard_map/ppermute | solution.py:207
  72.2 9.7 %collective-permute-start.3 = (bf16[4,192,256]{2,1,0:T(8,128)(2,1)S(1)}, bf16[4,192,256]{2,1,0:T(8,128)(2,1)S(1)}, u32[]{:S(2)}, u32[]{:S(2)}) collective-permute-start(bf16[4,192,256]{2,1,0:T(8,128)(2,1)S(1)} %bitcast.10), channel_id=1, source_target_pairs={{0,240},{16,0},{32,16},{48,32},{64,48},{80,64},{96,80},{112,96},{1... | collective-permute-start | bytes 1179656 | tf_op jit(solution)/shard_map/ppermute | solution.py:207
  75.0 9.7 %collective-permute-start.4 = (bf16[768,256]{1,0:T(8,128)(2,1)S(1)}, bf16[768,256]{1,0:T(8,128)(2,1)S(1)}, u32[]{:S(2)}, u32[]{:S(2)}) collective-permute-start(bf16[768,256]{1,0:T(8,128)(2,1)S(1)} %copy-done.4), channel_id=1, source_target_pairs={{0,0},{8,256},{256,8},{264,264},{1,1},{9,257},{257,9},{265,265},{2... | collective-permute-start | bytes 1179656 | tf_op jit(solution)/shard_map/ppermute | solution.py:199
  84.7 0.7 copy-start.1
  100.2 9.9 %collective-permute-start.5 = (bf16[768,256]{1,0:T(8,128)(2,1)}, bf16[768,256]{1,0:T(8,128)(2,1)S(1)}, u32[]{:S(2)}, u32[]{:S(2)}) collective-permute-start(bf16[768,256]{1,0:T(8,128)(2,1)} %get-tuple-element.23), channel_id=1, source_target_pairs={{0,0},{8,256},{256,8},{264,264},{1,1},{9,257},{257,9},{265,265},{2... | collective-permute-start | bytes 1179656 | tf_op jit(solution)/shard_map/ppermute | solution.py:199
  103.8 9.9 %collective-permute-start.6 = (bf16[768,256]{1,0:T(8,128)(2,1)}, bf16[768,256]{1,0:T(8,128)(2,1)S(1)}, u32[]{:S(2)}, u32[]{:S(2)}) collective-permute-start(bf16[768,256]{1,0:T(8,128)(2,1)} %get-tuple-element.24), channel_id=1, source_target_pairs={{0,256},{8,0},{256,264},{264,8},{1,257},{9,1},{257,265},{265,9},{2... | collective-permute-start | bytes 1179656 | tf_op jit(solution)/shard_map/ppermute | solution.py:199
  110.0 3.6 %copy-start.2 = (bf16[768,256]{1,0:T(8,128)(2,1)}, bf16[768,256]{1,0:T(8,128)(2,1)S(1)}, u32[]{:S(2)}) copy-start(bf16[768,256]{1,0:T(8,128)(2,1)S(1)} %collective-permute-done.5.one_ref) | copy-start | bytes 1179652
  113.7 0.8 copy-start.3
  161.9 6.7 %collective-permute-start.7 = (bf16[192,256]{1,0:T(8,128)(2,1)}, bf16[192,256]{1,0:T(8,128)(2,1)S(1)}, u32[]{:S(2)}, u32[]{:S(2)}) collective-permute-start(bf16[192,256]{1,0:T(8,128)(2,1)} %reduce-scatter.2.cloned.1.call-done), channel_id=1, source_target_pairs={{0,0},{8,256},{256,8},{264,264},{1,1},{9,257},{257,9},{265,265},{2... | collective-permute-start | bytes 294920 | tf_op jit(solution)/shard_map/ppermute | solution.py:199
Sparse Core Ops, SparseCore 0:
  10.2 69.0 all-gather.3
  92.7 69.1 reduce-scatter.1

commit v16 on v15

--- a/solution.py
+++ b/solution.py
@@ -209,9 +209,9 @@
 
 def gather_rows(own_rows):
     same = lax.all_gather(own_rows, ("za", "zm"), axis=0)
-    other = jnp.concatenate([along(same[:4], 1), along(same[4:], -1)])
-    blocks = jnp.stack([same, other, same])
-    return lax.dynamic_slice_in_dim(blocks, lax.axis_index("zl"), 2, axis=0)
+    came = along(same[:4], 1), along(same[4:], -1)
+    blocks = jnp.stack([same, jnp.concatenate(came), same])
+    return lax.dynamic_slice_in_dim(blocks, lax.axis_index("zl"), 2, axis=0), came
 
 
 def sum_over(array, axis, count):
@@ -228,8 +228,8 @@
     attn_same = turned(attn)
     attn_other = swap_y(attn, lambda low, up: (up, 1 - low))
     own_rows, attn_other = lax.optimization_barrier((turned(out_weight), attn_other))
-    weights = gather_rows(own_rows)
-    grads, weights = lax.optimization_barrier((grads, weights))
+    weights, came = gather_rows(own_rows)
+    grads, _ = lax.optimization_barrier((grads, came))
 
     wgrad = weight_product(high, grads, attn_same, attn_other)
     shard = lax.psum_scatter(wgrad, Z, scatter_dimension=0, tiled=True)

time: 177 us -> 177 us (level)
  the two profiles are of different devices: /device:TPU:8 before, /device:TPU:16 now
where the time goes in v16:
time: 177 us; the launch traced here: 176 us
  blocking collectives  73.6 us (42%)
  waiting for transfers between devices  29.7 us (17%)
  Pallas kernels  27.2 us (15%)
  starting transfers between devices  25.9 us (15%)
  between operations  14.2 us (8%)
  other arithmetic  3.42 us (2%)
  local copies, waits for them, and re-layouts  2.27 us (1%)
    all_gather x1, blocking collectives, gather_rows(): same = lax.all_gather(own_rows, ('za', 'zm'), axis=0)  38.3 us
    all_to_all x2, blocking collectives, sum_over(): lax.all_to_all(jnp.broadcast_to(array[None], (count,) + array.shape), axi...  35.3 us
    ppermute x6, waiting for transfers between devices, swap_y(): return lax.ppermute(array, ('yl', 'yh'), pairs)  22.2 us
    ppermute x6, starting transfers between devices, swap_y(): return lax.ppermute(array, ('yl', 'yh'), pairs)  18.8 us
    pallas_call x1, Pallas kernels, token_product(): pl.pallas_call(token_kernel, grid_spec=pltpu.PrefetchScalarGridSpec(num_s...  7.62 us
    pallas_call x1, Pallas kernels, backward(): pl.pallas_call(backward_kernel, grid=(tokens // PATCH,), in_specs=[block]...  7.37 us
    pallas_call x1, Pallas kernels, weight_product(): pl.pallas_call(weight_kernel, grid_spec=pltpu.PrefetchScalarGridSpec(num_...  7.1 us
    ppermute x2, starting transfers between devices, along(): return lax.ppermute(array, Z, [(z, (z + step) % 16) for z in range(16)])  7.05 us
  transfers between devices with their start and end apart: 10, of which 8 were waited for; matrix products, arithmetic and copies ran while one was open for 2% of the time, Pallas kernels for 11%

profile of v16, /device:TPU:16, one launch (start us, length us, event | category | flops | bytes accessed | tf_op | source)
XLA Modules:
  0.0 176.2 jit_solution(14033934928525961679)
XLA Ops:
  7.2 0.0 copy-start.5
  7.2 0.0 all-gather.4.cloned.1.call-start
  7.2 0.7 all-gather.4.cloned.1.call-update
  7.9 0.0 reduce-scatter.2.cloned.1.call-start
  8.0 5.1 %shard_map.101 = bf16[768,256]{1,0:T(8,128)(2,1)} custom-call(bf16[768,256]{1,0:T(8,128)(2,1)} %q_ref.3, bf16[768,256]{1,0:T(8,128)(2,1)} %k_ref.3, bf16[768,256]{1,0:T(8,128)(2,1)} %v_ref.3, f32[2,128]{1,0:T(2,128)} %gains_ref.3), custom_call_target="tpu_custom_call" | custom-call | tf_op jit(solution)/shard_map/pallas_call | solution.py:56
  13.0 0.0 copy-start.4
  13.0 3.3 %collective-permute-start.1 = (bf16[768,256]{1,0:T(8,128)(2,1)}, bf16[768,256]{1,0:T(8,128)(2,1)S(1)}, u32[]{:S(2)}, u32[]{:S(2)}) collective-permute-start(bf16[768,256]{1,0:T(8,128)(2,1)} %shard_map.101), channel_id=1, source_target_pairs={{0,8},{8,264},{256,0},{264,256},{1,9},{9,265},{257,1},{265,257},{2... | collective-permute-start | bytes 1179656 | tf_op jit(solution)/shard_map/ppermute | solution.py:199
  16.4 0.0 copy-done.5
  16.4 6.9 %collective-permute-start = (bf16[192,256]{1,0:T(8,128)(2,1)S(1)}, bf16[192,256]{1,0:T(8,128)(2,1)S(1)}, u32[]{:S(2)}, u32[]{:S(2)}) collective-permute-start(bf16[192,256]{1,0:T(8,128)(2,1)S(1)} %copy-done.5), channel_id=1, source_target_pairs={{0,0},{8,256},{256,8},{264,264},{1,1},{9,257},{257,9},{265,265},{2... | collective-permute-start | bytes 294920 | tf_op jit(solution)/shard_map/ppermute | solution.py:199
  23.3 6.5 %collective-permute-done = bf16[192,256]{1,0:T(8,128)(2,1)S(1)} collective-permute-done((bf16[192,256]{1,0:T(8,128)(2,1)S(1)}, bf16[192,256]{1,0:T(8,128)(2,1)S(1)}, u32[]{:S(2)}, u32[]{:S(2)}) %collective-permute-start) | collective-permute-done | bytes 98336 | tf_op jit(solution)/shard_map/ppermute | solution.py:199
  29.7 0.0 collective-permute-done.1.other_ref
  29.7 0.0 copy-start
  29.7 38.3 %all-gather.1 = bf16[1536,256]{1,0:T(8,128)(2,1)S(1)} all-gather(bf16[192,256]{1,0:T(8,128)(2,1)S(1)} %collective-permute-done), channel_id=3, replica_groups=mesh['yl'=2,'za'=4,'zm'=2,'zl'=2,'yh'=2,'x'=4,'c'=2] {'za','zm'}, dimensions={0}, use_global_device_ids=true | all-gather | bytes 884736 | tf_op jit(solution)/shard_map/all_gather | solution.py:211
  68.0 0.1 fusion.2
  68.1 3.7 %collective-permute-start.2 = (bf16[4,192,256]{2,1,0:T(8,128)(2,1)S(1)}, bf16[4,192,256]{2,1,0:T(8,128)(2,1)S(1)}, u32[]{:S(2)}, u32[]{:S(2)}) collective-permute-start(bf16[4,192,256]{2,1,0:T(8,128)(2,1)S(1)} %bitcast.11), channel_id=1, source_target_pairs={{0,16},{16,32},{32,48},{48,64},{64,80},{80,96},{96,112},{112,128},... | collective-permute-start | bytes 1179656 | tf_op jit(solution)/shard_map/ppermute | solution.py:207
  71.8 3.3 %collective-permute-start.3 = (bf16[4,192,256]{2,1,0:T(8,128)(2,1)S(1)}, bf16[4,192,256]{2,1,0:T(8,128)(2,1)S(1)}, u32[]{:S(2)}, u32[]{:S(2)}) collective-permute-start(bf16[4,192,256]{2,1,0:T(8,128)(2,1)S(1)} %bitcast.10), channel_id=1, source_target_pairs={{0,240},{16,0},{32,16},{48,32},{64,48},{80,64},{96,80},{112,96},{1... | collective-permute-start | bytes 1179656 | tf_op jit(solution)/shard_map/ppermute | solution.py:207
  75.1 0.0 copy-done.4
  75.2 2.2 %collective-permute-start.4 = (bf16[768,256]{1,0:T(8,128)(2,1)S(1)}, bf16[768,256]{1,0:T(8,128)(2,1)S(1)}, u32[]{:S(2)}, u32[]{:S(2)}) collective-permute-start(bf16[768,256]{1,0:T(8,128)(2,1)S(1)} %copy-done.4), channel_id=1, source_target_pairs={{0,0},{8,256},{256,8},{264,264},{1,1},{9,257},{257,9},{265,265},{2... | collective-permute-start | bytes 1179656 | tf_op jit(solution)/shard_map/ppermute | solution.py:199
  77.4 1.6 collective-permute-done.2
  79.0 2.5 %collective-permute-done.3 = bf16[4,192,256]{2,1,0:T(8,128)(2,1)S(1)} collective-permute-done((bf16[4,192,256]{2,1,0:T(8,128)(2,1)S(1)}, bf16[4,192,256]{2,1,0:T(8,128)(2,1)S(1)}, u32[]{:S(2)}, u32[]{:S(2)}) %collective-permute-start.3) | collective-permute-done | bytes 393248 | tf_op jit(solution)/shard_map/ppermute | solution.py:207
  81.5 0.0 all-gather.4.cloned.1.call-done
  81.5 3.3 %collective-permute-done.4.same_ref = bf16[768,256]{1,0:T(8,128)(2,1)S(1)} collective-permute-done((bf16[768,256]{1,0:T(8,128)(2,1)S(1)}, bf16[768,256]{1,0:T(8,128)(2,1)S(1)}, u32[]{:S(2)}, u32[]{:S(2)}) %collective-permute-start.4) | collective-permute-done | bytes 393248 | tf_op jit(solution)/shard_map/ppermute | solution.py:199
  84.8 0.0 copy-start.1
  84.8 0.0 copy-done
  84.8 0.7 copy-done.1
  85.6 7.1 %shard_map.102 = bf16[3072,256]{1,0:T(8,128)(2,1)} custom-call(s32[1]{0:T(128)} %bitcast.high_ref, bf16[2,4,2,768,384]{4,3,2,1,0:T(8,128)(2,1)} %bitcast.7, bf16[768,256]{1,0:T(8,128)(2,1)} %copy-done.1, bf16[768,256]{1,0:T(8,128)(2,1)} %copy-done), custom_call_target="tpu_custom_call" | custom-call | flops 2415919104 | bytes 11010048 | tf_op jit(solution)/shard_map/pallas_call | solution.py:129
  92.7 0.0 reduce-scatter.2.cloned.1.call-update
  92.7 0.1 maximum_bitcast_fusion
  92.8 2.0 %fusion.1.weight_ref = bf16[2,8,192,256]{3,2,1,0:T(8,128)(2,1)} fusion(s32[]{:T(128)S(6)} %select_n.3, bf16[1,8,192,256]{3,2,1,0:T(8,128)(2,1)S(1)} %bitcast.9, bf16[1,8,192,256]{3,2,1,0:T(8,128)(2,1)S(1)} %maximum_bitcast_fusion), kind=kLoop, calls=%fused_computation.4 | loop fusion | flops 1572864 | bytes 3145732 | tf_op jit(solution)/shard_map/stack | solution.py:213
  94.8 7.6 %shard_map.103 = (bf16[768,256]{1,0:T(8,128)(2,1)}, bf16[768,256]{1,0:T(8,128)(2,1)}) custom-call(s32[1]{0:T(128)} %bitcast.high_ref, bf16[2,4,2,768,384]{4,3,2,1,0:T(8,128)(2,1)} %bitcast.8, bf16[2,8,192,256]{3,2,1,0:T(8,128)(2,1)} %fusion.1.weight_ref), custom_call_target="tpu_custom_call" | custom-call | flops 2415919104 | bytes 11010048 | tf_op jit(solution)/shard_map/pallas_call | solution.py:171
  102.4 2.2 %collective-permute-start.5 = (bf16[768,256]{1,0:T(8,128)(2,1)}, bf16[768,256]{1,0:T(8,128)(2,1)S(1)}, u32[]{:S(2)}, u32[]{:S(2)}) collective-permute-start(bf16[768,256]{1,0:T(8,128)(2,1)} %get-tuple-element.21), channel_id=1, source_target_pairs={{0,0},{8,256},{256,8},{264,264},{1,1},{9,257},{257,9},{265,265},{2... | collective-permute-start | bytes 1179656 | tf_op jit(solution)/shard_map/ppermute | solution.py:199
  104.6 1.9 %collective-permute-start.6 = (bf16[768,256]{1,0:T(8,128)(2,1)}, bf16[768,256]{1,0:T(8,128)(2,1)S(1)}, u32[]{:S(2)}, u32[]{:S(2)}) collective-permute-start(bf16[768,256]{1,0:T(8,128)(2,1)} %get-tuple-element.22), channel_id=1, source_target_pairs={{0,256},{8,0},{256,264},{264,8},{1,257},{9,1},{257,265},{265,9},{2... | collective-permute-start | bytes 1179656 | tf_op jit(solution)/shard_map/ppermute | solution.py:199
  106.6 5.7 %collective-permute-done.5.one_ref = bf16[768,256]{1,0:T(8,128)(2,1)S(1)} collective-permute-done((bf16[768,256]{1,0:T(8,128)(2,1)}, bf16[768,256]{1,0:T(8,128)(2,1)S(1)}, u32[]{:S(2)}, u32[]{:S(2)}) %collective-permute-start.5) | collective-permute-done | bytes 393248 | tf_op jit(solution)/shard_map/ppermute | solution.py:199
  112.3 0.0 copy-start.2
  112.3 2.2 %collective-permute-done.6.two_ref = bf16[768,256]{1,0:T(8,128)(2,1)S(1)} collective-permute-done((bf16[768,256]{1,0:T(8,128)(2,1)}, bf16[768,256]{1,0:T(8,128)(2,1)S(1)}, u32[]{:S(2)}, u32[]{:S(2)}) %collective-permute-start.6) | collective-permute-done | bytes 393248 | tf_op jit(solution)/shard_map/ppermute | solution.py:199
  114.5 0.0 copy-done.2
  114.5 0.0 copy-start.3
  114.5 0.8 copy-done.3
  115.3 7.4 %shard_map.104 = (bf16[768,256]{1,0:T(8,128)(2,1)}, bf16[768,256]{1,0:T(8,128)(2,1)}, bf16[768,256]{1,0:T(8,128)(2,1)}, f32[2,128]{1,0:T(2,128)}) custom-call(bf16[768,256]{1,0:T(8,128)(2,1)} %q_ref.3, bf16[768,256]{1,0:T(8,128)(2,1)} %k_ref.3, bf16[768,256]{1,0:T(8,128)(2,1)} %v_ref.3, bf16[768,256]{1,0:T(8,128)(2,1)} %copy-done.2, ...), custom_call_target="tpu_custom_call" | custom-call | tf_op jit(solution)/shard_map/pallas_call | solution.py:102
  122.7 0.7 broadcast_in_dim.4
  123.3 13.1 %all_to_all.10 = f32[32,2,128]{2,1,0:T(2,128)S(1)} all-to-all(f32[32,2,128]{2,1,0:T(2,128)S(1)} %broadcast_in_dim.4), channel_id=1, replica_groups=mesh['yl'=2,'za'=4,'zm'=2,'zl'=2,'yh'=2,'x'=4,'c'=2] {'yl','yh','x','c'}, dimensions={0} | all-to-all | bytes 65536 | tf_op jit(solution)/shard_map/all_to_all | solution.py:218
  136.5 22.2 %all_to_all.11 = f32[16,2,128]{2,1,0:T(2,128)S(1)} all-to-all(f32[16,2,128]{2,1,0:T(2,128)S(1)} %broadcast_in_dim.5), channel_id=1, replica_groups=mesh['yl'=2,'za'=4,'zm'=2,'zl'=2,'yh'=2,'x'=4,'c'=2] {'za','zm','zl'}, dimensions={0} | all-to-all | bytes 32768 | tf_op jit(solution)/shard_map/all_to_all | solution.py:218
  158.7 0.6 reduce_sum.19
  159.3 2.7 %reduce-scatter.2.cloned.1.call-done = bf16[192,256]{1,0:T(8,128)(2,1)} async-done(((bf16[3072,256]{1,0:T(8,128)(2,1)}), bf16[192,256]{1,0:T(8,128)(2,1)}) %reduce-scatter.2.cloned.1.call-update) | async-done | bytes 98320 | tf_op jit(solution)/shard_map/reduce_scatter | solution.py:235
  162.0 2.2 %collective-permute-start.7 = (bf16[192,256]{1,0:T(8,128)(2,1)}, bf16[192,256]{1,0:T(8,128)(2,1)S(1)}, u32[]{:S(2)}, u32[]{:S(2)}) collective-permute-start(bf16[192,256]{1,0:T(8,128)(2,1)} %reduce-scatter.2.cloned.1.call-done), channel_id=1, source_target_pairs={{0,0},{8,256},{256,8},{264,264},{1,1},{9,257},{257,9},{265,265},{2... | collective-permute-start | bytes 294920 | tf_op jit(solution)/shard_map/ppermute | solution.py:199
  164.2 4.5 %collective-permute-done.7 = bf16[192,256]{1,0:T(8,128)(2,1)S(1)} collective-permute-done((bf16[192,256]{1,0:T(8,128)(2,1)}, bf16[192,256]{1,0:T(8,128)(2,1)S(1)}, u32[]{:S(2)}, u32[]{:S(2)}) %collective-permute-start.7) | collective-permute-done | bytes 98336 | tf_op jit(solution)/shard_map/ppermute | solution.py:199
  168.7 0.7 convert_element_type.3
  (2 shorter events, 0.1 us)
Async XLA Ops:
  7.2 9.2 %copy-start.5 = (bf16[192,256]{1,0:T(8,128)(2,1)S(1)}, bf16[192,256]{1,0:T(8,128)(2,1)}, u32[]{:S(2)}) copy-start(bf16[192,256]{1,0:T(8,128)(2,1)} %param.10) | copy-start | bytes 294916
  7.2 74.3 %all-gather.4.cloned.1.call-start = ((), (), s32[]{:S(2)}) async-start(), calls=%async_computation.4 | async-start | bytes 10027008 | tf_op jit(solution)/shard_map/all_gather | solution.py:224
  7.9 154.1 %reduce-scatter.2.cloned.1.call-start = ((), (), s32[]{:S(2)}) async-start(), calls=%async_computation.3 | async-start | bytes 1671168 | tf_op jit(solution)/shard_map/reduce_scatter | solution.py:235
  13.0 62.1 %copy-start.4 = (bf16[768,256]{1,0:T(8,128)(2,1)S(1)}, bf16[768,256]{1,0:T(8,128)(2,1)}, u32[]{:S(2)}) copy-start(bf16[768,256]{1,0:T(8,128)(2,1)} %shard_map.101) | copy-start | bytes 1179652
  13.0 16.7 %collective-permute-start.1 = (bf16[768,256]{1,0:T(8,128)(2,1)}, bf16[768,256]{1,0:T(8,128)(2,1)S(1)}, u32[]{:S(2)}, u32[]{:S(2)}) collective-permute-start(bf16[768,256]{1,0:T(8,128)(2,1)} %shard_map.101), channel_id=1, source_target_pairs={{0,8},{8,264},{256,0},{264,256},{1,9},{9,265},{257,1},{265,257},{2... | collective-permute-start | bytes 1179656 | tf_op jit(solution)/shard_map/ppermute | solution.py:199
  16.4 13.4 %collective-permute-start = (bf16[192,256]{1,0:T(8,128)(2,1)S(1)}, bf16[192,256]{1,0:T(8,128)(2,1)S(1)}, u32[]{:S(2)}, u32[]{:S(2)}) collective-permute-start(bf16[192,256]{1,0:T(8,128)(2,1)S(1)} %copy-done.5), channel_id=1, source_target_pairs={{0,0},{8,256},{256,8},{264,264},{1,1},{9,257},{257,9},{265,265},{2... | collective-permute-start | bytes 294920 | tf_op jit(solution)/shard_map/ppermute | solution.py:199
  29.7 55.1 %copy-start = (bf16[768,256]{1,0:T(8,128)(2,1)}, bf16[768,256]{1,0:T(8,128)(2,1)S(1)}, u32[]{:S(2)}) copy-start(bf16[768,256]{1,0:T(8,128)(2,1)S(1)} %collective-permute-done.1.other_ref) | copy-start | bytes 1179652
  68.1 10.9 %collective-permute-start.2 = (bf16[4,192,256]{2,1,0:T(8,128)(2,1)S(1)}, bf16[4,192,256]{2,1,0:T(8,128)(2,1)S(1)}, u32[]{:S(2)}, u32[]{:S(2)}) collective-permute-start(bf16[4,192,256]{2,1,0:T(8,128)(2,1)S(1)} %bitcast.11), channel_id=1, source_target_pairs={{0,16},{16,32},{32,48},{48,64},{64,80},{80,96},{96,112},{112,128},... | collective-permute-start | bytes 1179656 | tf_op jit(solution)/shard_map/ppermute | solution.py:207
  71.8 9.7 %collective-permute-start.3 = (bf16[4,192,256]{2,1,0:T(8,128)(2,1)S(1)}, bf16[4,192,256]{2,1,0:T(8,128)(2,1)S(1)}, u32[]{:S(2)}, u32[]{:S(2)}) collective-permute-start(bf16[4,192,256]{2,1,0:T(8,128)(2,1)S(1)} %bitcast.10), channel_id=1, source_target_pairs={{0,240},{16,0},{32,16},{48,32},{64,48},{80,64},{96,80},{112,96},{1... | collective-permute-start | bytes 1179656 | tf_op jit(solution)/shard_map/ppermute | solution.py:207
  75.2 9.7 %collective-permute-start.4 = (bf16[768,256]{1,0:T(8,128)(2,1)S(1)}, bf16[768,256]{1,0:T(8,128)(2,1)S(1)}, u32[]{:S(2)}, u32[]{:S(2)}) collective-permute-start(bf16[768,256]{1,0:T(8,128)(2,1)S(1)} %copy-done.4), channel_id=1, source_target_pairs={{0,0},{8,256},{256,8},{264,264},{1,1},{9,257},{257,9},{265,265},{2... | collective-permute-start | bytes 1179656 | tf_op jit(solution)/shard_map/ppermute | solution.py:199
  84.8 0.7 copy-start.1
  102.4 9.9 %collective-permute-start.5 = (bf16[768,256]{1,0:T(8,128)(2,1)}, bf16[768,256]{1,0:T(8,128)(2,1)S(1)}, u32[]{:S(2)}, u32[]{:S(2)}) collective-permute-start(bf16[768,256]{1,0:T(8,128)(2,1)} %get-tuple-element.21), channel_id=1, source_target_pairs={{0,0},{8,256},{256,8},{264,264},{1,1},{9,257},{257,9},{265,265},{2... | collective-permute-start | bytes 1179656 | tf_op jit(solution)/shard_map/ppermute | solution.py:199
  104.6 9.9 %collective-permute-start.6 = (bf16[768,256]{1,0:T(8,128)(2,1)}, bf16[768,256]{1,0:T(8,128)(2,1)S(1)}, u32[]{:S(2)}, u32[]{:S(2)}) collective-permute-start(bf16[768,256]{1,0:T(8,128)(2,1)} %get-tuple-element.22), channel_id=1, source_target_pairs={{0,256},{8,0},{256,264},{264,8},{1,257},{9,1},{257,265},{265,9},{2... | collective-permute-start | bytes 1179656 | tf_op jit(solution)/shard_map/ppermute | solution.py:199
  112.3 2.2 %copy-start.2 = (bf16[768,256]{1,0:T(8,128)(2,1)}, bf16[768,256]{1,0:T(8,128)(2,1)S(1)}, u32[]{:S(2)}) copy-start(bf16[768,256]{1,0:T(8,128)(2,1)S(1)} %collective-permute-done.5.one_ref) | copy-start | bytes 1179652
  114.5 0.8 copy-start.3
  162.0 6.7 %collective-permute-start.7 = (bf16[192,256]{1,0:T(8,128)(2,1)}, bf16[192,256]{1,0:T(8,128)(2,1)S(1)}, u32[]{:S(2)}, u32[]{:S(2)}) collective-permute-start(bf16[192,256]{1,0:T(8,128)(2,1)} %reduce-scatter.2.cloned.1.call-done), channel_id=1, source_target_pairs={{0,0},{8,256},{256,8},{264,264},{1,1},{9,257},{257,9},{265,265},{2... | collective-permute-start | bytes 294920 | tf_op jit(solution)/shard_map/ppermute | solution.py:199
Sparse Core Ops, SparseCore 0:
  10.2 68.8 all-gather.3
  92.8 69.1 reduce-scatter.1
